TPU v7x, 32 devices: a whole 2x2x4 slice. The times are simulated.
32 devices in a mesh: groups: 2 (over y), expert: 8 (over z, core), sub: 2 (over x).
Axes of the slice: x: 2, y: 2, z: 4, core: 2. Of those that a mesh axis runs over, the one named last changes fastest.
Arguments:
- latent: bfloat16 [4096, 1024], P(('groups', 'expert', 'sub')), parts along dimension 0, may hold values from -6 to 6
- routes: int32 [4096, 4], P(('groups', 'expert', 'sub')), parts along dimension 0, may hold values from 0 to 7, all different within a row; in each aligned block of 128 rows (0 to 127, 128 to 255, ...) at most 96 rows name the same one
- gates: float32 [4096, 4], P(('groups', 'expert', 'sub')), parts along dimension 0, may hold values from 0.1 to 1
- up_weight: bfloat16 [8, 1024, 2688], P('expert', None, 'sub'), may hold values from -0.1875 to 0.1875
- down_weight: bfloat16 [8, 1024, 2688], P('expert', None, 'sub'), may hold values from -0.125 to 0.125
Outputs:
- mixed: bfloat16 [4096, 1024], P(('groups', 'expert', 'sub')), parts along dimension 0
There are 2 independent parts, one for each index of `groups`. A program takes and returns all parts, laid end to end along the dimension named above; an argument that names none is the same for every part. Nothing has to cross between parts.
Inputs may be any that keep to these rules, and one draw needn't show every extreme that they name: `routes`: each token names 4 different experts; among the 128 tokens of one device no expert is named more than 96 times, a bound that some block reaches.
All inputs are finite; a program needn't handle non-finite values.
Results may differ from a plain program's by a relative error of at most 0.0058.
Values may be sent and summed in bfloat16 or wider, within the bound.
No kernel may reach another device: no remote copies, remote signals or barrier semaphores. Data moves between devices by JAX's collectives and lax.ppermute only.
A program may use at most 128 MiB of HBM per device.

v0:
```python
import jax
import jax.numpy as jnp
from jax import lax
from jax.sharding import PartitionSpec as P


def expert_part(row_block, up_part, down_part):
    preact = jnp.dot(row_block, up_part, preferred_element_type=jnp.float32)
    active = jnp.square(jnp.maximum(preact, 0.0)).astype(jnp.bfloat16)
    return lax.dot_general(
        active, down_part, (((1,), (1,)), ((), ())), preferred_element_type=jnp.float32
    )


def local(latent, routes, gates, up_weight, down_weight):
    tokens_here, row_width = latent.shape
    top_count = routes.shape[1]
    experts = lax.axis_size("expert")
    slot_most = min(tokens_here, 3 * tokens_here * top_count // (2 * experts))
    pair_count = tokens_here * top_count
    route_ids = routes.reshape(-1)
    one_hot = (route_ids[:, None] == jnp.arange(experts, dtype=jnp.int32)[None, :]).astype(
        jnp.int32
    )
    before = jnp.cumsum(one_hot, axis=0) - one_hot
    slot_rank = jnp.sum(before * one_hot, axis=1)
    slot_of = route_ids * slot_most + slot_rank
    source = (
        jnp.full((experts * slot_most,), pair_count, jnp.int32)
        .at[slot_of]
        .set(jnp.arange(pair_count, dtype=jnp.int32))
    )
    padded = jnp.concatenate([latent, jnp.zeros((1, row_width), latent.dtype)], axis=0)
    send_rows = padded[source // top_count].reshape(experts, slot_most, row_width)
    arrived = lax.all_to_all(send_rows, "expert", split_axis=0, concat_axis=0, tiled=True)
    flat_rows = arrived.reshape(-1, row_width)
    summed = expert_part(
        flat_rows,
        lax.all_gather(up_weight, "sub", axis=2, tiled=True)[0],
        lax.all_gather(down_weight, "sub", axis=2, tiled=True)[0],
    )
    expert_out = lax.all_to_all(
        summed.astype(jnp.bfloat16).reshape(arrived.shape),
        "expert",
        split_axis=0,
        concat_axis=0,
        tiled=True,
    )
    values = expert_out.reshape(experts * slot_most, row_width)[slot_of].astype(jnp.float32)
    mixed_out = jnp.sum(
        values.reshape(tokens_here, top_count, row_width) * gates[:, :, None], axis=1
    )
    return mixed_out.astype(jnp.bfloat16)


def solution(mesh):
    placed = (
        P(("groups", "expert", "sub"), None),
        P(("groups", "expert", "sub"), None),
        P(("groups", "expert", "sub"), None),
        P("expert", None, "sub"),
        P("expert", None, "sub"),
    )
    return jax.shard_map(
        local,
        mesh=mesh,
        in_specs=placed,
        out_specs=P(("groups", "expert", "sub"), None),
        check_vma=False,
    )
```

profile of v0, /device:TPU:0, one launch (start us, length us, event | category | flops | bytes accessed | tf_op | source)
XLA Modules:
  0.0 220.1 jit_solution(8751266270399759051)
XLA Ops:
  6.5 0.0 copy-start.1
  6.5 0.0 copy-start
  6.5 0.0 all-gather.3.cloned.1.call-start
  6.5 0.7 all-gather.3.cloned.1.call-update
  7.3 0.0 all-gather.5.cloned.1.call-start
  7.3 0.7 all-gather.5.cloned.1.call-update
  8.0 0.0 copy-done.1
  8.0 0.1 copy.8
  8.1 0.1 eq.29
  8.2 0.1 eq.25
  8.4 1.1 reduce-window.6
  9.5 0.2 slice_reduce_fusion
  9.8 0.1 copy.7
  9.9 0.1 mul.29
  10.0 0.0 copy-done
  10.0 0.1 fusion.7
  10.1 2.4 %scatter_custom_fusion = s32[768]{0:T(1024)S(1)} fusion(s32[512]{0:T(512)S(1)} %bitcast.27, s32[512]{0:T(512)S(1)} %iota.11, s32[]{:T(128)} %constant.13.clone.1), kind=kCustom, calls=%fused_computation.27 | custom fusion | bytes 3076 | tf_op jit(solution)/shard_map/scatter | solution.py:31
  12.6 2.8 %gather_fusion = bf16[768,1024]{1,0:T(8,128)(2,1)S(1)} fusion(bf16[129,1024]{1,0:T(8,128)(2,1)S(1)} %concatenate.3, s32[1024]{0:T(1024)S(1)} %pad_clamp_fusion.1), kind=kCustom, calls=%fused_computation | custom fusion | bytes 3148800 | tf_op jit(solution)/shard_map/gather | solution.py:34
  15.5 44.0 %all_to_all.10 = bf16[8,96,1024]{2,1,0:T(8,128)(2,1)S(1)} all-to-all(bf16[8,96,1024]{2,1,0:T(8,128)(2,1)S(1)} %bitcast.25), channel_id=1, replica_groups=mesh['groups'=2,'expert'=8,'sub'=2] {'expert'}, dimensions={0} | all-to-all | bytes 3145728 | tf_op jit(solution)/shard_map/all_to_all | solution.py:35
  59.4 23.7 %all-gather.3.cloned.1.call-done = bf16[1,1024,2688]{1,2,0:T(8,128)(2,1)} async-done(((bf16[1,1024,1344]{1,2,0:T(8,128)(2,1)}), bf16[1,1024,2688]{1,2,0:T(8,128)(2,1)}) %all-gather.3.cloned.1.call-update) | async-done | bytes 5505040 | tf_op jit(solution)/shard_map/all_gather | solution.py:39
  83.1 8.8 %multiply_convert_fusion = bf16[768,2688]{1,0:T(8,128)(2,1)} fusion(bf16[768,1024]{1,0:T(8,128)(2,1)S(1)} %bitcast.26, bf16[1,1024,2688]{1,2,0:T(8,128)(2,1)} %all-gather.3.cloned.1.call-done), kind=kOutput, calls=%fused_computation.3 | convolution fusion | flops 4234051584 | bytes 11206656 | tf_op jit(solution)/shard_map/dot_general | solution.py:8
  91.9 64.3 %all-gather.5.cloned.1.call-done = bf16[1,1024,2688]{1,2,0:T(8,128)(2,1)} async-done(((bf16[1,1024,1344]{1,2,0:T(8,128)(2,1)}), bf16[1,1024,2688]{1,2,0:T(8,128)(2,1)}) %all-gather.5.cloned.1.call-update) | async-done | bytes 5505040 | tf_op jit(solution)/shard_map/all_gather | solution.py:40
  156.2 9.6 %fusion.3 = bf16[768,1024]{1,0:T(8,128)(2,1)} fusion(bf16[768,2688]{1,0:T(8,128)(2,1)} %multiply_convert_fusion, bf16[1,1024,2688]{1,2,0:T(8,128)(2,1)} %all-gather.5.cloned.1.call-done), kind=kOutput, calls=%fused_computation.8 | convolution fusion | flops 4228644864 | bytes 11206656 | tf_op jit(solution)/shard_map/dot_general | solution.py:10
  165.9 0.0 copy-start.2
  165.9 4.7 %all-to-all-start.1 = ((bf16[8,96,1024]{2,1,0:T(8,128)(2,1)}), bf16[8,96,1024]{2,1,0:T(8,128)(2,1)S(1)}, u32[]{:S(2)}, u32[]{:S(2)}) async-start(bf16[8,96,1024]{2,1,0:T(8,128)(2,1)} %bitcast.8), calls=%async_computation.1 | async-start | bytes 3145728 | tf_op jit(solution)/shard_map/all_to_all | solution.py:42
  170.6 0.0 copy-done.2
  170.6 0.1 copy.10
  170.7 37.7 %all-to-all-done.1 = bf16[8,96,1024]{2,1,0:T(8,128)(2,1)S(1)} async-done(((bf16[8,96,1024]{2,1,0:T(8,128)(2,1)}), bf16[8,96,1024]{2,1,0:T(8,128)(2,1)S(1)}, u32[]{:S(2)}, u32[]{:S(2)}) %all-to-all-start.1) | async-done | bytes 1572896 | tf_op jit(solution)/shard_map/all_to_all | solution.py:42
  208.4 2.0 gather_fusion.1
  210.5 0.7 reshape.68
  211.2 2.1 multiply_reduce_fusion
  (10 shorter events, 0.1 us)
Async XLA Ops:
  6.5 1.5 copy-start.1
  6.5 3.5 %copy-start = (bf16[128,1024]{1,0:T(8,128)(2,1)S(1)}, bf16[128,1024]{1,0:T(8,128)(2,1)}, u32[]{:S(2)}) copy-start(bf16[128,1024]{1,0:T(8,128)(2,1)} %param.5) | copy-start | bytes 786436
  6.5 76.6 %all-gather.3.cloned.1.call-start = ((), (), s32[]{:S(2)}) async-start(), calls=%async_computation.2 | async-start | bytes 8257536 | tf_op jit(solution)/shard_map/all_gather | solution.py:39
  7.3 149.0 %all-gather.5.cloned.1.call-start = ((), (), s32[]{:S(2)}) async-start(), calls=%async_computation.3 | async-start | bytes 8257536 | tf_op jit(solution)/shard_map/all_gather | solution.py:40
  165.9 4.7 %copy-start.2 = (f32[128,4]{0,1:T(4,128)S(1)}, f32[128,4]{0,1:T(4,128)}, u32[]{:S(2)}) copy-start(f32[128,4]{0,1:T(4,128)} %param.7) | copy-start | bytes 6148
  165.9 42.6 %all-to-all-start.1 = ((bf16[8,96,1024]{2,1,0:T(8,128)(2,1)}), bf16[8,96,1024]{2,1,0:T(8,128)(2,1)S(1)}, u32[]{:S(2)}, u32[]{:S(2)}) async-start(bf16[8,96,1024]{2,1,0:T(8,128)(2,1)} %bitcast.8), calls=%async_computation.1 | async-start | bytes 3145728 | tf_op jit(solution)/shard_map/all_to_all | solution.py:42
Sparse Core Ops, SparseCore 0:
  8.9 74.2 all-gather.2
  84.7 71.5 all-gather.4
where the time goes:
time: 220 us
  waiting for transfers between devices  127 us (58%)
  blocking collectives  44 us (20%)
  matrix products  18.4 us (8%)
  between operations  13.5 us (6%)
  local copies, waits for them, and re-layouts  8.93 us (4%)
  starting transfers between devices  4.78 us (2%)
  other arithmetic  3.39 us (2%)
    all_gather x1, waiting for transfers between devices, local(): lax.all_gather(down_weight, 'sub', axis=2, tiled=True)[0]  64.3 us
    all_to_all x1, blocking collectives, local(): lax.all_to_all(send_rows, 'expert', split_axis=0, concat_axis=0, tiled=True)  44 us
    all_to_all x1, waiting for transfers between devices, local(): lax.all_to_all(summed.astype(jnp.bfloat16).reshape(arrived.shape), 'exper...  37.7 us
    all_gather x1, waiting for transfers between devices, local(): lax.all_gather(up_weight, 'sub', axis=2, tiled=True)[0]  23.7 us
    dot_general x1, matrix products, expert_part(): lax.dot_general(active, down_part, (((1,), (1,)), ((), ())), preferred_el...  9.62 us
    dot_general x1, matrix products, expert_part(): preact = jnp.dot(row_block, up_part, preferred_element_type=jnp.float32)  8.77 us
    all_to_all x1, starting transfers between devices, local(): lax.all_to_all(summed.astype(jnp.bfloat16).reshape(arrived.shape), 'exper...  4.74 us
  transfers between devices with their start and end apart: 3, of which 3 were waited for; matrix products, arithmetic and copies ran while one was open for 7% of the time, Pallas kernels for 0%

commit v1 on v0

v1 whole, which is shorter than its diff:
```python
import functools
import math

import jax
import jax.numpy as jnp
from jax import lax
from jax.experimental import pallas as pl
from jax.experimental.pallas import tpu as pltpu
from jax.sharding import PartitionSpec as P


def expert_kernel(block, slots, unit, w_ref, x_ref, up_ref, down_ref, out_ref):
    blocks = w_ref.shape[1]
    weight = w_ref[0]
    named = (weight > 0).astype(jnp.bfloat16)
    earlier = lax.broadcasted_iota(jnp.int32, (block, block), 0)
    later = lax.broadcasted_iota(jnp.int32, (block, block), 1)
    before = (earlier < later).astype(jnp.bfloat16)
    rank = jnp.dot(named, before, preferred_element_type=jnp.float32).astype(jnp.int32)
    picks, scales, rows = [], [], []
    for u in range(blocks // unit):
        slot = lax.broadcasted_iota(jnp.int32, (unit * slots, block), 0)
        parts = []
        scale = 0.0
        for j in range(unit):
            b = u * unit + j
            here = (slot == rank[b : b + 1] + j * slots) & (weight[b : b + 1] > 0)
            scale = scale + jnp.sum(jnp.where(here, weight[b : b + 1], 0.0), axis=1, keepdims=True)
            parts.append(here.astype(jnp.bfloat16))
        pick = jnp.concatenate(parts, axis=1) if unit > 1 else parts[0]
        tokens = x_ref[u * unit * block : (u + 1) * unit * block, :]
        rows.append(jnp.dot(pick, tokens, preferred_element_type=jnp.float32).astype(jnp.bfloat16))
        picks.append(pick)
        scales.append(scale)
    picked = jnp.concatenate(rows, axis=0)
    preact = jnp.dot(picked, up_ref[0], preferred_element_type=jnp.float32)
    active = jnp.square(jnp.maximum(preact, 0.0)).astype(jnp.bfloat16)
    summed = lax.dot_general(
        active, down_ref[0], (((1,), (1,)), ((), ())), preferred_element_type=jnp.float32
    )
    size = unit * slots
    for u in range(blocks // unit):
        gated = (summed[u * size : (u + 1) * size] * scales[u]).astype(jnp.bfloat16)
        out_ref[u * unit * block : (u + 1) * unit * block, :] = lax.dot_general(
            picks[u], gated, (((0,), (0,)), ((), ())), preferred_element_type=jnp.float32
        ).astype(jnp.bfloat16)


def run_expert(weight, rows, up_weight, down_weight, block, slots):
    total, width = rows.shape
    hidden = up_weight.shape[2]
    unit = 16 // math.gcd(16, slots)
    blocks = total // block
    each = unit
    while each * 2 <= blocks and blocks % (each * 2) == 0 and each * 2 * slots <= 512:
        each *= 2
    steps = blocks // each
    return pl.pallas_call(
        functools.partial(expert_kernel, block, slots, unit),
        grid=(steps,),
        out_shape=jax.ShapeDtypeStruct((total, width), jnp.bfloat16),
        in_specs=[
            pl.BlockSpec((1, each, block), lambda i: (i, 0, 0)),
            pl.BlockSpec((each * block, width), lambda i: (i, 0)),
            pl.BlockSpec((1, width, hidden), lambda i: (0, 0, 0)),
            pl.BlockSpec((1, width, hidden), lambda i: (0, 0, 0)),
        ],
        out_specs=pl.BlockSpec((each * block, width), lambda i: (i, 0)),
        compiler_params=pltpu.CompilerParams(vmem_limit_bytes=48 * 1024 * 1024),
        cost_estimate=pl.CostEstimate(
            flops=4 * blocks * slots * width * (hidden + block),
            bytes_accessed=4 * total * width + 4 * width * hidden,
            transcendentals=0,
        ),
    )(weight.reshape(steps, each, block), rows, up_weight, down_weight)


def local(latent, routes, gates, up_weight, down_weight):
    block, width = latent.shape
    top = routes.shape[1]
    experts = lax.axis_size("expert")
    slots = min(block, 3 * block * top // (2 * experts))
    rows = lax.all_gather(latent, ("expert", "sub"), axis=0, tiled=True)
    ids = jnp.arange(experts, dtype=jnp.int32)
    weight = jnp.sum(
        jnp.where(routes.T[None] == ids[:, None, None], gates.T[None], 0.0), axis=1
    )
    weights = lax.all_gather(weight, ("expert", "sub"), axis=0, tiled=False)
    mine = lax.dynamic_index_in_dim(weights, lax.axis_index("expert"), 1, keepdims=False)
    partial = run_expert(mine, rows, up_weight, down_weight, block, slots)
    return lax.psum_scatter(partial, ("expert", "sub"), scatter_dimension=0, tiled=True)


def solution(mesh):
    placed = (
        P(("groups", "expert", "sub"), None),
        P(("groups", "expert", "sub"), None),
        P(("groups", "expert", "sub"), None),
        P("expert", None, "sub"),
        P("expert", None, "sub"),
    )
    return jax.shard_map(
        local,
        mesh=mesh,
        in_specs=placed,
        out_specs=P(("groups", "expert", "sub"), None),
        check_vma=False,
    )
```

time: 220 us -> 159 us (0.72)
  waiting for transfers between devices: 127 us -> 85.8 us
  matrix products: 18.4 us -> 0 us
  Pallas kernels: 0 us -> 15.2 us
  blocking collectives: 44 us -> 34.8 us
  starting transfers between devices: 4.78 us -> 0.04 us
  other arithmetic: 3.39 us -> 0.01 us
    all_gather x2 -> x1, waiting for transfers between devices: 88.1 us -> 12.9 us  [local(): rows = lax.all_gather(latent, ('expert', 'sub'), axis=0, tiled=True)]
    reduce_scatter x0 -> x1, waiting for transfers between devices: none -> 72.2 us  [local(): lax.psum_scatter(partial, ('expert', 'sub'), scatter_dimension=0, tiled=T...]
    all_to_all x1 -> x0, blocking collectives: 44 us -> none  [local(): lax.all_to_all(send_rows, 'expert', split_axis=0, concat_axis=0, tiled=True)]
    all_to_all x1 -> x0, waiting for transfers between devices: 37.7 us -> none  [local(): lax.all_to_all(summed.astype(jnp.bfloat16).reshape(arrived.shape), 'exper...]
    all_gather x0 -> x1, blocking collectives: none -> 34.8 us  [local(): weights = lax.all_gather(weight, ('expert', 'sub'), axis=0, tiled=False)]
    dot_general x2 -> x0, matrix products: 18.4 us -> none  [the longest x1 9.62 us: expert_part(): lax.dot_general(active, down_part, (((1,), (1,)), ((), ())), preferred_el...]
    pallas_call x0 -> x1, Pallas kernels: none -> 15.2 us  [run_expert(): pl.pallas_call(functools.partial(expert_kernel, block, slots, unit), grid...]
    unnamed x8, local copies, waits for them, and re-layouts: 0.24 us -> 9.64 us
  transfers between devices with their start and end apart: 3 -> 2, of which waited for: 3 -> 2; matrix products, arithmetic and copies ran while one was open for 7% -> 5% of each run, Pallas kernels for 0% -> 0%
where the time goes in v1:
time: 159 us
  waiting for transfers between devices  85.8 us (54%)
  blocking collectives  34.8 us (22%)
  Pallas kernels  15.2 us (10%)
  between operations  13.4 us (8%)
  local copies, waits for them, and re-layouts  9.65 us (6%)
    reduce_scatter x1, waiting for transfers between devices, local(): lax.psum_scatter(partial, ('expert', 'sub'), scatter_dimension=0, tiled=T...  72.2 us
    all_gather x1, blocking collectives, local(): weights = lax.all_gather(weight, ('expert', 'sub'), axis=0, tiled=False)  34.8 us
    pallas_call x1, Pallas kernels, run_expert(): pl.pallas_call(functools.partial(expert_kernel, block, slots, unit), grid...  15.2 us
    all_gather x1, waiting for transfers between devices, local(): rows = lax.all_gather(latent, ('expert', 'sub'), axis=0, tiled=True)  12.9 us
    unnamed x8, local copies, waits for them, and re-layouts  9.64 us
  transfers between devices with their start and end apart: 2, of which 2 were waited for; matrix products, arithmetic and copies ran while one was open for 5% of the time, Pallas kernels for 0%

profile of v1, /device:TPU:0, one launch (start us, length us, event | category | flops | bytes accessed | tf_op | source)
XLA Modules:
  0.0 159.0 jit_solution(10453054731178176519)
XLA Ops:
  6.5 0.0 all-gather.3.cloned.1.call-start
  6.5 0.7 all-gather.3.cloned.1.call-update
  7.3 0.0 reduce-scatter.2.cloned.1.call-start
  7.3 3.3 %copy.10.up_ref = bf16[1,1024,1344]{2,1,0:T(8,128)(2,1)S(1)} copy(bf16[1,1024,1344]{1,2,0:T(8,128)(2,1)} %param.8) | data formatting | bytes 5505024 | tf_op args[3]
  10.6 0.0 copy-start.1
  10.6 0.0 copy-start.2
  10.6 4.5 %copy.11.down_ref = bf16[1,1024,1344]{2,1,0:T(8,128)(2,1)} copy(bf16[1,1024,1344]{1,2,0:T(8,128)(2,1)} %param.9) | data formatting | bytes 5505024 | tf_op args[4]
  15.1 0.0 copy-done.1
  15.2 0.0 copy-done.2
  15.2 34.8 %all-gather = f32[128,128]{1,0:T(8,128)S(1)} all-gather(f32[8,128]{1,0:T(8,128)S(1)} %select_reduce_fusion), channel_id=2, replica_groups=mesh['groups'=2,'expert'=8,'sub'=2] {'expert','sub'}, dimensions={0}, use_global_device_ids=true | all-gather | bytes 69632 | tf_op jit(solution)/shard_map/all_gather | solution.py:88
  50.0 12.9 %all-gather.3.cloned.1.call-done.x_ref = bf16[2048,1024]{1,0:T(8,128)(2,1)} async-done(((bf16[128,1024]{1,0:T(8,128)(2,1)}), bf16[2048,1024]{1,0:T(8,128)(2,1)}) %all-gather.3.cloned.1.call-update) | async-done | bytes 4194320 | tf_op jit(solution)/shard_map/all_gather | solution.py:83
  62.9 0.0 copy-start
  62.9 1.8 %copy-done = bf16[1,1024,1344]{2,1,0:T(8,128)(2,1)S(1)} copy-done((bf16[1,1024,1344]{2,1,0:T(8,128)(2,1)S(1)}, bf16[1,1024,1344]{2,1,0:T(8,128)(2,1)}, u32[]{:S(2)}) %copy-start) | copy-done | bytes 2752536
  64.7 15.2 %shard_map.55 = bf16[2048,1024]{1,0:T(8,128)(2,1)} custom-call(f32[4,4,128]{2,1,0:T(4,128)S(1)} %bitcast.4, bf16[2048,1024]{1,0:T(8,128)(2,1)} %all-gather.3.cloned.1.call-done.x_ref, bf16[1,1024,1344]{2,1,0:T(8,128)(2,1)S(1)} %copy.10.up_ref, bf16[1,1024,1344]{2,1,0:T(8,128)(2,1)S(1)} %copy-done), custom_call_target="tpu_custom_call" | custom-call | flops 9261023232 | bytes 13893632 | tf_op jit(solution)/shard_map/pallas_call | solution.py:58
  79.9 0.0 reduce-scatter.2.cloned.1.call-update
  79.9 72.2 %reduce-scatter.2.cloned.1.call-done = bf16[128,1024]{1,0:T(8,128)(2,1)} async-done(((bf16[2048,1024]{1,0:T(8,128)(2,1)}), bf16[128,1024]{1,0:T(8,128)(2,1)}) %reduce-scatter.2.cloned.1.call-update) | async-done | bytes 262160 | tf_op jit(solution)/shard_map/reduce_scatter | solution.py:91
  (2 shorter events, 0.0 us)
Async XLA Ops:
  6.5 56.4 %all-gather.3.cloned.1.call-start = ((), (), s32[]{:S(2)}) async-start(), calls=%async_computation.1 | async-start | bytes 4456448 | tf_op jit(solution)/shard_map/all_gather | solution.py:83
  7.3 144.9 %reduce-scatter.2.cloned.1.call-start = ((), (), s32[]{:S(2)}) async-start(), calls=%async_computation.2 | async-start | bytes 4456448 | tf_op jit(solution)/shard_map/reduce_scatter | solution.py:91
  10.6 4.5 %copy-start.1 = (f32[128,4]{0,1:T(4,128)S(1)}, f32[128,4]{0,1:T(4,128)}, u32[]{:S(2)}) copy-start(f32[128,4]{0,1:T(4,128)} %param.7) | copy-start | bytes 6148
  10.6 4.5 %copy-start.2 = (s32[128,4]{0,1:T(4,128)S(1)}, s32[128,4]{0,1:T(4,128)}, u32[]{:S(2)}) copy-start(s32[128,4]{0,1:T(4,128)} %param.6) | copy-start | bytes 6148
  62.9 1.8 %copy-start = (bf16[1,1024,1344]{2,1,0:T(8,128)(2,1)S(1)}, bf16[1,1024,1344]{2,1,0:T(8,128)(2,1)}, u32[]{:S(2)}) copy-start(bf16[1,1024,1344]{2,1,0:T(8,128)(2,1)} %copy.11.down_ref) | copy-start | bytes 8257540
Sparse Core Ops, SparseCore 0:
  9.6 53.2 all-gather.2
  80.1 71.9 reduce-scatter.1

commit v2 on v1

v2 whole, which is shorter than its diff:
```python
import functools
import math

import jax
import jax.numpy as jnp
from jax import lax
from jax.experimental import pallas as pl
from jax.experimental.pallas import tpu as pltpu
from jax.sharding import Mesh, PartitionSpec as P

CORES = 2
NT = (((1,), (1,)), ((), ()))
TN = (((0,), (0,)), ((), ()))


def expert_kernel(block, slots, unit, w_ref, x_ref, *refs):
    out_ref = refs[-1]
    blocks = w_ref.shape[2]
    earlier = lax.broadcasted_iota(jnp.int32, (block, block), 0)
    later = lax.broadcasted_iota(jnp.int32, (block, block), 1)
    before = (earlier < later).astype(jnp.bfloat16)
    size = unit * slots
    slot = lax.broadcasted_iota(jnp.int32, (size, block), 0)
    sums = [0.0] * (blocks // unit)
    for n in range(w_ref.shape[0]):
        up_ref, down_ref = refs[2 * n], refs[2 * n + 1]
        weight = w_ref[n, 0]
        named = (weight > 0).astype(jnp.bfloat16)
        rank = jnp.dot(named, before, preferred_element_type=jnp.float32).astype(jnp.int32)
        picks, scales, rows = [], [], []
        for u in range(blocks // unit):
            parts = []
            scale = 0.0
            for j in range(unit):
                b = u * unit + j
                here = (slot == rank[b : b + 1] + j * slots) & (weight[b : b + 1] > 0)
                scale = scale + jnp.sum(
                    jnp.where(here, weight[b : b + 1], 0.0), axis=1, keepdims=True
                )
                parts.append(here.astype(jnp.bfloat16))
            pick = jnp.concatenate(parts, axis=1) if unit > 1 else parts[0]
            tokens = x_ref[u * unit * block : (u + 1) * unit * block, :]
            rows.append(
                jnp.dot(pick, tokens, preferred_element_type=jnp.float32).astype(jnp.bfloat16)
            )
            picks.append(pick)
            scales.append(scale)
        picked = jnp.concatenate(rows, axis=0)
        preact = lax.dot_general(picked, up_ref[0], NT, preferred_element_type=jnp.float32)
        active = jnp.square(jnp.maximum(preact, 0.0)).astype(jnp.bfloat16)
        summed = jnp.dot(active, down_ref[0], preferred_element_type=jnp.float32)
        for u in range(blocks // unit):
            gated = (summed[u * size : (u + 1) * size] * scales[u]).astype(jnp.bfloat16)
            sums[u] = sums[u] + lax.dot_general(
                picks[u], gated, TN, preferred_element_type=jnp.float32
            )
    for u in range(blocks // unit):
        out_ref[u * unit * block : (u + 1) * unit * block, :] = sums[u].astype(jnp.bfloat16)


def run_experts(weights, rows, tables, block, slots):
    total, width = rows.shape
    number = weights.shape[0]
    hidden = tables[0].shape[1]
    unit = 16 // math.gcd(16, slots)
    blocks = total // block
    each = unit
    while blocks % (each * 2) == 0 and each * 2 * slots <= 512:
        each *= 2
    steps = blocks // each
    return pl.pallas_call(
        functools.partial(expert_kernel, block, slots, unit),
        grid=(steps,),
        out_shape=jax.ShapeDtypeStruct((total, width), jnp.bfloat16),
        in_specs=[
            pl.BlockSpec((number, 1, each, block), lambda i: (0, i, 0, 0)),
            pl.BlockSpec((each * block, width), lambda i: (i, 0)),
        ]
        + [pl.BlockSpec(memory_space=pltpu.VMEM)] * len(tables),
        out_specs=pl.BlockSpec((each * block, width), lambda i: (i, 0)),
        compiler_params=pltpu.CompilerParams(vmem_limit_bytes=56 * 1024 * 1024),
        cost_estimate=pl.CostEstimate(
            flops=4 * number * blocks * slots * width * (hidden + block),
            bytes_accessed=4 * total * width + 2 * len(tables) * width * hidden,
            transcendentals=0,
        ),
    )(weights.reshape(number, steps, each, block), rows, *tables)


def local(latent, routes, gates, up_weight, down_weight):
    block, width = latent.shape
    top = routes.shape[1]
    cores = lax.axis_size("core")
    experts = lax.axis_size("z") * cores
    slots = min(block, 3 * block * top // (2 * experts))
    own_up, own_down = jnp.swapaxes(up_weight, 1, 2), jnp.swapaxes(down_weight, 1, 2)
    rows = lax.all_gather(latent, ("z", "sub"), axis=0, tiled=True)
    tables = [own_up, own_down]
    for step in range(1, cores):
        turn = [(c, (c + step) % cores) for c in range(cores)]
        tables += [lax.ppermute(own_up, "core", turn), lax.ppermute(own_down, "core", turn)]
    ids = jnp.arange(experts, dtype=jnp.int32)
    weight = jnp.sum(
        jnp.where(routes.T[None] == ids[:, None, None], gates.T[None], 0.0), axis=1
    )
    weights = lax.all_gather(weight, ("z", "sub"), axis=1, tiled=False)
    first, core = lax.axis_index("z") * cores, lax.axis_index("core")
    mine = jnp.stack(
        [
            lax.dynamic_index_in_dim(weights, first + (core + cores - s) % cores, 0, keepdims=False)
            for s in range(cores)
        ]
    )
    partial = run_experts(mine, rows, tables, block, slots)
    return lax.psum_scatter(partial, ("z", "sub"), scatter_dimension=0, tiled=True)


def solution(mesh):
    groups, experts, sub = (mesh.shape[a] for a in ("groups", "expert", "sub"))
    inner = Mesh(
        mesh.devices.reshape(groups, experts // CORES, CORES, sub),
        ("groups", "z", "core", "sub"),
    )
    tokens = P(("groups", "z", "core", "sub"), None)
    table = P(("z", "core"), None, "sub")
    return jax.shard_map(
        local,
        mesh=inner,
        in_specs=(tokens, tokens, tokens, table, table),
        out_specs=tokens,
        check_vma=False,
    )
```

time: 159 us -> 154 us (0.969)
  local copies, waits for them, and re-layouts: 9.65 us -> 0.01 us
  Pallas kernels: 15.2 us -> 18.5 us
  blocking collectives: 34.8 us -> 32.4 us
  waiting for transfers between devices: 85.8 us -> 87.6 us
    unnamed x8 -> x2, local copies, waits for them, and re-layouts: 9.64 us -> 0.01 us
    all_gather x1, waiting for transfers between devices: 12.9 us -> 20.1 us  [local(): rows = lax.all_gather(latent, ('z', 'sub'), axis=0, tiled=True)]
    reduce_scatter x1, waiting for transfers between devices: 72.2 us -> 66.8 us  [local(): lax.psum_scatter(partial, ('z', 'sub'), scatter_dimension=0, tiled=True)]
    pallas_call x1, Pallas kernels: 15.2 us -> 18.5 us  [run_experts(): pl.pallas_call(functools.partial(expert_kernel, block, slots, unit), grid...]
    all_gather x1, blocking collectives: 34.8 us -> 32.4 us  [local(): weights = lax.all_gather(weight, ('z', 'sub'), axis=1, tiled=False)]
  transfers between devices with their start and end apart: 2 -> 4, of which waited for: 2 -> 2; matrix products, arithmetic and copies ran while one was open for 5% -> 1% of each run, Pallas kernels for 0% -> 0%
where the time goes in v2:
time: 154 us
  waiting for transfers between devices  87.6 us (57%)
  blocking collectives  32.4 us (21%)
  Pallas kernels  18.5 us (12%)
  between operations  13.4 us (9%)
    reduce_scatter x1, waiting for transfers between devices, local(): lax.psum_scatter(partial, ('z', 'sub'), scatter_dimension=0, tiled=True)  66.8 us
    all_gather x1, blocking collectives, local(): weights = lax.all_gather(weight, ('z', 'sub'), axis=1, tiled=False)  32.4 us
    all_gather x1, waiting for transfers between devices, local(): rows = lax.all_gather(latent, ('z', 'sub'), axis=0, tiled=True)  20.1 us
    pallas_call x1, Pallas kernels, run_experts(): pl.pallas_call(functools.partial(expert_kernel, block, slots, unit), grid...  18.5 us
  transfers between devices with their start and end apart: 4, of which 2 were waited for; matrix products, arithmetic and copies ran while one was open for 1% of the time, Pallas kernels for 0%

profile of v2, /device:TPU:0, one launch (start us, length us, event | category | flops | bytes accessed | tf_op | source)
XLA Modules:
  0.0 153.8 jit_solution(1002194047178279913)
XLA Ops:
  6.5 0.0 all-gather.3.cloned.1.call-start
  6.5 0.7 all-gather.3.cloned.1.call-update
  7.3 0.0 reduce-scatter.2.cloned.1.call-start
  7.3 0.5 collective-permute-start
  7.8 0.1 collective-permute-start.1
  7.9 0.7 select_reduce_fusion
  8.6 32.4 %all-gather = f32[8,1024]{1,0:T(8,128)S(1)} all-gather(f32[8,128]{1,0:T(8,128)S(1)} %select_reduce_fusion), channel_id=2, replica_groups=mesh['groups'=2,'z'=4,'core'=2,'sub'=2] {'z','sub'}, dimensions={1}, use_global_device_ids=true | all-gather | bytes 36864 | tf_op jit(solution)/shard_map/all_gather | solution.py:106
  41.0 0.6 pad_maximum_fusion
  41.6 0.0 collective-permute-done.refs_2_
  41.6 0.0 copy-start
  41.6 0.0 collective-permute-done.1.refs_3_
  41.6 20.1 %all-gather.3.cloned.1.call-done.x_ref = bf16[1024,1024]{1,0:T(8,128)(2,1)} async-done(((bf16[128,1024]{1,0:T(8,128)(2,1)}), bf16[1024,1024]{1,0:T(8,128)(2,1)}) %all-gather.3.cloned.1.call-update) | async-done | bytes 2097168 | tf_op jit(solution)/shard_map/all_gather | solution.py:97
  61.7 0.0 copy-done
  61.7 18.5 %shard_map.55 = bf16[1024,1024]{1,0:T(8,128)(2,1)} custom-call(f32[2,2,4,128]{3,2,1,0:T(4,128)} %bitcast.11, bf16[1024,1024]{1,0:T(8,128)(2,1)} %all-gather.3.cloned.1.call-done.x_ref, bf16[1,1344,1024]{2,1,0:T(8,128)(2,1)} %bitcast.15, bf16[1,1344,1024]{2,1,0:T(8,128)(2,1)} %bitcast.17, bf16[1,1344,1024]{2,1,0:T(8,128)(2,1)} %copy-done, ...), custom_call_target="tpu_custom_call" | custom-call | flops 9261023232 | bytes 15204352 | tf_op jit(solution)/shard_map/pallas_call | solution.py:71
  80.2 0.0 reduce-scatter.2.cloned.1.call-update
  80.2 66.8 %reduce-scatter.2.cloned.1.call-done = bf16[128,1024]{1,0:T(8,128)(2,1)} async-done(((bf16[1024,1024]{1,0:T(8,128)(2,1)}), bf16[128,1024]{1,0:T(8,128)(2,1)}) %reduce-scatter.2.cloned.1.call-update) | async-done | bytes 262160 | tf_op jit(solution)/shard_map/reduce_scatter | solution.py:115
  (1 shorter events, 0.0 us)
Async XLA Ops:
  6.5 55.1 %all-gather.3.cloned.1.call-start = ((), (), s32[]{:S(2)}) async-start(), calls=%async_computation.1 | async-start | bytes 2359296 | tf_op jit(solution)/shard_map/all_gather | solution.py:97
  7.3 139.7 %reduce-scatter.2.cloned.1.call-start = ((), (), s32[]{:S(2)}) async-start(), calls=%async_computation.2 | async-start | bytes 2359296 | tf_op jit(solution)/shard_map/reduce_scatter | solution.py:115
  7.3 34.3 %collective-permute-start = (bf16[1,1344,1024]{2,1,0:T(8,128)(2,1)}, bf16[1,1344,1024]{2,1,0:T(8,128)(2,1)S(1)}, u32[]{:S(2)}, u32[]{:S(2)}) collective-permute-start(bf16[1,1344,1024]{2,1,0:T(8,128)(2,1)} %bitcast.14), channel_id=1, source_target_pairs={{0,2},{2,0},{1,3},{3,1},{4,6},{6,4},{5,7},{7,5},{8,10},{10,8},{9,1... | collective-permute-start | bytes 8257544 | tf_op jit(solution)/shard_map/ppermute | solution.py:101
  7.8 33.8 %collective-permute-start.1 = (bf16[1,1344,1024]{2,1,0:T(8,128)(2,1)}, bf16[1,1344,1024]{2,1,0:T(8,128)(2,1)}, u32[]{:S(2)}, u32[]{:S(2)}) collective-permute-start(bf16[1,1344,1024]{2,1,0:T(8,128)(2,1)} %bitcast.16), channel_id=1, source_target_pairs={{0,2},{2,0},{1,3},{3,1},{4,6},{6,4},{5,7},{7,5},{8,10},{10,8},{9,1... | collective-permute-start | bytes 8257544 | tf_op jit(solution)/shard_map/ppermute | solution.py:101
  41.6 20.1 %copy-start = (bf16[1,1344,1024]{2,1,0:T(8,128)(2,1)}, bf16[1,1344,1024]{2,1,0:T(8,128)(2,1)S(1)}, u32[]{:S(2)}) copy-start(bf16[1,1344,1024]{2,1,0:T(8,128)(2,1)S(1)} %collective-permute-done.refs_2_) | copy-start | bytes 8257540
Sparse Core Ops, SparseCore 0:
  9.5 52.1 all-gather.2
  80.3 66.6 reduce-scatter.1

commit v3 on v2

v3 whole, which is shorter than its diff:
```python
import functools
import math

import jax
import jax.numpy as jnp
from jax import lax
from jax.experimental import pallas as pl
from jax.experimental.pallas import tpu as pltpu
from jax.sharding import Mesh, PartitionSpec as P

CORES = 2
ROUNDS = 2
TERMS = 3
NT = (((1,), (1,)), ((), ()))
TN = (((0,), (0,)), ((), ()))


def pack_kernel(experts, extra, latent_ref, routes_ref, gates_ref, out_ref):
    block, width = latent_ref.shape
    out_ref[:block, :] = latent_ref[...]
    ids = lax.broadcasted_iota(jnp.int32, (extra, block), 0)
    weight = jnp.zeros((extra, block), jnp.float32)
    for k in range(routes_ref.shape[0]):
        weight = weight + jnp.where(routes_ref[k : k + 1, :] == ids, gates_ref[k : k + 1, :], 0.0)
    out_ref[block:, :] = jnp.zeros((extra, width), jnp.bfloat16)
    for t in range(TERMS):
        term = weight.astype(jnp.bfloat16)
        out_ref[block:, t * block : (t + 1) * block] = term
        weight = weight - term.astype(jnp.float32)


def pack(latent, routes, gates, experts):
    block, width = latent.shape
    extra = -(-experts // 16) * 16
    return pl.pallas_call(
        functools.partial(pack_kernel, experts, extra),
        out_shape=jax.ShapeDtypeStruct((block + extra, width), jnp.bfloat16),
        in_specs=[pl.BlockSpec(memory_space=pltpu.VMEM)] * 3,
        out_specs=pl.BlockSpec(memory_space=pltpu.VMEM),
    )(latent, routes.T, gates.T)


def expert_kernel(block, slots, unit, number, blocks, ids_ref, after_ref, *refs):
    x_refs, tables, out_refs = refs[:blocks], refs[blocks : blocks + 2 * number], refs[blocks + 2 * number :]
    extra = x_refs[0].shape[0] - block
    earlier = lax.broadcasted_iota(jnp.int32, (block, block), 0)
    later = lax.broadcasted_iota(jnp.int32, (block, block), 1)
    before = (earlier < later).astype(jnp.bfloat16)
    size = unit * slots
    slot = lax.broadcasted_iota(jnp.int32, (size, block), 0)
    row = lax.broadcasted_iota(jnp.int32, (extra, block), 0)
    gates, ranks = [], []
    for x_ref in x_refs:
        gate = 0.0
        for t in range(TERMS):
            gate = gate + x_ref[block:, t * block : (t + 1) * block].astype(jnp.float32)
        gates.append(gate)
        ranks.append(
            jnp.dot((gate > 0).astype(jnp.bfloat16), before, preferred_element_type=jnp.float32)
        )
    sums = [0.0] * blocks
    for n in range(number):
        up_ref, down_ref = tables[2 * n], tables[2 * n + 1]
        mine = row == ids_ref[n]
        picks, scales, rows = [], [], []
        for u in range(blocks // unit):
            parts = []
            scale = 0.0
            for j in range(unit):
                b = u * unit + j
                weight = jnp.sum(jnp.where(mine, gates[b], 0.0), axis=0, keepdims=True)
                rank = jnp.sum(jnp.where(mine, ranks[b], 0.0), axis=0, keepdims=True)
                here = (slot == rank.astype(jnp.int32) + j * slots) & (weight > 0)
                scale = scale + jnp.sum(jnp.where(here, weight, 0.0), axis=1, keepdims=True)
                parts.append(here.astype(jnp.bfloat16))
            tokens = [x_refs[u * unit + j][:block, :] for j in range(unit)]
            pick = jnp.concatenate(parts, axis=1) if unit > 1 else parts[0]
            token = jnp.concatenate(tokens, axis=0) if unit > 1 else tokens[0]
            rows.append(
                jnp.dot(pick, token, preferred_element_type=jnp.float32).astype(jnp.bfloat16)
            )
            picks.append(parts)
            scales.append(scale)
        picked = jnp.concatenate(rows, axis=0)
        preact = lax.dot_general(picked, up_ref[0], NT, preferred_element_type=jnp.float32)
        active = jnp.square(jnp.maximum(preact, 0.0)).astype(jnp.bfloat16)
        summed = jnp.dot(active, down_ref[0], preferred_element_type=jnp.float32)
        for u in range(blocks // unit):
            gated = (summed[u * size : (u + 1) * size] * scales[u]).astype(jnp.bfloat16)
            for j in range(unit):
                b = u * unit + j
                sums[b] = sums[b] + lax.dot_general(
                    picks[u][j], gated, TN, preferred_element_type=jnp.float32
                )
    for b in range(blocks):
        out_refs[b][...] = sums[b].astype(out_refs[b].dtype)


def run_experts(ids, after, arrived, tables, kinds, block, slots):
    blocks, number = len(arrived), len(tables) // 2
    hidden, width = tables[0].shape[1:]
    unit = 16 // math.gcd(16, slots)
    whole = pl.BlockSpec(memory_space=pltpu.VMEM)
    return pl.pallas_call(
        functools.partial(expert_kernel, block, slots, unit, number, blocks),
        out_shape=[jax.ShapeDtypeStruct((block, width), kind) for kind in kinds],
        in_specs=[pl.BlockSpec(memory_space=pltpu.SMEM), pl.BlockSpec(memory_space=pl.ANY)]
        + [whole] * (blocks + len(tables)),
        out_specs=[whole] * blocks,
        compiler_params=pltpu.CompilerParams(vmem_limit_bytes=34 * 1024 * 1024),
        cost_estimate=pl.CostEstimate(
            flops=4 * number * blocks * slots * width * (hidden + block),
            bytes_accessed=5 * blocks * block * width + 2 * len(tables) * width * hidden,
            transcendentals=0,
        ),
    )(ids, after, *arrived, *tables)


def shift(array, axis, step):
    size = lax.axis_size(axis)
    return lax.ppermute(array, axis, [(i, (i + step) % size) for i in range(size)])


def local(latent, routes, gates, up_weight, down_weight):
    block, width = latent.shape
    top = routes.shape[1]
    cores, depth, subs = (lax.axis_size(a) for a in ("core", "z", "sub"))
    experts = depth * cores
    slots = min(block, 3 * block * top // (2 * experts))
    tables = [jnp.swapaxes(up_weight, 1, 2), jnp.swapaxes(down_weight, 1, 2)]
    for step in range(1, cores):
        tables += [shift(tables[0], "core", step), shift(tables[1], "core", step)]
    core = lax.axis_index("core")
    ids = lax.axis_index("z") * cores + (core + cores - jnp.arange(cores, dtype=jnp.int32)) % cores
    ring = [pack(latent, routes, gates, experts)]
    for r in range(1, depth):
        ring.append(shift(ring[-1], "z", 1))
    arrived = [[held] + [shift(held, "sub", s) for s in range(1, subs)] for held in ring]
    home = 0.0
    kinds = [jnp.float32] + [jnp.bfloat16] * (subs - 1)
    for first in range(0, depth, ROUNDS):
        now = range(first, min(depth, first + ROUNDS))
        after = partial[0] if first else ring[min(depth - 1, ROUNDS)]
        partial = run_experts(
            ids, after, sum([arrived[r] for r in now], []), tables, kinds * len(now), block, slots
        )
        for r in now:
            own, *others = partial[(r - first) * subs : (r - first + 1) * subs]
            for s, other in enumerate(others, 1):
                own = own + shift(other, "sub", -s).astype(jnp.float32)
            if r:
                own = shift(own.astype(jnp.bfloat16), "z", -r).astype(jnp.float32)
            home = home + own
    return home.astype(jnp.bfloat16)


def solution(mesh):
    groups, experts, sub = (mesh.shape[a] for a in ("groups", "expert", "sub"))
    inner = Mesh(
        mesh.devices.reshape(groups, experts // CORES, CORES, sub),
        ("groups", "z", "core", "sub"),
    )
    tokens = P(("groups", "z", "core", "sub"), None)
    table = P(("z", "core"), None, "sub")
    return jax.shard_map(
        local,
        mesh=inner,
        in_specs=(tokens, tokens, tokens, table, table),
        out_specs=tokens,
        check_vma=False,
    )
```

time: 154 us -> 83.2 us (0.54)
  waiting for transfers between devices: 87.6 us -> 42.6 us
  blocking collectives: 32.4 us -> 0 us
  starting transfers between devices: 0.64 us -> 16.3 us
  between operations: 13.4 us -> 0.08 us
  local copies, waits for them, and re-layouts: 0.01 us -> 4.52 us
    reduce_scatter x1 -> x0, waiting for transfers between devices: 66.8 us -> none  [local(): lax.psum_scatter(partial, ('z', 'sub'), scatter_dimension=0, tiled=True)]
    ppermute x2 -> x16, waiting for transfers between devices: 0.01 us -> 42.6 us  [shift(): lax.ppermute(array, axis, [(i, (i + step) % size) for i in range(size)])]
    all_gather x1 -> x0, blocking collectives: 32.4 us -> none  [local(): weights = lax.all_gather(weight, ('z', 'sub'), axis=1, tiled=False)]
    all_gather x1 -> x0, waiting for transfers between devices: 20.1 us -> none  [local(): rows = lax.all_gather(latent, ('z', 'sub'), axis=0, tiled=True)]
    ppermute x2 -> x16, starting transfers between devices: 0.6 us -> 16.3 us  [shift(): lax.ppermute(array, axis, [(i, (i + step) % size) for i in range(size)])]
    unnamed x2 -> x8, local copies, waits for them, and re-layouts: 0.01 us -> 4.52 us
    pallas_call x1 -> x3, Pallas kernels: 18.5 us -> 18.3 us  [the longest x2 16.6 us: run_experts(): pl.pallas_call(functools.partial(expert_kernel, block, slots, unit, numbe...]
  transfers between devices with their start and end apart: 4 -> 16, of which waited for: 2 -> 7; matrix products, arithmetic and copies ran while one was open for 1% -> 0% of each run, Pallas kernels for 0% -> 22%
where the time goes in v3:
time: 83.2 us; the launch traced here: 82.9 us
  waiting for transfers between devices  42.6 us (51%)
  Pallas kernels  18.3 us (22%)
  starting transfers between devices  16.3 us (20%)
  local copies, waits for them, and re-layouts  4.52 us (5%)
  other arithmetic  1.07 us (1%)
    ppermute x16, waiting for transfers between devices, shift(): lax.ppermute(array, axis, [(i, (i + step) % size) for i in range(size)])  42.6 us
    pallas_call x2, Pallas kernels, run_experts(): pl.pallas_call(functools.partial(expert_kernel, block, slots, unit, numbe...  16.6 us
    ppermute x16, starting transfers between devices, shift(): lax.ppermute(array, axis, [(i, (i + step) % size) for i in range(size)])  16.3 us
    unnamed x8, local copies, waits for them, and re-layouts  4.52 us
    pallas_call x1, Pallas kernels, pack(): pl.pallas_call(functools.partial(pack_kernel, experts, extra), out_shape=...  1.73 us
  transfers between devices with their start and end apart: 16, of which 7 were waited for; matrix products, arithmetic and copies ran while one was open for 0% of the time, Pallas kernels for 22%

profile of v3, /device:TPU:0, one launch (start us, length us, event | category | flops | bytes accessed | tf_op | source)
XLA Modules:
  0.0 82.9 jit_solution(7917190257730549991)
XLA Ops:
  0.0 0.5 collective-permute-start.4
  0.5 0.1 collective-permute-start.5
  0.5 1.7 %shard_map.55.refs_0_ = bf16[144,1024]{1,0:T(8,128)(2,1)} custom-call(bf16[128,1024]{1,0:T(8,128)(2,1)} %latent_ref.1, s32[4,128]{1,0:T(4,128)} %bitcast.10, f32[4,128]{1,0:T(4,128)} %bitcast.11), custom_call_target="tpu_custom_call" | custom-call | tf_op jit(solution)/shard_map/pallas_call | solution.py:35
  2.2 3.0 %collective-permute-start = (bf16[144,1024]{1,0:T(8,128)(2,1)}, bf16[144,1024]{1,0:T(8,128)(2,1)}, u32[]{:S(2)}, u32[]{:S(2)}) collective-permute-start(bf16[144,1024]{1,0:T(8,128)(2,1)} %shard_map.55.refs_0_), channel_id=1, source_target_pairs={{0,4},{4,8},{8,12},{12,0},{1,5},{5,9},{9,13},{13,1},{2,6},{6,10},{... | collective-permute-start | bytes 884744 | tf_op jit(solution)/shard_map/ppermute | solution.py:121
  5.3 9.5 %collective-permute-done.refs_2_ = bf16[144,1024]{1,0:T(8,128)(2,1)} collective-permute-done((bf16[144,1024]{1,0:T(8,128)(2,1)}, bf16[144,1024]{1,0:T(8,128)(2,1)}, u32[]{:S(2)}, u32[]{:S(2)}) %collective-permute-start) | collective-permute-done | bytes 294944 | tf_op jit(solution)/shard_map/ppermute | solution.py:121
  14.8 0.0 collective-permute-start.1
  14.8 1.5 %collective-permute-start.2 = (bf16[144,1024]{1,0:T(8,128)(2,1)}, bf16[144,1024]{1,0:T(8,128)(2,1)}, u32[]{:S(2)}, u32[]{:S(2)}) collective-permute-start(bf16[144,1024]{1,0:T(8,128)(2,1)} %shard_map.55.refs_0_), channel_id=1, source_target_pairs={{0,1},{1,0},{2,3},{3,2},{4,5},{5,4},{6,7},{7,6},{8,9},{9,8},{10,11... | collective-permute-start | bytes 884744 | tf_op jit(solution)/shard_map/ppermute | solution.py:121
  16.3 8.9 %collective-permute-done.1.after_ref.refs_0_ = bf16[144,1024]{1,0:T(8,128)(2,1)S(1)} collective-permute-done((bf16[144,1024]{1,0:T(8,128)(2,1)}, bf16[144,1024]{1,0:T(8,128)(2,1)S(1)}, u32[]{:S(2)}, u32[]{:S(2)}) %collective-permute-start.1) | collective-permute-done | bytes 294944 | tf_op jit(solution)/shard_map/ppermute | solution.py:121
  25.2 0.0 collective-permute-start.10
  25.2 1.2 %collective-permute-start.3 = (bf16[144,1024]{1,0:T(8,128)(2,1)}, bf16[144,1024]{1,0:T(8,128)(2,1)}, u32[]{:S(2)}, u32[]{:S(2)}) collective-permute-start(bf16[144,1024]{1,0:T(8,128)(2,1)} %collective-permute-done.refs_2_), channel_id=1, source_target_pairs={{0,1},{1,0},{2,3},{3,2},{4,5},{5,4},{6,7},{7,6},{8,9},{9,8},{10,11... | collective-permute-start | bytes 884744 | tf_op jit(solution)/shard_map/ppermute | solution.py:121
  26.4 0.0 collective-permute-done.2.refs_1_
  26.4 0.8 %collective-permute-start.9 = (bf16[144,1024]{1,0:T(8,128)(2,1)S(1)}, bf16[144,1024]{1,0:T(8,128)(2,1)S(1)}, u32[]{:S(2)}, u32[]{:S(2)}) collective-permute-start(bf16[144,1024]{1,0:T(8,128)(2,1)S(1)} %collective-permute-done.1.after_ref.refs_0_), channel_id=1, source_target_pairs={{0,1},{1,0},{2,3},{3,2},{4,5},{5,4},{6,7},{7,6},{8,9},{9,8},{10,11... | collective-permute-start | bytes 884744 | tf_op jit(solution)/shard_map/ppermute | solution.py:121
  27.3 7.1 %collective-permute-done.10.refs_2_ = bf16[144,1024]{1,0:T(8,128)(2,1)S(1)} collective-permute-done((bf16[144,1024]{1,0:T(8,128)(2,1)S(1)}, bf16[144,1024]{1,0:T(8,128)(2,1)S(1)}, u32[]{:S(2)}, u32[]{:S(2)}) %collective-permute-start.10) | collective-permute-done | bytes 294944 | tf_op jit(solution)/shard_map/ppermute | solution.py:121
  34.4 1.0 %collective-permute-start.11 = (bf16[144,1024]{1,0:T(8,128)(2,1)S(1)}, bf16[144,1024]{1,0:T(8,128)(2,1)S(1)}, u32[]{:S(2)}, u32[]{:S(2)}) collective-permute-start(bf16[144,1024]{1,0:T(8,128)(2,1)S(1)} %collective-permute-done.10.refs_2_), channel_id=1, source_target_pairs={{0,1},{1,0},{2,3},{3,2},{4,5},{5,4},{6,7},{7,6},{8,9},{9,8},{10,11... | collective-permute-start | bytes 884744 | tf_op jit(solution)/shard_map/ppermute | solution.py:121
  35.4 0.0 collective-permute-done.3.refs_3_
  35.4 0.0 collective-permute-done.4.refs_6_
  35.4 0.0 collective-permute-done.5.refs_7_
  35.4 0.0 copy-start
  35.5 1.0 %copy-done = bf16[144,1024]{1,0:T(8,128)(2,1)S(1)} copy-done((bf16[144,1024]{1,0:T(8,128)(2,1)S(1)}, bf16[144,1024]{1,0:T(8,128)(2,1)}, u32[]{:S(2)}) %copy-start) | copy-done | bytes 294936
  36.4 0.0 copy-start.1
  36.4 1.8 %copy-done.1 = bf16[1,1024,1344]{1,2,0:T(8,128)(2,1)S(1)} copy-done((bf16[1,1024,1344]{1,2,0:T(8,128)(2,1)S(1)}, bf16[1,1024,1344]{1,2,0:T(8,128)(2,1)}, u32[]{:S(2)}) %copy-start.1) | copy-done | bytes 2752536
  38.2 0.0 copy-start.3
  38.2 1.8 %copy-done.3 = bf16[1,1024,1344]{1,2,0:T(8,128)(2,1)S(1)} copy-done((bf16[1,1024,1344]{1,2,0:T(8,128)(2,1)S(1)}, bf16[1,1024,1344]{1,2,0:T(8,128)(2,1)}, u32[]{:S(2)}) %copy-start.3) | copy-done | bytes 2752536
  40.0 0.0 copy-start.2
  40.0 8.5 %shard_map.56 = (f32[128,1024]{1,0:T(8,128)S(1)}, bf16[128,1024]{1,0:T(8,128)(2,1)S(1)}, f32[128,1024]{1,0:T(8,128)S(1)}, bf16[128,1024]{1,0:T(8,128)(2,1)S(1)}) custom-call(s32[2]{0:T(128)S(1)} %fusion.ids_ref, bf16[144,1024]{1,0:T(8,128)(2,1)S(1)} %collective-permute-done.1.after_ref.refs_0_, bf16[144,1024]{1,0:T(8,128)(2,1)S(1)} %copy-done, ...), custom_call_target="tpu_custom_call" | custom-call | flops 4630511616 | bytes 13631488 | tf_op jit(solution)/shard_map/pallas_call | solution.py:104
  48.5 1.3 %collective-permute-start.7 = (bf16[128,1024]{1,0:T(8,128)(2,1)S(1)}, bf16[128,1024]{1,0:T(8,128)(2,1)S(1)}, u32[]{:S(2)}, u32[]{:S(2)}) collective-permute-start(bf16[128,1024]{1,0:T(8,128)(2,1)S(1)} %get-tuple-element.16), channel_id=1, source_target_pairs={{0,1},{1,0},{2,3},{3,2},{4,5},{5,4},{6,7},{7,6},{8,9},{9,8},{10,11... | collective-permute-start | bytes 786440 | tf_op jit(solution)/shard_map/ppermute | solution.py:121
  49.8 0.0 collective-permute-done.9.refs_1_
  49.8 0.0 collective-permute-done.11.refs_3_
  49.8 0.0 copy-done.2
  49.8 8.1 %shard_map.57 = (f32[128,1024]{1,0:T(8,128)S(1)}, bf16[128,1024]{1,0:T(8,128)(2,1)S(1)}, f32[128,1024]{1,0:T(8,128)S(1)}, bf16[128,1024]{1,0:T(8,128)(2,1)S(1)}) custom-call(s32[2]{0:T(128)S(1)} %fusion.ids_ref, f32[128,1024]{1,0:T(8,128)S(1)} %get-tuple-element.13.after_ref, bf16[144,1024]{1,0:T(8,128)(2,1)S(1)} %collective-permute-done.1.after_ref.refs_0_, ...), custom_call_target="tpu_custom_call" | custom-call | flops 4630511616 | bytes 13631488 | tf_op jit(solution)/shard_map/pallas_call | solution.py:104
  57.9 0.8 %collective-permute-start.12 = (bf16[128,1024]{1,0:T(8,128)(2,1)S(1)}, bf16[128,1024]{1,0:T(8,128)(2,1)S(1)}, u32[]{:S(2)}, u32[]{:S(2)}) collective-permute-start(bf16[128,1024]{1,0:T(8,128)(2,1)S(1)} %get-tuple-element.18), channel_id=1, source_target_pairs={{0,1},{1,0},{2,3},{3,2},{4,5},{5,4},{6,7},{7,6},{8,9},{9,8},{10,11... | collective-permute-start | bytes 786440 | tf_op jit(solution)/shard_map/ppermute | solution.py:121
  58.7 1.3 %collective-permute-start.14 = (bf16[128,1024]{1,0:T(8,128)(2,1)S(1)}, bf16[128,1024]{1,0:T(8,128)(2,1)S(1)}, u32[]{:S(2)}, u32[]{:S(2)}) collective-permute-start(bf16[128,1024]{1,0:T(8,128)(2,1)S(1)} %get-tuple-element.20), channel_id=1, source_target_pairs={{0,1},{1,0},{2,3},{3,2},{4,5},{5,4},{6,7},{7,6},{8,9},{9,8},{10,11... | collective-permute-start | bytes 786440 | tf_op jit(solution)/shard_map/ppermute | solution.py:121
  60.0 0.8 collective-permute-start.6
  60.8 0.0 collective-permute-done.7
  60.8 0.1 add_convert_fusion.3
  60.8 3.9 %collective-permute-start.8 = (bf16[128,1024]{1,0:T(8,128)(2,1)S(1)}, bf16[128,1024]{1,0:T(8,128)(2,1)S(1)}, u32[]{:S(2)}, u32[]{:S(2)}) collective-permute-start(bf16[128,1024]{1,0:T(8,128)(2,1)S(1)} %add_convert_fusion.3), channel_id=1, source_target_pairs={{0,12},{4,0},{8,4},{12,8},{1,13},{5,1},{9,5},{13,9},{2,14},{6,2},{... | collective-permute-start | bytes 786440 | tf_op jit(solution)/shard_map/ppermute | solution.py:121
  64.7 2.5 %collective-permute-done.12 = bf16[128,1024]{1,0:T(8,128)(2,1)S(1)} collective-permute-done((bf16[128,1024]{1,0:T(8,128)(2,1)S(1)}, bf16[128,1024]{1,0:T(8,128)(2,1)S(1)}, u32[]{:S(2)}, u32[]{:S(2)}) %collective-permute-start.12) | collective-permute-done | bytes 262176 | tf_op jit(solution)/shard_map/ppermute | solution.py:121
  67.2 0.1 add_convert_fusion.2
  67.3 0.1 collective-permute-start.13
  67.4 4.1 %collective-permute-done.14 = bf16[128,1024]{1,0:T(8,128)(2,1)S(1)} collective-permute-done((bf16[128,1024]{1,0:T(8,128)(2,1)S(1)}, bf16[128,1024]{1,0:T(8,128)(2,1)S(1)}, u32[]{:S(2)}, u32[]{:S(2)}) %collective-permute-start.14) | collective-permute-done | bytes 262176 | tf_op jit(solution)/shard_map/ppermute | solution.py:121
  71.4 0.1 add_convert_fusion.1
  71.5 0.1 collective-permute-start.15
  71.6 2.7 %collective-permute-done.6 = bf16[128,1024]{1,0:T(8,128)(2,1)S(1)} collective-permute-done((bf16[128,1024]{1,0:T(8,128)(2,1)S(1)}, bf16[128,1024]{1,0:T(8,128)(2,1)S(1)}, u32[]{:S(2)}, u32[]{:S(2)}) %collective-permute-start.6) | collective-permute-done | bytes 262176 | tf_op jit(solution)/shard_map/ppermute | solution.py:121
  74.2 0.0 collective-permute-done.8
  74.2 7.8 %collective-permute-done.13 = bf16[128,1024]{1,0:T(8,128)(2,1)S(1)} collective-permute-done((bf16[128,1024]{1,0:T(8,128)(2,1)S(1)}, bf16[128,1024]{1,0:T(8,128)(2,1)S(1)}, u32[]{:S(2)}, u32[]{:S(2)}) %collective-permute-start.13) | collective-permute-done | bytes 262176 | tf_op jit(solution)/shard_map/ppermute | solution.py:121
  82.0 0.0 collective-permute-done.15
  82.0 0.9 %add_convert_fusion = bf16[128,1024]{1,0:T(8,128)(2,1)} fusion(bf16[128,1024]{1,0:T(8,128)(2,1)S(1)} %collective-permute-done.15, bf16[128,1024]{1,0:T(8,128)(2,1)S(1)} %collective-permute-done.13, bf16[128,1024]{1,0:T(8,128)(2,1)S(1)} %collective-permute-done.8, f32[128,1024]{1,0:T(8,128)S(1)} %get-tuple-element.13.after_ref, ...), kind=kLoop, calls=%fused_computation | loop fusion | flops 1179648 | bytes 1835008 | tf_op jit(solution)/shard_map/convert_element_type | solution.py:154
  (1 shorter events, 0.0 us)
Async XLA Ops:
  0.0 35.4 %collective-permute-start.4 = (bf16[1,1344,1024]{2,1,0:T(8,128)(2,1)}, bf16[1,1344,1024]{2,1,0:T(8,128)(2,1)S(1)}, u32[]{:S(2)}, u32[]{:S(2)}) collective-permute-start(bf16[1,1344,1024]{2,1,0:T(8,128)(2,1)} %bitcast.4), channel_id=1, source_target_pairs={{0,2},{2,0},{1,3},{3,1},{4,6},{6,4},{5,7},{7,5},{8,10},{10,8},{9,1... | collective-permute-start | bytes 8257544 | tf_op jit(solution)/shard_map/ppermute | solution.py:121
  0.5 35.0 %collective-permute-start.5 = (bf16[1,1344,1024]{2,1,0:T(8,128)(2,1)}, bf16[1,1344,1024]{2,1,0:T(8,128)(2,1)}, u32[]{:S(2)}, u32[]{:S(2)}) collective-permute-start(bf16[1,1344,1024]{2,1,0:T(8,128)(2,1)} %bitcast.7), channel_id=1, source_target_pairs={{0,2},{2,0},{1,3},{3,1},{4,6},{6,4},{5,7},{7,5},{8,10},{10,8},{9,1... | collective-permute-start | bytes 8257544 | tf_op jit(solution)/shard_map/ppermute | solution.py:121
  2.2 12.5 %collective-permute-start = (bf16[144,1024]{1,0:T(8,128)(2,1)}, bf16[144,1024]{1,0:T(8,128)(2,1)}, u32[]{:S(2)}, u32[]{:S(2)}) collective-permute-start(bf16[144,1024]{1,0:T(8,128)(2,1)} %shard_map.55.refs_0_), channel_id=1, source_target_pairs={{0,4},{4,8},{8,12},{12,0},{1,5},{5,9},{9,13},{13,1},{2,6},{6,10},{... | collective-permute-start | bytes 884744 | tf_op jit(solution)/shard_map/ppermute | solution.py:121
  14.8 10.4 %collective-permute-start.1 = (bf16[144,1024]{1,0:T(8,128)(2,1)}, bf16[144,1024]{1,0:T(8,128)(2,1)S(1)}, u32[]{:S(2)}, u32[]{:S(2)}) collective-permute-start(bf16[144,1024]{1,0:T(8,128)(2,1)} %collective-permute-done.refs_2_), channel_id=1, source_target_pairs={{0,4},{4,8},{8,12},{12,0},{1,5},{5,9},{9,13},{13,1},{2,6},{6,10},{... | collective-permute-start | bytes 884744 | tf_op jit(solution)/shard_map/ppermute | solution.py:121
  14.8 11.6 %collective-permute-start.2 = (bf16[144,1024]{1,0:T(8,128)(2,1)}, bf16[144,1024]{1,0:T(8,128)(2,1)}, u32[]{:S(2)}, u32[]{:S(2)}) collective-permute-start(bf16[144,1024]{1,0:T(8,128)(2,1)} %shard_map.55.refs_0_), channel_id=1, source_target_pairs={{0,1},{1,0},{2,3},{3,2},{4,5},{5,4},{6,7},{7,6},{8,9},{9,8},{10,11... | collective-permute-start | bytes 884744 | tf_op jit(solution)/shard_map/ppermute | solution.py:121
  25.2 9.3 %collective-permute-start.10 = (bf16[144,1024]{1,0:T(8,128)(2,1)S(1)}, bf16[144,1024]{1,0:T(8,128)(2,1)S(1)}, u32[]{:S(2)}, u32[]{:S(2)}) collective-permute-start(bf16[144,1024]{1,0:T(8,128)(2,1)S(1)} %collective-permute-done.1.after_ref.refs_0_), channel_id=1, source_target_pairs={{0,4},{4,8},{8,12},{12,0},{1,5},{5,9},{9,13},{13,1},{2,6},{6,10},{... | collective-permute-start | bytes 884744 | tf_op jit(solution)/shard_map/ppermute | solution.py:121
  25.2 10.3 %collective-permute-start.3 = (bf16[144,1024]{1,0:T(8,128)(2,1)}, bf16[144,1024]{1,0:T(8,128)(2,1)}, u32[]{:S(2)}, u32[]{:S(2)}) collective-permute-start(bf16[144,1024]{1,0:T(8,128)(2,1)} %collective-permute-done.refs_2_), channel_id=1, source_target_pairs={{0,1},{1,0},{2,3},{3,2},{4,5},{5,4},{6,7},{7,6},{8,9},{9,8},{10,11... | collective-permute-start | bytes 884744 | tf_op jit(solution)/shard_map/ppermute | solution.py:121
  26.4 23.3 %collective-permute-start.9 = (bf16[144,1024]{1,0:T(8,128)(2,1)S(1)}, bf16[144,1024]{1,0:T(8,128)(2,1)S(1)}, u32[]{:S(2)}, u32[]{:S(2)}) collective-permute-start(bf16[144,1024]{1,0:T(8,128)(2,1)S(1)} %collective-permute-done.1.after_ref.refs_0_), channel_id=1, source_target_pairs={{0,1},{1,0},{2,3},{3,2},{4,5},{5,4},{6,7},{7,6},{8,9},{9,8},{10,11... | collective-permute-start | bytes 884744 | tf_op jit(solution)/shard_map/ppermute | solution.py:121
  34.4 15.4 %collective-permute-start.11 = (bf16[144,1024]{1,0:T(8,128)(2,1)S(1)}, bf16[144,1024]{1,0:T(8,128)(2,1)S(1)}, u32[]{:S(2)}, u32[]{:S(2)}) collective-permute-start(bf16[144,1024]{1,0:T(8,128)(2,1)S(1)} %collective-permute-done.10.refs_2_), channel_id=1, source_target_pairs={{0,1},{1,0},{2,3},{3,2},{4,5},{5,4},{6,7},{7,6},{8,9},{9,8},{10,11... | collective-permute-start | bytes 884744 | tf_op jit(solution)/shard_map/ppermute | solution.py:121
  35.4 1.0 %copy-start = (bf16[144,1024]{1,0:T(8,128)(2,1)S(1)}, bf16[144,1024]{1,0:T(8,128)(2,1)}, u32[]{:S(2)}) copy-start(bf16[144,1024]{1,0:T(8,128)(2,1)} %shard_map.55.refs_0_) | copy-start | bytes 884740
  36.4 1.8 %copy-start.1 = (bf16[1,1024,1344]{1,2,0:T(8,128)(2,1)S(1)}, bf16[1,1024,1344]{1,2,0:T(8,128)(2,1)}, u32[]{:S(2)}) copy-start(bf16[1,1024,1344]{1,2,0:T(8,128)(2,1)} %param.8) | copy-start | bytes 8257540
  38.2 1.8 %copy-start.3 = (bf16[1,1024,1344]{1,2,0:T(8,128)(2,1)S(1)}, bf16[1,1024,1344]{1,2,0:T(8,128)(2,1)}, u32[]{:S(2)}) copy-start(bf16[1,1024,1344]{1,2,0:T(8,128)(2,1)} %param.9) | copy-start | bytes 8257540
  40.0 9.8 %copy-start.2 = (bf16[1,1024,1344]{1,2,0:T(8,128)(2,1)S(1)}, bf16[1,1024,1344]{1,2,0:T(8,128)(2,1)}, u32[]{:S(2)}) copy-start(bf16[1,1024,1344]{1,2,0:T(8,128)(2,1)} %param.8) | copy-start | bytes 8257540
  48.5 12.3 %collective-permute-start.7 = (bf16[128,1024]{1,0:T(8,128)(2,1)S(1)}, bf16[128,1024]{1,0:T(8,128)(2,1)S(1)}, u32[]{:S(2)}, u32[]{:S(2)}) collective-permute-start(bf16[128,1024]{1,0:T(8,128)(2,1)S(1)} %get-tuple-element.16), channel_id=1, source_target_pairs={{0,1},{1,0},{2,3},{3,2},{4,5},{5,4},{6,7},{7,6},{8,9},{9,8},{10,11... | collective-permute-start | bytes 786440 | tf_op jit(solution)/shard_map/ppermute | solution.py:121
  57.9 9.3 %collective-permute-start.12 = (bf16[128,1024]{1,0:T(8,128)(2,1)S(1)}, bf16[128,1024]{1,0:T(8,128)(2,1)S(1)}, u32[]{:S(2)}, u32[]{:S(2)}) collective-permute-start(bf16[128,1024]{1,0:T(8,128)(2,1)S(1)} %get-tuple-element.18), channel_id=1, source_target_pairs={{0,1},{1,0},{2,3},{3,2},{4,5},{5,4},{6,7},{7,6},{8,9},{9,8},{10,11... | collective-permute-start | bytes 786440 | tf_op jit(solution)/shard_map/ppermute | solution.py:121
  58.7 12.7 %collective-permute-start.14 = (bf16[128,1024]{1,0:T(8,128)(2,1)S(1)}, bf16[128,1024]{1,0:T(8,128)(2,1)S(1)}, u32[]{:S(2)}, u32[]{:S(2)}) collective-permute-start(bf16[128,1024]{1,0:T(8,128)(2,1)S(1)} %get-tuple-element.20), channel_id=1, source_target_pairs={{0,1},{1,0},{2,3},{3,2},{4,5},{5,4},{6,7},{7,6},{8,9},{9,8},{10,11... | collective-permute-start | bytes 786440 | tf_op jit(solution)/shard_map/ppermute | solution.py:121
  60.0 14.2 %collective-permute-start.6 = (bf16[128,1024]{1,0:T(8,128)(2,1)S(1)}, bf16[128,1024]{1,0:T(8,128)(2,1)S(1)}, u32[]{:S(2)}, u32[]{:S(2)}) collective-permute-start(bf16[128,1024]{1,0:T(8,128)(2,1)S(1)} %get-tuple-element.14), channel_id=1, source_target_pairs={{0,1},{1,0},{2,3},{3,2},{4,5},{5,4},{6,7},{7,6},{8,9},{9,8},{10,11... | collective-permute-start | bytes 786440 | tf_op jit(solution)/shard_map/ppermute | solution.py:121
  60.8 13.4 %collective-permute-start.8 = (bf16[128,1024]{1,0:T(8,128)(2,1)S(1)}, bf16[128,1024]{1,0:T(8,128)(2,1)S(1)}, u32[]{:S(2)}, u32[]{:S(2)}) collective-permute-start(bf16[128,1024]{1,0:T(8,128)(2,1)S(1)} %add_convert_fusion.3), channel_id=1, source_target_pairs={{0,12},{4,0},{8,4},{12,8},{1,13},{5,1},{9,5},{13,9},{2,14},{6,2},{... | collective-permute-start | bytes 786440 | tf_op jit(solution)/shard_map/ppermute | solution.py:121
  67.3 14.7 %collective-permute-start.13 = (bf16[128,1024]{1,0:T(8,128)(2,1)S(1)}, bf16[128,1024]{1,0:T(8,128)(2,1)S(1)}, u32[]{:S(2)}, u32[]{:S(2)}) collective-permute-start(bf16[128,1024]{1,0:T(8,128)(2,1)S(1)} %add_convert_fusion.2), channel_id=1, source_target_pairs={{0,8},{4,12},{8,0},{12,4},{1,9},{5,13},{9,1},{13,5},{2,10},{6,14},... | collective-permute-start | bytes 786440 | tf_op jit(solution)/shard_map/ppermute | solution.py:121
  71.5 10.5 %collective-permute-start.15 = (bf16[128,1024]{1,0:T(8,128)(2,1)S(1)}, bf16[128,1024]{1,0:T(8,128)(2,1)S(1)}, u32[]{:S(2)}, u32[]{:S(2)}) collective-permute-start(bf16[128,1024]{1,0:T(8,128)(2,1)S(1)} %add_convert_fusion.1), channel_id=1, source_target_pairs={{0,4},{4,8},{8,12},{12,0},{1,5},{5,9},{9,13},{13,1},{2,6},{6,10},{... | collective-permute-start | bytes 786440 | tf_op jit(solution)/shard_map/ppermute | solution.py:121

commit v4 on v3

--- a/solution.py
+++ b/solution.py
@@ -9,7 +9,6 @@
 from jax.sharding import Mesh, PartitionSpec as P
 
 CORES = 2
-ROUNDS = 2
 TERMS = 3
 NT = (((1,), (1,)), ((), ()))
 TN = (((0,), (0,)), ((), ()))
@@ -40,7 +39,31 @@
     )(latent, routes.T, gates.T)
 
 
-def expert_kernel(block, slots, unit, number, blocks, ids_ref, after_ref, *refs):
+def stage_kernel(after_ref, *refs):
+    number = (len(refs) - 1) // 2
+    copies = [
+        pltpu.make_async_copy(refs[n], refs[number + n], refs[-1].at[n]) for n in range(number)
+    ]
+    for copy in copies:
+        copy.start()
+    for copy in copies:
+        copy.wait()
+
+
+def stage(after, arrays):
+    return pl.pallas_call(
+        stage_kernel,
+        out_shape=[jax.ShapeDtypeStruct(a.shape, a.dtype) for a in arrays],
+        in_specs=[pl.BlockSpec(memory_space=pl.ANY)]
+        + [pl.BlockSpec(memory_space=pltpu.HBM)] * len(arrays),
+        out_specs=[pl.BlockSpec(memory_space=pltpu.VMEM)] * len(arrays),
+        scratch_shapes=[pltpu.SemaphoreType.DMA((len(arrays),))],
+        compiler_params=pltpu.CompilerParams(vmem_limit_bytes=16 * 1024 * 1024),
+    )(after, *arrays)
+
+
+def expert_kernel(block, slots, unit, number, blocks, waits, ids_ref, *refs):
+    refs = refs[waits:]
     x_refs, tables, out_refs = refs[:blocks], refs[blocks : blocks + 2 * number], refs[blocks + 2 * number :]
     extra = x_refs[0].shape[0] - block
     earlier = lax.broadcasted_iota(jnp.int32, (block, block), 0)
@@ -102,18 +125,19 @@
     unit = 16 // math.gcd(16, slots)
     whole = pl.BlockSpec(memory_space=pltpu.VMEM)
     return pl.pallas_call(
-        functools.partial(expert_kernel, block, slots, unit, number, blocks),
+        functools.partial(expert_kernel, block, slots, unit, number, blocks, len(after)),
         out_shape=[jax.ShapeDtypeStruct((block, width), kind) for kind in kinds],
-        in_specs=[pl.BlockSpec(memory_space=pltpu.SMEM), pl.BlockSpec(memory_space=pl.ANY)]
+        in_specs=[pl.BlockSpec(memory_space=pltpu.SMEM)]
+        + [pl.BlockSpec(memory_space=pl.ANY)] * len(after)
         + [whole] * (blocks + len(tables)),
         out_specs=[whole] * blocks,
-        compiler_params=pltpu.CompilerParams(vmem_limit_bytes=34 * 1024 * 1024),
+        compiler_params=pltpu.CompilerParams(vmem_limit_bytes=30 * 1024 * 1024),
         cost_estimate=pl.CostEstimate(
             flops=4 * number * blocks * slots * width * (hidden + block),
             bytes_accessed=5 * blocks * block * width + 2 * len(tables) * width * hidden,
             transcendentals=0,
         ),
-    )(ids, after, *arrived, *tables)
+    )(ids, *after, *arrived, *tables)
 
 
 def shift(array, axis, step):
@@ -127,30 +151,33 @@
     cores, depth, subs = (lax.axis_size(a) for a in ("core", "z", "sub"))
     experts = depth * cores
     slots = min(block, 3 * block * top // (2 * experts))
-    tables = [jnp.swapaxes(up_weight, 1, 2), jnp.swapaxes(down_weight, 1, 2)]
-    for step in range(1, cores):
-        tables += [shift(tables[0], "core", step), shift(tables[1], "core", step)]
+    own = [jnp.swapaxes(up_weight, 1, 2), jnp.swapaxes(down_weight, 1, 2)]
+    moved = [shift(table, "core", step) for step in range(1, cores) for table in own]
     core = lax.axis_index("core")
     ids = lax.axis_index("z") * cores + (core + cores - jnp.arange(cores, dtype=jnp.int32)) % cores
     ring = [pack(latent, routes, gates, experts)]
-    for r in range(1, depth):
-        ring.append(shift(ring[-1], "z", 1))
-    arrived = [[held] + [shift(held, "sub", s) for s in range(1, subs)] for held in ring]
+    tables = [*stage(ring[0], own), *moved]
+    ring.append(shift(ring[0], "z", 1))
     home = 0.0
     kinds = [jnp.float32] + [jnp.bfloat16] * (subs - 1)
-    for first in range(0, depth, ROUNDS):
-        now = range(first, min(depth, first + ROUNDS))
-        after = partial[0] if first else ring[min(depth - 1, ROUNDS)]
-        partial = run_experts(
-            ids, after, sum([arrived[r] for r in now], []), tables, kinds * len(now), block, slots
-        )
-        for r in now:
-            own, *others = partial[(r - first) * subs : (r - first + 1) * subs]
-            for s, other in enumerate(others, 1):
-                own = own + shift(other, "sub", -s).astype(jnp.float32)
-            if r:
-                own = shift(own.astype(jnp.bfloat16), "z", -r).astype(jnp.float32)
-            home = home + own
+    partial, summed, back = [], [], []
+    for r in range(depth):
+        arrived = [ring[r]] + [shift(ring[r], "sub", s) for s in range(1, subs)]
+        after = [ring[min(r + 1, depth - 1)], *partial[:1], *summed[1:][r - 3 : r - 2]]
+        partial = list(run_experts(ids, after, arrived, tables, kinds, block, slots))
+        if r + 2 < depth:
+            held, partial[0] = lax.optimization_barrier((shift(ring[-1], "z", 1), partial[0]))
+            ring.append(held)
+        total = partial[0]
+        for s in range(1, subs):
+            other = shift(partial[s], "sub", -s)
+            if r > 1 and s == 1:
+                other, back[r - 2] = lax.optimization_barrier((other, back[r - 2]))
+            total = total + other.astype(jnp.float32)
+        summed.append(total.astype(jnp.bfloat16))
+        back.append(shift(summed[r], "z", -r) if r else total)
+    for part in back:
+        home = home + part.astype(jnp.float32)
     return home.astype(jnp.bfloat16)
 
 

time: 83.2 us -> 79.4 us (0.954)
  waiting for transfers between devices: 42.6 us -> 26.7 us
  Pallas kernels: 18.3 us -> 24.9 us
  starting transfers between devices: 16.3 us -> 21.5 us
    ppermute x16, waiting for transfers between devices: 42.6 us -> 26.7 us  [shift(): lax.ppermute(array, axis, [(i, (i + step) % size) for i in range(size)])]
    pallas_call x2 -> x4, Pallas kernels: 16.6 us -> 22.4 us  [run_experts(): pl.pallas_call(functools.partial(expert_kernel, block, slots, unit, numbe...]
    ppermute x16, starting transfers between devices: 16.3 us -> 21.5 us  [shift(): lax.ppermute(array, axis, [(i, (i + step) % size) for i in range(size)])]
  transfers between devices with their start and end apart: 16 -> 16, of which waited for: 7 -> 5; matrix products, arithmetic and copies ran while one was open for 0% -> 0% of each run, Pallas kernels for 22% -> 31%
where the time goes in v4:
time: 79.4 us; the launch traced here: 79 us
  waiting for transfers between devices  26.7 us (34%)
  Pallas kernels  24.9 us (31%)
  starting transfers between devices  21.5 us (27%)
  local copies, waits for them, and re-layouts  4.72 us (6%)
  other arithmetic  1.08 us (1%)
    ppermute x16, waiting for transfers between devices, shift(): lax.ppermute(array, axis, [(i, (i + step) % size) for i in range(size)])  26.7 us
    pallas_call x4, Pallas kernels, run_experts(): pl.pallas_call(functools.partial(expert_kernel, block, slots, unit, numbe...  22.4 us
    ppermute x16, starting transfers between devices, shift(): lax.ppermute(array, axis, [(i, (i + step) % size) for i in range(size)])  21.5 us
    unnamed x8, local copies, waits for them, and re-layouts  4.72 us
    pallas_call x1, Pallas kernels, pack(): pl.pallas_call(functools.partial(pack_kernel, experts, extra), out_shape=...  1.71 us
  transfers between devices with their start and end apart: 16, of which 5 were waited for; matrix products, arithmetic and copies ran while one was open for 0% of the time, Pallas kernels for 31%

profile of v4, /device:TPU:0, one launch (start us, length us, event | category | flops | bytes accessed | tf_op | source)
XLA Modules:
  0.0 79.0 jit_solution(5507887629652716553)
XLA Ops:
  0.0 0.5 collective-permute-start.3
  0.5 0.1 collective-permute-start.4
  0.5 1.7 %shard_map.55.after_ref.refs_1_ = bf16[144,1024]{1,0:T(8,128)(2,1)} custom-call(bf16[128,1024]{1,0:T(8,128)(2,1)} %latent_ref.1, s32[4,128]{1,0:T(4,128)} %bitcast.8, f32[4,128]{1,0:T(4,128)} %bitcast.9), custom_call_target="tpu_custom_call" | custom-call | tf_op jit(solution)/shard_map/pallas_call | solution.py:34
  2.2 3.0 %collective-permute-start = (bf16[144,1024]{1,0:T(8,128)(2,1)}, bf16[144,1024]{1,0:T(8,128)(2,1)S(1)}, u32[]{:S(2)}, u32[]{:S(2)}) collective-permute-start(bf16[144,1024]{1,0:T(8,128)(2,1)} %shard_map.55.after_ref.refs_1_), channel_id=1, source_target_pairs={{0,4},{4,8},{8,12},{12,0},{1,5},{5,9},{9,13},{13,1},{2,6},{6,10},{... | collective-permute-start | bytes 884744 | tf_op jit(solution)/shard_map/ppermute | solution.py:145
  5.3 1.5 %collective-permute-start.2 = (bf16[144,1024]{1,0:T(8,128)(2,1)}, bf16[144,1024]{1,0:T(8,128)(2,1)S(1)}, u32[]{:S(2)}, u32[]{:S(2)}) collective-permute-start(bf16[144,1024]{1,0:T(8,128)(2,1)} %shard_map.55.after_ref.refs_1_), channel_id=1, source_target_pairs={{0,1},{1,0},{2,3},{3,2},{4,5},{5,4},{6,7},{7,6},{8,9},{9,8},{10,11... | collective-permute-start | bytes 884744 | tf_op jit(solution)/shard_map/ppermute | solution.py:145
  6.7 7.9 %collective-permute-done.refs_0_.refs_2_ = bf16[144,1024]{1,0:T(8,128)(2,1)S(1)} collective-permute-done((bf16[144,1024]{1,0:T(8,128)(2,1)}, bf16[144,1024]{1,0:T(8,128)(2,1)S(1)}, u32[]{:S(2)}, u32[]{:S(2)}) %collective-permute-start) | collective-permute-done | bytes 294944 | tf_op jit(solution)/shard_map/ppermute | solution.py:145
  14.7 0.0 collective-permute-start.1
  14.7 1.5 %collective-permute-start.6 = (bf16[144,1024]{1,0:T(8,128)(2,1)S(1)}, bf16[144,1024]{1,0:T(8,128)(2,1)S(1)}, u32[]{:S(2)}, u32[]{:S(2)}) collective-permute-start(bf16[144,1024]{1,0:T(8,128)(2,1)S(1)} %collective-permute-done.refs_0_.refs_2_), channel_id=1, source_target_pairs={{0,1},{1,0},{2,3},{3,2},{4,5},{5,4},{6,7},{7,6},{8,9},{9,8},{10,11... | collective-permute-start | bytes 884744 | tf_op jit(solution)/shard_map/ppermute | solution.py:145
  16.2 0.0 copy-start
  16.2 1.8 %copy-done = bf16[1,1024,1344]{1,2,0:T(8,128)(2,1)S(1)} copy-done((bf16[1,1024,1344]{1,2,0:T(8,128)(2,1)S(1)}, bf16[1,1024,1344]{1,2,0:T(8,128)(2,1)}, u32[]{:S(2)}) %copy-start) | copy-done | bytes 2752536
  17.9 1.8 %copy-done.1 = bf16[1,1024,1344]{1,2,0:T(8,128)(2,1)S(1)} copy-done((bf16[1,1024,1344]{1,2,0:T(8,128)(2,1)S(1)}, bf16[1,1024,1344]{1,2,0:T(8,128)(2,1)}, u32[]{:S(2)}) %copy-start.1) | copy-done | bytes 2752536
  19.7 1.0 %copy-done.2 = bf16[144,1024]{1,0:T(8,128)(2,1)S(1)} copy-done((bf16[144,1024]{1,0:T(8,128)(2,1)S(1)}, bf16[144,1024]{1,0:T(8,128)(2,1)}, u32[]{:S(2)}) %copy-start.2) | copy-done | bytes 294936
  20.7 0.7 shard_map.56
  21.4 0.0 collective-permute-done.2.refs_2_
  21.4 0.0 collective-permute-done.3.refs_5_.refs_6_.refs_7_
  21.4 0.0 collective-permute-done.4.refs_6_.refs_7_.refs_8_
  21.4 0.2 copy-done.3
  21.6 5.6 %shard_map.57 = (f32[128,1024]{1,0:T(8,128)S(1)}, bf16[128,1024]{1,0:T(8,128)(2,1)S(1)}) custom-call(s32[2]{0:T(128)S(1)} %fusion.ids_ref, bf16[144,1024]{1,0:T(8,128)(2,1)S(1)} %collective-permute-done.refs_0_.refs_2_, bf16[144,1024]{1,0:T(8,128)(2,1)S(1)} %copy-done.3, bf16[144,1024]{1,0:T(8,128)(2,1)S(1)} %collective-permute-done.2.refs_2_, ...), custom_call_target="tpu_custom_call" | custom-call | flops 2315255808 | bytes 12320768 | tf_op jit(solution)/shard_map/pallas_call | solution.py:127
  27.3 0.0 collective-permute-done.1.refs_0_.refs_2_
  27.3 1.3 %collective-permute-start.5 = (bf16[144,1024]{1,0:T(8,128)(2,1)S(1)}, bf16[144,1024]{1,0:T(8,128)(2,1)S(1)}, u32[]{:S(2)}, u32[]{:S(2)}) collective-permute-start(bf16[144,1024]{1,0:T(8,128)(2,1)S(1)} %collective-permute-done.1.refs_0_.refs_2_), channel_id=1, source_target_pairs={{0,4},{4,8},{8,12},{12,0},{1,5},{5,9},{9,13},{13,1},{2,6},{6,10},{... | collective-permute-start | bytes 884744 | tf_op jit(solution)/shard_map/ppermute | solution.py:145
  28.6 0.5 collective-permute-start.7
  29.1 0.0 collective-permute-done.6.refs_3_
  29.2 5.6 %shard_map.58 = (f32[128,1024]{1,0:T(8,128)S(1)}, bf16[128,1024]{1,0:T(8,128)(2,1)S(1)}) custom-call(s32[2]{0:T(128)S(1)} %fusion.ids_ref, bf16[144,1024]{1,0:T(8,128)(2,1)S(1)} %collective-permute-done.1.refs_0_.refs_2_, f32[128,1024]{1,0:T(8,128)S(1)} %get-tuple-element.27.refs_1_, bf16[144,1024]{1,0:T(8,128)(2,1)S(1)} %collective-permute-done.refs_0_.refs_2_, ...), custom_call_target="tpu_custom_call" | custom-call | flops 2315255808 | bytes 12320768 | tf_op jit(solution)/shard_map/pallas_call | solution.py:127
  34.8 1.6 %collective-permute-start.10 = (bf16[128,1024]{1,0:T(8,128)(2,1)S(1)}, bf16[128,1024]{1,0:T(8,128)(2,1)S(1)}, u32[]{:S(2)}, u32[]{:S(2)}) collective-permute-start(bf16[128,1024]{1,0:T(8,128)(2,1)S(1)} %get-tuple-element.35), channel_id=1, source_target_pairs={{0,1},{1,0},{2,3},{3,2},{4,5},{5,4},{6,7},{7,6},{8,9},{9,8},{10,11... | collective-permute-start | bytes 786440 | tf_op jit(solution)/shard_map/ppermute | solution.py:145
  36.3 0.5 collective-permute-start.9
  36.9 0.1 collective-permute-done.5.refs_0_.refs_3_
  37.0 1.4 %collective-permute-start.11 = (bf16[144,1024]{1,0:T(8,128)(2,1)S(1)}, bf16[144,1024]{1,0:T(8,128)(2,1)S(1)}, u32[]{:S(2)}, u32[]{:S(2)}) collective-permute-start(bf16[144,1024]{1,0:T(8,128)(2,1)S(1)} %collective-permute-done.5.refs_0_.refs_3_), channel_id=1, source_target_pairs={{0,1},{1,0},{2,3},{3,2},{4,5},{5,4},{6,7},{7,6},{8,9},{9,8},{10,11... | collective-permute-start | bytes 884744 | tf_op jit(solution)/shard_map/ppermute | solution.py:145
  38.3 0.0 collective-permute-done.7.refs_3_
  38.3 5.6 %shard_map.59 = (f32[128,1024]{1,0:T(8,128)S(1)}, bf16[128,1024]{1,0:T(8,128)(2,1)S(1)}) custom-call(s32[2]{0:T(128)S(1)} %fusion.ids_ref, bf16[144,1024]{1,0:T(8,128)(2,1)S(1)} %collective-permute-done.5.refs_0_.refs_3_, f32[128,1024]{1,0:T(8,128)S(1)} %get-tuple-element.30.refs_1_, bf16[144,1024]{1,0:T(8,128)(2,1)S(1)} %collective-permute-done.1.refs_0_.refs_2_, ...), custom_call_target="tpu_custom_call" | custom-call | flops 2315255808 | bytes 12320768 | tf_op jit(solution)/shard_map/pallas_call | solution.py:127
  44.0 0.7 collective-permute-start.8
  44.7 0.0 collective-permute-done.10
  44.7 0.1 add_convert_fusion.3.refs_2_
  44.8 2.7 %collective-permute-start.13 = (bf16[128,1024]{1,0:T(8,128)(2,1)S(1)}, bf16[128,1024]{1,0:T(8,128)(2,1)S(1)}, u32[]{:S(2)}, u32[]{:S(2)}) collective-permute-start(bf16[128,1024]{1,0:T(8,128)(2,1)S(1)} %add_convert_fusion.3.refs_2_), channel_id=1, source_target_pairs={{0,12},{4,0},{8,4},{12,8},{1,13},{5,1},{9,5},{13,9},{2,14},{6,2},{... | collective-permute-start | bytes 786440 | tf_op jit(solution)/shard_map/ppermute | solution.py:145
  47.5 8.5 %collective-permute-done.11.refs_4_ = bf16[144,1024]{1,0:T(8,128)(2,1)S(1)} collective-permute-done((bf16[144,1024]{1,0:T(8,128)(2,1)S(1)}, bf16[144,1024]{1,0:T(8,128)(2,1)S(1)}, u32[]{:S(2)}, u32[]{:S(2)}) %collective-permute-start.11) | collective-permute-done | bytes 294944 | tf_op jit(solution)/shard_map/ppermute | solution.py:145
  56.0 5.6 %shard_map.60 = (f32[128,1024]{1,0:T(8,128)S(1)}, bf16[128,1024]{1,0:T(8,128)(2,1)S(1)}) custom-call(s32[2]{0:T(128)S(1)} %fusion.ids_ref, bf16[144,1024]{1,0:T(8,128)(2,1)S(1)} %collective-permute-done.5.refs_0_.refs_3_, f32[128,1024]{1,0:T(8,128)S(1)} %get-tuple-element.34.refs_1_, bf16[128,1024]{1,0:T(8,128)(2,1)S(1)} %add_convert_fusion.3.refs_2_, ...), custom_call_target="tpu_custom_call" | custom-call | flops 2315255808 | bytes 12320768 | tf_op jit(solution)/shard_map/pallas_call | solution.py:127
  61.6 1.4 %collective-permute-start.12 = (bf16[128,1024]{1,0:T(8,128)(2,1)S(1)}, bf16[128,1024]{1,0:T(8,128)(2,1)S(1)}, u32[]{:S(2)}, u32[]{:S(2)}) collective-permute-start(bf16[128,1024]{1,0:T(8,128)(2,1)S(1)} %get-tuple-element.36), channel_id=1, source_target_pairs={{0,1},{1,0},{2,3},{3,2},{4,5},{5,4},{6,7},{7,6},{8,9},{9,8},{10,11... | collective-permute-start | bytes 786440 | tf_op jit(solution)/shard_map/ppermute | solution.py:145
  63.0 0.0 collective-permute-done.9
  63.0 0.1 convert_add_fusion
  63.0 0.0 collective-permute-done.8
  63.0 0.1 add_convert_fusion.2
  63.1 3.2 %collective-permute-start.14 = (bf16[128,1024]{1,0:T(8,128)(2,1)S(1)}, bf16[128,1024]{1,0:T(8,128)(2,1)S(1)}, u32[]{:S(2)}, u32[]{:S(2)}) collective-permute-start(bf16[128,1024]{1,0:T(8,128)(2,1)S(1)} %add_convert_fusion.2), channel_id=1, source_target_pairs={{0,8},{4,12},{8,0},{12,4},{1,9},{5,13},{9,1},{13,5},{2,10},{6,14},... | collective-permute-start | bytes 786440 | tf_op jit(solution)/shard_map/ppermute | solution.py:145
  66.3 0.0 collective-permute-done.13
  66.3 1.7 %collective-permute-done.12 = bf16[128,1024]{1,0:T(8,128)(2,1)S(1)} collective-permute-done((bf16[128,1024]{1,0:T(8,128)(2,1)S(1)}, bf16[128,1024]{1,0:T(8,128)(2,1)S(1)}, u32[]{:S(2)}, u32[]{:S(2)}) %collective-permute-start.12) | collective-permute-done | bytes 262176 | tf_op jit(solution)/shard_map/ppermute | solution.py:145
  68.1 0.1 add_convert_fusion.1
  68.1 1.6 %collective-permute-start.15 = (bf16[128,1024]{1,0:T(8,128)(2,1)S(1)}, bf16[128,1024]{1,0:T(8,128)(2,1)S(1)}, u32[]{:S(2)}, u32[]{:S(2)}) collective-permute-start(bf16[128,1024]{1,0:T(8,128)(2,1)S(1)} %add_convert_fusion.1), channel_id=1, source_target_pairs={{0,4},{4,8},{8,12},{12,0},{1,5},{5,9},{9,13},{13,1},{2,6},{6,10},{... | collective-permute-start | bytes 786440 | tf_op jit(solution)/shard_map/ppermute | solution.py:145
  69.8 8.4 %collective-permute-done.14 = bf16[128,1024]{1,0:T(8,128)(2,1)S(1)} collective-permute-done((bf16[128,1024]{1,0:T(8,128)(2,1)S(1)}, bf16[128,1024]{1,0:T(8,128)(2,1)S(1)}, u32[]{:S(2)}, u32[]{:S(2)}) %collective-permute-start.14) | collective-permute-done | bytes 262176 | tf_op jit(solution)/shard_map/ppermute | solution.py:145
  78.1 0.0 collective-permute-done.15
  78.1 0.8 %add_convert_fusion = bf16[128,1024]{1,0:T(8,128)(2,1)} fusion(bf16[128,1024]{1,0:T(8,128)(2,1)S(1)} %collective-permute-done.15, bf16[128,1024]{1,0:T(8,128)(2,1)S(1)} %collective-permute-done.14, f32[128,1024]{1,0:T(8,128)S(1)} %convert_add_fusion, bf16[128,1024]{1,0:T(8,128)(2,1)S(1)} %collective-permute-done.13), kind=kLoop, calls=%fused_computation | loop fusion | flops 917504 | bytes 1572864 | tf_op jit(solution)/shard_map/convert_element_type | solution.py:181
  (4 shorter events, 0.0 us)
Async XLA Ops:
  0.0 21.4 %collective-permute-start.3 = (bf16[1,1344,1024]{2,1,0:T(8,128)(2,1)}, bf16[1,1344,1024]{2,1,0:T(8,128)(2,1)S(1)}, u32[]{:S(2)}, u32[]{:S(2)}) collective-permute-start(bf16[1,1344,1024]{2,1,0:T(8,128)(2,1)} %bitcast.4), channel_id=1, source_target_pairs={{0,2},{2,0},{1,3},{3,1},{4,6},{6,4},{5,7},{7,5},{8,10},{10,8},{9,1... | collective-permute-start | bytes 8257544 | tf_op jit(solution)/shard_map/ppermute | solution.py:145
  0.5 21.0 %collective-permute-start.4 = (bf16[1,1344,1024]{2,1,0:T(8,128)(2,1)}, bf16[1,1344,1024]{2,1,0:T(8,128)(2,1)}, u32[]{:S(2)}, u32[]{:S(2)}) collective-permute-start(bf16[1,1344,1024]{2,1,0:T(8,128)(2,1)} %bitcast.6), channel_id=1, source_target_pairs={{0,2},{2,0},{1,3},{3,1},{4,6},{6,4},{5,7},{7,5},{8,10},{10,8},{9,1... | collective-permute-start | bytes 8257544 | tf_op jit(solution)/shard_map/ppermute | solution.py:145
  2.2 12.4 %collective-permute-start = (bf16[144,1024]{1,0:T(8,128)(2,1)}, bf16[144,1024]{1,0:T(8,128)(2,1)S(1)}, u32[]{:S(2)}, u32[]{:S(2)}) collective-permute-start(bf16[144,1024]{1,0:T(8,128)(2,1)} %shard_map.55.after_ref.refs_1_), channel_id=1, source_target_pairs={{0,4},{4,8},{8,12},{12,0},{1,5},{5,9},{9,13},{13,1},{2,6},{6,10},{... | collective-permute-start | bytes 884744 | tf_op jit(solution)/shard_map/ppermute | solution.py:145
  5.3 16.2 %collective-permute-start.2 = (bf16[144,1024]{1,0:T(8,128)(2,1)}, bf16[144,1024]{1,0:T(8,128)(2,1)S(1)}, u32[]{:S(2)}, u32[]{:S(2)}) collective-permute-start(bf16[144,1024]{1,0:T(8,128)(2,1)} %shard_map.55.after_ref.refs_1_), channel_id=1, source_target_pairs={{0,1},{1,0},{2,3},{3,2},{4,5},{5,4},{6,7},{7,6},{8,9},{9,8},{10,11... | collective-permute-start | bytes 884744 | tf_op jit(solution)/shard_map/ppermute | solution.py:145
  14.7 12.6 %collective-permute-start.1 = (bf16[144,1024]{1,0:T(8,128)(2,1)S(1)}, bf16[144,1024]{1,0:T(8,128)(2,1)S(1)}, u32[]{:S(2)}, u32[]{:S(2)}) collective-permute-start(bf16[144,1024]{1,0:T(8,128)(2,1)S(1)} %collective-permute-done.refs_0_.refs_2_), channel_id=1, source_target_pairs={{0,4},{4,8},{8,12},{12,0},{1,5},{5,9},{9,13},{13,1},{2,6},{6,10},{... | collective-permute-start | bytes 884744 | tf_op jit(solution)/shard_map/ppermute | solution.py:145
  14.7 14.5 %collective-permute-start.6 = (bf16[144,1024]{1,0:T(8,128)(2,1)S(1)}, bf16[144,1024]{1,0:T(8,128)(2,1)S(1)}, u32[]{:S(2)}, u32[]{:S(2)}) collective-permute-start(bf16[144,1024]{1,0:T(8,128)(2,1)S(1)} %collective-permute-done.refs_0_.refs_2_), channel_id=1, source_target_pairs={{0,1},{1,0},{2,3},{3,2},{4,5},{5,4},{6,7},{7,6},{8,9},{9,8},{10,11... | collective-permute-start | bytes 884744 | tf_op jit(solution)/shard_map/ppermute | solution.py:145
  16.2 1.8 %copy-start = (bf16[1,1024,1344]{1,2,0:T(8,128)(2,1)S(1)}, bf16[1,1024,1344]{1,2,0:T(8,128)(2,1)}, u32[]{:S(2)}) copy-start(bf16[1,1024,1344]{1,2,0:T(8,128)(2,1)} %param.8) | copy-start | bytes 8257540
  17.9 1.8 %copy-start.1 = (bf16[1,1024,1344]{1,2,0:T(8,128)(2,1)S(1)}, bf16[1,1024,1344]{1,2,0:T(8,128)(2,1)}, u32[]{:S(2)}) copy-start(bf16[1,1024,1344]{1,2,0:T(8,128)(2,1)} %param.9) | copy-start | bytes 8257540
  19.7 1.0 %copy-start.2 = (bf16[144,1024]{1,0:T(8,128)(2,1)S(1)}, bf16[144,1024]{1,0:T(8,128)(2,1)}, u32[]{:S(2)}) copy-start(bf16[144,1024]{1,0:T(8,128)(2,1)} %shard_map.55.after_ref.refs_1_) | copy-start | bytes 884740
  20.7 1.0 %copy-start.3 = (bf16[144,1024]{1,0:T(8,128)(2,1)S(1)}, bf16[144,1024]{1,0:T(8,128)(2,1)}, u32[]{:S(2)}) copy-start(bf16[144,1024]{1,0:T(8,128)(2,1)} %shard_map.55.after_ref.refs_1_) | copy-start | bytes 884740
  27.3 9.7 %collective-permute-start.5 = (bf16[144,1024]{1,0:T(8,128)(2,1)S(1)}, bf16[144,1024]{1,0:T(8,128)(2,1)S(1)}, u32[]{:S(2)}, u32[]{:S(2)}) collective-permute-start(bf16[144,1024]{1,0:T(8,128)(2,1)S(1)} %collective-permute-done.1.refs_0_.refs_2_), channel_id=1, source_target_pairs={{0,4},{4,8},{8,12},{12,0},{1,5},{5,9},{9,13},{13,1},{2,6},{6,10},{... | collective-permute-start | bytes 884744 | tf_op jit(solution)/shard_map/ppermute | solution.py:145
  28.6 9.7 %collective-permute-start.7 = (bf16[144,1024]{1,0:T(8,128)(2,1)S(1)}, bf16[144,1024]{1,0:T(8,128)(2,1)S(1)}, u32[]{:S(2)}, u32[]{:S(2)}) collective-permute-start(bf16[144,1024]{1,0:T(8,128)(2,1)S(1)} %collective-permute-done.1.refs_0_.refs_2_), channel_id=1, source_target_pairs={{0,1},{1,0},{2,3},{3,2},{4,5},{5,4},{6,7},{7,6},{8,9},{9,8},{10,11... | collective-permute-start | bytes 884744 | tf_op jit(solution)/shard_map/ppermute | solution.py:145
  34.8 9.9 %collective-permute-start.10 = (bf16[128,1024]{1,0:T(8,128)(2,1)S(1)}, bf16[128,1024]{1,0:T(8,128)(2,1)S(1)}, u32[]{:S(2)}, u32[]{:S(2)}) collective-permute-start(bf16[128,1024]{1,0:T(8,128)(2,1)S(1)} %get-tuple-element.35), channel_id=1, source_target_pairs={{0,1},{1,0},{2,3},{3,2},{4,5},{5,4},{6,7},{7,6},{8,9},{9,8},{10,11... | collective-permute-start | bytes 786440 | tf_op jit(solution)/shard_map/ppermute | solution.py:145
  36.3 26.7 %collective-permute-start.9 = (bf16[128,1024]{1,0:T(8,128)(2,1)S(1)}, bf16[128,1024]{1,0:T(8,128)(2,1)S(1)}, u32[]{:S(2)}, u32[]{:S(2)}) collective-permute-start(bf16[128,1024]{1,0:T(8,128)(2,1)S(1)} %get-tuple-element.32), channel_id=1, source_target_pairs={{0,1},{1,0},{2,3},{3,2},{4,5},{5,4},{6,7},{7,6},{8,9},{9,8},{10,11... | collective-permute-start | bytes 786440 | tf_op jit(solution)/shard_map/ppermute | solution.py:145
  37.0 19.0 %collective-permute-start.11 = (bf16[144,1024]{1,0:T(8,128)(2,1)S(1)}, bf16[144,1024]{1,0:T(8,128)(2,1)S(1)}, u32[]{:S(2)}, u32[]{:S(2)}) collective-permute-start(bf16[144,1024]{1,0:T(8,128)(2,1)S(1)} %collective-permute-done.5.refs_0_.refs_3_), channel_id=1, source_target_pairs={{0,1},{1,0},{2,3},{3,2},{4,5},{5,4},{6,7},{7,6},{8,9},{9,8},{10,11... | collective-permute-start | bytes 884744 | tf_op jit(solution)/shard_map/ppermute | solution.py:145
  44.0 19.1 %collective-permute-start.8 = (bf16[128,1024]{1,0:T(8,128)(2,1)S(1)}, bf16[128,1024]{1,0:T(8,128)(2,1)S(1)}, u32[]{:S(2)}, u32[]{:S(2)}) collective-permute-start(bf16[128,1024]{1,0:T(8,128)(2,1)S(1)} %get-tuple-element.31), channel_id=1, source_target_pairs={{0,1},{1,0},{2,3},{3,2},{4,5},{5,4},{6,7},{7,6},{8,9},{9,8},{10,11... | collective-permute-start | bytes 786440 | tf_op jit(solution)/shard_map/ppermute | solution.py:145
  44.8 21.6 %collective-permute-start.13 = (bf16[128,1024]{1,0:T(8,128)(2,1)S(1)}, bf16[128,1024]{1,0:T(8,128)(2,1)S(1)}, u32[]{:S(2)}, u32[]{:S(2)}) collective-permute-start(bf16[128,1024]{1,0:T(8,128)(2,1)S(1)} %add_convert_fusion.3.refs_2_), channel_id=1, source_target_pairs={{0,12},{4,0},{8,4},{12,8},{1,13},{5,1},{9,5},{13,9},{2,14},{6,2},{... | collective-permute-start | bytes 786440 | tf_op jit(solution)/shard_map/ppermute | solution.py:145
  61.6 6.4 %collective-permute-start.12 = (bf16[128,1024]{1,0:T(8,128)(2,1)S(1)}, bf16[128,1024]{1,0:T(8,128)(2,1)S(1)}, u32[]{:S(2)}, u32[]{:S(2)}) collective-permute-start(bf16[128,1024]{1,0:T(8,128)(2,1)S(1)} %get-tuple-element.36), channel_id=1, source_target_pairs={{0,1},{1,0},{2,3},{3,2},{4,5},{5,4},{6,7},{7,6},{8,9},{9,8},{10,11... | collective-permute-start | bytes 786440 | tf_op jit(solution)/shard_map/ppermute | solution.py:145
  63.1 15.0 %collective-permute-start.14 = (bf16[128,1024]{1,0:T(8,128)(2,1)S(1)}, bf16[128,1024]{1,0:T(8,128)(2,1)S(1)}, u32[]{:S(2)}, u32[]{:S(2)}) collective-permute-start(bf16[128,1024]{1,0:T(8,128)(2,1)S(1)} %add_convert_fusion.2), channel_id=1, source_target_pairs={{0,8},{4,12},{8,0},{12,4},{1,9},{5,13},{9,1},{13,5},{2,10},{6,14},... | collective-permute-start | bytes 786440 | tf_op jit(solution)/shard_map/ppermute | solution.py:145
  68.1 10.0 %collective-permute-start.15 = (bf16[128,1024]{1,0:T(8,128)(2,1)S(1)}, bf16[128,1024]{1,0:T(8,128)(2,1)S(1)}, u32[]{:S(2)}, u32[]{:S(2)}) collective-permute-start(bf16[128,1024]{1,0:T(8,128)(2,1)S(1)} %add_convert_fusion.1), channel_id=1, source_target_pairs={{0,4},{4,8},{8,12},{12,0},{1,5},{5,9},{9,13},{13,1},{2,6},{6,10},{... | collective-permute-start | bytes 786440 | tf_op jit(solution)/shard_map/ppermute | solution.py:145

commit v5 on v4

--- a/solution.py
+++ b/solution.py
@@ -69,8 +69,8 @@
     earlier = lax.broadcasted_iota(jnp.int32, (block, block), 0)
     later = lax.broadcasted_iota(jnp.int32, (block, block), 1)
     before = (earlier < later).astype(jnp.bfloat16)
-    size = unit * slots
-    slot = lax.broadcasted_iota(jnp.int32, (size, block), 0)
+    groups = [range(g, min(g + unit, blocks)) for g in range(0, blocks, unit)]
+    sizes = [-(-len(g) * slots // 16) * 16 for g in groups]
     row = lax.broadcasted_iota(jnp.int32, (extra, block), 0)
     gates, ranks = [], []
     for x_ref in x_refs:
@@ -86,34 +86,35 @@
         up_ref, down_ref = tables[2 * n], tables[2 * n + 1]
         mine = row == ids_ref[n]
         picks, scales, rows = [], [], []
-        for u in range(blocks // unit):
+        for group, size in zip(groups, sizes):
+            slot = lax.broadcasted_iota(jnp.int32, (size, block), 0)
             parts = []
             scale = 0.0
-            for j in range(unit):
-                b = u * unit + j
+            for j, b in enumerate(group):
                 weight = jnp.sum(jnp.where(mine, gates[b], 0.0), axis=0, keepdims=True)
                 rank = jnp.sum(jnp.where(mine, ranks[b], 0.0), axis=0, keepdims=True)
                 here = (slot == rank.astype(jnp.int32) + j * slots) & (weight > 0)
                 scale = scale + jnp.sum(jnp.where(here, weight, 0.0), axis=1, keepdims=True)
                 parts.append(here.astype(jnp.bfloat16))
-            tokens = [x_refs[u * unit + j][:block, :] for j in range(unit)]
-            pick = jnp.concatenate(parts, axis=1) if unit > 1 else parts[0]
-            token = jnp.concatenate(tokens, axis=0) if unit > 1 else tokens[0]
+            tokens = [x_refs[b][:block, :] for b in group]
+            pick = jnp.concatenate(parts, axis=1) if len(group) > 1 else parts[0]
+            token = jnp.concatenate(tokens, axis=0) if len(group) > 1 else tokens[0]
             rows.append(
                 jnp.dot(pick, token, preferred_element_type=jnp.float32).astype(jnp.bfloat16)
             )
             picks.append(parts)
             scales.append(scale)
-        picked = jnp.concatenate(rows, axis=0)
+        picked = jnp.concatenate(rows, axis=0) if len(rows) > 1 else rows[0]
         preact = lax.dot_general(picked, up_ref[0], NT, preferred_element_type=jnp.float32)
         active = jnp.square(jnp.maximum(preact, 0.0)).astype(jnp.bfloat16)
         summed = jnp.dot(active, down_ref[0], preferred_element_type=jnp.float32)
-        for u in range(blocks // unit):
-            gated = (summed[u * size : (u + 1) * size] * scales[u]).astype(jnp.bfloat16)
-            for j in range(unit):
-                b = u * unit + j
+        start = 0
+        for g, (group, size) in enumerate(zip(groups, sizes)):
+            gated = (summed[start : start + size] * scales[g]).astype(jnp.bfloat16)
+            start += size
+            for j, b in enumerate(group):
                 sums[b] = sums[b] + lax.dot_general(
-                    picks[u][j], gated, TN, preferred_element_type=jnp.float32
+                    picks[g][j], gated, TN, preferred_element_type=jnp.float32
                 )
     for b in range(blocks):
         out_refs[b][...] = sums[b].astype(out_refs[b].dtype)
@@ -145,6 +146,20 @@
     return lax.ppermute(array, axis, [(i, (i + step) % size) for i in range(size)])
 
 
+def follow(array, first):
+    return lax.optimization_barrier((array, first))[0]
+
+
+def shift_both(array, outer, step, inner, turn):
+    sizes = lax.axis_size(outer), lax.axis_size(inner)
+    pairs = [
+        (i * sizes[1] + k, (i + step) % sizes[0] * sizes[1] + (k + turn) % sizes[1])
+        for i in range(sizes[0])
+        for k in range(sizes[1])
+    ]
+    return lax.ppermute(array, (outer, inner), pairs)
+
+
 def local(latent, routes, gates, up_weight, down_weight):
     block, width = latent.shape
     top = routes.shape[1]
@@ -157,27 +172,50 @@
     ids = lax.axis_index("z") * cores + (core + cores - jnp.arange(cores, dtype=jnp.int32)) % cores
     ring = [pack(latent, routes, gates, experts)]
     tables = [*stage(ring[0], own), *moved]
-    ring.append(shift(ring[0], "z", 1))
-    home = 0.0
-    kinds = [jnp.float32] + [jnp.bfloat16] * (subs - 1)
-    partial, summed, back = [], [], []
-    for r in range(depth):
-        arrived = [ring[r]] + [shift(ring[r], "sub", s) for s in range(1, subs)]
-        after = [ring[min(r + 1, depth - 1)], *partial[:1], *summed[1:][r - 3 : r - 2]]
-        partial = list(run_experts(ids, after, arrived, tables, kinds, block, slots))
-        if r + 2 < depth:
-            held, partial[0] = lax.optimization_barrier((shift(ring[-1], "z", 1), partial[0]))
-            ring.append(held)
-        total = partial[0]
-        for s in range(1, subs):
-            other = shift(partial[s], "sub", -s)
-            if r > 1 and s == 1:
-                other, back[r - 2] = lax.optimization_barrier((other, back[r - 2]))
-            total = total + other.astype(jnp.float32)
-        summed.append(total.astype(jnp.bfloat16))
-        back.append(shift(summed[r], "z", -r) if r else total)
-    for part in back:
-        home = home + part.astype(jnp.float32)
+    ring.append(follow(shift(ring[0], "z", 1), tables[0]))
+    last = depth - 1
+    kept = [None] * depth
+    others, totals = [], {}
+    after = []
+
+    def total(j, behind=None):
+        rows = kept[j]
+        for s, other in enumerate(others[j], 1):
+            other = shift(other, "sub", -s)
+            if behind is not None:
+                other = follow(other, behind)
+            rows = rows + other.astype(jnp.float32)
+        return rows.astype(jnp.bfloat16) if j else rows
+
+    for j in range(depth):
+        handed = [shift(ring[j], "sub", s) for s in range(1, subs)]
+        fresh = ([0] if j == 0 else []) + [j + 1] * (j < last)
+        kinds = [jnp.bfloat16] * len(handed)
+        kinds += [jnp.bfloat16 if r == last else jnp.float32 for r in fresh]
+        if j > 2:
+            totals[j - 2] = total(j - 2, after[0])
+            after.append(totals[j - 2])
+        partial = run_experts(
+            ids, after, handed + [ring[r] for r in fresh], tables, kinds, block, slots
+        )
+        after = [partial[0]]
+        if j + 2 < depth:
+            ring.append(follow(shift(ring[-1], "z", 1), partial[0]))
+        for r, rows in zip(fresh, partial[subs - 1 :]):
+            kept[r] = rows
+        others.append(partial[: subs - 1])
+    corner = [shift_both(other, "z", -last, "sub", -s) for s, other in enumerate(others[last], 1)]
+    others[0] = [follow(other, others[last][0]) for other in others[0]]
+    for j in range(last):
+        if j not in totals:
+            totals[j] = total(j, others[last][0])
+    back = [shift(kept[last], "z", -last)] + [shift(totals[j], "z", -j) for j in range(1, last)]
+    late = back.pop()
+    home = sum(rows.astype(jnp.float32) for rows in back)
+    home, *corner = lax.optimization_barrier((home, *corner))
+    home = home + totals[0] + sum(rows.astype(jnp.float32) for rows in corner)
+    home, late = lax.optimization_barrier((home, late))
+    home = home + late.astype(jnp.float32)
     return home.astype(jnp.bfloat16)
 
 

time: 79.4 us -> 75.1 us (0.946)
  waiting for transfers between devices: 26.7 us -> 18.4 us
  local copies, waits for them, and re-layouts: 4.72 us -> 11.2 us
  starting transfers between devices: 21.5 us -> 18.3 us
    ppermute x16 -> x15, waiting for transfers between devices: 26.7 us -> 18.4 us  [shift(): lax.ppermute(array, axis, [(i, (i + step) % size) for i in range(size)])]
    unnamed x8 -> x20, local copies, waits for them, and re-layouts: 4.72 us -> 11.2 us
    ppermute x16 -> x15, starting transfers between devices: 21.5 us -> 18.1 us  [shift(): lax.ppermute(array, axis, [(i, (i + step) % size) for i in range(size)])]
  transfers between devices with their start and end apart: 16 -> 16, of which waited for: 5 -> 5; matrix products, arithmetic and copies ran while one was open for 0% -> 0% of each run, Pallas kernels for 31% -> 34%
where the time goes in v5:
time: 75.1 us; the launch traced here: 74.7 us
  Pallas kernels  25.6 us (34%)
  waiting for transfers between devices  18.4 us (25%)
  starting transfers between devices  18.3 us (24%)
  local copies, waits for them, and re-layouts  11.2 us (15%)
  other arithmetic  1.07 us (1%)
    pallas_call x4, Pallas kernels, run_experts(): pl.pallas_call(functools.partial(expert_kernel, block, slots, unit, numbe...  23.2 us
    ppermute x15, waiting for transfers between devices, shift(): lax.ppermute(array, axis, [(i, (i + step) % size) for i in range(size)])  18.4 us
    ppermute x15, starting transfers between devices, shift(): lax.ppermute(array, axis, [(i, (i + step) % size) for i in range(size)])  18.1 us
    unnamed x20, local copies, waits for them, and re-layouts  11.2 us
    pallas_call x1, Pallas kernels, pack(): pl.pallas_call(functools.partial(pack_kernel, experts, extra), out_shape=...  1.72 us
  transfers between devices with their start and end apart: 16, of which 5 were waited for; matrix products, arithmetic and copies ran while one was open for 0% of the time, Pallas kernels for 34%

profile of v5, /device:TPU:0, one launch (start us, length us, event | category | flops | bytes accessed | tf_op | source)
XLA Modules:
  0.0 74.7 jit_solution(18366274975842844037)
XLA Ops:
  0.0 0.5 collective-permute-start.2
  0.5 0.1 collective-permute-start.3
  0.5 1.7 %shard_map.55.after_ref.refs_1_ = bf16[144,1024]{1,0:T(8,128)(2,1)} custom-call(bf16[128,1024]{1,0:T(8,128)(2,1)} %latent_ref.1, s32[4,128]{1,0:T(4,128)} %bitcast.8, f32[4,128]{1,0:T(4,128)} %bitcast.9), custom_call_target="tpu_custom_call" | custom-call | tf_op jit(solution)/shard_map/pallas_call | solution.py:34
  2.2 3.0 %collective-permute-start.1 = (bf16[144,1024]{1,0:T(8,128)(2,1)}, bf16[144,1024]{1,0:T(8,128)(2,1)S(1)}, u32[]{:S(2)}, u32[]{:S(2)}) collective-permute-start(bf16[144,1024]{1,0:T(8,128)(2,1)} %shard_map.55.after_ref.refs_1_), channel_id=1, source_target_pairs={{0,4},{4,8},{8,12},{12,0},{1,5},{5,9},{9,13},{13,1},{2,6},{6,10},{... | collective-permute-start | bytes 884744 | tf_op jit(solution)/shard_map/ppermute | solution.py:146
  5.3 1.5 %collective-permute-start = (bf16[144,1024]{1,0:T(8,128)(2,1)}, bf16[144,1024]{1,0:T(8,128)(2,1)}, u32[]{:S(2)}, u32[]{:S(2)}) collective-permute-start(bf16[144,1024]{1,0:T(8,128)(2,1)} %shard_map.55.after_ref.refs_1_), channel_id=1, source_target_pairs={{0,1},{1,0},{2,3},{3,2},{4,5},{5,4},{6,7},{7,6},{8,9},{9,8},{10,11... | collective-permute-start | bytes 884744 | tf_op jit(solution)/shard_map/ppermute | solution.py:146
  6.8 1.8 %copy-done.6 = bf16[1,1024,1344]{1,2,0:T(8,128)(2,1)S(1)} copy-done((bf16[1,1024,1344]{1,2,0:T(8,128)(2,1)S(1)}, bf16[1,1024,1344]{1,2,0:T(8,128)(2,1)}, u32[]{:S(2)}) %copy-start.6) | copy-done | bytes 2752536
  8.5 1.8 %copy-done.7 = bf16[1,1024,1344]{1,2,0:T(8,128)(2,1)S(1)} copy-done((bf16[1,1024,1344]{1,2,0:T(8,128)(2,1)S(1)}, bf16[1,1024,1344]{1,2,0:T(8,128)(2,1)}, u32[]{:S(2)}) %copy-start.7) | copy-done | bytes 2752536
  10.3 1.0 %copy-done.8 = bf16[144,1024]{1,0:T(8,128)(2,1)S(1)} copy-done((bf16[144,1024]{1,0:T(8,128)(2,1)S(1)}, bf16[144,1024]{1,0:T(8,128)(2,1)}, u32[]{:S(2)}) %copy-start.8) | copy-done | bytes 294936
  11.3 0.7 shard_map.56
  12.0 1.5 %copy-done = bf16[1,1344,1024]{2,1,0:T(8,128)(2,1)} copy-done((bf16[1,1344,1024]{2,1,0:T(8,128)(2,1)}, bf16[1,1344,1024]{2,1,0:T(8,128)(2,1)S(1)}, u32[]{:S(2)}) %copy-start) | copy-done | bytes 2752536
  13.5 1.6 %copy-done.3 = bf16[1,1344,1024]{2,1,0:T(8,128)(2,1)} copy-done((bf16[1,1344,1024]{2,1,0:T(8,128)(2,1)}, bf16[1,1344,1024]{2,1,0:T(8,128)(2,1)S(1)}, u32[]{:S(2)}) %copy-start.3) | copy-done | bytes 2752536
  15.1 0.0 collective-permute-done.1.refs_2_
  15.1 1.6 %collective-permute-start.5 = (bf16[144,1024]{1,0:T(8,128)(2,1)S(1)}, bf16[144,1024]{1,0:T(8,128)(2,1)S(1)}, u32[]{:S(2)}, u32[]{:S(2)}) collective-permute-start(bf16[144,1024]{1,0:T(8,128)(2,1)S(1)} %collective-permute-done.1.refs_2_), channel_id=1, source_target_pairs={{0,4},{4,8},{8,12},{12,0},{1,5},{5,9},{9,13},{13,1},{2,6},{6,10},{... | collective-permute-start | bytes 884744 | tf_op jit(solution)/shard_map/ppermute | solution.py:146
  16.7 0.5 collective-permute-start.4
  17.3 0.0 collective-permute-done.refs_0_
  17.3 0.0 collective-permute-done.2.refs_5_
  17.3 0.0 collective-permute-done.3.refs_6_
  17.3 1.8 %copy-done.1 = bf16[1,1344,1024]{2,1,0:T(8,128)(2,1)S(1)} copy-done((bf16[1,1344,1024]{2,1,0:T(8,128)(2,1)S(1)}, bf16[1,1344,1024]{2,1,0:T(8,128)(2,1)}, u32[]{:S(2)}) %copy-start.1) | copy-done | bytes 2752536
  19.1 1.8 %copy-done.4 = bf16[1,1344,1024]{2,1,0:T(8,128)(2,1)S(1)} copy-done((bf16[1,1344,1024]{2,1,0:T(8,128)(2,1)S(1)}, bf16[1,1344,1024]{2,1,0:T(8,128)(2,1)}, u32[]{:S(2)}) %copy-start.4) | copy-done | bytes 2752536
  20.9 6.9 %shard_map.57 = (bf16[128,1024]{1,0:T(8,128)(2,1)S(1)}, f32[128,1024]{1,0:T(8,128)S(1)}, f32[128,1024]{1,0:T(8,128)S(1)}) custom-call(s32[2]{0:T(128)S(1)} %fusion.ids_ref, bf16[144,1024]{1,0:T(8,128)(2,1)} %collective-permute-done.refs_0_, bf16[144,1024]{1,0:T(8,128)(2,1)S(1)} %copy-done.9, bf16[144,1024]{1,0:T(8,128)(2,1)S(1)} %collective-permute-done.1.refs_2_, ...), custom_call_target="tpu_custom_call" | custom-call | flops 3472883712 | bytes 12976128 | tf_op jit(solution)/shard_map/pallas_call | solution.py:128
  27.8 0.0 collective-permute-done.5.refs_2_
  27.8 1.6 %collective-permute-start.7 = (bf16[144,1024]{1,0:T(8,128)(2,1)S(1)}, bf16[144,1024]{1,0:T(8,128)(2,1)S(1)}, u32[]{:S(2)}, u32[]{:S(2)}) collective-permute-start(bf16[144,1024]{1,0:T(8,128)(2,1)S(1)} %collective-permute-done.5.refs_2_), channel_id=1, source_target_pairs={{0,4},{4,8},{8,12},{12,0},{1,5},{5,9},{9,13},{13,1},{2,6},{6,10},{... | collective-permute-start | bytes 884744 | tf_op jit(solution)/shard_map/ppermute | solution.py:146
  29.4 1.5 %collective-permute-start.6 = (bf16[144,1024]{1,0:T(8,128)(2,1)S(1)}, bf16[144,1024]{1,0:T(8,128)(2,1)S(1)}, u32[]{:S(2)}, u32[]{:S(2)}) collective-permute-start(bf16[144,1024]{1,0:T(8,128)(2,1)S(1)} %collective-permute-done.5.refs_2_), channel_id=1, source_target_pairs={{0,1},{1,0},{2,3},{3,2},{4,5},{5,4},{6,7},{7,6},{8,9},{9,8},{10,11... | collective-permute-start | bytes 884744 | tf_op jit(solution)/shard_map/ppermute | solution.py:146
  30.9 0.0 collective-permute-done.4.refs_1_
  30.9 5.6 %shard_map.58 = (bf16[128,1024]{1,0:T(8,128)(2,1)S(1)}, f32[128,1024]{1,0:T(8,128)S(1)}) custom-call(s32[2]{0:T(128)S(1)} %fusion.ids_ref, bf16[128,1024]{1,0:T(8,128)(2,1)S(1)} %get-tuple-element.38.refs_0_, bf16[144,1024]{1,0:T(8,128)(2,1)S(1)} %collective-permute-done.4.refs_1_, bf16[144,1024]{1,0:T(8,128)(2,1)S(1)} %collective-permute-done.5.refs_2_, ...), custom_call_target="tpu_custom_call" | custom-call | flops 2315255808 | bytes 12320768 | tf_op jit(solution)/shard_map/pallas_call | solution.py:128
  36.5 0.6 collective-permute-start.9
  37.1 0.3 collective-permute-done.7.refs_2_
  37.4 1.5 %collective-permute-start.11 = (bf16[144,1024]{1,0:T(8,128)(2,1)S(1)}, bf16[144,1024]{1,0:T(8,128)(2,1)S(1)}, u32[]{:S(2)}, u32[]{:S(2)}) collective-permute-start(bf16[144,1024]{1,0:T(8,128)(2,1)S(1)} %collective-permute-done.7.refs_2_), channel_id=1, source_target_pairs={{0,1},{1,0},{2,3},{3,2},{4,5},{5,4},{6,7},{7,6},{8,9},{9,8},{10,11... | collective-permute-start | bytes 884744 | tf_op jit(solution)/shard_map/ppermute | solution.py:146
  38.9 5.6 %shard_map.59 = (bf16[128,1024]{1,0:T(8,128)(2,1)S(1)}, bf16[128,1024]{1,0:T(8,128)(2,1)S(1)}) custom-call(s32[2]{0:T(128)S(1)} %fusion.ids_ref, bf16[128,1024]{1,0:T(8,128)(2,1)S(1)} %get-tuple-element.30.refs_0_, bf16[144,1024]{1,0:T(8,128)(2,1)S(1)} %collective-permute-done.6.refs_1_, bf16[144,1024]{1,0:T(8,128)(2,1)S(1)} %collective-permute-done.7.refs_2_, ...), custom_call_target="tpu_custom_call" | custom-call | flops 2315255808 | bytes 12320768 | tf_op jit(solution)/shard_map/pallas_call | solution.py:128
  44.5 1.3 %collective-permute-done.9 = bf16[128,1024]{1,0:T(8,128)(2,1)S(1)} collective-permute-done((bf16[128,1024]{1,0:T(8,128)(2,1)S(1)}, bf16[128,1024]{1,0:T(8,128)(2,1)S(1)}, u32[]{:S(2)}, u32[]{:S(2)}) %collective-permute-start.9) | collective-permute-done | bytes 262176 | tf_op jit(solution)/shard_map/ppermute | solution.py:146
  45.8 0.1 add_convert_fusion.2.refs_1_
  45.9 2.3 %collective-permute-start.10 = (bf16[128,1024]{1,0:T(8,128)(2,1)S(1)}, bf16[128,1024]{1,0:T(8,128)(2,1)S(1)}, u32[]{:S(2)}, u32[]{:S(2)}) collective-permute-start(bf16[128,1024]{1,0:T(8,128)(2,1)S(1)} %add_convert_fusion.2.refs_1_), channel_id=1, source_target_pairs={{0,12},{4,0},{8,4},{12,8},{1,13},{5,1},{9,5},{13,9},{2,14},{6,2},{... | collective-permute-start | bytes 786440 | tf_op jit(solution)/shard_map/ppermute | solution.py:146
  48.2 0.0 collective-permute-start.8
  48.2 0.5 collective-permute-start.14
  48.7 3.4 %collective-permute-done.11.refs_2_ = bf16[144,1024]{1,0:T(8,128)(2,1)S(1)} collective-permute-done((bf16[144,1024]{1,0:T(8,128)(2,1)S(1)}, bf16[144,1024]{1,0:T(8,128)(2,1)S(1)}, u32[]{:S(2)}, u32[]{:S(2)}) %collective-permute-start.11) | collective-permute-done | bytes 294944 | tf_op jit(solution)/shard_map/ppermute | solution.py:146
  52.1 5.0 %shard_map.60 = bf16[128,1024]{1,0:T(8,128)(2,1)S(1)} custom-call(s32[2]{0:T(128)S(1)} %fusion.ids_ref, bf16[128,1024]{1,0:T(8,128)(2,1)S(1)} %get-tuple-element.34.refs_0_, bf16[128,1024]{1,0:T(8,128)(2,1)S(1)} %add_convert_fusion.2.refs_1_, bf16[144,1024]{1,0:T(8,128)(2,1)S(1)} %collective-permute-done.11.refs_2_, bf16[1,1344,1024]{2,1,0:T(8,128)(2,1)S(1)} %copy-done.2, ...), custom_call_target="tpu_custom_call" | custom-call | flops 1157627904 | bytes 11665408 | tf_op jit(solution)/shard_map/pallas_call | solution.py:128
  57.2 0.2 collective-permute-start.12
  57.4 1.6 %collective-permute-start.13 = (bf16[128,1024]{1,0:T(8,128)(2,1)S(1)}, bf16[128,1024]{1,0:T(8,128)(2,1)S(1)}, u32[]{:S(2)}, u32[]{:S(2)}) collective-permute-start(bf16[128,1024]{1,0:T(8,128)(2,1)S(1)} %get-tuple-element.38.refs_0_), channel_id=1, source_target_pairs={{0,1},{1,0},{2,3},{3,2},{4,5},{5,4},{6,7},{7,6},{8,9},{9,8},{10,11... | collective-permute-start | bytes 786440 | tf_op jit(solution)/shard_map/ppermute | solution.py:146
  58.9 0.0 collective-permute-done.10
  59.0 0.0 collective-permute-done.8
  59.0 0.1 convert_add_fusion.1
  59.0 0.0 collective-permute-done.14
  59.0 0.1 add_convert_fusion.1
  59.1 1.3 %collective-permute-start.15 = (bf16[128,1024]{1,0:T(8,128)(2,1)S(1)}, bf16[128,1024]{1,0:T(8,128)(2,1)S(1)}, u32[]{:S(2)}, u32[]{:S(2)}) collective-permute-start(bf16[128,1024]{1,0:T(8,128)(2,1)S(1)} %add_convert_fusion.1), channel_id=1, source_target_pairs={{0,8},{4,12},{8,0},{12,4},{1,9},{5,13},{9,1},{13,5},{2,10},{6,14},... | collective-permute-start | bytes 786440 | tf_op jit(solution)/shard_map/ppermute | solution.py:146
  60.4 6.3 %collective-permute-done.13 = bf16[128,1024]{1,0:T(8,128)(2,1)S(1)} collective-permute-done((bf16[128,1024]{1,0:T(8,128)(2,1)S(1)}, bf16[128,1024]{1,0:T(8,128)(2,1)S(1)}, u32[]{:S(2)}, u32[]{:S(2)}) %collective-permute-start.13) | collective-permute-done | bytes 262176 | tf_op jit(solution)/shard_map/ppermute | solution.py:146
  66.8 0.1 convert_add_fusion
  66.9 7.0 %collective-permute-done.15 = bf16[128,1024]{1,0:T(8,128)(2,1)S(1)} collective-permute-done((bf16[128,1024]{1,0:T(8,128)(2,1)S(1)}, bf16[128,1024]{1,0:T(8,128)(2,1)S(1)}, u32[]{:S(2)}, u32[]{:S(2)}) %collective-permute-start.15) | collective-permute-done | bytes 262176 | tf_op jit(solution)/shard_map/ppermute | solution.py:146
  73.9 0.8 %add_convert_fusion = bf16[128,1024]{1,0:T(8,128)(2,1)} fusion(f32[128,1024]{1,0:T(8,128)S(1)} %convert_add_fusion, bf16[128,1024]{1,0:T(8,128)(2,1)S(1)} %collective-permute-done.15), kind=kLoop, calls=%fused_computation | loop fusion | flops 393216 | bytes 1048576 | tf_op jit(solution)/shard_map/convert_element_type | solution.py:219
  (16 shorter events, 0.0 us)
Async XLA Ops:
  0.0 17.3 %collective-permute-start.2 = (bf16[1,1344,1024]{2,1,0:T(8,128)(2,1)}, bf16[1,1344,1024]{2,1,0:T(8,128)(2,1)S(1)}, u32[]{:S(2)}, u32[]{:S(2)}) collective-permute-start(bf16[1,1344,1024]{2,1,0:T(8,128)(2,1)} %bitcast.4), channel_id=1, source_target_pairs={{0,2},{2,0},{1,3},{3,1},{4,6},{6,4},{5,7},{7,5},{8,10},{10,8},{9,1... | collective-permute-start | bytes 8257544 | tf_op jit(solution)/shard_map/ppermute | solution.py:146
  0.5 16.8 %collective-permute-start.3 = (bf16[1,1344,1024]{2,1,0:T(8,128)(2,1)}, bf16[1,1344,1024]{2,1,0:T(8,128)(2,1)}, u32[]{:S(2)}, u32[]{:S(2)}) collective-permute-start(bf16[1,1344,1024]{2,1,0:T(8,128)(2,1)} %bitcast.6), channel_id=1, source_target_pairs={{0,2},{2,0},{1,3},{3,1},{4,6},{6,4},{5,7},{7,5},{8,10},{10,8},{9,1... | collective-permute-start | bytes 8257544 | tf_op jit(solution)/shard_map/ppermute | solution.py:146
  2.2 12.9 %collective-permute-start.1 = (bf16[144,1024]{1,0:T(8,128)(2,1)}, bf16[144,1024]{1,0:T(8,128)(2,1)S(1)}, u32[]{:S(2)}, u32[]{:S(2)}) collective-permute-start(bf16[144,1024]{1,0:T(8,128)(2,1)} %shard_map.55.after_ref.refs_1_), channel_id=1, source_target_pairs={{0,4},{4,8},{8,12},{12,0},{1,5},{5,9},{9,13},{13,1},{2,6},{6,10},{... | collective-permute-start | bytes 884744 | tf_op jit(solution)/shard_map/ppermute | solution.py:146
  5.3 12.0 %collective-permute-start = (bf16[144,1024]{1,0:T(8,128)(2,1)}, bf16[144,1024]{1,0:T(8,128)(2,1)}, u32[]{:S(2)}, u32[]{:S(2)}) collective-permute-start(bf16[144,1024]{1,0:T(8,128)(2,1)} %shard_map.55.after_ref.refs_1_), channel_id=1, source_target_pairs={{0,1},{1,0},{2,3},{3,2},{4,5},{5,4},{6,7},{7,6},{8,9},{9,8},{10,11... | collective-permute-start | bytes 884744 | tf_op jit(solution)/shard_map/ppermute | solution.py:146
  6.7 1.8 %copy-start.6 = (bf16[1,1024,1344]{1,2,0:T(8,128)(2,1)S(1)}, bf16[1,1024,1344]{1,2,0:T(8,128)(2,1)}, u32[]{:S(2)}) copy-start(bf16[1,1024,1344]{1,2,0:T(8,128)(2,1)} %param.8) | copy-start | bytes 8257540
  8.5 1.8 %copy-start.7 = (bf16[1,1024,1344]{1,2,0:T(8,128)(2,1)S(1)}, bf16[1,1024,1344]{1,2,0:T(8,128)(2,1)}, u32[]{:S(2)}) copy-start(bf16[1,1024,1344]{1,2,0:T(8,128)(2,1)} %param.9) | copy-start | bytes 8257540
  10.3 1.0 %copy-start.8 = (bf16[144,1024]{1,0:T(8,128)(2,1)S(1)}, bf16[144,1024]{1,0:T(8,128)(2,1)}, u32[]{:S(2)}) copy-start(bf16[144,1024]{1,0:T(8,128)(2,1)} %shard_map.55.after_ref.refs_1_) | copy-start | bytes 884740
  11.3 6.0 %copy-start.9 = (bf16[144,1024]{1,0:T(8,128)(2,1)S(1)}, bf16[144,1024]{1,0:T(8,128)(2,1)}, u32[]{:S(2)}) copy-start(bf16[144,1024]{1,0:T(8,128)(2,1)} %shard_map.55.after_ref.refs_1_) | copy-start | bytes 884740
  12.0 1.5 %copy-start = (bf16[1,1344,1024]{2,1,0:T(8,128)(2,1)}, bf16[1,1344,1024]{2,1,0:T(8,128)(2,1)S(1)}, u32[]{:S(2)}) copy-start(bf16[1,1344,1024]{2,1,0:T(8,128)(2,1)S(1)} %get-tuple-element.25.refs_3_) | copy-start | bytes 8257540
  13.5 1.6 %copy-start.3 = (bf16[1,1344,1024]{2,1,0:T(8,128)(2,1)}, bf16[1,1344,1024]{2,1,0:T(8,128)(2,1)S(1)}, u32[]{:S(2)}) copy-start(bf16[1,1344,1024]{2,1,0:T(8,128)(2,1)S(1)} %get-tuple-element.27.refs_4_) | copy-start | bytes 8257540
  15.1 12.7 %collective-permute-start.5 = (bf16[144,1024]{1,0:T(8,128)(2,1)S(1)}, bf16[144,1024]{1,0:T(8,128)(2,1)S(1)}, u32[]{:S(2)}, u32[]{:S(2)}) collective-permute-start(bf16[144,1024]{1,0:T(8,128)(2,1)S(1)} %collective-permute-done.1.refs_2_), channel_id=1, source_target_pairs={{0,4},{4,8},{8,12},{12,0},{1,5},{5,9},{9,13},{13,1},{2,6},{6,10},{... | collective-permute-start | bytes 884744 | tf_op jit(solution)/shard_map/ppermute | solution.py:146
  16.7 14.2 %collective-permute-start.4 = (bf16[144,1024]{1,0:T(8,128)(2,1)S(1)}, bf16[144,1024]{1,0:T(8,128)(2,1)S(1)}, u32[]{:S(2)}, u32[]{:S(2)}) collective-permute-start(bf16[144,1024]{1,0:T(8,128)(2,1)S(1)} %collective-permute-done.1.refs_2_), channel_id=1, source_target_pairs={{0,1},{1,0},{2,3},{3,2},{4,5},{5,4},{6,7},{7,6},{8,9},{9,8},{10,11... | collective-permute-start | bytes 884744 | tf_op jit(solution)/shard_map/ppermute | solution.py:146
  17.3 1.8 %copy-start.1 = (bf16[1,1344,1024]{2,1,0:T(8,128)(2,1)S(1)}, bf16[1,1344,1024]{2,1,0:T(8,128)(2,1)}, u32[]{:S(2)}) copy-start(bf16[1,1344,1024]{2,1,0:T(8,128)(2,1)} %copy-done) | copy-start | bytes 8257540
  19.1 1.8 %copy-start.4 = (bf16[1,1344,1024]{2,1,0:T(8,128)(2,1)S(1)}, bf16[1,1344,1024]{2,1,0:T(8,128)(2,1)}, u32[]{:S(2)}) copy-start(bf16[1,1344,1024]{2,1,0:T(8,128)(2,1)} %copy-done.3) | copy-start | bytes 8257540
  20.9 10.0 %copy-start.2 = (bf16[1,1344,1024]{2,1,0:T(8,128)(2,1)S(1)}, bf16[1,1344,1024]{2,1,0:T(8,128)(2,1)}, u32[]{:S(2)}) copy-start(bf16[1,1344,1024]{2,1,0:T(8,128)(2,1)} %copy-done) | copy-start | bytes 8257540
  20.9 10.0 %copy-start.5 = (bf16[1,1344,1024]{2,1,0:T(8,128)(2,1)S(1)}, bf16[1,1344,1024]{2,1,0:T(8,128)(2,1)}, u32[]{:S(2)}) copy-start(bf16[1,1344,1024]{2,1,0:T(8,128)(2,1)} %copy-done.3) | copy-start | bytes 8257540
  27.8 9.6 %collective-permute-start.7 = (bf16[144,1024]{1,0:T(8,128)(2,1)S(1)}, bf16[144,1024]{1,0:T(8,128)(2,1)S(1)}, u32[]{:S(2)}, u32[]{:S(2)}) collective-permute-start(bf16[144,1024]{1,0:T(8,128)(2,1)S(1)} %collective-permute-done.5.refs_2_), channel_id=1, source_target_pairs={{0,4},{4,8},{8,12},{12,0},{1,5},{5,9},{9,13},{13,1},{2,6},{6,10},{... | collective-permute-start | bytes 884744 | tf_op jit(solution)/shard_map/ppermute | solution.py:146
  29.4 9.5 %collective-permute-start.6 = (bf16[144,1024]{1,0:T(8,128)(2,1)S(1)}, bf16[144,1024]{1,0:T(8,128)(2,1)S(1)}, u32[]{:S(2)}, u32[]{:S(2)}) collective-permute-start(bf16[144,1024]{1,0:T(8,128)(2,1)S(1)} %collective-permute-done.5.refs_2_), channel_id=1, source_target_pairs={{0,1},{1,0},{2,3},{3,2},{4,5},{5,4},{6,7},{7,6},{8,9},{9,8},{10,11... | collective-permute-start | bytes 884744 | tf_op jit(solution)/shard_map/ppermute | solution.py:146
  36.5 9.3 %collective-permute-start.9 = (bf16[128,1024]{1,0:T(8,128)(2,1)S(1)}, bf16[128,1024]{1,0:T(8,128)(2,1)S(1)}, u32[]{:S(2)}, u32[]{:S(2)}) collective-permute-start(bf16[128,1024]{1,0:T(8,128)(2,1)S(1)} %get-tuple-element.30.refs_0_), channel_id=1, source_target_pairs={{0,1},{1,0},{2,3},{3,2},{4,5},{5,4},{6,7},{7,6},{8,9},{9,8},{10,11... | collective-permute-start | bytes 786440 | tf_op jit(solution)/shard_map/ppermute | solution.py:146
  37.4 14.7 %collective-permute-start.11 = (bf16[144,1024]{1,0:T(8,128)(2,1)S(1)}, bf16[144,1024]{1,0:T(8,128)(2,1)S(1)}, u32[]{:S(2)}, u32[]{:S(2)}) collective-permute-start(bf16[144,1024]{1,0:T(8,128)(2,1)S(1)} %collective-permute-done.7.refs_2_), channel_id=1, source_target_pairs={{0,1},{1,0},{2,3},{3,2},{4,5},{5,4},{6,7},{7,6},{8,9},{9,8},{10,11... | collective-permute-start | bytes 884744 | tf_op jit(solution)/shard_map/ppermute | solution.py:146
  45.9 13.1 %collective-permute-start.10 = (bf16[128,1024]{1,0:T(8,128)(2,1)S(1)}, bf16[128,1024]{1,0:T(8,128)(2,1)S(1)}, u32[]{:S(2)}, u32[]{:S(2)}) collective-permute-start(bf16[128,1024]{1,0:T(8,128)(2,1)S(1)} %add_convert_fusion.2.refs_1_), channel_id=1, source_target_pairs={{0,12},{4,0},{8,4},{12,8},{1,13},{5,1},{9,5},{13,9},{2,14},{6,2},{... | collective-permute-start | bytes 786440 | tf_op jit(solution)/shard_map/ppermute | solution.py:146
  48.2 10.8 %collective-permute-start.8 = (bf16[128,1024]{1,0:T(8,128)(2,1)S(1)}, bf16[128,1024]{1,0:T(8,128)(2,1)S(1)}, u32[]{:S(2)}, u32[]{:S(2)}) collective-permute-start(bf16[128,1024]{1,0:T(8,128)(2,1)S(1)} %get-tuple-element.32), channel_id=1, source_target_pairs={{0,4},{4,8},{8,12},{12,0},{1,5},{5,9},{9,13},{13,1},{2,6},{6,10},{... | collective-permute-start | bytes 786440 | tf_op jit(solution)/shard_map/ppermute | solution.py:146
  48.2 10.8 %collective-permute-start.14 = (bf16[128,1024]{1,0:T(8,128)(2,1)S(1)}, bf16[128,1024]{1,0:T(8,128)(2,1)S(1)}, u32[]{:S(2)}, u32[]{:S(2)}) collective-permute-start(bf16[128,1024]{1,0:T(8,128)(2,1)S(1)} %get-tuple-element.34.refs_0_), channel_id=1, source_target_pairs={{0,1},{1,0},{2,3},{3,2},{4,5},{5,4},{6,7},{7,6},{8,9},{9,8},{10,11... | collective-permute-start | bytes 786440 | tf_op jit(solution)/shard_map/ppermute | solution.py:146
  57.2 9.6 %collective-permute-start.12 = (bf16[128,1024]{1,0:T(8,128)(2,1)S(1)}, bf16[128,1024]{1,0:T(8,128)(2,1)S(1)}, u32[]{:S(2)}, u32[]{:S(2)}) collective-permute-start(bf16[128,1024]{1,0:T(8,128)(2,1)S(1)} %shard_map.60), channel_id=1, source_target_pairs={{0,5},{1,4},{4,9},{5,8},{8,13},{9,12},{12,1},{13,0},{2,7},{3,6},{6... | collective-permute-start | bytes 786440 | tf_op jit(solution)/shard_map/ppermute | solution.py:160
  57.4 9.4 %collective-permute-start.13 = (bf16[128,1024]{1,0:T(8,128)(2,1)S(1)}, bf16[128,1024]{1,0:T(8,128)(2,1)S(1)}, u32[]{:S(2)}, u32[]{:S(2)}) collective-permute-start(bf16[128,1024]{1,0:T(8,128)(2,1)S(1)} %get-tuple-element.38.refs_0_), channel_id=1, source_target_pairs={{0,1},{1,0},{2,3},{3,2},{4,5},{5,4},{6,7},{7,6},{8,9},{9,8},{10,11... | collective-permute-start | bytes 786440 | tf_op jit(solution)/shard_map/ppermute | solution.py:146
  59.1 14.8 %collective-permute-start.15 = (bf16[128,1024]{1,0:T(8,128)(2,1)S(1)}, bf16[128,1024]{1,0:T(8,128)(2,1)S(1)}, u32[]{:S(2)}, u32[]{:S(2)}) collective-permute-start(bf16[128,1024]{1,0:T(8,128)(2,1)S(1)} %add_convert_fusion.1), channel_id=1, source_target_pairs={{0,8},{4,12},{8,0},{12,4},{1,9},{5,13},{9,1},{13,5},{2,10},{6,14},... | collective-permute-start | bytes 786440 | tf_op jit(solution)/shard_map/ppermute | solution.py:146

commit v6 on v5

--- a/solution.py
+++ b/solution.py
@@ -36,6 +36,7 @@
         out_shape=jax.ShapeDtypeStruct((block + extra, width), jnp.bfloat16),
         in_specs=[pl.BlockSpec(memory_space=pltpu.VMEM)] * 3,
         out_specs=pl.BlockSpec(memory_space=pltpu.VMEM),
+        compiler_params=pltpu.CompilerParams(vmem_limit_bytes=4 * 1024 * 1024),
     )(latent, routes.T, gates.T)
 
 
@@ -62,7 +63,8 @@
     )(after, *arrays)
 
 
-def expert_kernel(block, slots, unit, number, blocks, waits, ids_ref, *refs):
+def expert_kernel(block, slots, unit, number, blocks, waits, *refs):
+    first, core = lax.axis_index("z") * number, lax.axis_index("core")
     refs = refs[waits:]
     x_refs, tables, out_refs = refs[:blocks], refs[blocks : blocks + 2 * number], refs[blocks + 2 * number :]
     extra = x_refs[0].shape[0] - block
@@ -84,7 +86,7 @@
     sums = [0.0] * blocks
     for n in range(number):
         up_ref, down_ref = tables[2 * n], tables[2 * n + 1]
-        mine = row == ids_ref[n]
+        mine = row == first + lax.rem(core + number - n, number)
         picks, scales, rows = [], [], []
         for group, size in zip(groups, sizes):
             slot = lax.broadcasted_iota(jnp.int32, (size, block), 0)
@@ -120,7 +122,7 @@
         out_refs[b][...] = sums[b].astype(out_refs[b].dtype)
 
 
-def run_experts(ids, after, arrived, tables, kinds, block, slots):
+def run_experts(after, arrived, tables, kinds, block, slots):
     blocks, number = len(arrived), len(tables) // 2
     hidden, width = tables[0].shape[1:]
     unit = 16 // math.gcd(16, slots)
@@ -128,8 +130,7 @@
     return pl.pallas_call(
         functools.partial(expert_kernel, block, slots, unit, number, blocks, len(after)),
         out_shape=[jax.ShapeDtypeStruct((block, width), kind) for kind in kinds],
-        in_specs=[pl.BlockSpec(memory_space=pltpu.SMEM)]
-        + [pl.BlockSpec(memory_space=pl.ANY)] * len(after)
+        in_specs=[pl.BlockSpec(memory_space=pl.ANY)] * len(after)
         + [whole] * (blocks + len(tables)),
         out_specs=[whole] * blocks,
         compiler_params=pltpu.CompilerParams(vmem_limit_bytes=30 * 1024 * 1024),
@@ -138,7 +139,7 @@
             bytes_accessed=5 * blocks * block * width + 2 * len(tables) * width * hidden,
             transcendentals=0,
         ),
-    )(ids, *after, *arrived, *tables)
+    )(*after, *arrived, *tables)
 
 
 def shift(array, axis, step):
@@ -168,8 +169,6 @@
     slots = min(block, 3 * block * top // (2 * experts))
     own = [jnp.swapaxes(up_weight, 1, 2), jnp.swapaxes(down_weight, 1, 2)]
     moved = [shift(table, "core", step) for step in range(1, cores) for table in own]
-    core = lax.axis_index("core")
-    ids = lax.axis_index("z") * cores + (core + cores - jnp.arange(cores, dtype=jnp.int32)) % cores
     ring = [pack(latent, routes, gates, experts)]
     tables = [*stage(ring[0], own), *moved]
     ring.append(follow(shift(ring[0], "z", 1), tables[0]))
@@ -196,7 +195,7 @@
             totals[j - 2] = total(j - 2, after[0])
             after.append(totals[j - 2])
         partial = run_experts(
-            ids, after, handed + [ring[r] for r in fresh], tables, kinds, block, slots
+            after, handed + [ring[r] for r in fresh], tables, kinds, block, slots
         )
         after = [partial[0]]
         if j + 2 < depth:

time: 75.1 us -> 70.9 us (0.944)
  waiting for transfers between devices: 18.4 us -> 31.7 us
  Pallas kernels: 25.6 us -> 16.5 us
  local copies, waits for them, and re-layouts: 11.2 us -> 5.87 us
  starting transfers between devices: 18.3 us -> 15.5 us
    ppermute x15, waiting for transfers between devices: 18.4 us -> 31.5 us  [shift(): lax.ppermute(array, axis, [(i, (i + step) % size) for i in range(size)])]
    pallas_call x4, Pallas kernels: 23.2 us -> 15.8 us  [run_experts(): pl.pallas_call(functools.partial(expert_kernel, block, slots, unit, numbe...]
    unnamed x20 -> x10, local copies, waits for them, and re-layouts: 11.2 us -> 5.87 us
    ppermute x15, starting transfers between devices: 18.1 us -> 15.4 us  [shift(): lax.ppermute(array, axis, [(i, (i + step) % size) for i in range(size)])]
    pallas_call x1, Pallas kernels: 1.72 us -> 0.03 us  [pack(): pl.pallas_call(functools.partial(pack_kernel, experts, extra), out_shape=...]
  transfers between devices with their start and end apart: 16 -> 16, of which waited for: 5 -> 9; matrix products, arithmetic and copies ran while one was open for 0% -> 0% of each run, Pallas kernels for 34% -> 23%
where the time goes in v6:
time: 70.9 us; the launch traced here: 70.7 us
  waiting for transfers between devices  31.7 us (45%)
  Pallas kernels  16.5 us (23%)
  starting transfers between devices  15.5 us (22%)
  local copies, waits for them, and re-layouts  5.87 us (8%)
  other arithmetic  1.05 us (1%)
    ppermute x15, waiting for transfers between devices, shift(): lax.ppermute(array, axis, [(i, (i + step) % size) for i in range(size)])  31.5 us
    pallas_call x4, Pallas kernels, run_experts(): pl.pallas_call(functools.partial(expert_kernel, block, slots, unit, numbe...  15.8 us
    ppermute x15, starting transfers between devices, shift(): lax.ppermute(array, axis, [(i, (i + step) % size) for i in range(size)])  15.4 us
    unnamed x10, local copies, waits for them, and re-layouts  5.87 us
  transfers between devices with their start and end apart: 16, of which 9 were waited for; matrix products, arithmetic and copies ran while one was open for 0% of the time, Pallas kernels for 23%

profile of v6, /device:TPU:0, one launch (start us, length us, event | category | flops | bytes accessed | tf_op | source)
XLA Modules:
  0.0 70.7 jit_solution(3394268181579034619)
XLA Ops:
  0.0 0.5 collective-permute-start.2
  0.5 0.1 collective-permute-start.3
  0.5 0.0 copy-start.2
  0.5 0.9 %copy-done.2 = bf16[128,1024]{1,0:T(8,128)(2,1)S(1)} copy-done((bf16[128,1024]{1,0:T(8,128)(2,1)S(1)}, bf16[128,1024]{1,0:T(8,128)(2,1)}, u32[]{:S(2)}) %copy-start.2) | copy-done | bytes 262168
  1.5 0.7 copy-done.3
  2.1 0.7 copy-done.4
  2.9 3.1 %collective-permute-start.1 = (bf16[144,1024]{1,0:T(8,128)(2,1)S(1)}, bf16[144,1024]{1,0:T(8,128)(2,1)S(1)}, u32[]{:S(2)}, u32[]{:S(2)}) collective-permute-start(bf16[144,1024]{1,0:T(8,128)(2,1)S(1)} %shard_map.55.after_ref.refs_1_), channel_id=1, source_target_pairs={{0,4},{4,8},{8,12},{12,0},{1,5},{5,9},{9,13},{13,1},{2,6},{6,10},{... | collective-permute-start | bytes 884744 | tf_op jit(solution)/shard_map/ppermute | solution.py:147
  5.9 1.5 %collective-permute-start = (bf16[144,1024]{1,0:T(8,128)(2,1)S(1)}, bf16[144,1024]{1,0:T(8,128)(2,1)S(1)}, u32[]{:S(2)}, u32[]{:S(2)}) collective-permute-start(bf16[144,1024]{1,0:T(8,128)(2,1)S(1)} %shard_map.55.after_ref.refs_1_), channel_id=1, source_target_pairs={{0,1},{1,0},{2,3},{3,2},{4,5},{5,4},{6,7},{7,6},{8,9},{9,8},{10,11... | collective-permute-start | bytes 884744 | tf_op jit(solution)/shard_map/ppermute | solution.py:147
  7.4 1.8 %copy-done = bf16[1,1024,1344]{1,2,0:T(8,128)(2,1)S(1)} copy-done((bf16[1,1024,1344]{1,2,0:T(8,128)(2,1)S(1)}, bf16[1,1024,1344]{1,2,0:T(8,128)(2,1)}, u32[]{:S(2)}) %copy-start) | copy-done | bytes 2752536
  9.2 1.8 %copy-done.1 = bf16[1,1024,1344]{1,2,0:T(8,128)(2,1)S(1)} copy-done((bf16[1,1024,1344]{1,2,0:T(8,128)(2,1)S(1)}, bf16[1,1024,1344]{1,2,0:T(8,128)(2,1)}, u32[]{:S(2)}) %copy-start.1) | copy-done | bytes 2752536
  11.0 0.7 %shard_map.56 = (bf16[1,1344,1024]{2,1,0:T(8,128)(2,1)S(1)}, bf16[1,1344,1024]{2,1,0:T(8,128)(2,1)S(1)}) custom-call(bf16[144,1024]{1,0:T(8,128)(2,1)S(1)} %shard_map.55.after_ref.refs_1_, bf16[1,1344,1024]{2,1,0:T(8,128)(2,1)S(1)} %bitcast.5, bf16[1,1344,1024]{2,1,0:T(8,128)(2,1)S(1)} %bitcast.7), custom_call_target="tpu_custom_call" | custom-call | tf_op jit(solution)/shard_map/pallas_call | solution.py:55
  11.7 3.4 %collective-permute-done.1.refs_2_ = bf16[144,1024]{1,0:T(8,128)(2,1)S(1)} collective-permute-done((bf16[144,1024]{1,0:T(8,128)(2,1)S(1)}, bf16[144,1024]{1,0:T(8,128)(2,1)S(1)}, u32[]{:S(2)}, u32[]{:S(2)}) %collective-permute-start.1) | collective-permute-done | bytes 294944 | tf_op jit(solution)/shard_map/ppermute | solution.py:147
  15.1 0.0 collective-permute-start.5
  15.1 1.5 %collective-permute-start.4 = (bf16[144,1024]{1,0:T(8,128)(2,1)S(1)}, bf16[144,1024]{1,0:T(8,128)(2,1)S(1)}, u32[]{:S(2)}, u32[]{:S(2)}) collective-permute-start(bf16[144,1024]{1,0:T(8,128)(2,1)S(1)} %collective-permute-done.1.refs_2_), channel_id=1, source_target_pairs={{0,1},{1,0},{2,3},{3,2},{4,5},{5,4},{6,7},{7,6},{8,9},{9,8},{10,11... | collective-permute-start | bytes 884744 | tf_op jit(solution)/shard_map/ppermute | solution.py:147
  16.6 0.0 collective-permute-done.refs_0_
  16.6 0.0 collective-permute-done.2.refs_5_
  16.6 0.0 collective-permute-done.3.refs_6_
  16.6 4.9 %shard_map.57 = (bf16[128,1024]{1,0:T(8,128)(2,1)S(1)}, f32[128,1024]{1,0:T(8,128)S(1)}, f32[128,1024]{1,0:T(8,128)S(1)}) custom-call(bf16[144,1024]{1,0:T(8,128)(2,1)S(1)} %collective-permute-done.refs_0_, bf16[144,1024]{1,0:T(8,128)(2,1)S(1)} %shard_map.55.after_ref.refs_1_, bf16[144,1024]{1,0:T(8,128)(2,1)S(1)} %collective-permute-done.1.refs_2_, ...), custom_call_target="tpu_custom_call" | custom-call | flops 3472883712 | bytes 12976128 | tf_op jit(solution)/shard_map/pallas_call | solution.py:130
  21.5 3.8 %collective-permute-done.5.refs_2_ = bf16[144,1024]{1,0:T(8,128)(2,1)S(1)} collective-permute-done((bf16[144,1024]{1,0:T(8,128)(2,1)S(1)}, bf16[144,1024]{1,0:T(8,128)(2,1)S(1)}, u32[]{:S(2)}, u32[]{:S(2)}) %collective-permute-start.5) | collective-permute-done | bytes 294944 | tf_op jit(solution)/shard_map/ppermute | solution.py:147
  25.3 0.0 collective-permute-start.7
  25.3 1.3 %collective-permute-start.6 = (bf16[144,1024]{1,0:T(8,128)(2,1)S(1)}, bf16[144,1024]{1,0:T(8,128)(2,1)S(1)}, u32[]{:S(2)}, u32[]{:S(2)}) collective-permute-start(bf16[144,1024]{1,0:T(8,128)(2,1)S(1)} %collective-permute-done.5.refs_2_), channel_id=1, source_target_pairs={{0,1},{1,0},{2,3},{3,2},{4,5},{5,4},{6,7},{7,6},{8,9},{9,8},{10,11... | collective-permute-start | bytes 884744 | tf_op jit(solution)/shard_map/ppermute | solution.py:147
  26.6 0.0 collective-permute-done.4.refs_1_
  26.6 3.8 %shard_map.58 = (bf16[128,1024]{1,0:T(8,128)(2,1)S(1)}, f32[128,1024]{1,0:T(8,128)S(1)}) custom-call(bf16[128,1024]{1,0:T(8,128)(2,1)S(1)} %get-tuple-element.38.refs_0_, bf16[144,1024]{1,0:T(8,128)(2,1)S(1)} %collective-permute-done.4.refs_1_, bf16[144,1024]{1,0:T(8,128)(2,1)S(1)} %collective-permute-done.5.refs_2_, ...), custom_call_target="tpu_custom_call" | custom-call | flops 2315255808 | bytes 12320768 | tf_op jit(solution)/shard_map/pallas_call | solution.py:130
  30.4 0.8 %collective-permute-start.9 = (bf16[128,1024]{1,0:T(8,128)(2,1)S(1)}, bf16[128,1024]{1,0:T(8,128)(2,1)S(1)}, u32[]{:S(2)}, u32[]{:S(2)}) collective-permute-start(bf16[128,1024]{1,0:T(8,128)(2,1)S(1)} %get-tuple-element.30.refs_0_), channel_id=1, source_target_pairs={{0,1},{1,0},{2,3},{3,2},{4,5},{5,4},{6,7},{7,6},{8,9},{9,8},{10,11... | collective-permute-start | bytes 786440 | tf_op jit(solution)/shard_map/ppermute | solution.py:147
  31.2 3.3 %collective-permute-done.7.refs_2_ = bf16[144,1024]{1,0:T(8,128)(2,1)S(1)} collective-permute-done((bf16[144,1024]{1,0:T(8,128)(2,1)S(1)}, bf16[144,1024]{1,0:T(8,128)(2,1)S(1)}, u32[]{:S(2)}, u32[]{:S(2)}) %collective-permute-start.7) | collective-permute-done | bytes 294944 | tf_op jit(solution)/shard_map/ppermute | solution.py:147
  34.6 1.0 %collective-permute-start.11 = (bf16[144,1024]{1,0:T(8,128)(2,1)S(1)}, bf16[144,1024]{1,0:T(8,128)(2,1)S(1)}, u32[]{:S(2)}, u32[]{:S(2)}) collective-permute-start(bf16[144,1024]{1,0:T(8,128)(2,1)S(1)} %collective-permute-done.7.refs_2_), channel_id=1, source_target_pairs={{0,1},{1,0},{2,3},{3,2},{4,5},{5,4},{6,7},{7,6},{8,9},{9,8},{10,11... | collective-permute-start | bytes 884744 | tf_op jit(solution)/shard_map/ppermute | solution.py:147
  35.6 0.0 collective-permute-done.6.refs_1_
  35.6 3.8 %shard_map.59 = (bf16[128,1024]{1,0:T(8,128)(2,1)S(1)}, bf16[128,1024]{1,0:T(8,128)(2,1)S(1)}) custom-call(bf16[128,1024]{1,0:T(8,128)(2,1)S(1)} %get-tuple-element.30.refs_0_, bf16[144,1024]{1,0:T(8,128)(2,1)S(1)} %collective-permute-done.6.refs_1_, bf16[144,1024]{1,0:T(8,128)(2,1)S(1)} %collective-permute-done.7.refs_2_, ...), custom_call_target="tpu_custom_call" | custom-call | flops 2315255808 | bytes 12320768 | tf_op jit(solution)/shard_map/pallas_call | solution.py:130
  39.4 0.6 collective-permute-done.9
  40.0 0.1 add_convert_fusion.2.refs_1_
  40.1 3.6 %collective-permute-start.10 = (bf16[128,1024]{1,0:T(8,128)(2,1)S(1)}, bf16[128,1024]{1,0:T(8,128)(2,1)S(1)}, u32[]{:S(2)}, u32[]{:S(2)}) collective-permute-start(bf16[128,1024]{1,0:T(8,128)(2,1)S(1)} %add_convert_fusion.2.refs_1_), channel_id=1, source_target_pairs={{0,12},{4,0},{8,4},{12,8},{1,13},{5,1},{9,5},{13,9},{2,14},{6,2},{... | collective-permute-start | bytes 786440 | tf_op jit(solution)/shard_map/ppermute | solution.py:147
  43.7 0.0 collective-permute-start.8
  43.7 1.0 %collective-permute-start.14 = (bf16[128,1024]{1,0:T(8,128)(2,1)S(1)}, bf16[128,1024]{1,0:T(8,128)(2,1)S(1)}, u32[]{:S(2)}, u32[]{:S(2)}) collective-permute-start(bf16[128,1024]{1,0:T(8,128)(2,1)S(1)} %get-tuple-element.34.refs_0_), channel_id=1, source_target_pairs={{0,1},{1,0},{2,3},{3,2},{4,5},{5,4},{6,7},{7,6},{8,9},{9,8},{10,11... | collective-permute-start | bytes 786440 | tf_op jit(solution)/shard_map/ppermute | solution.py:147
  44.7 1.7 %collective-permute-done.11.refs_2_ = bf16[144,1024]{1,0:T(8,128)(2,1)S(1)} collective-permute-done((bf16[144,1024]{1,0:T(8,128)(2,1)S(1)}, bf16[144,1024]{1,0:T(8,128)(2,1)S(1)}, u32[]{:S(2)}, u32[]{:S(2)}) %collective-permute-start.11) | collective-permute-done | bytes 294944 | tf_op jit(solution)/shard_map/ppermute | solution.py:147
  46.3 3.3 %shard_map.60 = bf16[128,1024]{1,0:T(8,128)(2,1)S(1)} custom-call(bf16[128,1024]{1,0:T(8,128)(2,1)S(1)} %get-tuple-element.34.refs_0_, bf16[128,1024]{1,0:T(8,128)(2,1)S(1)} %add_convert_fusion.2.refs_1_, bf16[144,1024]{1,0:T(8,128)(2,1)S(1)} %collective-permute-done.11.refs_2_, bf16[1,1344,1024]{2,1,0:T(8,128)(2,1)S(1)} %get-tuple-element.25.refs_3_, ...), custom_call_target="tpu_custom_call" | custom-call | flops 1157627904 | bytes 11665408 | tf_op jit(solution)/shard_map/pallas_call | solution.py:130
  49.6 0.1 collective-permute-start.12
  49.7 1.1 %collective-permute-start.13 = (bf16[128,1024]{1,0:T(8,128)(2,1)S(1)}, bf16[128,1024]{1,0:T(8,128)(2,1)S(1)}, u32[]{:S(2)}, u32[]{:S(2)}) collective-permute-start(bf16[128,1024]{1,0:T(8,128)(2,1)S(1)} %get-tuple-element.38.refs_0_), channel_id=1, source_target_pairs={{0,1},{1,0},{2,3},{3,2},{4,5},{5,4},{6,7},{7,6},{8,9},{9,8},{10,11... | collective-permute-start | bytes 786440 | tf_op jit(solution)/shard_map/ppermute | solution.py:147
  50.7 0.0 collective-permute-done.10
  50.7 5.3 %collective-permute-done.8 = bf16[128,1024]{1,0:T(8,128)(2,1)S(1)} collective-permute-done((bf16[128,1024]{1,0:T(8,128)(2,1)S(1)}, bf16[128,1024]{1,0:T(8,128)(2,1)S(1)}, u32[]{:S(2)}, u32[]{:S(2)}) %collective-permute-start.8) | collective-permute-done | bytes 262176 | tf_op jit(solution)/shard_map/ppermute | solution.py:147
  56.1 0.1 convert_add_fusion.1
  56.1 0.0 collective-permute-done.14
  56.1 0.1 add_convert_fusion.1
  56.2 0.1 collective-permute-start.15
  56.3 5.2 %collective-permute-done.13 = bf16[128,1024]{1,0:T(8,128)(2,1)S(1)} collective-permute-done((bf16[128,1024]{1,0:T(8,128)(2,1)S(1)}, bf16[128,1024]{1,0:T(8,128)(2,1)S(1)}, u32[]{:S(2)}, u32[]{:S(2)}) %collective-permute-start.13) | collective-permute-done | bytes 262176 | tf_op jit(solution)/shard_map/ppermute | solution.py:147
  61.5 0.2 collective-permute-done.12
  61.7 0.1 convert_add_fusion
  61.8 8.1 %collective-permute-done.15 = bf16[128,1024]{1,0:T(8,128)(2,1)S(1)} collective-permute-done((bf16[128,1024]{1,0:T(8,128)(2,1)S(1)}, bf16[128,1024]{1,0:T(8,128)(2,1)S(1)}, u32[]{:S(2)}, u32[]{:S(2)}) %collective-permute-start.15) | collective-permute-done | bytes 262176 | tf_op jit(solution)/shard_map/ppermute | solution.py:147
  69.9 0.8 %add_convert_fusion = bf16[128,1024]{1,0:T(8,128)(2,1)} fusion(f32[128,1024]{1,0:T(8,128)S(1)} %convert_add_fusion, bf16[128,1024]{1,0:T(8,128)(2,1)S(1)} %collective-permute-done.15), kind=kLoop, calls=%fused_computation | loop fusion | flops 393216 | bytes 1048576 | tf_op jit(solution)/shard_map/convert_element_type | solution.py:218
  (5 shorter events, 0.0 us)
Async XLA Ops:
  0.0 16.6 %collective-permute-start.2 = (bf16[1,1344,1024]{2,1,0:T(8,128)(2,1)}, bf16[1,1344,1024]{2,1,0:T(8,128)(2,1)S(1)}, u32[]{:S(2)}, u32[]{:S(2)}) collective-permute-start(bf16[1,1344,1024]{2,1,0:T(8,128)(2,1)} %bitcast.4), channel_id=1, source_target_pairs={{0,2},{2,0},{1,3},{3,1},{4,6},{6,4},{5,7},{7,5},{8,10},{10,8},{9,1... | collective-permute-start | bytes 8257544 | tf_op jit(solution)/shard_map/ppermute | solution.py:147
  0.5 16.2 %collective-permute-start.3 = (bf16[1,1344,1024]{2,1,0:T(8,128)(2,1)}, bf16[1,1344,1024]{2,1,0:T(8,128)(2,1)S(1)}, u32[]{:S(2)}, u32[]{:S(2)}) collective-permute-start(bf16[1,1344,1024]{2,1,0:T(8,128)(2,1)} %bitcast.6), channel_id=1, source_target_pairs={{0,2},{2,0},{1,3},{3,1},{4,6},{6,4},{5,7},{7,5},{8,10},{10,8},{9,1... | collective-permute-start | bytes 8257544 | tf_op jit(solution)/shard_map/ppermute | solution.py:147
  0.5 0.9 %copy-start.2 = (bf16[128,1024]{1,0:T(8,128)(2,1)S(1)}, bf16[128,1024]{1,0:T(8,128)(2,1)}, u32[]{:S(2)}) copy-start(bf16[128,1024]{1,0:T(8,128)(2,1)} %latent_ref.1) | copy-start | bytes 786436
  1.5 0.7 copy-start.3
  2.1 0.7 copy-start.4
  2.9 12.3 %collective-permute-start.1 = (bf16[144,1024]{1,0:T(8,128)(2,1)S(1)}, bf16[144,1024]{1,0:T(8,128)(2,1)S(1)}, u32[]{:S(2)}, u32[]{:S(2)}) collective-permute-start(bf16[144,1024]{1,0:T(8,128)(2,1)S(1)} %shard_map.55.after_ref.refs_1_), channel_id=1, source_target_pairs={{0,4},{4,8},{8,12},{12,0},{1,5},{5,9},{9,13},{13,1},{2,6},{6,10},{... | collective-permute-start | bytes 884744 | tf_op jit(solution)/shard_map/ppermute | solution.py:147
  5.9 10.7 %collective-permute-start = (bf16[144,1024]{1,0:T(8,128)(2,1)S(1)}, bf16[144,1024]{1,0:T(8,128)(2,1)S(1)}, u32[]{:S(2)}, u32[]{:S(2)}) collective-permute-start(bf16[144,1024]{1,0:T(8,128)(2,1)S(1)} %shard_map.55.after_ref.refs_1_), channel_id=1, source_target_pairs={{0,1},{1,0},{2,3},{3,2},{4,5},{5,4},{6,7},{7,6},{8,9},{9,8},{10,11... | collective-permute-start | bytes 884744 | tf_op jit(solution)/shard_map/ppermute | solution.py:147
  7.4 1.8 %copy-start = (bf16[1,1024,1344]{1,2,0:T(8,128)(2,1)S(1)}, bf16[1,1024,1344]{1,2,0:T(8,128)(2,1)}, u32[]{:S(2)}) copy-start(bf16[1,1024,1344]{1,2,0:T(8,128)(2,1)} %param.8) | copy-start | bytes 8257540
  9.2 1.8 %copy-start.1 = (bf16[1,1024,1344]{1,2,0:T(8,128)(2,1)S(1)}, bf16[1,1024,1344]{1,2,0:T(8,128)(2,1)}, u32[]{:S(2)}) copy-start(bf16[1,1024,1344]{1,2,0:T(8,128)(2,1)} %param.9) | copy-start | bytes 8257540
  15.1 10.2 %collective-permute-start.5 = (bf16[144,1024]{1,0:T(8,128)(2,1)S(1)}, bf16[144,1024]{1,0:T(8,128)(2,1)S(1)}, u32[]{:S(2)}, u32[]{:S(2)}) collective-permute-start(bf16[144,1024]{1,0:T(8,128)(2,1)S(1)} %collective-permute-done.1.refs_2_), channel_id=1, source_target_pairs={{0,4},{4,8},{8,12},{12,0},{1,5},{5,9},{9,13},{13,1},{2,6},{6,10},{... | collective-permute-start | bytes 884744 | tf_op jit(solution)/shard_map/ppermute | solution.py:147
  15.1 11.4 %collective-permute-start.4 = (bf16[144,1024]{1,0:T(8,128)(2,1)S(1)}, bf16[144,1024]{1,0:T(8,128)(2,1)S(1)}, u32[]{:S(2)}, u32[]{:S(2)}) collective-permute-start(bf16[144,1024]{1,0:T(8,128)(2,1)S(1)} %collective-permute-done.1.refs_2_), channel_id=1, source_target_pairs={{0,1},{1,0},{2,3},{3,2},{4,5},{5,4},{6,7},{7,6},{8,9},{9,8},{10,11... | collective-permute-start | bytes 884744 | tf_op jit(solution)/shard_map/ppermute | solution.py:147
  25.3 9.3 %collective-permute-start.7 = (bf16[144,1024]{1,0:T(8,128)(2,1)S(1)}, bf16[144,1024]{1,0:T(8,128)(2,1)S(1)}, u32[]{:S(2)}, u32[]{:S(2)}) collective-permute-start(bf16[144,1024]{1,0:T(8,128)(2,1)S(1)} %collective-permute-done.5.refs_2_), channel_id=1, source_target_pairs={{0,4},{4,8},{8,12},{12,0},{1,5},{5,9},{9,13},{13,1},{2,6},{6,10},{... | collective-permute-start | bytes 884744 | tf_op jit(solution)/shard_map/ppermute | solution.py:147
  25.3 10.3 %collective-permute-start.6 = (bf16[144,1024]{1,0:T(8,128)(2,1)S(1)}, bf16[144,1024]{1,0:T(8,128)(2,1)S(1)}, u32[]{:S(2)}, u32[]{:S(2)}) collective-permute-start(bf16[144,1024]{1,0:T(8,128)(2,1)S(1)} %collective-permute-done.5.refs_2_), channel_id=1, source_target_pairs={{0,1},{1,0},{2,3},{3,2},{4,5},{5,4},{6,7},{7,6},{8,9},{9,8},{10,11... | collective-permute-start | bytes 884744 | tf_op jit(solution)/shard_map/ppermute | solution.py:147
  30.4 9.6 %collective-permute-start.9 = (bf16[128,1024]{1,0:T(8,128)(2,1)S(1)}, bf16[128,1024]{1,0:T(8,128)(2,1)S(1)}, u32[]{:S(2)}, u32[]{:S(2)}) collective-permute-start(bf16[128,1024]{1,0:T(8,128)(2,1)S(1)} %get-tuple-element.30.refs_0_), channel_id=1, source_target_pairs={{0,1},{1,0},{2,3},{3,2},{4,5},{5,4},{6,7},{7,6},{8,9},{9,8},{10,11... | collective-permute-start | bytes 786440 | tf_op jit(solution)/shard_map/ppermute | solution.py:147
  34.6 11.8 %collective-permute-start.11 = (bf16[144,1024]{1,0:T(8,128)(2,1)S(1)}, bf16[144,1024]{1,0:T(8,128)(2,1)S(1)}, u32[]{:S(2)}, u32[]{:S(2)}) collective-permute-start(bf16[144,1024]{1,0:T(8,128)(2,1)S(1)} %collective-permute-done.7.refs_2_), channel_id=1, source_target_pairs={{0,1},{1,0},{2,3},{3,2},{4,5},{5,4},{6,7},{7,6},{8,9},{9,8},{10,11... | collective-permute-start | bytes 884744 | tf_op jit(solution)/shard_map/ppermute | solution.py:147
  40.1 10.7 %collective-permute-start.10 = (bf16[128,1024]{1,0:T(8,128)(2,1)S(1)}, bf16[128,1024]{1,0:T(8,128)(2,1)S(1)}, u32[]{:S(2)}, u32[]{:S(2)}) collective-permute-start(bf16[128,1024]{1,0:T(8,128)(2,1)S(1)} %add_convert_fusion.2.refs_1_), channel_id=1, source_target_pairs={{0,12},{4,0},{8,4},{12,8},{1,13},{5,1},{9,5},{13,9},{2,14},{6,2},{... | collective-permute-start | bytes 786440 | tf_op jit(solution)/shard_map/ppermute | solution.py:147
  43.7 12.4 %collective-permute-start.8 = (bf16[128,1024]{1,0:T(8,128)(2,1)S(1)}, bf16[128,1024]{1,0:T(8,128)(2,1)S(1)}, u32[]{:S(2)}, u32[]{:S(2)}) collective-permute-start(bf16[128,1024]{1,0:T(8,128)(2,1)S(1)} %get-tuple-element.32), channel_id=1, source_target_pairs={{0,4},{4,8},{8,12},{12,0},{1,5},{5,9},{9,13},{13,1},{2,6},{6,10},{... | collective-permute-start | bytes 786440 | tf_op jit(solution)/shard_map/ppermute | solution.py:147
  43.7 12.4 %collective-permute-start.14 = (bf16[128,1024]{1,0:T(8,128)(2,1)S(1)}, bf16[128,1024]{1,0:T(8,128)(2,1)S(1)}, u32[]{:S(2)}, u32[]{:S(2)}) collective-permute-start(bf16[128,1024]{1,0:T(8,128)(2,1)S(1)} %get-tuple-element.34.refs_0_), channel_id=1, source_target_pairs={{0,1},{1,0},{2,3},{3,2},{4,5},{5,4},{6,7},{7,6},{8,9},{9,8},{10,11... | collective-permute-start | bytes 786440 | tf_op jit(solution)/shard_map/ppermute | solution.py:147
  49.6 12.1 %collective-permute-start.12 = (bf16[128,1024]{1,0:T(8,128)(2,1)S(1)}, bf16[128,1024]{1,0:T(8,128)(2,1)S(1)}, u32[]{:S(2)}, u32[]{:S(2)}) collective-permute-start(bf16[128,1024]{1,0:T(8,128)(2,1)S(1)} %shard_map.60), channel_id=1, source_target_pairs={{0,5},{1,4},{4,9},{5,8},{8,13},{9,12},{12,1},{13,0},{2,7},{3,6},{6... | collective-permute-start | bytes 786440 | tf_op jit(solution)/shard_map/ppermute | solution.py:161
  49.7 11.8 %collective-permute-start.13 = (bf16[128,1024]{1,0:T(8,128)(2,1)S(1)}, bf16[128,1024]{1,0:T(8,128)(2,1)S(1)}, u32[]{:S(2)}, u32[]{:S(2)}) collective-permute-start(bf16[128,1024]{1,0:T(8,128)(2,1)S(1)} %get-tuple-element.38.refs_0_), channel_id=1, source_target_pairs={{0,1},{1,0},{2,3},{3,2},{4,5},{5,4},{6,7},{7,6},{8,9},{9,8},{10,11... | collective-permute-start | bytes 786440 | tf_op jit(solution)/shard_map/ppermute | solution.py:147
  56.2 13.7 %collective-permute-start.15 = (bf16[128,1024]{1,0:T(8,128)(2,1)S(1)}, bf16[128,1024]{1,0:T(8,128)(2,1)S(1)}, u32[]{:S(2)}, u32[]{:S(2)}) collective-permute-start(bf16[128,1024]{1,0:T(8,128)(2,1)S(1)} %add_convert_fusion.1), channel_id=1, source_target_pairs={{0,8},{4,12},{8,0},{12,4},{1,9},{5,13},{9,1},{13,5},{2,10},{6,14},... | collective-permute-start | bytes 786440 | tf_op jit(solution)/shard_map/ppermute | solution.py:147

commit v7 on v6

--- a/solution.py
+++ b/solution.py
@@ -151,14 +151,13 @@
     return lax.optimization_barrier((array, first))[0]
 
 
-def shift_both(array, outer, step, inner, turn):
-    sizes = lax.axis_size(outer), lax.axis_size(inner)
-    pairs = [
-        (i * sizes[1] + k, (i + step) % sizes[0] * sizes[1] + (k + turn) % sizes[1])
-        for i in range(sizes[0])
-        for k in range(sizes[1])
-    ]
-    return lax.ppermute(array, (outer, inner), pairs)
+def arrival_order(depth):
+    ahead, behind = list(range(2, depth // 2 + 1)), list(range(depth - 1, depth // 2, -1))
+    order = list(range(min(depth, 2)))
+    while ahead or behind:
+        order += ahead[:1] + [r for r in behind[:1] if r > 1]
+        ahead, behind = ahead[1:], behind[1:]
+    return order
 
 
 def local(latent, routes, gates, up_weight, down_weight):
@@ -169,52 +168,58 @@
     slots = min(block, 3 * block * top // (2 * experts))
     own = [jnp.swapaxes(up_weight, 1, 2), jnp.swapaxes(down_weight, 1, 2)]
     moved = [shift(table, "core", step) for step in range(1, cores) for table in own]
-    ring = [pack(latent, routes, gates, experts)]
+    ring = {0: pack(latent, routes, gates, experts)}
     tables = [*stage(ring[0], own), *moved]
-    ring.append(follow(shift(ring[0], "z", 1), tables[0]))
-    last = depth - 1
-    kept = [None] * depth
-    others, totals = [], {}
-    after = []
-
-    def total(j, behind=None):
-        rows = kept[j]
-        for s, other in enumerate(others[j], 1):
-            other = shift(other, "sub", -s)
-            if behind is not None:
-                other = follow(other, behind)
-            rows = rows + other.astype(jnp.float32)
-        return rows.astype(jnp.bfloat16) if j else rows
-
-    for j in range(depth):
-        handed = [shift(ring[j], "sub", s) for s in range(1, subs)]
-        fresh = ([0] if j == 0 else []) + [j + 1] * (j < last)
-        kinds = [jnp.bfloat16] * len(handed)
-        kinds += [jnp.bfloat16 if r == last else jnp.float32 for r in fresh]
-        if j > 2:
-            totals[j - 2] = total(j - 2, after[0])
-            after.append(totals[j - 2])
-        partial = run_experts(
-            after, handed + [ring[r] for r in fresh], tables, kinds, block, slots
-        )
-        after = [partial[0]]
-        if j + 2 < depth:
-            ring.append(follow(shift(ring[-1], "z", 1), partial[0]))
-        for r, rows in zip(fresh, partial[subs - 1 :]):
-            kept[r] = rows
-        others.append(partial[: subs - 1])
-    corner = [shift_both(other, "z", -last, "sub", -s) for s, other in enumerate(others[last], 1)]
-    others[0] = [follow(other, others[last][0]) for other in others[0]]
-    for j in range(last):
-        if j not in totals:
-            totals[j] = total(j, others[last][0])
-    back = [shift(kept[last], "z", -last)] + [shift(totals[j], "z", -j) for j in range(1, last)]
-    late = back.pop()
-    home = sum(rows.astype(jnp.float32) for rows in back)
-    home, *corner = lax.optimization_barrier((home, *corner))
-    home = home + totals[0] + sum(rows.astype(jnp.float32) for rows in corner)
-    home, late = lax.optimization_barrier((home, late))
-    home = home + late.astype(jnp.float32)
+    turns = arrival_order(depth)
+    ring[1] = follow(shift(ring[0], "z", 1), tables[0])
+    kept, others, totals = {}, {}, {}
+    firsts = []
+
+    def fetch(p):
+        r = turns[p]
+        held = shift(ring[r - 1], "z", 1) if r <= depth // 2 else shift(ring[(r + 1) % depth], "z", -1)
+        ring[r] = follow(held, firsts[-1])
+
+    def total(r, behind):
+        rows = kept[r]
+        for s, other in enumerate(others[r], 1):
+            rows = rows + follow(shift(other, "sub", -s), behind).astype(jnp.float32)
+        return rows
+
+    def send_home(order, step):
+        passing = None
+        for r in order:
+            rows = totals[r] if passing is None else totals[r] + passing.astype(jnp.float32)
+            leaving = rows.astype(jnp.bfloat16)
+            passing = shift(leaving, "z", step)
+        return leaving, passing
+
+    for p, r in enumerate(turns):
+        handed = [shift(ring[r], "sub", s) for s in range(1, subs)]
+        fresh = turns[:2] if p == 0 else turns[p + 1 : p + 2]
+        kinds = [jnp.bfloat16] * len(handed) + [jnp.float32] * len(fresh)
+        after = firsts[-1:] + ([ring[turns[p + 2]]] if 0 < p < depth - 2 else [])
+        if p > 2:
+            early = turns[p - 2]
+            totals[early] = total(early, firsts[-1])
+            after.append(totals[early])
+        partial = run_experts(after, handed + [ring[f] for f in fresh], tables, kinds, block, slots)
+        firsts.append(partial[0])
+        for q in (2, 3) if p == 0 else (p + 3,):
+            if q < depth:
+                fetch(q)
+        for f, rows in zip(fresh, partial[subs - 1 :]):
+            kept[f] = rows
+        others[r] = partial[: subs - 1]
+    for r in turns[1:]:
+        if r not in totals:
+            totals[r] = total(r, others[turns[-1]][0])
+    homeward = [send_home(range(depth - 1, depth // 2, -1)[::-1], 1)] if depth > 2 else []
+    homeward.append(send_home(range(depth // 2, 0, -1), -1))
+    others[0] = [follow(other, homeward[0][0]) for other in others[0]]
+    home = total(0, homeward[0][0])
+    for _, rows in homeward:
+        home = home + rows.astype(jnp.float32)
     return home.astype(jnp.bfloat16)
 
 

time: 70.9 us -> 72.7 us (1.025)
  starting transfers between devices: 15.5 us -> 24.6 us
  waiting for transfers between devices: 31.7 us -> 24.3 us
    ppermute x15 -> x16, starting transfers between devices: 15.4 us -> 24.6 us  [shift(): lax.ppermute(array, axis, [(i, (i + step) % size) for i in range(size)])]
    ppermute x15 -> x16, waiting for transfers between devices: 31.5 us -> 24.3 us  [shift(): lax.ppermute(array, axis, [(i, (i + step) % size) for i in range(size)])]
  transfers between devices with their start and end apart: 16 -> 16, of which waited for: 9 -> 10; matrix products, arithmetic and copies ran while one was open for 0% -> 0% of each run, Pallas kernels for 23% -> 23%
where the time goes in v7:
time: 72.7 us; the launch traced here: 72.5 us
  starting transfers between devices  24.6 us (34%)
  waiting for transfers between devices  24.3 us (33%)
  Pallas kernels  16.5 us (23%)
  local copies, waits for them, and re-layouts  5.87 us (8%)
  other arithmetic  1.06 us (1%)
    ppermute x16, starting transfers between devices, shift(): lax.ppermute(array, axis, [(i, (i + step) % size) for i in range(size)])  24.6 us
    ppermute x16, waiting for transfers between devices, shift(): lax.ppermute(array, axis, [(i, (i + step) % size) for i in range(size)])  24.3 us
    pallas_call x4, Pallas kernels, run_experts(): pl.pallas_call(functools.partial(expert_kernel, block, slots, unit, numbe...  15.8 us
    unnamed x10, local copies, waits for them, and re-layouts  5.87 us
  transfers between devices with their start and end apart: 16, of which 10 were waited for; matrix products, arithmetic and copies ran while one was open for 0% of the time, Pallas kernels for 23%

profile of v7, /device:TPU:0, one launch (start us, length us, event | category | flops | bytes accessed | tf_op | source)
XLA Modules:
  0.0 72.5 jit_solution(6806525770637797864)
XLA Ops:
  0.0 0.5 collective-permute-start.2
  0.5 0.1 collective-permute-start.3
  0.5 0.0 copy-start.2
  0.5 0.9 %copy-done.2 = bf16[128,1024]{1,0:T(8,128)(2,1)S(1)} copy-done((bf16[128,1024]{1,0:T(8,128)(2,1)S(1)}, bf16[128,1024]{1,0:T(8,128)(2,1)}, u32[]{:S(2)}) %copy-start.2) | copy-done | bytes 262168
  1.5 0.7 copy-done.3
  2.1 0.7 copy-done.4
  2.9 3.1 %collective-permute-start.1 = (bf16[144,1024]{1,0:T(8,128)(2,1)S(1)}, bf16[144,1024]{1,0:T(8,128)(2,1)S(1)}, u32[]{:S(2)}, u32[]{:S(2)}) collective-permute-start(bf16[144,1024]{1,0:T(8,128)(2,1)S(1)} %shard_map.55.after_ref.refs_1_), channel_id=1, source_target_pairs={{0,4},{4,8},{8,12},{12,0},{1,5},{5,9},{9,13},{13,1},{2,6},{6,10},{... | collective-permute-start | bytes 884744 | tf_op jit(solution)/shard_map/ppermute | solution.py:147
  5.9 1.5 %collective-permute-start = (bf16[144,1024]{1,0:T(8,128)(2,1)S(1)}, bf16[144,1024]{1,0:T(8,128)(2,1)S(1)}, u32[]{:S(2)}, u32[]{:S(2)}) collective-permute-start(bf16[144,1024]{1,0:T(8,128)(2,1)S(1)} %shard_map.55.after_ref.refs_1_), channel_id=1, source_target_pairs={{0,1},{1,0},{2,3},{3,2},{4,5},{5,4},{6,7},{7,6},{8,9},{9,8},{10,11... | collective-permute-start | bytes 884744 | tf_op jit(solution)/shard_map/ppermute | solution.py:147
  7.4 2.2 %collective-permute-start.4 = (bf16[144,1024]{1,0:T(8,128)(2,1)S(1)}, bf16[144,1024]{1,0:T(8,128)(2,1)S(1)}, u32[]{:S(2)}, u32[]{:S(2)}) collective-permute-start(bf16[144,1024]{1,0:T(8,128)(2,1)S(1)} %shard_map.55.after_ref.refs_1_), channel_id=1, source_target_pairs={{0,12},{4,0},{8,4},{12,8},{1,13},{5,1},{9,5},{13,9},{2,14},{6,2},{... | collective-permute-start | bytes 884744 | tf_op jit(solution)/shard_map/ppermute | solution.py:147
  9.7 1.8 %copy-done = bf16[1,1024,1344]{1,2,0:T(8,128)(2,1)S(1)} copy-done((bf16[1,1024,1344]{1,2,0:T(8,128)(2,1)S(1)}, bf16[1,1024,1344]{1,2,0:T(8,128)(2,1)}, u32[]{:S(2)}) %copy-start) | copy-done | bytes 2752536
  11.5 1.8 %copy-done.1 = bf16[1,1024,1344]{1,2,0:T(8,128)(2,1)S(1)} copy-done((bf16[1,1024,1344]{1,2,0:T(8,128)(2,1)S(1)}, bf16[1,1024,1344]{1,2,0:T(8,128)(2,1)}, u32[]{:S(2)}) %copy-start.1) | copy-done | bytes 2752536
  13.2 0.7 shard_map.56
  13.9 1.9 %collective-permute-done.1.refs_2_ = bf16[144,1024]{1,0:T(8,128)(2,1)S(1)} collective-permute-done((bf16[144,1024]{1,0:T(8,128)(2,1)S(1)}, bf16[144,1024]{1,0:T(8,128)(2,1)S(1)}, u32[]{:S(2)}, u32[]{:S(2)}) %collective-permute-start.1) | collective-permute-done | bytes 294944 | tf_op jit(solution)/shard_map/ppermute | solution.py:147
  15.8 0.0 collective-permute-start.6
  15.8 0.0 collective-permute-done.refs_0_
  15.8 1.7 %collective-permute-start.5 = (bf16[144,1024]{1,0:T(8,128)(2,1)S(1)}, bf16[144,1024]{1,0:T(8,128)(2,1)S(1)}, u32[]{:S(2)}, u32[]{:S(2)}) collective-permute-start(bf16[144,1024]{1,0:T(8,128)(2,1)S(1)} %collective-permute-done.1.refs_2_), channel_id=1, source_target_pairs={{0,1},{1,0},{2,3},{3,2},{4,5},{5,4},{6,7},{7,6},{8,9},{9,8},{10,11... | collective-permute-start | bytes 884744 | tf_op jit(solution)/shard_map/ppermute | solution.py:147
  17.6 0.0 collective-permute-done.2.refs_5_.refs_6_
  17.6 0.0 collective-permute-done.3.refs_6_.refs_7_
  17.6 4.9 %shard_map.57 = (bf16[128,1024]{1,0:T(8,128)(2,1)S(1)}, f32[128,1024]{1,0:T(8,128)S(1)}, f32[128,1024]{1,0:T(8,128)S(1)}) custom-call(bf16[144,1024]{1,0:T(8,128)(2,1)S(1)} %collective-permute-done.refs_0_, bf16[144,1024]{1,0:T(8,128)(2,1)S(1)} %shard_map.55.after_ref.refs_1_, bf16[144,1024]{1,0:T(8,128)(2,1)S(1)} %collective-permute-done.1.refs_2_, ...), custom_call_target="tpu_custom_call" | custom-call | flops 3472883712 | bytes 12976128 | tf_op jit(solution)/shard_map/pallas_call | solution.py:130
  22.5 5.4 %collective-permute-done.6.refs_3_ = bf16[144,1024]{1,0:T(8,128)(2,1)S(1)} collective-permute-done((bf16[144,1024]{1,0:T(8,128)(2,1)S(1)}, bf16[144,1024]{1,0:T(8,128)(2,1)S(1)}, u32[]{:S(2)}, u32[]{:S(2)}) %collective-permute-start.6) | collective-permute-done | bytes 294944 | tf_op jit(solution)/shard_map/ppermute | solution.py:147
  27.8 1.5 %collective-permute-start.7 = (bf16[144,1024]{1,0:T(8,128)(2,1)S(1)}, bf16[144,1024]{1,0:T(8,128)(2,1)S(1)}, u32[]{:S(2)}, u32[]{:S(2)}) collective-permute-start(bf16[144,1024]{1,0:T(8,128)(2,1)S(1)} %collective-permute-done.6.refs_3_), channel_id=1, source_target_pairs={{0,1},{1,0},{2,3},{3,2},{4,5},{5,4},{6,7},{7,6},{8,9},{9,8},{10,11... | collective-permute-start | bytes 884744 | tf_op jit(solution)/shard_map/ppermute | solution.py:147
  29.3 0.0 collective-permute-done.4.refs_1_.refs_2_
  29.3 0.0 collective-permute-done.5.refs_2_
  29.3 3.8 %shard_map.58 = (bf16[128,1024]{1,0:T(8,128)(2,1)S(1)}, f32[128,1024]{1,0:T(8,128)S(1)}) custom-call(bf16[128,1024]{1,0:T(8,128)(2,1)S(1)} %get-tuple-element.35.refs_0_, bf16[144,1024]{1,0:T(8,128)(2,1)S(1)} %collective-permute-done.4.refs_1_.refs_2_, bf16[144,1024]{1,0:T(8,128)(2,1)S(1)} %collective-permute-done.5.refs_2_, ...), custom_call_target="tpu_custom_call" | custom-call | flops 2315255808 | bytes 12320768 | tf_op jit(solution)/shard_map/pallas_call | solution.py:130
  33.1 0.6 collective-permute-start.8
  33.7 1.5 %collective-permute-start.9 = (bf16[144,1024]{1,0:T(8,128)(2,1)S(1)}, bf16[144,1024]{1,0:T(8,128)(2,1)S(1)}, u32[]{:S(2)}, u32[]{:S(2)}) collective-permute-start(bf16[144,1024]{1,0:T(8,128)(2,1)S(1)} %collective-permute-done.4.refs_1_.refs_2_), channel_id=1, source_target_pairs={{0,1},{1,0},{2,3},{3,2},{4,5},{5,4},{6,7},{7,6},{8,9},{9,8},{10,11... | collective-permute-start | bytes 884744 | tf_op jit(solution)/shard_map/ppermute | solution.py:147
  35.2 0.7 %collective-permute-done.7.refs_1_ = bf16[144,1024]{1,0:T(8,128)(2,1)S(1)} collective-permute-done((bf16[144,1024]{1,0:T(8,128)(2,1)S(1)}, bf16[144,1024]{1,0:T(8,128)(2,1)S(1)}, u32[]{:S(2)}, u32[]{:S(2)}) %collective-permute-start.7) | collective-permute-done | bytes 294944 | tf_op jit(solution)/shard_map/ppermute | solution.py:147
  36.0 3.8 %shard_map.59 = (bf16[128,1024]{1,0:T(8,128)(2,1)S(1)}, f32[128,1024]{1,0:T(8,128)S(1)}) custom-call(bf16[128,1024]{1,0:T(8,128)(2,1)S(1)} %get-tuple-element.29.refs_0_, bf16[144,1024]{1,0:T(8,128)(2,1)S(1)} %collective-permute-done.7.refs_1_, bf16[144,1024]{1,0:T(8,128)(2,1)S(1)} %collective-permute-done.4.refs_1_.refs_2_, ...), custom_call_target="tpu_custom_call" | custom-call | flops 2315255808 | bytes 12320768 | tf_op jit(solution)/shard_map/pallas_call | solution.py:130
  39.8 2.5 %collective-permute-start.13 = (bf16[128,1024]{1,0:T(8,128)(2,1)S(1)}, bf16[128,1024]{1,0:T(8,128)(2,1)S(1)}, u32[]{:S(2)}, u32[]{:S(2)}) collective-permute-start(bf16[128,1024]{1,0:T(8,128)(2,1)S(1)} %get-tuple-element.31.refs_0_), channel_id=1, source_target_pairs={{0,1},{1,0},{2,3},{3,2},{4,5},{5,4},{6,7},{7,6},{8,9},{9,8},{10,11... | collective-permute-start | bytes 786440 | tf_op jit(solution)/shard_map/ppermute | solution.py:147
  42.4 0.1 collective-permute-done.8
  42.5 0.1 convert_add_fusion.refs_1_
  42.5 6.3 %collective-permute-done.9.refs_2_ = bf16[144,1024]{1,0:T(8,128)(2,1)S(1)} collective-permute-done((bf16[144,1024]{1,0:T(8,128)(2,1)S(1)}, bf16[144,1024]{1,0:T(8,128)(2,1)S(1)}, u32[]{:S(2)}, u32[]{:S(2)}) %collective-permute-start.9) | collective-permute-done | bytes 294944 | tf_op jit(solution)/shard_map/ppermute | solution.py:147
  48.8 3.3 %shard_map.60 = bf16[128,1024]{1,0:T(8,128)(2,1)S(1)} custom-call(bf16[128,1024]{1,0:T(8,128)(2,1)S(1)} %get-tuple-element.31.refs_0_, f32[128,1024]{1,0:T(8,128)S(1)} %convert_add_fusion.refs_1_, bf16[144,1024]{1,0:T(8,128)(2,1)S(1)} %collective-permute-done.9.refs_2_, bf16[1,1344,1024]{2,1,0:T(8,128)(2,1)S(1)} %get-tuple-element.22.refs_3_.refs_4_, ...), custom_call_target="tpu_custom_call" | custom-call | flops 1157627904 | bytes 11665408 | tf_op jit(solution)/shard_map/pallas_call | solution.py:130
  52.0 1.7 %collective-permute-start.10 = (bf16[128,1024]{1,0:T(8,128)(2,1)S(1)}, bf16[128,1024]{1,0:T(8,128)(2,1)S(1)}, u32[]{:S(2)}, u32[]{:S(2)}) collective-permute-start(bf16[128,1024]{1,0:T(8,128)(2,1)S(1)} %shard_map.60), channel_id=1, source_target_pairs={{0,1},{1,0},{2,3},{3,2},{4,5},{5,4},{6,7},{7,6},{8,9},{9,8},{10,11... | collective-permute-start | bytes 786440 | tf_op jit(solution)/shard_map/ppermute | solution.py:147
  53.7 0.2 collective-permute-done.13
  53.9 0.1 add_convert_fusion.2
  54.0 1.9 %collective-permute-start.14 = (bf16[128,1024]{1,0:T(8,128)(2,1)S(1)}, bf16[128,1024]{1,0:T(8,128)(2,1)S(1)}, u32[]{:S(2)}, u32[]{:S(2)}) collective-permute-start(bf16[128,1024]{1,0:T(8,128)(2,1)S(1)} %add_convert_fusion.2), channel_id=1, source_target_pairs={{0,12},{4,0},{8,4},{12,8},{1,13},{5,1},{9,5},{13,9},{2,14},{6,2},{... | collective-permute-start | bytes 786440 | tf_op jit(solution)/shard_map/ppermute | solution.py:147
  55.9 2.6 %collective-permute-done.10 = bf16[128,1024]{1,0:T(8,128)(2,1)S(1)} collective-permute-done((bf16[128,1024]{1,0:T(8,128)(2,1)S(1)}, bf16[128,1024]{1,0:T(8,128)(2,1)S(1)}, u32[]{:S(2)}, u32[]{:S(2)}) %collective-permute-start.10) | collective-permute-done | bytes 262176 | tf_op jit(solution)/shard_map/ppermute | solution.py:147
  58.5 0.1 add_convert_fusion.3
  58.5 0.4 collective-permute-start.12
  58.9 1.8 %collective-permute-start.11 = (bf16[128,1024]{1,0:T(8,128)(2,1)S(1)}, bf16[128,1024]{1,0:T(8,128)(2,1)S(1)}, u32[]{:S(2)}, u32[]{:S(2)}) collective-permute-start(bf16[128,1024]{1,0:T(8,128)(2,1)S(1)} %get-tuple-element.35.refs_0_), channel_id=1, source_target_pairs={{0,1},{1,0},{2,3},{3,2},{4,5},{5,4},{6,7},{7,6},{8,9},{9,8},{10,11... | collective-permute-start | bytes 786440 | tf_op jit(solution)/shard_map/ppermute | solution.py:147
  60.7 2.7 %collective-permute-done.14 = bf16[128,1024]{1,0:T(8,128)(2,1)S(1)} collective-permute-done((bf16[128,1024]{1,0:T(8,128)(2,1)S(1)}, bf16[128,1024]{1,0:T(8,128)(2,1)S(1)}, u32[]{:S(2)}, u32[]{:S(2)}) %collective-permute-start.14) | collective-permute-done | bytes 262176 | tf_op jit(solution)/shard_map/ppermute | solution.py:147
  63.4 0.1 add_convert_fusion.1
  63.5 3.6 %collective-permute-start.15 = (bf16[128,1024]{1,0:T(8,128)(2,1)S(1)}, bf16[128,1024]{1,0:T(8,128)(2,1)S(1)}, u32[]{:S(2)}, u32[]{:S(2)}) collective-permute-start(bf16[128,1024]{1,0:T(8,128)(2,1)S(1)} %add_convert_fusion.1), channel_id=1, source_target_pairs={{0,12},{4,0},{8,4},{12,8},{1,13},{5,1},{9,5},{13,9},{2,14},{6,2},{... | collective-permute-start | bytes 786440 | tf_op jit(solution)/shard_map/ppermute | solution.py:147
  67.0 0.0 collective-permute-done.11
  67.0 2.9 %collective-permute-done.12 = bf16[128,1024]{1,0:T(8,128)(2,1)S(1)} collective-permute-done((bf16[128,1024]{1,0:T(8,128)(2,1)S(1)}, bf16[128,1024]{1,0:T(8,128)(2,1)S(1)}, u32[]{:S(2)}, u32[]{:S(2)}) %collective-permute-start.12) | collective-permute-done | bytes 262176 | tf_op jit(solution)/shard_map/ppermute | solution.py:147
  69.9 1.7 %collective-permute-done.15 = bf16[128,1024]{1,0:T(8,128)(2,1)S(1)} collective-permute-done((bf16[128,1024]{1,0:T(8,128)(2,1)S(1)}, bf16[128,1024]{1,0:T(8,128)(2,1)S(1)}, u32[]{:S(2)}, u32[]{:S(2)}) %collective-permute-start.15) | collective-permute-done | bytes 262176 | tf_op jit(solution)/shard_map/ppermute | solution.py:147
  71.6 0.8 %add_convert_fusion = bf16[128,1024]{1,0:T(8,128)(2,1)} fusion(bf16[128,1024]{1,0:T(8,128)(2,1)S(1)} %collective-permute-done.15, bf16[128,1024]{1,0:T(8,128)(2,1)S(1)} %collective-permute-done.12, f32[128,1024]{1,0:T(8,128)S(1)} %get-tuple-element.25, bf16[128,1024]{1,0:T(8,128)(2,1)S(1)} %collective-permute-done.11), kind=kLoop, calls=%fused_computation | loop fusion | flops 917504 | bytes 1572864 | tf_op jit(solution)/shard_map/convert_element_type | solution.py:223
  (5 shorter events, 0.0 us)
Async XLA Ops:
  0.0 17.6 %collective-permute-start.2 = (bf16[1,1344,1024]{2,1,0:T(8,128)(2,1)}, bf16[1,1344,1024]{2,1,0:T(8,128)(2,1)S(1)}, u32[]{:S(2)}, u32[]{:S(2)}) collective-permute-start(bf16[1,1344,1024]{2,1,0:T(8,128)(2,1)} %bitcast.4), channel_id=1, source_target_pairs={{0,2},{2,0},{1,3},{3,1},{4,6},{6,4},{5,7},{7,5},{8,10},{10,8},{9,1... | collective-permute-start | bytes 8257544 | tf_op jit(solution)/shard_map/ppermute | solution.py:147
  0.5 17.1 %collective-permute-start.3 = (bf16[1,1344,1024]{2,1,0:T(8,128)(2,1)}, bf16[1,1344,1024]{2,1,0:T(8,128)(2,1)S(1)}, u32[]{:S(2)}, u32[]{:S(2)}) collective-permute-start(bf16[1,1344,1024]{2,1,0:T(8,128)(2,1)} %bitcast.6), channel_id=1, source_target_pairs={{0,2},{2,0},{1,3},{3,1},{4,6},{6,4},{5,7},{7,5},{8,10},{10,8},{9,1... | collective-permute-start | bytes 8257544 | tf_op jit(solution)/shard_map/ppermute | solution.py:147
  0.5 0.9 %copy-start.2 = (bf16[128,1024]{1,0:T(8,128)(2,1)S(1)}, bf16[128,1024]{1,0:T(8,128)(2,1)}, u32[]{:S(2)}) copy-start(bf16[128,1024]{1,0:T(8,128)(2,1)} %latent_ref.1) | copy-start | bytes 786436
  1.5 0.7 copy-start.3
  2.1 0.7 copy-start.4
  2.9 13.0 %collective-permute-start.1 = (bf16[144,1024]{1,0:T(8,128)(2,1)S(1)}, bf16[144,1024]{1,0:T(8,128)(2,1)S(1)}, u32[]{:S(2)}, u32[]{:S(2)}) collective-permute-start(bf16[144,1024]{1,0:T(8,128)(2,1)S(1)} %shard_map.55.after_ref.refs_1_), channel_id=1, source_target_pairs={{0,4},{4,8},{8,12},{12,0},{1,5},{5,9},{9,13},{13,1},{2,6},{6,10},{... | collective-permute-start | bytes 884744 | tf_op jit(solution)/shard_map/ppermute | solution.py:147
  5.9 9.9 %collective-permute-start = (bf16[144,1024]{1,0:T(8,128)(2,1)S(1)}, bf16[144,1024]{1,0:T(8,128)(2,1)S(1)}, u32[]{:S(2)}, u32[]{:S(2)}) collective-permute-start(bf16[144,1024]{1,0:T(8,128)(2,1)S(1)} %shard_map.55.after_ref.refs_1_), channel_id=1, source_target_pairs={{0,1},{1,0},{2,3},{3,2},{4,5},{5,4},{6,7},{7,6},{8,9},{9,8},{10,11... | collective-permute-start | bytes 884744 | tf_op jit(solution)/shard_map/ppermute | solution.py:147
  7.4 21.9 %collective-permute-start.4 = (bf16[144,1024]{1,0:T(8,128)(2,1)S(1)}, bf16[144,1024]{1,0:T(8,128)(2,1)S(1)}, u32[]{:S(2)}, u32[]{:S(2)}) collective-permute-start(bf16[144,1024]{1,0:T(8,128)(2,1)S(1)} %shard_map.55.after_ref.refs_1_), channel_id=1, source_target_pairs={{0,12},{4,0},{8,4},{12,8},{1,13},{5,1},{9,5},{13,9},{2,14},{6,2},{... | collective-permute-start | bytes 884744 | tf_op jit(solution)/shard_map/ppermute | solution.py:147
  9.7 1.8 %copy-start = (bf16[1,1024,1344]{1,2,0:T(8,128)(2,1)S(1)}, bf16[1,1024,1344]{1,2,0:T(8,128)(2,1)}, u32[]{:S(2)}) copy-start(bf16[1,1024,1344]{1,2,0:T(8,128)(2,1)} %param.8) | copy-start | bytes 8257540
  11.4 1.8 %copy-start.1 = (bf16[1,1024,1344]{1,2,0:T(8,128)(2,1)S(1)}, bf16[1,1024,1344]{1,2,0:T(8,128)(2,1)}, u32[]{:S(2)}) copy-start(bf16[1,1024,1344]{1,2,0:T(8,128)(2,1)} %param.9) | copy-start | bytes 8257540
  15.8 12.0 %collective-permute-start.6 = (bf16[144,1024]{1,0:T(8,128)(2,1)S(1)}, bf16[144,1024]{1,0:T(8,128)(2,1)S(1)}, u32[]{:S(2)}, u32[]{:S(2)}) collective-permute-start(bf16[144,1024]{1,0:T(8,128)(2,1)S(1)} %collective-permute-done.1.refs_2_), channel_id=1, source_target_pairs={{0,4},{4,8},{8,12},{12,0},{1,5},{5,9},{9,13},{13,1},{2,6},{6,10},{... | collective-permute-start | bytes 884744 | tf_op jit(solution)/shard_map/ppermute | solution.py:147
  15.8 13.5 %collective-permute-start.5 = (bf16[144,1024]{1,0:T(8,128)(2,1)S(1)}, bf16[144,1024]{1,0:T(8,128)(2,1)S(1)}, u32[]{:S(2)}, u32[]{:S(2)}) collective-permute-start(bf16[144,1024]{1,0:T(8,128)(2,1)S(1)} %collective-permute-done.1.refs_2_), channel_id=1, source_target_pairs={{0,1},{1,0},{2,3},{3,2},{4,5},{5,4},{6,7},{7,6},{8,9},{9,8},{10,11... | collective-permute-start | bytes 884744 | tf_op jit(solution)/shard_map/ppermute | solution.py:147
  27.8 8.2 %collective-permute-start.7 = (bf16[144,1024]{1,0:T(8,128)(2,1)S(1)}, bf16[144,1024]{1,0:T(8,128)(2,1)S(1)}, u32[]{:S(2)}, u32[]{:S(2)}) collective-permute-start(bf16[144,1024]{1,0:T(8,128)(2,1)S(1)} %collective-permute-done.6.refs_3_), channel_id=1, source_target_pairs={{0,1},{1,0},{2,3},{3,2},{4,5},{5,4},{6,7},{7,6},{8,9},{9,8},{10,11... | collective-permute-start | bytes 884744 | tf_op jit(solution)/shard_map/ppermute | solution.py:147
  33.1 9.3 %collective-permute-start.8 = (bf16[128,1024]{1,0:T(8,128)(2,1)S(1)}, bf16[128,1024]{1,0:T(8,128)(2,1)S(1)}, u32[]{:S(2)}, u32[]{:S(2)}) collective-permute-start(bf16[128,1024]{1,0:T(8,128)(2,1)S(1)} %get-tuple-element.29.refs_0_), channel_id=1, source_target_pairs={{0,1},{1,0},{2,3},{3,2},{4,5},{5,4},{6,7},{7,6},{8,9},{9,8},{10,11... | collective-permute-start | bytes 786440 | tf_op jit(solution)/shard_map/ppermute | solution.py:147
  33.7 15.0 %collective-permute-start.9 = (bf16[144,1024]{1,0:T(8,128)(2,1)S(1)}, bf16[144,1024]{1,0:T(8,128)(2,1)S(1)}, u32[]{:S(2)}, u32[]{:S(2)}) collective-permute-start(bf16[144,1024]{1,0:T(8,128)(2,1)S(1)} %collective-permute-done.4.refs_1_.refs_2_), channel_id=1, source_target_pairs={{0,1},{1,0},{2,3},{3,2},{4,5},{5,4},{6,7},{7,6},{8,9},{9,8},{10,11... | collective-permute-start | bytes 884744 | tf_op jit(solution)/shard_map/ppermute | solution.py:147
  39.8 14.1 %collective-permute-start.13 = (bf16[128,1024]{1,0:T(8,128)(2,1)S(1)}, bf16[128,1024]{1,0:T(8,128)(2,1)S(1)}, u32[]{:S(2)}, u32[]{:S(2)}) collective-permute-start(bf16[128,1024]{1,0:T(8,128)(2,1)S(1)} %get-tuple-element.31.refs_0_), channel_id=1, source_target_pairs={{0,1},{1,0},{2,3},{3,2},{4,5},{5,4},{6,7},{7,6},{8,9},{9,8},{10,11... | collective-permute-start | bytes 786440 | tf_op jit(solution)/shard_map/ppermute | solution.py:147
  52.0 6.4 %collective-permute-start.10 = (bf16[128,1024]{1,0:T(8,128)(2,1)S(1)}, bf16[128,1024]{1,0:T(8,128)(2,1)S(1)}, u32[]{:S(2)}, u32[]{:S(2)}) collective-permute-start(bf16[128,1024]{1,0:T(8,128)(2,1)S(1)} %shard_map.60), channel_id=1, source_target_pairs={{0,1},{1,0},{2,3},{3,2},{4,5},{5,4},{6,7},{7,6},{8,9},{9,8},{10,11... | collective-permute-start | bytes 786440 | tf_op jit(solution)/shard_map/ppermute | solution.py:147
  54.0 9.4 %collective-permute-start.14 = (bf16[128,1024]{1,0:T(8,128)(2,1)S(1)}, bf16[128,1024]{1,0:T(8,128)(2,1)S(1)}, u32[]{:S(2)}, u32[]{:S(2)}) collective-permute-start(bf16[128,1024]{1,0:T(8,128)(2,1)S(1)} %add_convert_fusion.2), channel_id=1, source_target_pairs={{0,12},{4,0},{8,4},{12,8},{1,13},{5,1},{9,5},{13,9},{2,14},{6,2},{... | collective-permute-start | bytes 786440 | tf_op jit(solution)/shard_map/ppermute | solution.py:147
  58.5 11.4 %collective-permute-start.12 = (bf16[128,1024]{1,0:T(8,128)(2,1)S(1)}, bf16[128,1024]{1,0:T(8,128)(2,1)S(1)}, u32[]{:S(2)}, u32[]{:S(2)}) collective-permute-start(bf16[128,1024]{1,0:T(8,128)(2,1)S(1)} %add_convert_fusion.3), channel_id=1, source_target_pairs={{0,4},{4,8},{8,12},{12,0},{1,5},{5,9},{9,13},{13,1},{2,6},{6,10},{... | collective-permute-start | bytes 786440 | tf_op jit(solution)/shard_map/ppermute | solution.py:147
  58.9 8.2 %collective-permute-start.11 = (bf16[128,1024]{1,0:T(8,128)(2,1)S(1)}, bf16[128,1024]{1,0:T(8,128)(2,1)S(1)}, u32[]{:S(2)}, u32[]{:S(2)}) collective-permute-start(bf16[128,1024]{1,0:T(8,128)(2,1)S(1)} %get-tuple-element.35.refs_0_), channel_id=1, source_target_pairs={{0,1},{1,0},{2,3},{3,2},{4,5},{5,4},{6,7},{7,6},{8,9},{9,8},{10,11... | collective-permute-start | bytes 786440 | tf_op jit(solution)/shard_map/ppermute | solution.py:147
  63.5 8.2 %collective-permute-start.15 = (bf16[128,1024]{1,0:T(8,128)(2,1)S(1)}, bf16[128,1024]{1,0:T(8,128)(2,1)S(1)}, u32[]{:S(2)}, u32[]{:S(2)}) collective-permute-start(bf16[128,1024]{1,0:T(8,128)(2,1)S(1)} %add_convert_fusion.1), channel_id=1, source_target_pairs={{0,12},{4,0},{8,4},{12,8},{1,13},{5,1},{9,5},{13,9},{2,14},{6,2},{... | collective-permute-start | bytes 786440 | tf_op jit(solution)/shard_map/ppermute | solution.py:147

commit v8 on v6

--- a/solution.py
+++ b/solution.py
@@ -151,16 +151,6 @@
     return lax.optimization_barrier((array, first))[0]
 
 
-def shift_both(array, outer, step, inner, turn):
-    sizes = lax.axis_size(outer), lax.axis_size(inner)
-    pairs = [
-        (i * sizes[1] + k, (i + step) % sizes[0] * sizes[1] + (k + turn) % sizes[1])
-        for i in range(sizes[0])
-        for k in range(sizes[1])
-    ]
-    return lax.ppermute(array, (outer, inner), pairs)
-
-
 def local(latent, routes, gates, up_weight, down_weight):
     block, width = latent.shape
     top = routes.shape[1]
@@ -173,48 +163,57 @@
     tables = [*stage(ring[0], own), *moved]
     ring.append(follow(shift(ring[0], "z", 1), tables[0]))
     last = depth - 1
-    kept = [None] * depth
-    others, totals = [], {}
-    after = []
-
-    def total(j, behind=None):
-        rows = kept[j]
-        for s, other in enumerate(others[j], 1):
+    kept, others = {}, {}
+    totals, home = {}, None
+    firsts = []
+
+    def total(r, *behind):
+        rows = kept[r]
+        for s, other in enumerate(others[r], 1):
             other = shift(other, "sub", -s)
-            if behind is not None:
-                other = follow(other, behind)
+            for first in behind:
+                other = follow(other, first)
             rows = rows + other.astype(jnp.float32)
-        return rows.astype(jnp.bfloat16) if j else rows
+        return rows
 
     for j in range(depth):
         handed = [shift(ring[j], "sub", s) for s in range(1, subs)]
         fresh = ([0] if j == 0 else []) + [j + 1] * (j < last)
         kinds = [jnp.bfloat16] * len(handed)
-        kinds += [jnp.bfloat16 if r == last else jnp.float32 for r in fresh]
-        if j > 2:
-            totals[j - 2] = total(j - 2, after[0])
-            after.append(totals[j - 2])
-        partial = run_experts(
-            after, handed + [ring[r] for r in fresh], tables, kinds, block, slots
-        )
-        after = [partial[0]]
+        kinds += [jnp.bfloat16 if r == 1 else jnp.float32 for r in fresh]
+        after = firsts[-1:]
+        if j == last and j > 1:
+            rows = follow(shift(kept[1], "z", -1), firsts[-1])
+            home = kept[0] + rows.astype(jnp.float32)
+            after = after + [home]
+        if j > 3:
+            totals[j - 2] = total(j - 2, firsts[-1]).astype(jnp.bfloat16)
+            after = after + [totals[j - 2]]
+        partial = run_experts(after, handed + [ring[r] for r in fresh], tables, kinds, block, slots)
+        firsts.append(partial[0])
         if j + 2 < depth:
             ring.append(follow(shift(ring[-1], "z", 1), partial[0]))
         for r, rows in zip(fresh, partial[subs - 1 :]):
             kept[r] = rows
-        others.append(partial[: subs - 1])
-    corner = [shift_both(other, "z", -last, "sub", -s) for s, other in enumerate(others[last], 1)]
-    others[0] = [follow(other, others[last][0]) for other in others[0]]
-    for j in range(last):
-        if j not in totals:
-            totals[j] = total(j, others[last][0])
-    back = [shift(kept[last], "z", -last)] + [shift(totals[j], "z", -j) for j in range(1, last)]
-    late = back.pop()
-    home = sum(rows.astype(jnp.float32) for rows in back)
-    home, *corner = lax.optimization_barrier((home, *corner))
-    home = home + totals[0] + sum(rows.astype(jnp.float32) for rows in corner)
-    home, late = lax.optimization_barrier((home, late))
-    home = home + late.astype(jnp.float32)
+        others[j] = partial[: subs - 1]
+    if home is None:
+        home = kept[0] + sum(shift(kept[r], "z", -r).astype(jnp.float32) for r in range(1, depth))
+    joined = others[0]
+    if depth > 1:
+        joined = [
+            (mine.astype(jnp.float32) + shift(rows, "z", -1).astype(jnp.float32)).astype(jnp.bfloat16)
+            for mine, rows in zip(others[0], others[1])
+        ]
+    for r in range(2, depth):
+        if r not in totals:
+            behind = [firsts[-1]] + (joined if r < last else [])
+            totals[r] = total(r, *behind).astype(jnp.bfloat16)
+    for s, rows in enumerate(joined, 1):
+        if depth > 2:
+            rows = follow(rows, totals[last])
+        home = home + shift(rows, "sub", -s).astype(jnp.float32)
+    for r in range(2, depth):
+        home = home + shift(totals[r], "z", -r).astype(jnp.float32)
     return home.astype(jnp.bfloat16)
 
 

time: 70.9 us -> 68.5 us (0.966)
  waiting for transfers between devices: 31.7 us -> 28 us
  starting transfers between devices: 15.5 us -> 16.7 us
    ppermute x15 -> x16, waiting for transfers between devices: 31.5 us -> 28 us  [shift(): lax.ppermute(array, axis, [(i, (i + step) % size) for i in range(size)])]
    ppermute x15 -> x16, starting transfers between devices: 15.4 us -> 16.7 us  [shift(): lax.ppermute(array, axis, [(i, (i + step) % size) for i in range(size)])]
  transfers between devices with their start and end apart: 16 -> 16, of which waited for: 9 -> 8; matrix products, arithmetic and copies ran while one was open for 0% -> 0% of each run, Pallas kernels for 23% -> 24%
where the time goes in v8:
time: 68.5 us; the launch traced here: 68.3 us
  waiting for transfers between devices  28 us (41%)
  starting transfers between devices  16.7 us (24%)
  Pallas kernels  16.5 us (24%)
  local copies, waits for them, and re-layouts  5.87 us (9%)
  other arithmetic  1.07 us (2%)
    ppermute x16, waiting for transfers between devices, shift(): lax.ppermute(array, axis, [(i, (i + step) % size) for i in range(size)])  28 us
    ppermute x16, starting transfers between devices, shift(): lax.ppermute(array, axis, [(i, (i + step) % size) for i in range(size)])  16.7 us
    pallas_call x4, Pallas kernels, run_experts(): pl.pallas_call(functools.partial(expert_kernel, block, slots, unit, numbe...  15.8 us
    unnamed x10, local copies, waits for them, and re-layouts  5.87 us
  transfers between devices with their start and end apart: 16, of which 8 were waited for; matrix products, arithmetic and copies ran while one was open for 0% of the time, Pallas kernels for 24%

profile of v8, /device:TPU:0, one launch (start us, length us, event | category | flops | bytes accessed | tf_op | source)
XLA Modules:
  0.0 68.3 jit_solution(52120680457479137)
XLA Ops:
  0.0 0.5 collective-permute-start.2
  0.5 0.1 collective-permute-start.3
  0.5 0.0 copy-start.2
  0.5 0.9 %copy-done.2 = bf16[128,1024]{1,0:T(8,128)(2,1)S(1)} copy-done((bf16[128,1024]{1,0:T(8,128)(2,1)S(1)}, bf16[128,1024]{1,0:T(8,128)(2,1)}, u32[]{:S(2)}) %copy-start.2) | copy-done | bytes 262168
  1.5 0.7 copy-done.3
  2.1 0.7 copy-done.4
  2.9 3.1 %collective-permute-start.1 = (bf16[144,1024]{1,0:T(8,128)(2,1)S(1)}, bf16[144,1024]{1,0:T(8,128)(2,1)S(1)}, u32[]{:S(2)}, u32[]{:S(2)}) collective-permute-start(bf16[144,1024]{1,0:T(8,128)(2,1)S(1)} %shard_map.55.after_ref.refs_1_), channel_id=1, source_target_pairs={{0,4},{4,8},{8,12},{12,0},{1,5},{5,9},{9,13},{13,1},{2,6},{6,10},{... | collective-permute-start | bytes 884744 | tf_op jit(solution)/shard_map/ppermute | solution.py:147
  5.9 1.5 %collective-permute-start = (bf16[144,1024]{1,0:T(8,128)(2,1)S(1)}, bf16[144,1024]{1,0:T(8,128)(2,1)S(1)}, u32[]{:S(2)}, u32[]{:S(2)}) collective-permute-start(bf16[144,1024]{1,0:T(8,128)(2,1)S(1)} %shard_map.55.after_ref.refs_1_), channel_id=1, source_target_pairs={{0,1},{1,0},{2,3},{3,2},{4,5},{5,4},{6,7},{7,6},{8,9},{9,8},{10,11... | collective-permute-start | bytes 884744 | tf_op jit(solution)/shard_map/ppermute | solution.py:147
  7.4 1.8 %copy-done = bf16[1,1024,1344]{1,2,0:T(8,128)(2,1)S(1)} copy-done((bf16[1,1024,1344]{1,2,0:T(8,128)(2,1)S(1)}, bf16[1,1024,1344]{1,2,0:T(8,128)(2,1)}, u32[]{:S(2)}) %copy-start) | copy-done | bytes 2752536
  9.2 1.8 %copy-done.1 = bf16[1,1024,1344]{1,2,0:T(8,128)(2,1)S(1)} copy-done((bf16[1,1024,1344]{1,2,0:T(8,128)(2,1)S(1)}, bf16[1,1024,1344]{1,2,0:T(8,128)(2,1)}, u32[]{:S(2)}) %copy-start.1) | copy-done | bytes 2752536
  11.0 0.7 %shard_map.56 = (bf16[1,1344,1024]{2,1,0:T(8,128)(2,1)S(1)}, bf16[1,1344,1024]{2,1,0:T(8,128)(2,1)S(1)}) custom-call(bf16[144,1024]{1,0:T(8,128)(2,1)S(1)} %shard_map.55.after_ref.refs_1_, bf16[1,1344,1024]{2,1,0:T(8,128)(2,1)S(1)} %bitcast.5, bf16[1,1344,1024]{2,1,0:T(8,128)(2,1)S(1)} %bitcast.7), custom_call_target="tpu_custom_call" | custom-call | tf_op jit(solution)/shard_map/pallas_call | solution.py:55
  11.7 3.4 %collective-permute-done.1.refs_2_ = bf16[144,1024]{1,0:T(8,128)(2,1)S(1)} collective-permute-done((bf16[144,1024]{1,0:T(8,128)(2,1)S(1)}, bf16[144,1024]{1,0:T(8,128)(2,1)S(1)}, u32[]{:S(2)}, u32[]{:S(2)}) %collective-permute-start.1) | collective-permute-done | bytes 294944 | tf_op jit(solution)/shard_map/ppermute | solution.py:147
  15.1 0.0 collective-permute-start.6
  15.1 1.5 %collective-permute-start.5 = (bf16[144,1024]{1,0:T(8,128)(2,1)S(1)}, bf16[144,1024]{1,0:T(8,128)(2,1)S(1)}, u32[]{:S(2)}, u32[]{:S(2)}) collective-permute-start(bf16[144,1024]{1,0:T(8,128)(2,1)S(1)} %collective-permute-done.1.refs_2_), channel_id=1, source_target_pairs={{0,1},{1,0},{2,3},{3,2},{4,5},{5,4},{6,7},{7,6},{8,9},{9,8},{10,11... | collective-permute-start | bytes 884744 | tf_op jit(solution)/shard_map/ppermute | solution.py:147
  16.6 0.0 collective-permute-done.refs_0_
  16.6 0.0 collective-permute-done.2.refs_5_
  16.6 0.0 collective-permute-done.3.refs_6_
  16.6 4.9 %shard_map.57 = (bf16[128,1024]{1,0:T(8,128)(2,1)S(1)}, f32[128,1024]{1,0:T(8,128)S(1)}, bf16[128,1024]{1,0:T(8,128)(2,1)S(1)}) custom-call(bf16[144,1024]{1,0:T(8,128)(2,1)S(1)} %collective-permute-done.refs_0_, bf16[144,1024]{1,0:T(8,128)(2,1)S(1)} %shard_map.55.after_ref.refs_1_, bf16[144,1024]{1,0:T(8,128)(2,1)S(1)} %collective-permute-done.1.refs_2_, ...), custom_call_target="tpu_custom_call" | custom-call | flops 3472883712 | bytes 12976128 | tf_op jit(solution)/shard_map/pallas_call | solution.py:130
  21.5 3.8 %collective-permute-done.6.refs_2_ = bf16[144,1024]{1,0:T(8,128)(2,1)S(1)} collective-permute-done((bf16[144,1024]{1,0:T(8,128)(2,1)S(1)}, bf16[144,1024]{1,0:T(8,128)(2,1)S(1)}, u32[]{:S(2)}, u32[]{:S(2)}) %collective-permute-start.6) | collective-permute-done | bytes 294944 | tf_op jit(solution)/shard_map/ppermute | solution.py:147
  25.3 0.0 collective-permute-start.8
  25.3 1.3 %collective-permute-start.7 = (bf16[144,1024]{1,0:T(8,128)(2,1)S(1)}, bf16[144,1024]{1,0:T(8,128)(2,1)S(1)}, u32[]{:S(2)}, u32[]{:S(2)}) collective-permute-start(bf16[144,1024]{1,0:T(8,128)(2,1)S(1)} %collective-permute-done.6.refs_2_), channel_id=1, source_target_pairs={{0,1},{1,0},{2,3},{3,2},{4,5},{5,4},{6,7},{7,6},{8,9},{9,8},{10,11... | collective-permute-start | bytes 884744 | tf_op jit(solution)/shard_map/ppermute | solution.py:147
  26.6 3.8 %collective-permute-start.4 = (bf16[128,1024]{1,0:T(8,128)(2,1)S(1)}, bf16[128,1024]{1,0:T(8,128)(2,1)S(1)}, u32[]{:S(2)}, u32[]{:S(2)}) collective-permute-start(bf16[128,1024]{1,0:T(8,128)(2,1)S(1)} %get-tuple-element.26), channel_id=1, source_target_pairs={{0,12},{4,0},{8,4},{12,8},{1,13},{5,1},{9,5},{13,9},{2,14},{6,2},{... | collective-permute-start | bytes 786440 | tf_op jit(solution)/shard_map/ppermute | solution.py:147
  30.4 0.0 collective-permute-done.5.refs_1_
  30.4 3.8 %shard_map.58 = (bf16[128,1024]{1,0:T(8,128)(2,1)S(1)}, f32[128,1024]{1,0:T(8,128)S(1)}) custom-call(bf16[128,1024]{1,0:T(8,128)(2,1)S(1)} %get-tuple-element.27.refs_0_, bf16[144,1024]{1,0:T(8,128)(2,1)S(1)} %collective-permute-done.5.refs_1_, bf16[144,1024]{1,0:T(8,128)(2,1)S(1)} %collective-permute-done.6.refs_2_, ...), custom_call_target="tpu_custom_call" | custom-call | flops 2315255808 | bytes 12320768 | tf_op jit(solution)/shard_map/pallas_call | solution.py:130
  34.2 0.2 collective-permute-start.9
  34.5 2.6 %collective-permute-done.8.refs_2_ = bf16[144,1024]{1,0:T(8,128)(2,1)S(1)} collective-permute-done((bf16[144,1024]{1,0:T(8,128)(2,1)S(1)}, bf16[144,1024]{1,0:T(8,128)(2,1)S(1)}, u32[]{:S(2)}, u32[]{:S(2)}) %collective-permute-start.8) | collective-permute-done | bytes 294944 | tf_op jit(solution)/shard_map/ppermute | solution.py:147
  37.1 1.3 %collective-permute-start.10 = (bf16[144,1024]{1,0:T(8,128)(2,1)S(1)}, bf16[144,1024]{1,0:T(8,128)(2,1)S(1)}, u32[]{:S(2)}, u32[]{:S(2)}) collective-permute-start(bf16[144,1024]{1,0:T(8,128)(2,1)S(1)} %collective-permute-done.8.refs_2_), channel_id=1, source_target_pairs={{0,1},{1,0},{2,3},{3,2},{4,5},{5,4},{6,7},{7,6},{8,9},{9,8},{10,11... | collective-permute-start | bytes 884744 | tf_op jit(solution)/shard_map/ppermute | solution.py:147
  38.3 0.0 collective-permute-done.7.refs_1_
  38.3 3.8 %shard_map.59 = (bf16[128,1024]{1,0:T(8,128)(2,1)S(1)}, f32[128,1024]{1,0:T(8,128)S(1)}) custom-call(bf16[128,1024]{1,0:T(8,128)(2,1)S(1)} %get-tuple-element.29.refs_0_, bf16[144,1024]{1,0:T(8,128)(2,1)S(1)} %collective-permute-done.7.refs_1_, bf16[144,1024]{1,0:T(8,128)(2,1)S(1)} %collective-permute-done.8.refs_2_, ...), custom_call_target="tpu_custom_call" | custom-call | flops 2315255808 | bytes 12320768 | tf_op jit(solution)/shard_map/pallas_call | solution.py:130
  42.1 0.8 %collective-permute-start.13 = (bf16[128,1024]{1,0:T(8,128)(2,1)S(1)}, bf16[128,1024]{1,0:T(8,128)(2,1)S(1)}, u32[]{:S(2)}, u32[]{:S(2)}) collective-permute-start(bf16[128,1024]{1,0:T(8,128)(2,1)S(1)} %get-tuple-element.31.refs_0_), channel_id=1, source_target_pairs={{0,1},{1,0},{2,3},{3,2},{4,5},{5,4},{6,7},{7,6},{8,9},{9,8},{10,11... | collective-permute-start | bytes 786440 | tf_op jit(solution)/shard_map/ppermute | solution.py:147
  43.0 0.0 collective-permute-done.4
  43.0 0.1 convert_add_fusion.refs_1_
  43.0 3.3 %collective-permute-done.10.refs_2_ = bf16[144,1024]{1,0:T(8,128)(2,1)S(1)} collective-permute-done((bf16[144,1024]{1,0:T(8,128)(2,1)S(1)}, bf16[144,1024]{1,0:T(8,128)(2,1)S(1)}, u32[]{:S(2)}, u32[]{:S(2)}) %collective-permute-start.10) | collective-permute-done | bytes 294944 | tf_op jit(solution)/shard_map/ppermute | solution.py:147
  46.3 3.3 %shard_map.60 = bf16[128,1024]{1,0:T(8,128)(2,1)S(1)} custom-call(bf16[128,1024]{1,0:T(8,128)(2,1)S(1)} %get-tuple-element.31.refs_0_, f32[128,1024]{1,0:T(8,128)S(1)} %convert_add_fusion.refs_1_, bf16[144,1024]{1,0:T(8,128)(2,1)S(1)} %collective-permute-done.10.refs_2_, bf16[1,1344,1024]{2,1,0:T(8,128)(2,1)S(1)} %get-tuple-element.22.refs_3_, ...), custom_call_target="tpu_custom_call" | custom-call | flops 1157627904 | bytes 11665408 | tf_op jit(solution)/shard_map/pallas_call | solution.py:130
  49.6 1.7 %collective-permute-start.11 = (bf16[128,1024]{1,0:T(8,128)(2,1)S(1)}, bf16[128,1024]{1,0:T(8,128)(2,1)S(1)}, u32[]{:S(2)}, u32[]{:S(2)}) collective-permute-start(bf16[128,1024]{1,0:T(8,128)(2,1)S(1)} %shard_map.60), channel_id=1, source_target_pairs={{0,1},{1,0},{2,3},{3,2},{4,5},{5,4},{6,7},{7,6},{8,9},{9,8},{10,11... | collective-permute-start | bytes 786440 | tf_op jit(solution)/shard_map/ppermute | solution.py:147
  51.3 0.0 collective-permute-done.9
  51.3 0.1 add_convert_fusion.3
  51.3 0.0 collective-permute-done.13
  51.3 0.1 add_convert_fusion.1
  51.4 0.1 collective-permute-start.14
  51.5 6.7 %collective-permute-done.11 = bf16[128,1024]{1,0:T(8,128)(2,1)S(1)} collective-permute-done((bf16[128,1024]{1,0:T(8,128)(2,1)S(1)}, bf16[128,1024]{1,0:T(8,128)(2,1)S(1)}, u32[]{:S(2)}, u32[]{:S(2)}) %collective-permute-start.11) | collective-permute-done | bytes 262176 | tf_op jit(solution)/shard_map/ppermute | solution.py:147
  58.2 0.1 add_convert_fusion.2
  58.3 1.0 %collective-permute-start.12 = (bf16[128,1024]{1,0:T(8,128)(2,1)S(1)}, bf16[128,1024]{1,0:T(8,128)(2,1)S(1)}, u32[]{:S(2)}, u32[]{:S(2)}) collective-permute-start(bf16[128,1024]{1,0:T(8,128)(2,1)S(1)} %add_convert_fusion.3), channel_id=1, source_target_pairs={{0,1},{1,0},{2,3},{3,2},{4,5},{5,4},{6,7},{7,6},{8,9},{9,8},{10,11... | collective-permute-start | bytes 786440 | tf_op jit(solution)/shard_map/ppermute | solution.py:147
  59.2 0.0 collective-permute-start.15
  59.2 4.2 %collective-permute-done.14 = bf16[128,1024]{1,0:T(8,128)(2,1)S(1)} collective-permute-done((bf16[128,1024]{1,0:T(8,128)(2,1)S(1)}, bf16[128,1024]{1,0:T(8,128)(2,1)S(1)}, u32[]{:S(2)}, u32[]{:S(2)}) %collective-permute-start.14) | collective-permute-done | bytes 262176 | tf_op jit(solution)/shard_map/ppermute | solution.py:147
  63.4 1.3 %collective-permute-done.12 = bf16[128,1024]{1,0:T(8,128)(2,1)S(1)} collective-permute-done((bf16[128,1024]{1,0:T(8,128)(2,1)S(1)}, bf16[128,1024]{1,0:T(8,128)(2,1)S(1)}, u32[]{:S(2)}, u32[]{:S(2)}) %collective-permute-start.12) | collective-permute-done | bytes 262176 | tf_op jit(solution)/shard_map/ppermute | solution.py:147
  64.7 2.7 %collective-permute-done.15 = bf16[128,1024]{1,0:T(8,128)(2,1)S(1)} collective-permute-done((bf16[128,1024]{1,0:T(8,128)(2,1)S(1)}, bf16[128,1024]{1,0:T(8,128)(2,1)S(1)}, u32[]{:S(2)}, u32[]{:S(2)}) %collective-permute-start.15) | collective-permute-done | bytes 262176 | tf_op jit(solution)/shard_map/ppermute | solution.py:147
  67.4 0.8 %add_convert_fusion = bf16[128,1024]{1,0:T(8,128)(2,1)} fusion(bf16[128,1024]{1,0:T(8,128)(2,1)S(1)} %collective-permute-done.15, bf16[128,1024]{1,0:T(8,128)(2,1)S(1)} %collective-permute-done.14, f32[128,1024]{1,0:T(8,128)S(1)} %convert_add_fusion.refs_1_, bf16[128,1024]{1,0:T(8,128)(2,1)S(1)} %collective-permute-done.12), kind=kLoop, calls=%fused_computation | loop fusion | flops 917504 | bytes 1572864 | tf_op jit(solution)/shard_map/convert_element_type | solution.py:217
  (5 shorter events, 0.0 us)
Async XLA Ops:
  0.0 16.6 %collective-permute-start.2 = (bf16[1,1344,1024]{2,1,0:T(8,128)(2,1)}, bf16[1,1344,1024]{2,1,0:T(8,128)(2,1)S(1)}, u32[]{:S(2)}, u32[]{:S(2)}) collective-permute-start(bf16[1,1344,1024]{2,1,0:T(8,128)(2,1)} %bitcast.4), channel_id=1, source_target_pairs={{0,2},{2,0},{1,3},{3,1},{4,6},{6,4},{5,7},{7,5},{8,10},{10,8},{9,1... | collective-permute-start | bytes 8257544 | tf_op jit(solution)/shard_map/ppermute | solution.py:147
  0.5 16.2 %collective-permute-start.3 = (bf16[1,1344,1024]{2,1,0:T(8,128)(2,1)}, bf16[1,1344,1024]{2,1,0:T(8,128)(2,1)S(1)}, u32[]{:S(2)}, u32[]{:S(2)}) collective-permute-start(bf16[1,1344,1024]{2,1,0:T(8,128)(2,1)} %bitcast.6), channel_id=1, source_target_pairs={{0,2},{2,0},{1,3},{3,1},{4,6},{6,4},{5,7},{7,5},{8,10},{10,8},{9,1... | collective-permute-start | bytes 8257544 | tf_op jit(solution)/shard_map/ppermute | solution.py:147
  0.5 0.9 %copy-start.2 = (bf16[128,1024]{1,0:T(8,128)(2,1)S(1)}, bf16[128,1024]{1,0:T(8,128)(2,1)}, u32[]{:S(2)}) copy-start(bf16[128,1024]{1,0:T(8,128)(2,1)} %latent_ref.1) | copy-start | bytes 786436
  1.5 0.7 copy-start.3
  2.1 0.7 copy-start.4
  2.9 12.3 %collective-permute-start.1 = (bf16[144,1024]{1,0:T(8,128)(2,1)S(1)}, bf16[144,1024]{1,0:T(8,128)(2,1)S(1)}, u32[]{:S(2)}, u32[]{:S(2)}) collective-permute-start(bf16[144,1024]{1,0:T(8,128)(2,1)S(1)} %shard_map.55.after_ref.refs_1_), channel_id=1, source_target_pairs={{0,4},{4,8},{8,12},{12,0},{1,5},{5,9},{9,13},{13,1},{2,6},{6,10},{... | collective-permute-start | bytes 884744 | tf_op jit(solution)/shard_map/ppermute | solution.py:147
  5.9 10.7 %collective-permute-start = (bf16[144,1024]{1,0:T(8,128)(2,1)S(1)}, bf16[144,1024]{1,0:T(8,128)(2,1)S(1)}, u32[]{:S(2)}, u32[]{:S(2)}) collective-permute-start(bf16[144,1024]{1,0:T(8,128)(2,1)S(1)} %shard_map.55.after_ref.refs_1_), channel_id=1, source_target_pairs={{0,1},{1,0},{2,3},{3,2},{4,5},{5,4},{6,7},{7,6},{8,9},{9,8},{10,11... | collective-permute-start | bytes 884744 | tf_op jit(solution)/shard_map/ppermute | solution.py:147
  7.4 1.8 %copy-start = (bf16[1,1024,1344]{1,2,0:T(8,128)(2,1)S(1)}, bf16[1,1024,1344]{1,2,0:T(8,128)(2,1)}, u32[]{:S(2)}) copy-start(bf16[1,1024,1344]{1,2,0:T(8,128)(2,1)} %param.8) | copy-start | bytes 8257540
  9.2 1.8 %copy-start.1 = (bf16[1,1024,1344]{1,2,0:T(8,128)(2,1)S(1)}, bf16[1,1024,1344]{1,2,0:T(8,128)(2,1)}, u32[]{:S(2)}) copy-start(bf16[1,1024,1344]{1,2,0:T(8,128)(2,1)} %param.9) | copy-start | bytes 8257540
  15.1 10.2 %collective-permute-start.6 = (bf16[144,1024]{1,0:T(8,128)(2,1)S(1)}, bf16[144,1024]{1,0:T(8,128)(2,1)S(1)}, u32[]{:S(2)}, u32[]{:S(2)}) collective-permute-start(bf16[144,1024]{1,0:T(8,128)(2,1)S(1)} %collective-permute-done.1.refs_2_), channel_id=1, source_target_pairs={{0,4},{4,8},{8,12},{12,0},{1,5},{5,9},{9,13},{13,1},{2,6},{6,10},{... | collective-permute-start | bytes 884744 | tf_op jit(solution)/shard_map/ppermute | solution.py:147
  15.1 15.3 %collective-permute-start.5 = (bf16[144,1024]{1,0:T(8,128)(2,1)S(1)}, bf16[144,1024]{1,0:T(8,128)(2,1)S(1)}, u32[]{:S(2)}, u32[]{:S(2)}) collective-permute-start(bf16[144,1024]{1,0:T(8,128)(2,1)S(1)} %collective-permute-done.1.refs_2_), channel_id=1, source_target_pairs={{0,1},{1,0},{2,3},{3,2},{4,5},{5,4},{6,7},{7,6},{8,9},{9,8},{10,11... | collective-permute-start | bytes 884744 | tf_op jit(solution)/shard_map/ppermute | solution.py:147
  25.3 11.7 %collective-permute-start.8 = (bf16[144,1024]{1,0:T(8,128)(2,1)S(1)}, bf16[144,1024]{1,0:T(8,128)(2,1)S(1)}, u32[]{:S(2)}, u32[]{:S(2)}) collective-permute-start(bf16[144,1024]{1,0:T(8,128)(2,1)S(1)} %collective-permute-done.6.refs_2_), channel_id=1, source_target_pairs={{0,4},{4,8},{8,12},{12,0},{1,5},{5,9},{9,13},{13,1},{2,6},{6,10},{... | collective-permute-start | bytes 884744 | tf_op jit(solution)/shard_map/ppermute | solution.py:147
  25.3 13.0 %collective-permute-start.7 = (bf16[144,1024]{1,0:T(8,128)(2,1)S(1)}, bf16[144,1024]{1,0:T(8,128)(2,1)S(1)}, u32[]{:S(2)}, u32[]{:S(2)}) collective-permute-start(bf16[144,1024]{1,0:T(8,128)(2,1)S(1)} %collective-permute-done.6.refs_2_), channel_id=1, source_target_pairs={{0,1},{1,0},{2,3},{3,2},{4,5},{5,4},{6,7},{7,6},{8,9},{9,8},{10,11... | collective-permute-start | bytes 884744 | tf_op jit(solution)/shard_map/ppermute | solution.py:147
  26.6 16.4 %collective-permute-start.4 = (bf16[128,1024]{1,0:T(8,128)(2,1)S(1)}, bf16[128,1024]{1,0:T(8,128)(2,1)S(1)}, u32[]{:S(2)}, u32[]{:S(2)}) collective-permute-start(bf16[128,1024]{1,0:T(8,128)(2,1)S(1)} %get-tuple-element.26), channel_id=1, source_target_pairs={{0,12},{4,0},{8,4},{12,8},{1,13},{5,1},{9,5},{13,9},{2,14},{6,2},{... | collective-permute-start | bytes 786440 | tf_op jit(solution)/shard_map/ppermute | solution.py:147
  34.2 17.0 %collective-permute-start.9 = (bf16[128,1024]{1,0:T(8,128)(2,1)S(1)}, bf16[128,1024]{1,0:T(8,128)(2,1)S(1)}, u32[]{:S(2)}, u32[]{:S(2)}) collective-permute-start(bf16[128,1024]{1,0:T(8,128)(2,1)S(1)} %get-tuple-element.29.refs_0_), channel_id=1, source_target_pairs={{0,12},{4,0},{8,4},{12,8},{1,13},{5,1},{9,5},{13,9},{2,14},{6,2},{... | collective-permute-start | bytes 786440 | tf_op jit(solution)/shard_map/ppermute | solution.py:147
  37.1 9.2 %collective-permute-start.10 = (bf16[144,1024]{1,0:T(8,128)(2,1)S(1)}, bf16[144,1024]{1,0:T(8,128)(2,1)S(1)}, u32[]{:S(2)}, u32[]{:S(2)}) collective-permute-start(bf16[144,1024]{1,0:T(8,128)(2,1)S(1)} %collective-permute-done.8.refs_2_), channel_id=1, source_target_pairs={{0,1},{1,0},{2,3},{3,2},{4,5},{5,4},{6,7},{7,6},{8,9},{9,8},{10,11... | collective-permute-start | bytes 884744 | tf_op jit(solution)/shard_map/ppermute | solution.py:147
  42.1 9.2 %collective-permute-start.13 = (bf16[128,1024]{1,0:T(8,128)(2,1)S(1)}, bf16[128,1024]{1,0:T(8,128)(2,1)S(1)}, u32[]{:S(2)}, u32[]{:S(2)}) collective-permute-start(bf16[128,1024]{1,0:T(8,128)(2,1)S(1)} %get-tuple-element.31.refs_0_), channel_id=1, source_target_pairs={{0,1},{1,0},{2,3},{3,2},{4,5},{5,4},{6,7},{7,6},{8,9},{9,8},{10,11... | collective-permute-start | bytes 786440 | tf_op jit(solution)/shard_map/ppermute | solution.py:147
  49.6 8.7 %collective-permute-start.11 = (bf16[128,1024]{1,0:T(8,128)(2,1)S(1)}, bf16[128,1024]{1,0:T(8,128)(2,1)S(1)}, u32[]{:S(2)}, u32[]{:S(2)}) collective-permute-start(bf16[128,1024]{1,0:T(8,128)(2,1)S(1)} %shard_map.60), channel_id=1, source_target_pairs={{0,1},{1,0},{2,3},{3,2},{4,5},{5,4},{6,7},{7,6},{8,9},{9,8},{10,11... | collective-permute-start | bytes 786440 | tf_op jit(solution)/shard_map/ppermute | solution.py:147
  51.4 12.0 %collective-permute-start.14 = (bf16[128,1024]{1,0:T(8,128)(2,1)S(1)}, bf16[128,1024]{1,0:T(8,128)(2,1)S(1)}, u32[]{:S(2)}, u32[]{:S(2)}) collective-permute-start(bf16[128,1024]{1,0:T(8,128)(2,1)S(1)} %add_convert_fusion.1), channel_id=1, source_target_pairs={{0,8},{4,12},{8,0},{12,4},{1,9},{5,13},{9,1},{13,5},{2,10},{6,14},... | collective-permute-start | bytes 786440 | tf_op jit(solution)/shard_map/ppermute | solution.py:147
  58.3 6.4 %collective-permute-start.12 = (bf16[128,1024]{1,0:T(8,128)(2,1)S(1)}, bf16[128,1024]{1,0:T(8,128)(2,1)S(1)}, u32[]{:S(2)}, u32[]{:S(2)}) collective-permute-start(bf16[128,1024]{1,0:T(8,128)(2,1)S(1)} %add_convert_fusion.3), channel_id=1, source_target_pairs={{0,1},{1,0},{2,3},{3,2},{4,5},{5,4},{6,7},{7,6},{8,9},{9,8},{10,11... | collective-permute-start | bytes 786440 | tf_op jit(solution)/shard_map/ppermute | solution.py:147
  59.2 8.2 %collective-permute-start.15 = (bf16[128,1024]{1,0:T(8,128)(2,1)S(1)}, bf16[128,1024]{1,0:T(8,128)(2,1)S(1)}, u32[]{:S(2)}, u32[]{:S(2)}) collective-permute-start(bf16[128,1024]{1,0:T(8,128)(2,1)S(1)} %add_convert_fusion.2), channel_id=1, source_target_pairs={{0,4},{4,8},{8,12},{12,0},{1,5},{5,9},{9,13},{13,1},{2,6},{6,10},{... | collective-permute-start | bytes 786440 | tf_op jit(solution)/shard_map/ppermute | solution.py:147

commit v9 on v8

--- a/solution.py
+++ b/solution.py
@@ -201,19 +201,28 @@
     joined = others[0]
     if depth > 1:
         joined = [
-            (mine.astype(jnp.float32) + shift(rows, "z", -1).astype(jnp.float32)).astype(jnp.bfloat16)
+            (
+                mine.astype(jnp.float32)
+                + shift(follow(rows, ring[last]), "z", -1).astype(jnp.float32)
+            ).astype(jnp.bfloat16)
             for mine, rows in zip(others[0], others[1])
         ]
     for r in range(2, depth):
         if r not in totals:
-            behind = [firsts[-1]] + (joined if r < last else [])
+            behind = [firsts[-1]] + (joined if r < last else [totals[r - 1]] * (r > 2))
             totals[r] = total(r, *behind).astype(jnp.bfloat16)
+    came = []
+    for r in range(2, depth):
+        rows = shift(totals[r], "z", -r)
+        came.append(follow(rows, came[-1]) if came else rows)
     for s, rows in enumerate(joined, 1):
-        if depth > 2:
-            rows = follow(rows, totals[last])
-        home = home + shift(rows, "sub", -s).astype(jnp.float32)
-    for r in range(2, depth):
-        home = home + shift(totals[r], "z", -r).astype(jnp.float32)
+        if came:
+            rows = follow(shift(follow(rows, totals[last]), "sub", -s), came[-1])
+        else:
+            rows = shift(rows, "sub", -s)
+        home = home + rows.astype(jnp.float32)
+    for rows in came:
+        home = home + rows.astype(jnp.float32)
     return home.astype(jnp.bfloat16)
 
 

time: 68.5 us -> 67.7 us (0.988)
  waiting for transfers between devices: 28 us -> 27.3 us
  transfers between devices with their start and end apart: 16 -> 16, of which waited for: 8 -> 7; matrix products, arithmetic and copies ran while one was open for 0% -> 0% of each run, Pallas kernels for 24% -> 25%
where the time goes in v9:
time: 67.7 us; the launch traced here: 67.4 us
  waiting for transfers between devices  27.3 us (40%)
  starting transfers between devices  16.5 us (24%)
  Pallas kernels  16.5 us (24%)
  local copies, waits for them, and re-layouts  5.87 us (9%)
  other arithmetic  1.07 us (2%)
    ppermute x16, waiting for transfers between devices, shift(): lax.ppermute(array, axis, [(i, (i + step) % size) for i in range(size)])  27.3 us
    ppermute x16, starting transfers between devices, shift(): lax.ppermute(array, axis, [(i, (i + step) % size) for i in range(size)])  16.5 us
    pallas_call x4, Pallas kernels, run_experts(): pl.pallas_call(functools.partial(expert_kernel, block, slots, unit, numbe...  15.8 us
    unnamed x10, local copies, waits for them, and re-layouts  5.87 us
  transfers between devices with their start and end apart: 16, of which 7 were waited for; matrix products, arithmetic and copies ran while one was open for 0% of the time, Pallas kernels for 25%

profile of v9, /device:TPU:0, one launch (start us, length us, event | category | flops | bytes accessed | tf_op | source)
XLA Modules:
  0.0 67.4 jit_solution(14709551477066397657)
XLA Ops:
  0.0 0.5 collective-permute-start.2
  0.5 0.1 collective-permute-start.3
  0.5 0.0 copy-start.2
  0.5 0.9 %copy-done.2 = bf16[128,1024]{1,0:T(8,128)(2,1)S(1)} copy-done((bf16[128,1024]{1,0:T(8,128)(2,1)S(1)}, bf16[128,1024]{1,0:T(8,128)(2,1)}, u32[]{:S(2)}) %copy-start.2) | copy-done | bytes 262168
  1.5 0.7 %copy-done.3 = s32[128,4]{0,1:T(4,128)S(1)} copy-done((s32[128,4]{0,1:T(4,128)S(1)}, s32[128,4]{0,1:T(4,128)}, u32[]{:S(2)}) %copy-start.3) | copy-done | bytes 2072
  2.1 0.7 %copy-done.4 = f32[128,4]{0,1:T(4,128)S(1)} copy-done((f32[128,4]{0,1:T(4,128)S(1)}, f32[128,4]{0,1:T(4,128)}, u32[]{:S(2)}) %copy-start.4) | copy-done | bytes 2072
  2.9 3.1 %collective-permute-start.1 = (bf16[144,1024]{1,0:T(8,128)(2,1)S(1)}, bf16[144,1024]{1,0:T(8,128)(2,1)S(1)}, u32[]{:S(2)}, u32[]{:S(2)}) collective-permute-start(bf16[144,1024]{1,0:T(8,128)(2,1)S(1)} %shard_map.55.after_ref.refs_1_), channel_id=1, source_target_pairs={{0,4},{4,8},{8,12},{12,0},{1,5},{5,9},{9,13},{13,1},{2,6},{6,10},{... | collective-permute-start | bytes 884744 | tf_op jit(solution)/shard_map/ppermute | solution.py:147
  5.9 1.5 %collective-permute-start = (bf16[144,1024]{1,0:T(8,128)(2,1)S(1)}, bf16[144,1024]{1,0:T(8,128)(2,1)S(1)}, u32[]{:S(2)}, u32[]{:S(2)}) collective-permute-start(bf16[144,1024]{1,0:T(8,128)(2,1)S(1)} %shard_map.55.after_ref.refs_1_), channel_id=1, source_target_pairs={{0,1},{1,0},{2,3},{3,2},{4,5},{5,4},{6,7},{7,6},{8,9},{9,8},{10,11... | collective-permute-start | bytes 884744 | tf_op jit(solution)/shard_map/ppermute | solution.py:147
  7.4 1.8 %copy-done = bf16[1,1024,1344]{1,2,0:T(8,128)(2,1)S(1)} copy-done((bf16[1,1024,1344]{1,2,0:T(8,128)(2,1)S(1)}, bf16[1,1024,1344]{1,2,0:T(8,128)(2,1)}, u32[]{:S(2)}) %copy-start) | copy-done | bytes 2752536
  9.2 1.8 %copy-done.1 = bf16[1,1024,1344]{1,2,0:T(8,128)(2,1)S(1)} copy-done((bf16[1,1024,1344]{1,2,0:T(8,128)(2,1)S(1)}, bf16[1,1024,1344]{1,2,0:T(8,128)(2,1)}, u32[]{:S(2)}) %copy-start.1) | copy-done | bytes 2752536
  11.0 0.7 %shard_map.56 = (bf16[1,1344,1024]{2,1,0:T(8,128)(2,1)S(1)}, bf16[1,1344,1024]{2,1,0:T(8,128)(2,1)S(1)}) custom-call(bf16[144,1024]{1,0:T(8,128)(2,1)S(1)} %shard_map.55.after_ref.refs_1_, bf16[1,1344,1024]{2,1,0:T(8,128)(2,1)S(1)} %bitcast.5, bf16[1,1344,1024]{2,1,0:T(8,128)(2,1)S(1)} %bitcast.7), custom_call_target="tpu_custom_call" | custom-call | tf_op jit(solution)/shard_map/pallas_call | solution.py:55
  11.7 3.4 %collective-permute-done.1.refs_2_ = bf16[144,1024]{1,0:T(8,128)(2,1)S(1)} collective-permute-done((bf16[144,1024]{1,0:T(8,128)(2,1)S(1)}, bf16[144,1024]{1,0:T(8,128)(2,1)S(1)}, u32[]{:S(2)}, u32[]{:S(2)}) %collective-permute-start.1) | collective-permute-done | bytes 294944 | tf_op jit(solution)/shard_map/ppermute | solution.py:147
  15.1 0.0 collective-permute-start.6
  15.1 1.5 %collective-permute-start.5 = (bf16[144,1024]{1,0:T(8,128)(2,1)S(1)}, bf16[144,1024]{1,0:T(8,128)(2,1)S(1)}, u32[]{:S(2)}, u32[]{:S(2)}) collective-permute-start(bf16[144,1024]{1,0:T(8,128)(2,1)S(1)} %collective-permute-done.1.refs_2_), channel_id=1, source_target_pairs={{0,1},{1,0},{2,3},{3,2},{4,5},{5,4},{6,7},{7,6},{8,9},{9,8},{10,11... | collective-permute-start | bytes 884744 | tf_op jit(solution)/shard_map/ppermute | solution.py:147
  16.6 0.0 collective-permute-done.refs_0_
  16.6 0.0 collective-permute-done.2.refs_5_
  16.6 0.0 collective-permute-done.3.refs_6_
  16.6 4.9 %shard_map.57 = (bf16[128,1024]{1,0:T(8,128)(2,1)S(1)}, f32[128,1024]{1,0:T(8,128)S(1)}, bf16[128,1024]{1,0:T(8,128)(2,1)S(1)}) custom-call(bf16[144,1024]{1,0:T(8,128)(2,1)S(1)} %collective-permute-done.refs_0_, bf16[144,1024]{1,0:T(8,128)(2,1)S(1)} %shard_map.55.after_ref.refs_1_, bf16[144,1024]{1,0:T(8,128)(2,1)S(1)} %collective-permute-done.1.refs_2_, ...), custom_call_target="tpu_custom_call" | custom-call | flops 3472883712 | bytes 12976128 | tf_op jit(solution)/shard_map/pallas_call | solution.py:130
  21.5 3.8 %collective-permute-done.6.refs_2_ = bf16[144,1024]{1,0:T(8,128)(2,1)S(1)} collective-permute-done((bf16[144,1024]{1,0:T(8,128)(2,1)S(1)}, bf16[144,1024]{1,0:T(8,128)(2,1)S(1)}, u32[]{:S(2)}, u32[]{:S(2)}) %collective-permute-start.6) | collective-permute-done | bytes 294944 | tf_op jit(solution)/shard_map/ppermute | solution.py:147
  25.3 0.0 collective-permute-start.8
  25.3 1.3 %collective-permute-start.7 = (bf16[144,1024]{1,0:T(8,128)(2,1)S(1)}, bf16[144,1024]{1,0:T(8,128)(2,1)S(1)}, u32[]{:S(2)}, u32[]{:S(2)}) collective-permute-start(bf16[144,1024]{1,0:T(8,128)(2,1)S(1)} %collective-permute-done.6.refs_2_), channel_id=1, source_target_pairs={{0,1},{1,0},{2,3},{3,2},{4,5},{5,4},{6,7},{7,6},{8,9},{9,8},{10,11... | collective-permute-start | bytes 884744 | tf_op jit(solution)/shard_map/ppermute | solution.py:147
  26.6 3.8 %collective-permute-start.4 = (bf16[128,1024]{1,0:T(8,128)(2,1)S(1)}, bf16[128,1024]{1,0:T(8,128)(2,1)S(1)}, u32[]{:S(2)}, u32[]{:S(2)}) collective-permute-start(bf16[128,1024]{1,0:T(8,128)(2,1)S(1)} %get-tuple-element.30), channel_id=1, source_target_pairs={{0,12},{4,0},{8,4},{12,8},{1,13},{5,1},{9,5},{13,9},{2,14},{6,2},{... | collective-permute-start | bytes 786440 | tf_op jit(solution)/shard_map/ppermute | solution.py:147
  30.4 0.0 collective-permute-done.5.refs_1_
  30.4 3.8 %shard_map.58 = (bf16[128,1024]{1,0:T(8,128)(2,1)S(1)}, f32[128,1024]{1,0:T(8,128)S(1)}) custom-call(bf16[128,1024]{1,0:T(8,128)(2,1)S(1)} %get-tuple-element.31.refs_0_, bf16[144,1024]{1,0:T(8,128)(2,1)S(1)} %collective-permute-done.5.refs_1_, bf16[144,1024]{1,0:T(8,128)(2,1)S(1)} %collective-permute-done.6.refs_2_, ...), custom_call_target="tpu_custom_call" | custom-call | flops 2315255808 | bytes 12320768 | tf_op jit(solution)/shard_map/pallas_call | solution.py:130
  34.2 2.8 %collective-permute-done.8.refs_2_ = bf16[144,1024]{1,0:T(8,128)(2,1)S(1)} collective-permute-done((bf16[144,1024]{1,0:T(8,128)(2,1)S(1)}, bf16[144,1024]{1,0:T(8,128)(2,1)S(1)}, u32[]{:S(2)}, u32[]{:S(2)}) %collective-permute-start.8) | collective-permute-done | bytes 294944 | tf_op jit(solution)/shard_map/ppermute | solution.py:147
  37.1 1.3 %collective-permute-start.10 = (bf16[144,1024]{1,0:T(8,128)(2,1)S(1)}, bf16[144,1024]{1,0:T(8,128)(2,1)S(1)}, u32[]{:S(2)}, u32[]{:S(2)}) collective-permute-start(bf16[144,1024]{1,0:T(8,128)(2,1)S(1)} %collective-permute-done.8.refs_2_), channel_id=1, source_target_pairs={{0,1},{1,0},{2,3},{3,2},{4,5},{5,4},{6,7},{7,6},{8,9},{9,8},{10,11... | collective-permute-start | bytes 884744 | tf_op jit(solution)/shard_map/ppermute | solution.py:147
  38.3 0.0 collective-permute-start.9
  38.3 0.0 collective-permute-done.7.refs_1_
  38.3 3.8 %shard_map.59 = (bf16[128,1024]{1,0:T(8,128)(2,1)S(1)}, f32[128,1024]{1,0:T(8,128)S(1)}) custom-call(bf16[128,1024]{1,0:T(8,128)(2,1)S(1)} %get-tuple-element.37.refs_0_, bf16[144,1024]{1,0:T(8,128)(2,1)S(1)} %collective-permute-done.7.refs_1_, bf16[144,1024]{1,0:T(8,128)(2,1)S(1)} %collective-permute-done.8.refs_2_, ...), custom_call_target="tpu_custom_call" | custom-call | flops 2315255808 | bytes 12320768 | tf_op jit(solution)/shard_map/pallas_call | solution.py:130
  42.1 0.8 %collective-permute-start.12 = (bf16[128,1024]{1,0:T(8,128)(2,1)S(1)}, bf16[128,1024]{1,0:T(8,128)(2,1)S(1)}, u32[]{:S(2)}, u32[]{:S(2)}) collective-permute-start(bf16[128,1024]{1,0:T(8,128)(2,1)S(1)} %get-tuple-element.35.refs_0_), channel_id=1, source_target_pairs={{0,1},{1,0},{2,3},{3,2},{4,5},{5,4},{6,7},{7,6},{8,9},{9,8},{10,11... | collective-permute-start | bytes 786440 | tf_op jit(solution)/shard_map/ppermute | solution.py:147
  43.0 0.0 collective-permute-done.4
  43.0 0.1 convert_add_fusion.refs_1_
  43.1 3.3 %collective-permute-done.10.refs_2_ = bf16[144,1024]{1,0:T(8,128)(2,1)S(1)} collective-permute-done((bf16[144,1024]{1,0:T(8,128)(2,1)S(1)}, bf16[144,1024]{1,0:T(8,128)(2,1)S(1)}, u32[]{:S(2)}, u32[]{:S(2)}) %collective-permute-start.10) | collective-permute-done | bytes 294944 | tf_op jit(solution)/shard_map/ppermute | solution.py:147
  46.3 3.3 %shard_map.60 = bf16[128,1024]{1,0:T(8,128)(2,1)S(1)} custom-call(bf16[128,1024]{1,0:T(8,128)(2,1)S(1)} %get-tuple-element.35.refs_0_, f32[128,1024]{1,0:T(8,128)S(1)} %convert_add_fusion.refs_1_, bf16[144,1024]{1,0:T(8,128)(2,1)S(1)} %collective-permute-done.10.refs_2_, bf16[1,1344,1024]{2,1,0:T(8,128)(2,1)S(1)} %get-tuple-element.26.refs_3_, ...), custom_call_target="tpu_custom_call" | custom-call | flops 1157627904 | bytes 11665408 | tf_op jit(solution)/shard_map/pallas_call | solution.py:130
  49.6 1.7 %collective-permute-start.11 = (bf16[128,1024]{1,0:T(8,128)(2,1)S(1)}, bf16[128,1024]{1,0:T(8,128)(2,1)S(1)}, u32[]{:S(2)}, u32[]{:S(2)}) collective-permute-start(bf16[128,1024]{1,0:T(8,128)(2,1)S(1)} %shard_map.60), channel_id=1, source_target_pairs={{0,1},{1,0},{2,3},{3,2},{4,5},{5,4},{6,7},{7,6},{8,9},{9,8},{10,11... | collective-permute-start | bytes 786440 | tf_op jit(solution)/shard_map/ppermute | solution.py:147
  51.3 0.0 collective-permute-done.9
  51.3 0.1 add_convert_fusion.3
  51.4 0.0 collective-permute-done.12
  51.4 0.1 add_convert_fusion.2
  51.4 0.1 collective-permute-start.15
  51.5 6.8 %collective-permute-done.11 = bf16[128,1024]{1,0:T(8,128)(2,1)S(1)} collective-permute-done((bf16[128,1024]{1,0:T(8,128)(2,1)S(1)}, bf16[128,1024]{1,0:T(8,128)(2,1)S(1)}, u32[]{:S(2)}, u32[]{:S(2)}) %collective-permute-start.11) | collective-permute-done | bytes 262176 | tf_op jit(solution)/shard_map/ppermute | solution.py:147
  58.3 0.1 add_convert_fusion.1
  58.3 0.1 collective-permute-start.14
  58.4 1.0 %collective-permute-start.13 = (bf16[128,1024]{1,0:T(8,128)(2,1)S(1)}, bf16[128,1024]{1,0:T(8,128)(2,1)S(1)}, u32[]{:S(2)}, u32[]{:S(2)}) collective-permute-start(bf16[128,1024]{1,0:T(8,128)(2,1)S(1)} %add_convert_fusion.3), channel_id=1, source_target_pairs={{0,1},{1,0},{2,3},{3,2},{4,5},{5,4},{6,7},{7,6},{8,9},{9,8},{10,11... | collective-permute-start | bytes 786440 | tf_op jit(solution)/shard_map/ppermute | solution.py:147
  59.4 3.4 %collective-permute-done.15 = bf16[128,1024]{1,0:T(8,128)(2,1)S(1)} collective-permute-done((bf16[128,1024]{1,0:T(8,128)(2,1)S(1)}, bf16[128,1024]{1,0:T(8,128)(2,1)S(1)}, u32[]{:S(2)}, u32[]{:S(2)}) %collective-permute-start.15) | collective-permute-done | bytes 262176 | tf_op jit(solution)/shard_map/ppermute | solution.py:147
  62.8 3.8 %collective-permute-done.14 = bf16[128,1024]{1,0:T(8,128)(2,1)S(1)} collective-permute-done((bf16[128,1024]{1,0:T(8,128)(2,1)S(1)}, bf16[128,1024]{1,0:T(8,128)(2,1)S(1)}, u32[]{:S(2)}, u32[]{:S(2)}) %collective-permute-start.14) | collective-permute-done | bytes 262176 | tf_op jit(solution)/shard_map/ppermute | solution.py:147
  66.6 0.0 collective-permute-done.13
  66.6 0.8 %add_convert_fusion = bf16[128,1024]{1,0:T(8,128)(2,1)} fusion(bf16[128,1024]{1,0:T(8,128)(2,1)S(1)} %collective-permute-done.14, bf16[128,1024]{1,0:T(8,128)(2,1)S(1)} %collective-permute-done.15, f32[128,1024]{1,0:T(8,128)S(1)} %convert_add_fusion.refs_1_, bf16[128,1024]{1,0:T(8,128)(2,1)S(1)} %collective-permute-done.13), kind=kLoop, calls=%fused_computation | loop fusion | flops 917504 | bytes 1572864 | tf_op jit(solution)/shard_map/convert_element_type | solution.py:226
  (5 shorter events, 0.0 us)
Async XLA Ops:
  0.0 16.6 %collective-permute-start.2 = (bf16[1,1344,1024]{2,1,0:T(8,128)(2,1)}, bf16[1,1344,1024]{2,1,0:T(8,128)(2,1)S(1)}, u32[]{:S(2)}, u32[]{:S(2)}) collective-permute-start(bf16[1,1344,1024]{2,1,0:T(8,128)(2,1)} %bitcast.4), channel_id=1, source_target_pairs={{0,2},{2,0},{1,3},{3,1},{4,6},{6,4},{5,7},{7,5},{8,10},{10,8},{9,1... | collective-permute-start | bytes 8257544 | tf_op jit(solution)/shard_map/ppermute | solution.py:147
  0.5 16.2 %collective-permute-start.3 = (bf16[1,1344,1024]{2,1,0:T(8,128)(2,1)}, bf16[1,1344,1024]{2,1,0:T(8,128)(2,1)S(1)}, u32[]{:S(2)}, u32[]{:S(2)}) collective-permute-start(bf16[1,1344,1024]{2,1,0:T(8,128)(2,1)} %bitcast.6), channel_id=1, source_target_pairs={{0,2},{2,0},{1,3},{3,1},{4,6},{6,4},{5,7},{7,5},{8,10},{10,8},{9,1... | collective-permute-start | bytes 8257544 | tf_op jit(solution)/shard_map/ppermute | solution.py:147
  0.5 0.9 %copy-start.2 = (bf16[128,1024]{1,0:T(8,128)(2,1)S(1)}, bf16[128,1024]{1,0:T(8,128)(2,1)}, u32[]{:S(2)}) copy-start(bf16[128,1024]{1,0:T(8,128)(2,1)} %latent_ref.1) | copy-start | bytes 786436
  1.5 0.7 %copy-start.3 = (s32[128,4]{0,1:T(4,128)S(1)}, s32[128,4]{0,1:T(4,128)}, u32[]{:S(2)}) copy-start(s32[128,4]{0,1:T(4,128)} %param.6) | copy-start | bytes 6148
  2.1 0.7 %copy-start.4 = (f32[128,4]{0,1:T(4,128)S(1)}, f32[128,4]{0,1:T(4,128)}, u32[]{:S(2)}) copy-start(f32[128,4]{0,1:T(4,128)} %param.7) | copy-start | bytes 6148
  2.9 12.3 %collective-permute-start.1 = (bf16[144,1024]{1,0:T(8,128)(2,1)S(1)}, bf16[144,1024]{1,0:T(8,128)(2,1)S(1)}, u32[]{:S(2)}, u32[]{:S(2)}) collective-permute-start(bf16[144,1024]{1,0:T(8,128)(2,1)S(1)} %shard_map.55.after_ref.refs_1_), channel_id=1, source_target_pairs={{0,4},{4,8},{8,12},{12,0},{1,5},{5,9},{9,13},{13,1},{2,6},{6,10},{... | collective-permute-start | bytes 884744 | tf_op jit(solution)/shard_map/ppermute | solution.py:147
  5.9 10.7 %collective-permute-start = (bf16[144,1024]{1,0:T(8,128)(2,1)S(1)}, bf16[144,1024]{1,0:T(8,128)(2,1)S(1)}, u32[]{:S(2)}, u32[]{:S(2)}) collective-permute-start(bf16[144,1024]{1,0:T(8,128)(2,1)S(1)} %shard_map.55.after_ref.refs_1_), channel_id=1, source_target_pairs={{0,1},{1,0},{2,3},{3,2},{4,5},{5,4},{6,7},{7,6},{8,9},{9,8},{10,11... | collective-permute-start | bytes 884744 | tf_op jit(solution)/shard_map/ppermute | solution.py:147
  7.4 1.8 %copy-start = (bf16[1,1024,1344]{1,2,0:T(8,128)(2,1)S(1)}, bf16[1,1024,1344]{1,2,0:T(8,128)(2,1)}, u32[]{:S(2)}) copy-start(bf16[1,1024,1344]{1,2,0:T(8,128)(2,1)} %param.8) | copy-start | bytes 8257540
  9.2 1.8 %copy-start.1 = (bf16[1,1024,1344]{1,2,0:T(8,128)(2,1)S(1)}, bf16[1,1024,1344]{1,2,0:T(8,128)(2,1)}, u32[]{:S(2)}) copy-start(bf16[1,1024,1344]{1,2,0:T(8,128)(2,1)} %param.9) | copy-start | bytes 8257540
  15.1 10.2 %collective-permute-start.6 = (bf16[144,1024]{1,0:T(8,128)(2,1)S(1)}, bf16[144,1024]{1,0:T(8,128)(2,1)S(1)}, u32[]{:S(2)}, u32[]{:S(2)}) collective-permute-start(bf16[144,1024]{1,0:T(8,128)(2,1)S(1)} %collective-permute-done.1.refs_2_), channel_id=1, source_target_pairs={{0,4},{4,8},{8,12},{12,0},{1,5},{5,9},{9,13},{13,1},{2,6},{6,10},{... | collective-permute-start | bytes 884744 | tf_op jit(solution)/shard_map/ppermute | solution.py:147
  15.1 15.3 %collective-permute-start.5 = (bf16[144,1024]{1,0:T(8,128)(2,1)S(1)}, bf16[144,1024]{1,0:T(8,128)(2,1)S(1)}, u32[]{:S(2)}, u32[]{:S(2)}) collective-permute-start(bf16[144,1024]{1,0:T(8,128)(2,1)S(1)} %collective-permute-done.1.refs_2_), channel_id=1, source_target_pairs={{0,1},{1,0},{2,3},{3,2},{4,5},{5,4},{6,7},{7,6},{8,9},{9,8},{10,11... | collective-permute-start | bytes 884744 | tf_op jit(solution)/shard_map/ppermute | solution.py:147
  25.3 11.7 %collective-permute-start.8 = (bf16[144,1024]{1,0:T(8,128)(2,1)S(1)}, bf16[144,1024]{1,0:T(8,128)(2,1)S(1)}, u32[]{:S(2)}, u32[]{:S(2)}) collective-permute-start(bf16[144,1024]{1,0:T(8,128)(2,1)S(1)} %collective-permute-done.6.refs_2_), channel_id=1, source_target_pairs={{0,4},{4,8},{8,12},{12,0},{1,5},{5,9},{9,13},{13,1},{2,6},{6,10},{... | collective-permute-start | bytes 884744 | tf_op jit(solution)/shard_map/ppermute | solution.py:147
  25.3 13.0 %collective-permute-start.7 = (bf16[144,1024]{1,0:T(8,128)(2,1)S(1)}, bf16[144,1024]{1,0:T(8,128)(2,1)S(1)}, u32[]{:S(2)}, u32[]{:S(2)}) collective-permute-start(bf16[144,1024]{1,0:T(8,128)(2,1)S(1)} %collective-permute-done.6.refs_2_), channel_id=1, source_target_pairs={{0,1},{1,0},{2,3},{3,2},{4,5},{5,4},{6,7},{7,6},{8,9},{9,8},{10,11... | collective-permute-start | bytes 884744 | tf_op jit(solution)/shard_map/ppermute | solution.py:147
  26.6 16.4 %collective-permute-start.4 = (bf16[128,1024]{1,0:T(8,128)(2,1)S(1)}, bf16[128,1024]{1,0:T(8,128)(2,1)S(1)}, u32[]{:S(2)}, u32[]{:S(2)}) collective-permute-start(bf16[128,1024]{1,0:T(8,128)(2,1)S(1)} %get-tuple-element.30), channel_id=1, source_target_pairs={{0,12},{4,0},{8,4},{12,8},{1,13},{5,1},{9,5},{13,9},{2,14},{6,2},{... | collective-permute-start | bytes 786440 | tf_op jit(solution)/shard_map/ppermute | solution.py:147
  37.1 9.2 %collective-permute-start.10 = (bf16[144,1024]{1,0:T(8,128)(2,1)S(1)}, bf16[144,1024]{1,0:T(8,128)(2,1)S(1)}, u32[]{:S(2)}, u32[]{:S(2)}) collective-permute-start(bf16[144,1024]{1,0:T(8,128)(2,1)S(1)} %collective-permute-done.8.refs_2_), channel_id=1, source_target_pairs={{0,1},{1,0},{2,3},{3,2},{4,5},{5,4},{6,7},{7,6},{8,9},{9,8},{10,11... | collective-permute-start | bytes 884744 | tf_op jit(solution)/shard_map/ppermute | solution.py:147
  38.3 13.0 %collective-permute-start.9 = (bf16[128,1024]{1,0:T(8,128)(2,1)S(1)}, bf16[128,1024]{1,0:T(8,128)(2,1)S(1)}, u32[]{:S(2)}, u32[]{:S(2)}) collective-permute-start(bf16[128,1024]{1,0:T(8,128)(2,1)S(1)} %get-tuple-element.37.refs_0_), channel_id=1, source_target_pairs={{0,12},{4,0},{8,4},{12,8},{1,13},{5,1},{9,5},{13,9},{2,14},{6,2},{... | collective-permute-start | bytes 786440 | tf_op jit(solution)/shard_map/ppermute | solution.py:147
  42.1 9.2 %collective-permute-start.12 = (bf16[128,1024]{1,0:T(8,128)(2,1)S(1)}, bf16[128,1024]{1,0:T(8,128)(2,1)S(1)}, u32[]{:S(2)}, u32[]{:S(2)}) collective-permute-start(bf16[128,1024]{1,0:T(8,128)(2,1)S(1)} %get-tuple-element.35.refs_0_), channel_id=1, source_target_pairs={{0,1},{1,0},{2,3},{3,2},{4,5},{5,4},{6,7},{7,6},{8,9},{9,8},{10,11... | collective-permute-start | bytes 786440 | tf_op jit(solution)/shard_map/ppermute | solution.py:147
  49.6 8.7 %collective-permute-start.11 = (bf16[128,1024]{1,0:T(8,128)(2,1)S(1)}, bf16[128,1024]{1,0:T(8,128)(2,1)S(1)}, u32[]{:S(2)}, u32[]{:S(2)}) collective-permute-start(bf16[128,1024]{1,0:T(8,128)(2,1)S(1)} %shard_map.60), channel_id=1, source_target_pairs={{0,1},{1,0},{2,3},{3,2},{4,5},{5,4},{6,7},{7,6},{8,9},{9,8},{10,11... | collective-permute-start | bytes 786440 | tf_op jit(solution)/shard_map/ppermute | solution.py:147
  51.4 11.4 %collective-permute-start.15 = (bf16[128,1024]{1,0:T(8,128)(2,1)S(1)}, bf16[128,1024]{1,0:T(8,128)(2,1)S(1)}, u32[]{:S(2)}, u32[]{:S(2)}) collective-permute-start(bf16[128,1024]{1,0:T(8,128)(2,1)S(1)} %add_convert_fusion.2), channel_id=1, source_target_pairs={{0,8},{4,12},{8,0},{12,4},{1,9},{5,13},{9,1},{13,5},{2,10},{6,14},... | collective-permute-start | bytes 786440 | tf_op jit(solution)/shard_map/ppermute | solution.py:147
  58.3 8.2 %collective-permute-start.14 = (bf16[128,1024]{1,0:T(8,128)(2,1)S(1)}, bf16[128,1024]{1,0:T(8,128)(2,1)S(1)}, u32[]{:S(2)}, u32[]{:S(2)}) collective-permute-start(bf16[128,1024]{1,0:T(8,128)(2,1)S(1)} %add_convert_fusion.1), channel_id=1, source_target_pairs={{0,4},{4,8},{8,12},{12,0},{1,5},{5,9},{9,13},{13,1},{2,6},{6,10},{... | collective-permute-start | bytes 786440 | tf_op jit(solution)/shard_map/ppermute | solution.py:147
  58.4 8.2 %collective-permute-start.13 = (bf16[128,1024]{1,0:T(8,128)(2,1)S(1)}, bf16[128,1024]{1,0:T(8,128)(2,1)S(1)}, u32[]{:S(2)}, u32[]{:S(2)}) collective-permute-start(bf16[128,1024]{1,0:T(8,128)(2,1)S(1)} %add_convert_fusion.3), channel_id=1, source_target_pairs={{0,1},{1,0},{2,3},{3,2},{4,5},{5,4},{6,7},{7,6},{8,9},{9,8},{10,11... | collective-permute-start | bytes 786440 | tf_op jit(solution)/shard_map/ppermute | solution.py:147

commit v10 on v9

--- a/solution.py
+++ b/solution.py
@@ -118,8 +118,11 @@
                 sums[b] = sums[b] + lax.dot_general(
                     picks[g][j], gated, TN, preferred_element_type=jnp.float32
                 )
-    for b in range(blocks):
-        out_refs[b][...] = sums[b].astype(out_refs[b].dtype)
+    b = 0
+    for out_ref in out_refs:
+        for start in range(0, out_ref.shape[0], block):
+            out_ref[start : start + block, :] = sums[b].astype(out_ref.dtype)
+            b += 1
 
 
 def run_experts(after, arrived, tables, kinds, block, slots):
@@ -129,10 +132,10 @@
     whole = pl.BlockSpec(memory_space=pltpu.VMEM)
     return pl.pallas_call(
         functools.partial(expert_kernel, block, slots, unit, number, blocks, len(after)),
-        out_shape=[jax.ShapeDtypeStruct((block, width), kind) for kind in kinds],
+        out_shape=[jax.ShapeDtypeStruct((count * block, width), kind) for kind, count in kinds],
         in_specs=[pl.BlockSpec(memory_space=pl.ANY)] * len(after)
         + [whole] * (blocks + len(tables)),
-        out_specs=[whole] * blocks,
+        out_specs=[whole] * len(kinds),
         compiler_params=pltpu.CompilerParams(vmem_limit_bytes=30 * 1024 * 1024),
         cost_estimate=pl.CostEstimate(
             flops=4 * number * blocks * slots * width * (hidden + block),
@@ -164,7 +167,7 @@
     ring.append(follow(shift(ring[0], "z", 1), tables[0]))
     last = depth - 1
     kept, others = {}, {}
-    totals, home = {}, None
+    totals = {}
     firsts = []
 
     def total(r, *behind):
@@ -178,14 +181,11 @@
 
     for j in range(depth):
         handed = [shift(ring[j], "sub", s) for s in range(1, subs)]
-        fresh = ([0] if j == 0 else []) + [j + 1] * (j < last)
-        kinds = [jnp.bfloat16] * len(handed)
-        kinds += [jnp.bfloat16 if r == 1 else jnp.float32 for r in fresh]
+        fresh = [[0], [1, 2][:last]][j] if j < 2 else [j + 1][: last - j]
+        kinds = [(jnp.bfloat16, 1)] * len(handed) + [(jnp.float32, 1)] * len(fresh)
+        if j == 1:
+            kinds = [(jnp.bfloat16, subs)] + kinds[subs:]
         after = firsts[-1:]
-        if j == last and j > 1:
-            rows = follow(shift(kept[1], "z", -1), firsts[-1])
-            home = kept[0] + rows.astype(jnp.float32)
-            after = after + [home]
         if j > 3:
             totals[j - 2] = total(j - 2, firsts[-1]).astype(jnp.bfloat16)
             after = after + [totals[j - 2]]
@@ -193,23 +193,25 @@
         firsts.append(partial[0])
         if j + 2 < depth:
             ring.append(follow(shift(ring[-1], "z", 1), partial[0]))
-        for r, rows in zip(fresh, partial[subs - 1 :]):
+        if j == 1:
+            joint, *partial = partial
+            fresh = fresh[1:]
+        else:
+            others[j], partial = partial[: subs - 1], partial[subs - 1 :]
+        for r, rows in zip(fresh, partial):
             kept[r] = rows
-        others[j] = partial[: subs - 1]
-    if home is None:
-        home = kept[0] + sum(shift(kept[r], "z", -r).astype(jnp.float32) for r in range(1, depth))
-    joined = others[0]
+    home, joined = kept[0], others[0]
     if depth > 1:
+        sent = follow(shift(follow(joint, ring[last]), "z", -1), firsts[-1])
+        sent = [sent[s * block : (s + 1) * block].astype(jnp.float32) for s in range(subs)]
         joined = [
-            (
-                mine.astype(jnp.float32)
-                + shift(follow(rows, ring[last]), "z", -1).astype(jnp.float32)
-            ).astype(jnp.bfloat16)
-            for mine, rows in zip(others[0], others[1])
+            (mine.astype(jnp.float32) + rows).astype(jnp.bfloat16)
+            for mine, rows in zip(others[0], sent)
         ]
+        home = home + sent[-1]
     for r in range(2, depth):
         if r not in totals:
-            behind = [firsts[-1]] + (joined if r < last else [totals[r - 1]] * (r > 2))
+            behind = [firsts[-1]] + ([home, *joined] if r < last else [totals[r - 1]] * (r > 2))
             totals[r] = total(r, *behind).astype(jnp.bfloat16)
     came = []
     for r in range(2, depth):

time: 67.7 us -> 68.4 us (1.010)
  waiting for transfers between devices: 27.3 us -> 28.4 us
    ppermute x16 -> x15, waiting for transfers between devices: 27.3 us -> 28.4 us  [shift(): lax.ppermute(array, axis, [(i, (i + step) % size) for i in range(size)])]
    ppermute x16 -> x15, starting transfers between devices: 16.5 us -> 16.2 us  [shift(): lax.ppermute(array, axis, [(i, (i + step) % size) for i in range(size)])]
  transfers between devices with their start and end apart: 16 -> 15, of which waited for: 7 -> 7; matrix products, arithmetic and copies ran while one was open for 0% -> 0% of each run, Pallas kernels for 25% -> 24%
where the time goes in v10:
time: 68.4 us; the launch traced here: 68.1 us
  waiting for transfers between devices  28.4 us (42%)
  Pallas kernels  16.5 us (24%)
  starting transfers between devices  16.2 us (24%)
  local copies, waits for them, and re-layouts  5.87 us (9%)
  other arithmetic  1.1 us (2%)
    ppermute x15, waiting for transfers between devices, shift(): lax.ppermute(array, axis, [(i, (i + step) % size) for i in range(size)])  28.4 us
    ppermute x15, starting transfers between devices, shift(): lax.ppermute(array, axis, [(i, (i + step) % size) for i in range(size)])  16.2 us
    pallas_call x4, Pallas kernels, run_experts(): pl.pallas_call(functools.partial(expert_kernel, block, slots, unit, numbe...  15.8 us
    unnamed x10, local copies, waits for them, and re-layouts  5.87 us
  transfers between devices with their start and end apart: 15, of which 7 were waited for; matrix products, arithmetic and copies ran while one was open for 0% of the time, Pallas kernels for 24%

profile of v10, /device:TPU:0, one launch (start us, length us, event | category | flops | bytes accessed | tf_op | source)
XLA Modules:
  0.0 68.1 jit_solution(4946562001396257269)
XLA Ops:
  0.0 0.5 collective-permute-start.1
  0.5 0.1 collective-permute-start.2
  0.5 0.0 copy-start.2
  0.5 0.9 %copy-done.2 = bf16[128,1024]{1,0:T(8,128)(2,1)S(1)} copy-done((bf16[128,1024]{1,0:T(8,128)(2,1)S(1)}, bf16[128,1024]{1,0:T(8,128)(2,1)}, u32[]{:S(2)}) %copy-start.2) | copy-done | bytes 262168
  1.5 0.0 copy-start.3
  1.5 0.7 copy-done.3
  2.1 0.0 copy-start.4
  2.1 0.7 copy-done.4
  2.9 3.1 %collective-permute-start.3 = (bf16[144,1024]{1,0:T(8,128)(2,1)S(1)}, bf16[144,1024]{1,0:T(8,128)(2,1)S(1)}, u32[]{:S(2)}, u32[]{:S(2)}) collective-permute-start(bf16[144,1024]{1,0:T(8,128)(2,1)S(1)} %shard_map.55.after_ref.refs_1_), channel_id=1, source_target_pairs={{0,4},{4,8},{8,12},{12,0},{1,5},{5,9},{9,13},{13,1},{2,6},{6,10},{... | collective-permute-start | bytes 884744 | tf_op jit(solution)/shard_map/ppermute | solution.py:150
  5.9 1.5 %collective-permute-start = (bf16[144,1024]{1,0:T(8,128)(2,1)S(1)}, bf16[144,1024]{1,0:T(8,128)(2,1)S(1)}, u32[]{:S(2)}, u32[]{:S(2)}) collective-permute-start(bf16[144,1024]{1,0:T(8,128)(2,1)S(1)} %shard_map.55.after_ref.refs_1_), channel_id=1, source_target_pairs={{0,1},{1,0},{2,3},{3,2},{4,5},{5,4},{6,7},{7,6},{8,9},{9,8},{10,11... | collective-permute-start | bytes 884744 | tf_op jit(solution)/shard_map/ppermute | solution.py:150
  7.4 0.0 copy-start
  7.4 1.8 %copy-done = bf16[1,1024,1344]{1,2,0:T(8,128)(2,1)S(1)} copy-done((bf16[1,1024,1344]{1,2,0:T(8,128)(2,1)S(1)}, bf16[1,1024,1344]{1,2,0:T(8,128)(2,1)}, u32[]{:S(2)}) %copy-start) | copy-done | bytes 2752536
  9.2 1.8 %copy-done.1 = bf16[1,1024,1344]{1,2,0:T(8,128)(2,1)S(1)} copy-done((bf16[1,1024,1344]{1,2,0:T(8,128)(2,1)S(1)}, bf16[1,1024,1344]{1,2,0:T(8,128)(2,1)}, u32[]{:S(2)}) %copy-start.1) | copy-done | bytes 2752536
  11.0 0.7 %shard_map.56 = (bf16[1,1344,1024]{2,1,0:T(8,128)(2,1)S(1)}, bf16[1,1344,1024]{2,1,0:T(8,128)(2,1)S(1)}) custom-call(bf16[144,1024]{1,0:T(8,128)(2,1)S(1)} %shard_map.55.after_ref.refs_1_, bf16[1,1344,1024]{2,1,0:T(8,128)(2,1)S(1)} %bitcast.5, bf16[1,1344,1024]{2,1,0:T(8,128)(2,1)S(1)} %bitcast.7), custom_call_target="tpu_custom_call" | custom-call | tf_op jit(solution)/shard_map/pallas_call | solution.py:55
  11.7 3.4 %collective-permute-done.3.refs_2_ = bf16[144,1024]{1,0:T(8,128)(2,1)S(1)} collective-permute-done((bf16[144,1024]{1,0:T(8,128)(2,1)S(1)}, bf16[144,1024]{1,0:T(8,128)(2,1)S(1)}, u32[]{:S(2)}, u32[]{:S(2)}) %collective-permute-start.3) | collective-permute-done | bytes 294944 | tf_op jit(solution)/shard_map/ppermute | solution.py:150
  15.1 0.0 collective-permute-start.5
  15.1 1.5 %collective-permute-start.4 = (bf16[144,1024]{1,0:T(8,128)(2,1)S(1)}, bf16[144,1024]{1,0:T(8,128)(2,1)S(1)}, u32[]{:S(2)}, u32[]{:S(2)}) collective-permute-start(bf16[144,1024]{1,0:T(8,128)(2,1)S(1)} %collective-permute-done.3.refs_2_), channel_id=1, source_target_pairs={{0,1},{1,0},{2,3},{3,2},{4,5},{5,4},{6,7},{7,6},{8,9},{9,8},{10,11... | collective-permute-start | bytes 884744 | tf_op jit(solution)/shard_map/ppermute | solution.py:150
  16.6 0.0 collective-permute-done.refs_0_
  16.6 0.0 collective-permute-done.1.refs_4_.refs_6_.refs_5_
  16.6 0.0 collective-permute-done.2.refs_5_.refs_7_.refs_6_
  16.6 3.8 %shard_map.57 = (bf16[128,1024]{1,0:T(8,128)(2,1)S(1)}, f32[128,1024]{1,0:T(8,128)S(1)}) custom-call(bf16[144,1024]{1,0:T(8,128)(2,1)S(1)} %collective-permute-done.refs_0_, bf16[144,1024]{1,0:T(8,128)(2,1)S(1)} %shard_map.55.after_ref.refs_1_, bf16[1,1344,1024]{2,1,0:T(8,128)(2,1)S(1)} %get-tuple-element.26.refs_2_.refs_4_.refs_3_, ...), custom_call_target="tpu_custom_call" | custom-call | flops 2315255808 | bytes 12320768 | tf_op jit(solution)/shard_map/pallas_call | solution.py:133
  20.5 4.8 %collective-permute-done.5.refs_3_ = bf16[144,1024]{1,0:T(8,128)(2,1)S(1)} collective-permute-done((bf16[144,1024]{1,0:T(8,128)(2,1)S(1)}, bf16[144,1024]{1,0:T(8,128)(2,1)S(1)}, u32[]{:S(2)}, u32[]{:S(2)}) %collective-permute-start.5) | collective-permute-done | bytes 294944 | tf_op jit(solution)/shard_map/ppermute | solution.py:150
  25.3 1.2 %collective-permute-start.8 = (bf16[144,1024]{1,0:T(8,128)(2,1)S(1)}, bf16[144,1024]{1,0:T(8,128)(2,1)S(1)}, u32[]{:S(2)}, u32[]{:S(2)}) collective-permute-start(bf16[144,1024]{1,0:T(8,128)(2,1)S(1)} %collective-permute-done.5.refs_3_), channel_id=1, source_target_pairs={{0,1},{1,0},{2,3},{3,2},{4,5},{5,4},{6,7},{7,6},{8,9},{9,8},{10,11... | collective-permute-start | bytes 884744 | tf_op jit(solution)/shard_map/ppermute | solution.py:150
  26.6 0.0 collective-permute-start.6
  26.6 0.0 collective-permute-done.4.refs_1_
  26.6 4.9 %shard_map.58 = (bf16[256,1024]{1,0:T(8,128)(2,1)S(1)}, f32[128,1024]{1,0:T(8,128)S(1)}) custom-call(bf16[128,1024]{1,0:T(8,128)(2,1)S(1)} %get-tuple-element.29.refs_0_, bf16[144,1024]{1,0:T(8,128)(2,1)S(1)} %collective-permute-done.4.refs_1_, bf16[144,1024]{1,0:T(8,128)(2,1)S(1)} %collective-permute-done.3.refs_2_, ...), custom_call_target="tpu_custom_call" | custom-call | flops 3472883712 | bytes 12976128 | tf_op jit(solution)/shard_map/pallas_call | solution.py:133
  31.5 5.0 %collective-permute-done.6.refs_2_ = bf16[144,1024]{1,0:T(8,128)(2,1)S(1)} collective-permute-done((bf16[144,1024]{1,0:T(8,128)(2,1)S(1)}, bf16[144,1024]{1,0:T(8,128)(2,1)S(1)}, u32[]{:S(2)}, u32[]{:S(2)}) %collective-permute-start.6) | collective-permute-done | bytes 294944 | tf_op jit(solution)/shard_map/ppermute | solution.py:150
  36.4 0.0 collective-permute-start.7
  36.4 1.0 %collective-permute-start.9 = (bf16[144,1024]{1,0:T(8,128)(2,1)S(1)}, bf16[144,1024]{1,0:T(8,128)(2,1)S(1)}, u32[]{:S(2)}, u32[]{:S(2)}) collective-permute-start(bf16[144,1024]{1,0:T(8,128)(2,1)S(1)} %collective-permute-done.6.refs_2_), channel_id=1, source_target_pairs={{0,1},{1,0},{2,3},{3,2},{4,5},{5,4},{6,7},{7,6},{8,9},{9,8},{10,11... | collective-permute-start | bytes 884744 | tf_op jit(solution)/shard_map/ppermute | solution.py:150
  37.4 0.0 collective-permute-done.8.refs_1_
  37.5 3.8 %shard_map.59 = (bf16[128,1024]{1,0:T(8,128)(2,1)S(1)}, f32[128,1024]{1,0:T(8,128)S(1)}) custom-call(bf16[256,1024]{1,0:T(8,128)(2,1)S(1)} %get-tuple-element.34.refs_0_, bf16[144,1024]{1,0:T(8,128)(2,1)S(1)} %collective-permute-done.8.refs_1_, bf16[144,1024]{1,0:T(8,128)(2,1)S(1)} %collective-permute-done.6.refs_2_, ...), custom_call_target="tpu_custom_call" | custom-call | flops 2315255808 | bytes 12320768 | tf_op jit(solution)/shard_map/pallas_call | solution.py:133
  41.3 1.1 %collective-permute-start.11 = (bf16[128,1024]{1,0:T(8,128)(2,1)S(1)}, bf16[128,1024]{1,0:T(8,128)(2,1)S(1)}, u32[]{:S(2)}, u32[]{:S(2)}) collective-permute-start(bf16[128,1024]{1,0:T(8,128)(2,1)S(1)} %get-tuple-element.35.refs_0_), channel_id=1, source_target_pairs={{0,1},{1,0},{2,3},{3,2},{4,5},{5,4},{6,7},{7,6},{8,9},{9,8},{10,11... | collective-permute-start | bytes 786440 | tf_op jit(solution)/shard_map/ppermute | solution.py:150
  42.3 3.8 %collective-permute-done.9.refs_1_ = bf16[144,1024]{1,0:T(8,128)(2,1)S(1)} collective-permute-done((bf16[144,1024]{1,0:T(8,128)(2,1)S(1)}, bf16[144,1024]{1,0:T(8,128)(2,1)S(1)}, u32[]{:S(2)}, u32[]{:S(2)}) %collective-permute-start.9) | collective-permute-done | bytes 294944 | tf_op jit(solution)/shard_map/ppermute | solution.py:150
  46.1 3.3 %shard_map.60 = bf16[128,1024]{1,0:T(8,128)(2,1)S(1)} custom-call(bf16[128,1024]{1,0:T(8,128)(2,1)S(1)} %get-tuple-element.35.refs_0_, bf16[144,1024]{1,0:T(8,128)(2,1)S(1)} %collective-permute-done.9.refs_1_, bf16[1,1344,1024]{2,1,0:T(8,128)(2,1)S(1)} %get-tuple-element.26.refs_2_.refs_4_.refs_3_, ...), custom_call_target="tpu_custom_call" | custom-call | flops 1157627904 | bytes 11665408 | tf_op jit(solution)/shard_map/pallas_call | solution.py:133
  49.4 1.1 %collective-permute-start.10 = (bf16[128,1024]{1,0:T(8,128)(2,1)S(1)}, bf16[128,1024]{1,0:T(8,128)(2,1)S(1)}, u32[]{:S(2)}, u32[]{:S(2)}) collective-permute-start(bf16[128,1024]{1,0:T(8,128)(2,1)S(1)} %shard_map.60), channel_id=1, source_target_pairs={{0,1},{1,0},{2,3},{3,2},{4,5},{5,4},{6,7},{7,6},{8,9},{9,8},{10,11... | collective-permute-start | bytes 786440 | tf_op jit(solution)/shard_map/ppermute | solution.py:150
  50.5 1.1 %collective-permute-done.11 = bf16[128,1024]{1,0:T(8,128)(2,1)S(1)} collective-permute-done((bf16[128,1024]{1,0:T(8,128)(2,1)S(1)}, bf16[128,1024]{1,0:T(8,128)(2,1)S(1)}, u32[]{:S(2)}, u32[]{:S(2)}) %collective-permute-start.11) | collective-permute-done | bytes 262176 | tf_op jit(solution)/shard_map/ppermute | solution.py:150
  51.6 0.0 collective-permute-done.7
  51.6 0.1 add_convert_fusion.3
  51.7 0.1 add_convert_fusion.2
  51.8 0.1 collective-permute-start.14
  51.9 4.6 %collective-permute-done.10 = bf16[128,1024]{1,0:T(8,128)(2,1)S(1)} collective-permute-done((bf16[128,1024]{1,0:T(8,128)(2,1)S(1)}, bf16[128,1024]{1,0:T(8,128)(2,1)S(1)}, u32[]{:S(2)}, u32[]{:S(2)}) %collective-permute-start.10) | collective-permute-done | bytes 262176 | tf_op jit(solution)/shard_map/ppermute | solution.py:150
  56.5 0.1 add_convert_fusion.1
  56.5 4.0 %collective-permute-start.13 = (bf16[128,1024]{1,0:T(8,128)(2,1)S(1)}, bf16[128,1024]{1,0:T(8,128)(2,1)S(1)}, u32[]{:S(2)}, u32[]{:S(2)}) collective-permute-start(bf16[128,1024]{1,0:T(8,128)(2,1)S(1)} %add_convert_fusion.1), channel_id=1, source_target_pairs={{0,4},{4,8},{8,12},{12,0},{1,5},{5,9},{9,13},{13,1},{2,6},{6,10},{... | collective-permute-start | bytes 786440 | tf_op jit(solution)/shard_map/ppermute | solution.py:150
  60.5 1.1 %collective-permute-start.12 = (bf16[128,1024]{1,0:T(8,128)(2,1)S(1)}, bf16[128,1024]{1,0:T(8,128)(2,1)S(1)}, u32[]{:S(2)}, u32[]{:S(2)}) collective-permute-start(bf16[128,1024]{1,0:T(8,128)(2,1)S(1)} %get-tuple-element.44), channel_id=1, source_target_pairs={{0,1},{1,0},{2,3},{3,2},{4,5},{5,4},{6,7},{7,6},{8,9},{9,8},{10,11... | collective-permute-start | bytes 786440 | tf_op jit(solution)/shard_map/ppermute | solution.py:150
  61.7 5.6 %collective-permute-done.14 = bf16[128,1024]{1,0:T(8,128)(2,1)S(1)} collective-permute-done((bf16[128,1024]{1,0:T(8,128)(2,1)S(1)}, bf16[128,1024]{1,0:T(8,128)(2,1)S(1)}, u32[]{:S(2)}, u32[]{:S(2)}) %collective-permute-start.14) | collective-permute-done | bytes 262176 | tf_op jit(solution)/shard_map/ppermute | solution.py:150
  67.3 0.0 collective-permute-done.13
  67.3 0.0 collective-permute-done.12
  67.3 0.8 %add_convert_fusion = bf16[128,1024]{1,0:T(8,128)(2,1)} fusion(bf16[128,1024]{1,0:T(8,128)(2,1)S(1)} %collective-permute-done.13, bf16[128,1024]{1,0:T(8,128)(2,1)S(1)} %collective-permute-done.14, f32[128,1024]{1,0:T(8,128)S(1)} %get-tuple-element.48, bf16[128,1024]{1,0:T(8,128)(2,1)S(1)} %collective-permute-done.12), kind=kLoop, calls=%fused_computation | loop fusion | flops 917504 | bytes 1572864 | tf_op jit(solution)/shard_map/convert_element_type | solution.py:228
  (2 shorter events, 0.0 us)
Async XLA Ops:
  0.0 16.6 %collective-permute-start.1 = (bf16[1,1344,1024]{2,1,0:T(8,128)(2,1)}, bf16[1,1344,1024]{2,1,0:T(8,128)(2,1)S(1)}, u32[]{:S(2)}, u32[]{:S(2)}) collective-permute-start(bf16[1,1344,1024]{2,1,0:T(8,128)(2,1)} %bitcast.4), channel_id=1, source_target_pairs={{0,2},{2,0},{1,3},{3,1},{4,6},{6,4},{5,7},{7,5},{8,10},{10,8},{9,1... | collective-permute-start | bytes 8257544 | tf_op jit(solution)/shard_map/ppermute | solution.py:150
  0.5 16.2 %collective-permute-start.2 = (bf16[1,1344,1024]{2,1,0:T(8,128)(2,1)}, bf16[1,1344,1024]{2,1,0:T(8,128)(2,1)S(1)}, u32[]{:S(2)}, u32[]{:S(2)}) collective-permute-start(bf16[1,1344,1024]{2,1,0:T(8,128)(2,1)} %bitcast.6), channel_id=1, source_target_pairs={{0,2},{2,0},{1,3},{3,1},{4,6},{6,4},{5,7},{7,5},{8,10},{10,8},{9,1... | collective-permute-start | bytes 8257544 | tf_op jit(solution)/shard_map/ppermute | solution.py:150
  0.5 0.9 %copy-start.2 = (bf16[128,1024]{1,0:T(8,128)(2,1)S(1)}, bf16[128,1024]{1,0:T(8,128)(2,1)}, u32[]{:S(2)}) copy-start(bf16[128,1024]{1,0:T(8,128)(2,1)} %latent_ref.1) | copy-start | bytes 786436
  1.5 0.7 %copy-start.3 = (s32[128,4]{0,1:T(4,128)S(1)}, s32[128,4]{0,1:T(4,128)}, u32[]{:S(2)}) copy-start(s32[128,4]{0,1:T(4,128)} %param.6) | copy-start | bytes 6148
  2.1 0.7 %copy-start.4 = (f32[128,4]{0,1:T(4,128)S(1)}, f32[128,4]{0,1:T(4,128)}, u32[]{:S(2)}) copy-start(f32[128,4]{0,1:T(4,128)} %param.7) | copy-start | bytes 6148
  2.9 12.3 %collective-permute-start.3 = (bf16[144,1024]{1,0:T(8,128)(2,1)S(1)}, bf16[144,1024]{1,0:T(8,128)(2,1)S(1)}, u32[]{:S(2)}, u32[]{:S(2)}) collective-permute-start(bf16[144,1024]{1,0:T(8,128)(2,1)S(1)} %shard_map.55.after_ref.refs_1_), channel_id=1, source_target_pairs={{0,4},{4,8},{8,12},{12,0},{1,5},{5,9},{9,13},{13,1},{2,6},{6,10},{... | collective-permute-start | bytes 884744 | tf_op jit(solution)/shard_map/ppermute | solution.py:150
  5.9 10.7 %collective-permute-start = (bf16[144,1024]{1,0:T(8,128)(2,1)S(1)}, bf16[144,1024]{1,0:T(8,128)(2,1)S(1)}, u32[]{:S(2)}, u32[]{:S(2)}) collective-permute-start(bf16[144,1024]{1,0:T(8,128)(2,1)S(1)} %shard_map.55.after_ref.refs_1_), channel_id=1, source_target_pairs={{0,1},{1,0},{2,3},{3,2},{4,5},{5,4},{6,7},{7,6},{8,9},{9,8},{10,11... | collective-permute-start | bytes 884744 | tf_op jit(solution)/shard_map/ppermute | solution.py:150
  7.4 1.8 %copy-start = (bf16[1,1024,1344]{1,2,0:T(8,128)(2,1)S(1)}, bf16[1,1024,1344]{1,2,0:T(8,128)(2,1)}, u32[]{:S(2)}) copy-start(bf16[1,1024,1344]{1,2,0:T(8,128)(2,1)} %param.8) | copy-start | bytes 8257540
  9.2 1.8 %copy-start.1 = (bf16[1,1024,1344]{1,2,0:T(8,128)(2,1)S(1)}, bf16[1,1024,1344]{1,2,0:T(8,128)(2,1)}, u32[]{:S(2)}) copy-start(bf16[1,1024,1344]{1,2,0:T(8,128)(2,1)} %param.9) | copy-start | bytes 8257540
  15.1 10.2 %collective-permute-start.5 = (bf16[144,1024]{1,0:T(8,128)(2,1)S(1)}, bf16[144,1024]{1,0:T(8,128)(2,1)S(1)}, u32[]{:S(2)}, u32[]{:S(2)}) collective-permute-start(bf16[144,1024]{1,0:T(8,128)(2,1)S(1)} %collective-permute-done.3.refs_2_), channel_id=1, source_target_pairs={{0,4},{4,8},{8,12},{12,0},{1,5},{5,9},{9,13},{13,1},{2,6},{6,10},{... | collective-permute-start | bytes 884744 | tf_op jit(solution)/shard_map/ppermute | solution.py:150
  15.1 11.4 %collective-permute-start.4 = (bf16[144,1024]{1,0:T(8,128)(2,1)S(1)}, bf16[144,1024]{1,0:T(8,128)(2,1)S(1)}, u32[]{:S(2)}, u32[]{:S(2)}) collective-permute-start(bf16[144,1024]{1,0:T(8,128)(2,1)S(1)} %collective-permute-done.3.refs_2_), channel_id=1, source_target_pairs={{0,1},{1,0},{2,3},{3,2},{4,5},{5,4},{6,7},{7,6},{8,9},{9,8},{10,11... | collective-permute-start | bytes 884744 | tf_op jit(solution)/shard_map/ppermute | solution.py:150
  25.3 12.1 %collective-permute-start.8 = (bf16[144,1024]{1,0:T(8,128)(2,1)S(1)}, bf16[144,1024]{1,0:T(8,128)(2,1)S(1)}, u32[]{:S(2)}, u32[]{:S(2)}) collective-permute-start(bf16[144,1024]{1,0:T(8,128)(2,1)S(1)} %collective-permute-done.5.refs_3_), channel_id=1, source_target_pairs={{0,1},{1,0},{2,3},{3,2},{4,5},{5,4},{6,7},{7,6},{8,9},{9,8},{10,11... | collective-permute-start | bytes 884744 | tf_op jit(solution)/shard_map/ppermute | solution.py:150
  26.6 9.9 %collective-permute-start.6 = (bf16[144,1024]{1,0:T(8,128)(2,1)S(1)}, bf16[144,1024]{1,0:T(8,128)(2,1)S(1)}, u32[]{:S(2)}, u32[]{:S(2)}) collective-permute-start(bf16[144,1024]{1,0:T(8,128)(2,1)S(1)} %collective-permute-done.5.refs_3_), channel_id=1, source_target_pairs={{0,4},{4,8},{8,12},{12,0},{1,5},{5,9},{9,13},{13,1},{2,6},{6,10},{... | collective-permute-start | bytes 884744 | tf_op jit(solution)/shard_map/ppermute | solution.py:150
  36.4 15.2 %collective-permute-start.7 = (bf16[256,1024]{1,0:T(8,128)(2,1)S(1)}, bf16[256,1024]{1,0:T(8,128)(2,1)S(1)}, u32[]{:S(2)}, u32[]{:S(2)}) collective-permute-start(bf16[256,1024]{1,0:T(8,128)(2,1)S(1)} %get-tuple-element.34.refs_0_), channel_id=1, source_target_pairs={{0,12},{4,0},{8,4},{12,8},{1,13},{5,1},{9,5},{13,9},{2,14},{6,2},{... | collective-permute-start | bytes 1572872 | tf_op jit(solution)/shard_map/ppermute | solution.py:150
  36.4 9.7 %collective-permute-start.9 = (bf16[144,1024]{1,0:T(8,128)(2,1)S(1)}, bf16[144,1024]{1,0:T(8,128)(2,1)S(1)}, u32[]{:S(2)}, u32[]{:S(2)}) collective-permute-start(bf16[144,1024]{1,0:T(8,128)(2,1)S(1)} %collective-permute-done.6.refs_2_), channel_id=1, source_target_pairs={{0,1},{1,0},{2,3},{3,2},{4,5},{5,4},{6,7},{7,6},{8,9},{9,8},{10,11... | collective-permute-start | bytes 884744 | tf_op jit(solution)/shard_map/ppermute | solution.py:150
  41.3 10.3 %collective-permute-start.11 = (bf16[128,1024]{1,0:T(8,128)(2,1)S(1)}, bf16[128,1024]{1,0:T(8,128)(2,1)S(1)}, u32[]{:S(2)}, u32[]{:S(2)}) collective-permute-start(bf16[128,1024]{1,0:T(8,128)(2,1)S(1)} %get-tuple-element.35.refs_0_), channel_id=1, source_target_pairs={{0,1},{1,0},{2,3},{3,2},{4,5},{5,4},{6,7},{7,6},{8,9},{9,8},{10,11... | collective-permute-start | bytes 786440 | tf_op jit(solution)/shard_map/ppermute | solution.py:150
  49.4 7.1 %collective-permute-start.10 = (bf16[128,1024]{1,0:T(8,128)(2,1)S(1)}, bf16[128,1024]{1,0:T(8,128)(2,1)S(1)}, u32[]{:S(2)}, u32[]{:S(2)}) collective-permute-start(bf16[128,1024]{1,0:T(8,128)(2,1)S(1)} %shard_map.60), channel_id=1, source_target_pairs={{0,1},{1,0},{2,3},{3,2},{4,5},{5,4},{6,7},{7,6},{8,9},{9,8},{10,11... | collective-permute-start | bytes 786440 | tf_op jit(solution)/shard_map/ppermute | solution.py:150
  51.8 15.5 %collective-permute-start.14 = (bf16[128,1024]{1,0:T(8,128)(2,1)S(1)}, bf16[128,1024]{1,0:T(8,128)(2,1)S(1)}, u32[]{:S(2)}, u32[]{:S(2)}) collective-permute-start(bf16[128,1024]{1,0:T(8,128)(2,1)S(1)} %add_convert_fusion.2), channel_id=1, source_target_pairs={{0,8},{4,12},{8,0},{12,4},{1,9},{5,13},{9,1},{13,5},{2,10},{6,14},... | collective-permute-start | bytes 786440 | tf_op jit(solution)/shard_map/ppermute | solution.py:150
  56.5 10.8 %collective-permute-start.13 = (bf16[128,1024]{1,0:T(8,128)(2,1)S(1)}, bf16[128,1024]{1,0:T(8,128)(2,1)S(1)}, u32[]{:S(2)}, u32[]{:S(2)}) collective-permute-start(bf16[128,1024]{1,0:T(8,128)(2,1)S(1)} %add_convert_fusion.1), channel_id=1, source_target_pairs={{0,4},{4,8},{8,12},{12,0},{1,5},{5,9},{9,13},{13,1},{2,6},{6,10},{... | collective-permute-start | bytes 786440 | tf_op jit(solution)/shard_map/ppermute | solution.py:150
  60.5 6.8 %collective-permute-start.12 = (bf16[128,1024]{1,0:T(8,128)(2,1)S(1)}, bf16[128,1024]{1,0:T(8,128)(2,1)S(1)}, u32[]{:S(2)}, u32[]{:S(2)}) collective-permute-start(bf16[128,1024]{1,0:T(8,128)(2,1)S(1)} %get-tuple-element.44), channel_id=1, source_target_pairs={{0,1},{1,0},{2,3},{3,2},{4,5},{5,4},{6,7},{7,6},{8,9},{9,8},{10,11... | collective-permute-start | bytes 786440 | tf_op jit(solution)/shard_map/ppermute | solution.py:150

commit v11 on v9

--- a/solution.py
+++ b/solution.py
@@ -9,38 +9,11 @@
 from jax.sharding import Mesh, PartitionSpec as P
 
 CORES = 2
-TERMS = 3
 NT = (((1,), (1,)), ((), ()))
 TN = (((0,), (0,)), ((), ()))
 
 
-def pack_kernel(experts, extra, latent_ref, routes_ref, gates_ref, out_ref):
-    block, width = latent_ref.shape
-    out_ref[:block, :] = latent_ref[...]
-    ids = lax.broadcasted_iota(jnp.int32, (extra, block), 0)
-    weight = jnp.zeros((extra, block), jnp.float32)
-    for k in range(routes_ref.shape[0]):
-        weight = weight + jnp.where(routes_ref[k : k + 1, :] == ids, gates_ref[k : k + 1, :], 0.0)
-    out_ref[block:, :] = jnp.zeros((extra, width), jnp.bfloat16)
-    for t in range(TERMS):
-        term = weight.astype(jnp.bfloat16)
-        out_ref[block:, t * block : (t + 1) * block] = term
-        weight = weight - term.astype(jnp.float32)
-
-
-def pack(latent, routes, gates, experts):
-    block, width = latent.shape
-    extra = -(-experts // 16) * 16
-    return pl.pallas_call(
-        functools.partial(pack_kernel, experts, extra),
-        out_shape=jax.ShapeDtypeStruct((block + extra, width), jnp.bfloat16),
-        in_specs=[pl.BlockSpec(memory_space=pltpu.VMEM)] * 3,
-        out_specs=pl.BlockSpec(memory_space=pltpu.VMEM),
-        compiler_params=pltpu.CompilerParams(vmem_limit_bytes=4 * 1024 * 1024),
-    )(latent, routes.T, gates.T)
-
-
-def stage_kernel(after_ref, *refs):
+def stage_kernel(*refs):
     number = (len(refs) - 1) // 2
     copies = [
         pltpu.make_async_copy(refs[n], refs[number + n], refs[-1].at[n]) for n in range(number)
@@ -51,34 +24,33 @@
         copy.wait()
 
 
-def stage(after, arrays):
+def stage(arrays):
     return pl.pallas_call(
         stage_kernel,
         out_shape=[jax.ShapeDtypeStruct(a.shape, a.dtype) for a in arrays],
-        in_specs=[pl.BlockSpec(memory_space=pl.ANY)]
-        + [pl.BlockSpec(memory_space=pltpu.HBM)] * len(arrays),
+        in_specs=[pl.BlockSpec(memory_space=pltpu.HBM)] * len(arrays),
         out_specs=[pl.BlockSpec(memory_space=pltpu.VMEM)] * len(arrays),
         scratch_shapes=[pltpu.SemaphoreType.DMA((len(arrays),))],
         compiler_params=pltpu.CompilerParams(vmem_limit_bytes=16 * 1024 * 1024),
-    )(after, *arrays)
-
-
-def expert_kernel(block, slots, unit, number, blocks, waits, *refs):
-    first, core = lax.axis_index("z") * number, lax.axis_index("core")
+    )(*arrays)
+
+
+def expert_kernel(block, slots, unit, number, sources, waits, gates_ref, *refs):
+    core, z, sub = (lax.axis_index(a) for a in ("core", "z", "sub"))
+    depth, subs = lax.axis_size("z"), lax.axis_size("sub")
+    blocks = len(sources)
     refs = refs[waits:]
     x_refs, tables, out_refs = refs[:blocks], refs[blocks : blocks + 2 * number], refs[blocks + 2 * number :]
-    extra = x_refs[0].shape[0] - block
     earlier = lax.broadcasted_iota(jnp.int32, (block, block), 0)
     later = lax.broadcasted_iota(jnp.int32, (block, block), 1)
     before = (earlier < later).astype(jnp.bfloat16)
     groups = [range(g, min(g + unit, blocks)) for g in range(0, blocks, unit)]
     sizes = [-(-len(g) * slots // 16) * 16 for g in groups]
-    row = lax.broadcasted_iota(jnp.int32, (extra, block), 0)
+    row = lax.broadcasted_iota(jnp.int32, (number, block), 0)
     gates, ranks = [], []
-    for x_ref in x_refs:
-        gate = 0.0
-        for t in range(TERMS):
-            gate = gate + x_ref[block:, t * block : (t + 1) * block].astype(jnp.float32)
+    for r, turn in sources:
+        source = lax.rem(z + depth - r, depth) * subs + lax.rem(sub + subs - turn, subs)
+        gate = gates_ref[source]
         gates.append(gate)
         ranks.append(
             jnp.dot((gate > 0).astype(jnp.bfloat16), before, preferred_element_type=jnp.float32)
@@ -86,7 +58,7 @@
     sums = [0.0] * blocks
     for n in range(number):
         up_ref, down_ref = tables[2 * n], tables[2 * n + 1]
-        mine = row == first + lax.rem(core + number - n, number)
+        mine = row == lax.rem(core + number - n, number)
         picks, scales, rows = [], [], []
         for group, size in zip(groups, sizes):
             slot = lax.broadcasted_iota(jnp.int32, (size, block), 0)
@@ -98,7 +70,7 @@
                 here = (slot == rank.astype(jnp.int32) + j * slots) & (weight > 0)
                 scale = scale + jnp.sum(jnp.where(here, weight, 0.0), axis=1, keepdims=True)
                 parts.append(here.astype(jnp.bfloat16))
-            tokens = [x_refs[b][:block, :] for b in group]
+            tokens = [x_refs[b][...] for b in group]
             pick = jnp.concatenate(parts, axis=1) if len(group) > 1 else parts[0]
             token = jnp.concatenate(tokens, axis=0) if len(group) > 1 else tokens[0]
             rows.append(
@@ -122,15 +94,16 @@
         out_refs[b][...] = sums[b].astype(out_refs[b].dtype)
 
 
-def run_experts(after, arrived, tables, kinds, block, slots):
-    blocks, number = len(arrived), len(tables) // 2
+def run_experts(after, gates, sources, arrived, tables, kinds, slots):
+    blocks, number, block = len(arrived), gates.shape[1], gates.shape[2]
     hidden, width = tables[0].shape[1:]
     unit = 16 // math.gcd(16, slots)
     whole = pl.BlockSpec(memory_space=pltpu.VMEM)
     return pl.pallas_call(
-        functools.partial(expert_kernel, block, slots, unit, number, blocks, len(after)),
+        functools.partial(expert_kernel, block, slots, unit, number, sources, len(after)),
         out_shape=[jax.ShapeDtypeStruct((block, width), kind) for kind in kinds],
-        in_specs=[pl.BlockSpec(memory_space=pl.ANY)] * len(after)
+        in_specs=[whole]
+        + [pl.BlockSpec(memory_space=pl.ANY)] * len(after)
         + [whole] * (blocks + len(tables)),
         out_specs=[whole] * blocks,
         compiler_params=pltpu.CompilerParams(vmem_limit_bytes=30 * 1024 * 1024),
@@ -139,7 +112,7 @@
             bytes_accessed=5 * blocks * block * width + 2 * len(tables) * width * hidden,
             transcendentals=0,
         ),
-    )(*after, *arrived, *tables)
+    )(gates, *after, *arrived, *tables)
 
 
 def shift(array, axis, step):
@@ -159,9 +132,15 @@
     slots = min(block, 3 * block * top // (2 * experts))
     own = [jnp.swapaxes(up_weight, 1, 2), jnp.swapaxes(down_weight, 1, 2)]
     moved = [shift(table, "core", step) for step in range(1, cores) for table in own]
-    ring = [pack(latent, routes, gates, experts)]
-    tables = [*stage(ring[0], own), *moved]
+    ring = [latent]
+    tables = [*stage(own), *moved]
     ring.append(follow(shift(ring[0], "z", 1), tables[0]))
+    ids = jnp.arange(experts, dtype=jnp.int32)
+    weight = jnp.sum(
+        jnp.where(routes.T[None] == ids[:, None, None], gates.T[None], 0.0), axis=1
+    ).reshape(depth, 1, cores, block)
+    weight = jnp.broadcast_to(weight, (depth, subs, cores, block)).reshape(-1, cores, block)
+    weight = lax.all_to_all(weight, ("z", "sub"), split_axis=0, concat_axis=0, tiled=True)
     last = depth - 1
     kept, others = {}, {}
     totals, home = {}, None
@@ -189,7 +168,9 @@
         if j > 3:
             totals[j - 2] = total(j - 2, firsts[-1]).astype(jnp.bfloat16)
             after = after + [totals[j - 2]]
-        partial = run_experts(after, handed + [ring[r] for r in fresh], tables, kinds, block, slots)
+        sources = [(j, s) for s in range(1, subs)] + [(r, 0) for r in fresh]
+        arrived = handed + [ring[r] for r in fresh]
+        partial = run_experts(after, weight, sources, arrived, tables, kinds, slots)
         firsts.append(partial[0])
         if j + 2 < depth:
             ring.append(follow(shift(ring[-1], "z", 1), partial[0]))

time: 67.7 us -> 74.8 us (1.10)
  waiting for transfers between devices: 27.3 us -> 14 us
  Pallas kernels: 16.5 us -> 23.8 us
  starting transfers between devices: 16.5 us -> 23.8 us
  local copies, waits for them, and re-layouts: 5.87 us -> 10.8 us
    ppermute x16, waiting for transfers between devices: 27.3 us -> 14 us  [shift(): lax.ppermute(array, axis, [(i, (i + step) % size) for i in range(size)])]
    pallas_call x4, Pallas kernels: 15.8 us -> 23.1 us  [run_experts(): pl.pallas_call(functools.partial(expert_kernel, block, slots, unit, numbe...]
    unnamed x10 -> x14, local copies, waits for them, and re-layouts: 5.87 us -> 10.2 us
    all_to_all x0 -> x1, starting transfers between devices: none -> 3.87 us  [local(): lax.all_to_all(weight, ('z', 'sub'), split_axis=0, concat_axis=0, tiled=T...]
    ppermute x16, starting transfers between devices: 16.5 us -> 20 us  [shift(): lax.ppermute(array, axis, [(i, (i + step) % size) for i in range(size)])]
  transfers between devices with their start and end apart: 16 -> 17, of which waited for: 7 -> 4; matrix products, arithmetic and copies ran while one was open for 0% -> 2% of each run, Pallas kernels for 25% -> 32%
where the time goes in v11:
time: 74.8 us; the launch traced here: 74.4 us
  starting transfers between devices  23.8 us (32%)
  Pallas kernels  23.8 us (32%)
  waiting for transfers between devices  14 us (19%)
  local copies, waits for them, and re-layouts  10.8 us (14%)
  other arithmetic  1.81 us (2%)
    pallas_call x4, Pallas kernels, run_experts(): pl.pallas_call(functools.partial(expert_kernel, block, slots, unit, numbe...  23.1 us
    ppermute x16, starting transfers between devices, shift(): lax.ppermute(array, axis, [(i, (i + step) % size) for i in range(size)])  20 us
    ppermute x16, waiting for transfers between devices, shift(): lax.ppermute(array, axis, [(i, (i + step) % size) for i in range(size)])  14 us
    unnamed x14, local copies, waits for them, and re-layouts  10.2 us
    all_to_all x1, starting transfers between devices, local(): lax.all_to_all(weight, ('z', 'sub'), split_axis=0, concat_axis=0, tiled=T...  3.87 us
  transfers between devices with their start and end apart: 17, of which 4 were waited for; matrix products, arithmetic and copies ran while one was open for 2% of the time, Pallas kernels for 32%

profile of v11, /device:TPU:0, one launch (start us, length us, event | category | flops | bytes accessed | tf_op | source)
XLA Modules:
  0.0 74.4 jit_solution(8574991717373232747)
XLA Ops:
  0.0 0.5 collective-permute-start.2
  0.5 0.1 collective-permute-start.3
  0.5 3.0 %collective-permute-start.1 = (bf16[128,1024]{1,0:T(8,128)(2,1)}, bf16[128,1024]{1,0:T(8,128)(2,1)}, u32[]{:S(2)}, u32[]{:S(2)}) collective-permute-start(bf16[128,1024]{1,0:T(8,128)(2,1)} %refs_1_.1), channel_id=1, source_target_pairs={{0,4},{4,8},{8,12},{12,0},{1,5},{5,9},{9,13},{13,1},{2,6},{6,10},{... | collective-permute-start | bytes 786440 | tf_op jit(solution)/shard_map/ppermute | solution.py:120
  3.5 1.5 %collective-permute-start = (bf16[128,1024]{1,0:T(8,128)(2,1)}, bf16[128,1024]{1,0:T(8,128)(2,1)}, u32[]{:S(2)}, u32[]{:S(2)}) collective-permute-start(bf16[128,1024]{1,0:T(8,128)(2,1)} %refs_1_.1), channel_id=1, source_target_pairs={{0,1},{1,0},{2,3},{3,2},{4,5},{5,4},{6,7},{7,6},{8,9},{9,8},{10,11... | collective-permute-start | bytes 786440 | tf_op jit(solution)/shard_map/ppermute | solution.py:120
  5.0 0.7 select_reduce_fusion
  5.7 0.6 broadcast_in_dim.25
  6.3 3.9 %all-to-all-start = ((f32[8,2,128]{2,1,0:T(2,128)}), f32[8,2,128]{2,1,0:T(2,128)S(1)}, u32[]{:S(2)}, u32[]{:S(2)}) async-start(f32[8,2,128]{2,1,0:T(2,128)} %bitcast.3), calls=%async_computation | async-start | bytes 16384 | tf_op jit(solution)/shard_map/all_to_all | solution.py:143
  10.2 1.8 %copy-done.4 = bf16[1,1024,1344]{1,2,0:T(8,128)(2,1)S(1)} copy-done((bf16[1,1024,1344]{1,2,0:T(8,128)(2,1)S(1)}, bf16[1,1024,1344]{1,2,0:T(8,128)(2,1)}, u32[]{:S(2)}) %copy-start.4) | copy-done | bytes 2752536
  12.0 1.8 %copy-done.5 = bf16[1,1024,1344]{1,2,0:T(8,128)(2,1)S(1)} copy-done((bf16[1,1024,1344]{1,2,0:T(8,128)(2,1)S(1)}, bf16[1,1024,1344]{1,2,0:T(8,128)(2,1)}, u32[]{:S(2)}) %copy-start.5) | copy-done | bytes 2752536
  13.8 0.7 shard_map.55
  14.5 1.5 %copy-done = bf16[1,1344,1024]{2,1,0:T(8,128)(2,1)} copy-done((bf16[1,1344,1024]{2,1,0:T(8,128)(2,1)}, bf16[1,1344,1024]{2,1,0:T(8,128)(2,1)S(1)}, u32[]{:S(2)}) %copy-start) | copy-done | bytes 2752536
  16.0 1.6 %copy-done.2 = bf16[1,1344,1024]{2,1,0:T(8,128)(2,1)} copy-done((bf16[1,1344,1024]{2,1,0:T(8,128)(2,1)}, bf16[1,1344,1024]{2,1,0:T(8,128)(2,1)S(1)}, u32[]{:S(2)}) %copy-start.2) | copy-done | bytes 2752536
  17.6 0.0 collective-permute-done.1.refs_2_
  17.6 2.0 %collective-permute-start.6 = (bf16[128,1024]{1,0:T(8,128)(2,1)}, bf16[128,1024]{1,0:T(8,128)(2,1)S(1)}, u32[]{:S(2)}, u32[]{:S(2)}) collective-permute-start(bf16[128,1024]{1,0:T(8,128)(2,1)} %collective-permute-done.1.refs_2_), channel_id=1, source_target_pairs={{0,4},{4,8},{8,12},{12,0},{1,5},{5,9},{9,13},{13,1},{2,6},{6,10},{... | collective-permute-start | bytes 786440 | tf_op jit(solution)/shard_map/ppermute | solution.py:120
  19.6 1.5 %collective-permute-start.5 = (bf16[128,1024]{1,0:T(8,128)(2,1)}, bf16[128,1024]{1,0:T(8,128)(2,1)S(1)}, u32[]{:S(2)}, u32[]{:S(2)}) collective-permute-start(bf16[128,1024]{1,0:T(8,128)(2,1)} %collective-permute-done.1.refs_2_), channel_id=1, source_target_pairs={{0,1},{1,0},{2,3},{3,2},{4,5},{5,4},{6,7},{7,6},{8,9},{9,8},{10,11... | collective-permute-start | bytes 786440 | tf_op jit(solution)/shard_map/ppermute | solution.py:120
  21.1 0.0 all-to-all-done.gates_ref
  21.1 0.0 collective-permute-done.refs_0_
  21.1 0.0 collective-permute-done.2.refs_5_
  21.1 0.0 collective-permute-done.3.refs_6_
  21.1 1.8 %copy-done.1 = bf16[1,1344,1024]{2,1,0:T(8,128)(2,1)S(1)} copy-done((bf16[1,1344,1024]{2,1,0:T(8,128)(2,1)S(1)}, bf16[1,1344,1024]{2,1,0:T(8,128)(2,1)}, u32[]{:S(2)}) %copy-start.1) | copy-done | bytes 2752536
  22.9 1.8 %copy-done.3 = bf16[1,1344,1024]{2,1,0:T(8,128)(2,1)S(1)} copy-done((bf16[1,1344,1024]{2,1,0:T(8,128)(2,1)S(1)}, bf16[1,1344,1024]{2,1,0:T(8,128)(2,1)}, u32[]{:S(2)}) %copy-start.3) | copy-done | bytes 2752536
  24.7 6.8 %shard_map.56 = (bf16[128,1024]{1,0:T(8,128)(2,1)S(1)}, f32[128,1024]{1,0:T(8,128)S(1)}, bf16[128,1024]{1,0:T(8,128)(2,1)S(1)}) custom-call(f32[8,2,128]{2,1,0:T(2,128)S(1)} %all-to-all-done.gates_ref, bf16[128,1024]{1,0:T(8,128)(2,1)} %collective-permute-done.refs_0_, bf16[128,1024]{1,0:T(8,128)(2,1)S(1)} %copy-done.6, ...), custom_call_target="tpu_custom_call" | custom-call | flops 3472883712 | bytes 12976128 | tf_op jit(solution)/shard_map/pallas_call | solution.py:102
  31.5 0.0 collective-permute-done.6.refs_2_
  31.5 1.5 %collective-permute-start.8 = (bf16[128,1024]{1,0:T(8,128)(2,1)S(1)}, bf16[128,1024]{1,0:T(8,128)(2,1)S(1)}, u32[]{:S(2)}, u32[]{:S(2)}) collective-permute-start(bf16[128,1024]{1,0:T(8,128)(2,1)S(1)} %collective-permute-done.6.refs_2_), channel_id=1, source_target_pairs={{0,4},{4,8},{8,12},{12,0},{1,5},{5,9},{9,13},{13,1},{2,6},{6,10},{... | collective-permute-start | bytes 786440 | tf_op jit(solution)/shard_map/ppermute | solution.py:120
  33.0 0.6 collective-permute-start.7
  33.6 2.4 %collective-permute-start.4 = (bf16[128,1024]{1,0:T(8,128)(2,1)S(1)}, bf16[128,1024]{1,0:T(8,128)(2,1)S(1)}, u32[]{:S(2)}, u32[]{:S(2)}) collective-permute-start(bf16[128,1024]{1,0:T(8,128)(2,1)S(1)} %get-tuple-element.30), channel_id=1, source_target_pairs={{0,12},{4,0},{8,4},{12,8},{1,13},{5,1},{9,5},{13,9},{2,14},{6,2},{... | collective-permute-start | bytes 786440 | tf_op jit(solution)/shard_map/ppermute | solution.py:120
  36.0 5.6 %shard_map.57 = (bf16[128,1024]{1,0:T(8,128)(2,1)S(1)}, f32[128,1024]{1,0:T(8,128)S(1)}) custom-call(f32[8,2,128]{2,1,0:T(2,128)S(1)} %all-to-all-done.gates_ref, bf16[128,1024]{1,0:T(8,128)(2,1)S(1)} %get-tuple-element.31.refs_0_, bf16[128,1024]{1,0:T(8,128)(2,1)S(1)} %collective-permute-done.5.refs_1_, ...), custom_call_target="tpu_custom_call" | custom-call | flops 2315255808 | bytes 12320768 | tf_op jit(solution)/shard_map/pallas_call | solution.py:102
  41.6 1.1 %collective-permute-done.8.refs_2_ = bf16[128,1024]{1,0:T(8,128)(2,1)S(1)} collective-permute-done((bf16[128,1024]{1,0:T(8,128)(2,1)S(1)}, bf16[128,1024]{1,0:T(8,128)(2,1)S(1)}, u32[]{:S(2)}, u32[]{:S(2)}) %collective-permute-start.8) | collective-permute-done | bytes 262176 | tf_op jit(solution)/shard_map/ppermute | solution.py:120
  42.6 0.6 collective-permute-start.10
  43.2 0.5 collective-permute-start.9
  43.7 0.0 collective-permute-done.7.refs_1_
  43.7 5.6 %shard_map.58 = (bf16[128,1024]{1,0:T(8,128)(2,1)S(1)}, f32[128,1024]{1,0:T(8,128)S(1)}) custom-call(f32[8,2,128]{2,1,0:T(2,128)S(1)} %all-to-all-done.gates_ref, bf16[128,1024]{1,0:T(8,128)(2,1)S(1)} %get-tuple-element.37.refs_0_, bf16[128,1024]{1,0:T(8,128)(2,1)S(1)} %collective-permute-done.7.refs_1_, ...), custom_call_target="tpu_custom_call" | custom-call | flops 2315255808 | bytes 12320768 | tf_op jit(solution)/shard_map/pallas_call | solution.py:102
  49.3 1.0 %collective-permute-start.12 = (bf16[128,1024]{1,0:T(8,128)(2,1)S(1)}, bf16[128,1024]{1,0:T(8,128)(2,1)S(1)}, u32[]{:S(2)}, u32[]{:S(2)}) collective-permute-start(bf16[128,1024]{1,0:T(8,128)(2,1)S(1)} %get-tuple-element.35.refs_0_), channel_id=1, source_target_pairs={{0,1},{1,0},{2,3},{3,2},{4,5},{5,4},{6,7},{7,6},{8,9},{9,8},{10,11... | collective-permute-start | bytes 786440 | tf_op jit(solution)/shard_map/ppermute | solution.py:120
  50.3 0.1 convert_add_fusion.refs_1_
  50.4 0.0 collective-permute-done.10.refs_2_
  50.4 5.0 %shard_map.59 = bf16[128,1024]{1,0:T(8,128)(2,1)S(1)} custom-call(f32[8,2,128]{2,1,0:T(2,128)S(1)} %all-to-all-done.gates_ref, bf16[128,1024]{1,0:T(8,128)(2,1)S(1)} %get-tuple-element.35.refs_0_, f32[128,1024]{1,0:T(8,128)S(1)} %convert_add_fusion.refs_1_, bf16[128,1024]{1,0:T(8,128)(2,1)S(1)} %collective-permute-done.10.refs_2_, ...), custom_call_target="tpu_custom_call" | custom-call | flops 1157627904 | bytes 11665408 | tf_op jit(solution)/shard_map/pallas_call | solution.py:102
  55.4 1.1 %collective-permute-start.11 = (bf16[128,1024]{1,0:T(8,128)(2,1)S(1)}, bf16[128,1024]{1,0:T(8,128)(2,1)S(1)}, u32[]{:S(2)}, u32[]{:S(2)}) collective-permute-start(bf16[128,1024]{1,0:T(8,128)(2,1)S(1)} %shard_map.59), channel_id=1, source_target_pairs={{0,1},{1,0},{2,3},{3,2},{4,5},{5,4},{6,7},{7,6},{8,9},{9,8},{10,11... | collective-permute-start | bytes 786440 | tf_op jit(solution)/shard_map/ppermute | solution.py:120
  56.5 0.0 collective-permute-done.9
  56.6 0.1 add_convert_fusion.3
  56.6 0.5 collective-permute-done.12
  57.1 0.1 add_convert_fusion.2
  57.2 0.6 collective-permute-start.15
  57.7 4.1 %collective-permute-done.11 = bf16[128,1024]{1,0:T(8,128)(2,1)S(1)} collective-permute-done((bf16[128,1024]{1,0:T(8,128)(2,1)S(1)}, bf16[128,1024]{1,0:T(8,128)(2,1)S(1)}, u32[]{:S(2)}, u32[]{:S(2)}) %collective-permute-start.11) | collective-permute-done | bytes 262176 | tf_op jit(solution)/shard_map/ppermute | solution.py:120
  61.9 0.1 add_convert_fusion.1
  61.9 3.3 %collective-permute-start.14 = (bf16[128,1024]{1,0:T(8,128)(2,1)S(1)}, bf16[128,1024]{1,0:T(8,128)(2,1)S(1)}, u32[]{:S(2)}, u32[]{:S(2)}) collective-permute-start(bf16[128,1024]{1,0:T(8,128)(2,1)S(1)} %add_convert_fusion.1), channel_id=1, source_target_pairs={{0,4},{4,8},{8,12},{12,0},{1,5},{5,9},{9,13},{13,1},{2,6},{6,10},{... | collective-permute-start | bytes 786440 | tf_op jit(solution)/shard_map/ppermute | solution.py:120
  65.2 0.0 collective-permute-start.13
  65.2 8.3 %collective-permute-done.15 = bf16[128,1024]{1,0:T(8,128)(2,1)S(1)} collective-permute-done((bf16[128,1024]{1,0:T(8,128)(2,1)S(1)}, bf16[128,1024]{1,0:T(8,128)(2,1)S(1)}, u32[]{:S(2)}, u32[]{:S(2)}) %collective-permute-start.15) | collective-permute-done | bytes 262176 | tf_op jit(solution)/shard_map/ppermute | solution.py:120
  73.5 0.9 %add_convert_fusion = bf16[128,1024]{1,0:T(8,128)(2,1)} fusion(bf16[128,1024]{1,0:T(8,128)(2,1)S(1)} %collective-permute-done.14, bf16[128,1024]{1,0:T(8,128)(2,1)S(1)} %collective-permute-done.15, f32[128,1024]{1,0:T(8,128)S(1)} %convert_add_fusion.refs_1_, bf16[128,1024]{1,0:T(8,128)(2,1)S(1)} %collective-permute-done.13), kind=kLoop, calls=%fused_computation | loop fusion | flops 917504 | bytes 1572864 | tf_op jit(solution)/shard_map/convert_element_type | solution.py:207
  (12 shorter events, 0.0 us)
Async XLA Ops:
  0.0 21.1 %collective-permute-start.2 = (bf16[1,1344,1024]{2,1,0:T(8,128)(2,1)}, bf16[1,1344,1024]{2,1,0:T(8,128)(2,1)S(1)}, u32[]{:S(2)}, u32[]{:S(2)}) collective-permute-start(bf16[1,1344,1024]{2,1,0:T(8,128)(2,1)} %bitcast.6), channel_id=1, source_target_pairs={{0,2},{2,0},{1,3},{3,1},{4,6},{6,4},{5,7},{7,5},{8,10},{10,8},{9,1... | collective-permute-start | bytes 8257544 | tf_op jit(solution)/shard_map/ppermute | solution.py:120
  0.5 20.6 %collective-permute-start.3 = (bf16[1,1344,1024]{2,1,0:T(8,128)(2,1)}, bf16[1,1344,1024]{2,1,0:T(8,128)(2,1)}, u32[]{:S(2)}, u32[]{:S(2)}) collective-permute-start(bf16[1,1344,1024]{2,1,0:T(8,128)(2,1)} %bitcast.8), channel_id=1, source_target_pairs={{0,2},{2,0},{1,3},{3,1},{4,6},{6,4},{5,7},{7,5},{8,10},{10,8},{9,1... | collective-permute-start | bytes 8257544 | tf_op jit(solution)/shard_map/ppermute | solution.py:120
  0.5 17.1 %collective-permute-start.1 = (bf16[128,1024]{1,0:T(8,128)(2,1)}, bf16[128,1024]{1,0:T(8,128)(2,1)}, u32[]{:S(2)}, u32[]{:S(2)}) collective-permute-start(bf16[128,1024]{1,0:T(8,128)(2,1)} %refs_1_.1), channel_id=1, source_target_pairs={{0,4},{4,8},{8,12},{12,0},{1,5},{5,9},{9,13},{13,1},{2,6},{6,10},{... | collective-permute-start | bytes 786440 | tf_op jit(solution)/shard_map/ppermute | solution.py:120
  3.5 17.6 %collective-permute-start = (bf16[128,1024]{1,0:T(8,128)(2,1)}, bf16[128,1024]{1,0:T(8,128)(2,1)}, u32[]{:S(2)}, u32[]{:S(2)}) collective-permute-start(bf16[128,1024]{1,0:T(8,128)(2,1)} %refs_1_.1), channel_id=1, source_target_pairs={{0,1},{1,0},{2,3},{3,2},{4,5},{5,4},{6,7},{7,6},{8,9},{9,8},{10,11... | collective-permute-start | bytes 786440 | tf_op jit(solution)/shard_map/ppermute | solution.py:120
  6.3 14.7 %all-to-all-start = ((f32[8,2,128]{2,1,0:T(2,128)}), f32[8,2,128]{2,1,0:T(2,128)S(1)}, u32[]{:S(2)}, u32[]{:S(2)}) async-start(f32[8,2,128]{2,1,0:T(2,128)} %bitcast.3), calls=%async_computation | async-start | bytes 16384 | tf_op jit(solution)/shard_map/all_to_all | solution.py:143
  10.2 1.8 %copy-start.4 = (bf16[1,1024,1344]{1,2,0:T(8,128)(2,1)S(1)}, bf16[1,1024,1344]{1,2,0:T(8,128)(2,1)}, u32[]{:S(2)}) copy-start(bf16[1,1024,1344]{1,2,0:T(8,128)(2,1)} %param.8) | copy-start | bytes 8257540
  12.0 1.8 %copy-start.5 = (bf16[1,1024,1344]{1,2,0:T(8,128)(2,1)S(1)}, bf16[1,1024,1344]{1,2,0:T(8,128)(2,1)}, u32[]{:S(2)}) copy-start(bf16[1,1024,1344]{1,2,0:T(8,128)(2,1)} %param.9) | copy-start | bytes 8257540
  13.8 7.3 %copy-start.6 = (bf16[128,1024]{1,0:T(8,128)(2,1)S(1)}, bf16[128,1024]{1,0:T(8,128)(2,1)}, u32[]{:S(2)}) copy-start(bf16[128,1024]{1,0:T(8,128)(2,1)} %refs_1_.1) | copy-start | bytes 786436
  14.5 1.6 %copy-start = (bf16[1,1344,1024]{2,1,0:T(8,128)(2,1)}, bf16[1,1344,1024]{2,1,0:T(8,128)(2,1)S(1)}, u32[]{:S(2)}) copy-start(bf16[1,1344,1024]{2,1,0:T(8,128)(2,1)S(1)} %get-tuple-element.26.refs_3_) | copy-start | bytes 8257540
  16.0 1.6 %copy-start.2 = (bf16[1,1344,1024]{2,1,0:T(8,128)(2,1)}, bf16[1,1344,1024]{2,1,0:T(8,128)(2,1)S(1)}, u32[]{:S(2)}) copy-start(bf16[1,1344,1024]{2,1,0:T(8,128)(2,1)S(1)} %get-tuple-element.28.refs_4_) | copy-start | bytes 8257540
  17.6 13.9 %collective-permute-start.6 = (bf16[128,1024]{1,0:T(8,128)(2,1)}, bf16[128,1024]{1,0:T(8,128)(2,1)S(1)}, u32[]{:S(2)}, u32[]{:S(2)}) collective-permute-start(bf16[128,1024]{1,0:T(8,128)(2,1)} %collective-permute-done.1.refs_2_), channel_id=1, source_target_pairs={{0,4},{4,8},{8,12},{12,0},{1,5},{5,9},{9,13},{13,1},{2,6},{6,10},{... | collective-permute-start | bytes 786440 | tf_op jit(solution)/shard_map/ppermute | solution.py:120
  19.6 16.3 %collective-permute-start.5 = (bf16[128,1024]{1,0:T(8,128)(2,1)}, bf16[128,1024]{1,0:T(8,128)(2,1)S(1)}, u32[]{:S(2)}, u32[]{:S(2)}) collective-permute-start(bf16[128,1024]{1,0:T(8,128)(2,1)} %collective-permute-done.1.refs_2_), channel_id=1, source_target_pairs={{0,1},{1,0},{2,3},{3,2},{4,5},{5,4},{6,7},{7,6},{8,9},{9,8},{10,11... | collective-permute-start | bytes 786440 | tf_op jit(solution)/shard_map/ppermute | solution.py:120
  21.1 1.8 %copy-start.1 = (bf16[1,1344,1024]{2,1,0:T(8,128)(2,1)S(1)}, bf16[1,1344,1024]{2,1,0:T(8,128)(2,1)}, u32[]{:S(2)}) copy-start(bf16[1,1344,1024]{2,1,0:T(8,128)(2,1)} %copy-done) | copy-start | bytes 8257540
  22.9 1.8 %copy-start.3 = (bf16[1,1344,1024]{2,1,0:T(8,128)(2,1)S(1)}, bf16[1,1344,1024]{2,1,0:T(8,128)(2,1)}, u32[]{:S(2)}) copy-start(bf16[1,1344,1024]{2,1,0:T(8,128)(2,1)} %copy-done.2) | copy-start | bytes 8257540
  31.5 11.1 %collective-permute-start.8 = (bf16[128,1024]{1,0:T(8,128)(2,1)S(1)}, bf16[128,1024]{1,0:T(8,128)(2,1)S(1)}, u32[]{:S(2)}, u32[]{:S(2)}) collective-permute-start(bf16[128,1024]{1,0:T(8,128)(2,1)S(1)} %collective-permute-done.6.refs_2_), channel_id=1, source_target_pairs={{0,4},{4,8},{8,12},{12,0},{1,5},{5,9},{9,13},{13,1},{2,6},{6,10},{... | collective-permute-start | bytes 786440 | tf_op jit(solution)/shard_map/ppermute | solution.py:120
  33.0 10.6 %collective-permute-start.7 = (bf16[128,1024]{1,0:T(8,128)(2,1)S(1)}, bf16[128,1024]{1,0:T(8,128)(2,1)S(1)}, u32[]{:S(2)}, u32[]{:S(2)}) collective-permute-start(bf16[128,1024]{1,0:T(8,128)(2,1)S(1)} %collective-permute-done.6.refs_2_), channel_id=1, source_target_pairs={{0,1},{1,0},{2,3},{3,2},{4,5},{5,4},{6,7},{7,6},{8,9},{9,8},{10,11... | collective-permute-start | bytes 786440 | tf_op jit(solution)/shard_map/ppermute | solution.py:120
  33.6 16.7 %collective-permute-start.4 = (bf16[128,1024]{1,0:T(8,128)(2,1)S(1)}, bf16[128,1024]{1,0:T(8,128)(2,1)S(1)}, u32[]{:S(2)}, u32[]{:S(2)}) collective-permute-start(bf16[128,1024]{1,0:T(8,128)(2,1)S(1)} %get-tuple-element.30), channel_id=1, source_target_pairs={{0,12},{4,0},{8,4},{12,8},{1,13},{5,1},{9,5},{13,9},{2,14},{6,2},{... | collective-permute-start | bytes 786440 | tf_op jit(solution)/shard_map/ppermute | solution.py:120
  42.6 7.8 %collective-permute-start.10 = (bf16[128,1024]{1,0:T(8,128)(2,1)S(1)}, bf16[128,1024]{1,0:T(8,128)(2,1)S(1)}, u32[]{:S(2)}, u32[]{:S(2)}) collective-permute-start(bf16[128,1024]{1,0:T(8,128)(2,1)S(1)} %collective-permute-done.8.refs_2_), channel_id=1, source_target_pairs={{0,1},{1,0},{2,3},{3,2},{4,5},{5,4},{6,7},{7,6},{8,9},{9,8},{10,11... | collective-permute-start | bytes 786440 | tf_op jit(solution)/shard_map/ppermute | solution.py:120
  43.2 13.4 %collective-permute-start.9 = (bf16[128,1024]{1,0:T(8,128)(2,1)S(1)}, bf16[128,1024]{1,0:T(8,128)(2,1)S(1)}, u32[]{:S(2)}, u32[]{:S(2)}) collective-permute-start(bf16[128,1024]{1,0:T(8,128)(2,1)S(1)} %get-tuple-element.37.refs_0_), channel_id=1, source_target_pairs={{0,12},{4,0},{8,4},{12,8},{1,13},{5,1},{9,5},{13,9},{2,14},{6,2},{... | collective-permute-start | bytes 786440 | tf_op jit(solution)/shard_map/ppermute | solution.py:120
  49.3 7.8 %collective-permute-start.12 = (bf16[128,1024]{1,0:T(8,128)(2,1)S(1)}, bf16[128,1024]{1,0:T(8,128)(2,1)S(1)}, u32[]{:S(2)}, u32[]{:S(2)}) collective-permute-start(bf16[128,1024]{1,0:T(8,128)(2,1)S(1)} %get-tuple-element.35.refs_0_), channel_id=1, source_target_pairs={{0,1},{1,0},{2,3},{3,2},{4,5},{5,4},{6,7},{7,6},{8,9},{9,8},{10,11... | collective-permute-start | bytes 786440 | tf_op jit(solution)/shard_map/ppermute | solution.py:120
  55.4 6.4 %collective-permute-start.11 = (bf16[128,1024]{1,0:T(8,128)(2,1)S(1)}, bf16[128,1024]{1,0:T(8,128)(2,1)S(1)}, u32[]{:S(2)}, u32[]{:S(2)}) collective-permute-start(bf16[128,1024]{1,0:T(8,128)(2,1)S(1)} %shard_map.59), channel_id=1, source_target_pairs={{0,1},{1,0},{2,3},{3,2},{4,5},{5,4},{6,7},{7,6},{8,9},{9,8},{10,11... | collective-permute-start | bytes 786440 | tf_op jit(solution)/shard_map/ppermute | solution.py:120
  57.2 16.3 %collective-permute-start.15 = (bf16[128,1024]{1,0:T(8,128)(2,1)S(1)}, bf16[128,1024]{1,0:T(8,128)(2,1)S(1)}, u32[]{:S(2)}, u32[]{:S(2)}) collective-permute-start(bf16[128,1024]{1,0:T(8,128)(2,1)S(1)} %add_convert_fusion.2), channel_id=1, source_target_pairs={{0,8},{4,12},{8,0},{12,4},{1,9},{5,13},{9,1},{13,5},{2,10},{6,14},... | collective-permute-start | bytes 786440 | tf_op jit(solution)/shard_map/ppermute | solution.py:120
  61.9 11.5 %collective-permute-start.14 = (bf16[128,1024]{1,0:T(8,128)(2,1)S(1)}, bf16[128,1024]{1,0:T(8,128)(2,1)S(1)}, u32[]{:S(2)}, u32[]{:S(2)}) collective-permute-start(bf16[128,1024]{1,0:T(8,128)(2,1)S(1)} %add_convert_fusion.1), channel_id=1, source_target_pairs={{0,4},{4,8},{8,12},{12,0},{1,5},{5,9},{9,13},{13,1},{2,6},{6,10},{... | collective-permute-start | bytes 786440 | tf_op jit(solution)/shard_map/ppermute | solution.py:120
  65.2 8.3 %collective-permute-start.13 = (bf16[128,1024]{1,0:T(8,128)(2,1)S(1)}, bf16[128,1024]{1,0:T(8,128)(2,1)S(1)}, u32[]{:S(2)}, u32[]{:S(2)}) collective-permute-start(bf16[128,1024]{1,0:T(8,128)(2,1)S(1)} %add_convert_fusion.3), channel_id=1, source_target_pairs={{0,1},{1,0},{2,3},{3,2},{4,5},{5,4},{6,7},{7,6},{8,9},{9,8},{10,11... | collective-permute-start | bytes 786440 | tf_op jit(solution)/shard_map/ppermute | solution.py:120

commit v12 on v11

--- a/solution.py
+++ b/solution.py
@@ -35,10 +35,11 @@
     )(*arrays)
 
 
-def expert_kernel(block, slots, unit, number, sources, waits, gates_ref, *refs):
-    core, z, sub = (lax.axis_index(a) for a in ("core", "z", "sub"))
-    depth, subs = lax.axis_size("z"), lax.axis_size("sub")
-    blocks = len(sources)
+def expert_kernel(block, slots, unit, number, sources, waits, *refs):
+    rounds = sorted({r for r, _ in sources})
+    gate_refs, refs = refs[: len(rounds)], refs[len(rounds) :]
+    first, core = lax.axis_index("z") * number, lax.axis_index("core")
+    blocks, experts = len(sources), gate_refs[0].shape[0] // lax.axis_size("sub")
     refs = refs[waits:]
     x_refs, tables, out_refs = refs[:blocks], refs[blocks : blocks + 2 * number], refs[blocks + 2 * number :]
     earlier = lax.broadcasted_iota(jnp.int32, (block, block), 0)
@@ -46,11 +47,10 @@
     before = (earlier < later).astype(jnp.bfloat16)
     groups = [range(g, min(g + unit, blocks)) for g in range(0, blocks, unit)]
     sizes = [-(-len(g) * slots // 16) * 16 for g in groups]
-    row = lax.broadcasted_iota(jnp.int32, (number, block), 0)
+    row = lax.broadcasted_iota(jnp.int32, (experts, block), 0)
     gates, ranks = [], []
     for r, turn in sources:
-        source = lax.rem(z + depth - r, depth) * subs + lax.rem(sub + subs - turn, subs)
-        gate = gates_ref[source]
+        gate = gate_refs[rounds.index(r)][turn * experts : (turn + 1) * experts, :]
         gates.append(gate)
         ranks.append(
             jnp.dot((gate > 0).astype(jnp.bfloat16), before, preferred_element_type=jnp.float32)
@@ -58,7 +58,7 @@
     sums = [0.0] * blocks
     for n in range(number):
         up_ref, down_ref = tables[2 * n], tables[2 * n + 1]
-        mine = row == lax.rem(core + number - n, number)
+        mine = row == first + lax.rem(core + number - n, number)
         picks, scales, rows = [], [], []
         for group, size in zip(groups, sizes):
             slot = lax.broadcasted_iota(jnp.int32, (size, block), 0)
@@ -95,14 +95,15 @@
 
 
 def run_experts(after, gates, sources, arrived, tables, kinds, slots):
-    blocks, number, block = len(arrived), gates.shape[1], gates.shape[2]
+    blocks, number, block = len(arrived), len(tables) // 2, gates[0].shape[1]
+    gates = [gates[r] for r in sorted({r for r, _ in sources})]
     hidden, width = tables[0].shape[1:]
     unit = 16 // math.gcd(16, slots)
     whole = pl.BlockSpec(memory_space=pltpu.VMEM)
     return pl.pallas_call(
         functools.partial(expert_kernel, block, slots, unit, number, sources, len(after)),
         out_shape=[jax.ShapeDtypeStruct((block, width), kind) for kind in kinds],
-        in_specs=[whole]
+        in_specs=[whole] * len(gates)
         + [pl.BlockSpec(memory_space=pl.ANY)] * len(after)
         + [whole] * (blocks + len(tables)),
         out_specs=[whole] * blocks,
@@ -112,7 +113,7 @@
             bytes_accessed=5 * blocks * block * width + 2 * len(tables) * width * hidden,
             transcendentals=0,
         ),
-    )(gates, *after, *arrived, *tables)
+    )(*gates, *after, *arrived, *tables)
 
 
 def shift(array, axis, step):
@@ -138,9 +139,10 @@
     ids = jnp.arange(experts, dtype=jnp.int32)
     weight = jnp.sum(
         jnp.where(routes.T[None] == ids[:, None, None], gates.T[None], 0.0), axis=1
-    ).reshape(depth, 1, cores, block)
-    weight = jnp.broadcast_to(weight, (depth, subs, cores, block)).reshape(-1, cores, block)
-    weight = lax.all_to_all(weight, ("z", "sub"), split_axis=0, concat_axis=0, tiled=True)
+    )
+    near = [weight] + [follow(shift(weight, "sub", s), tables[0]) for s in range(1, subs)]
+    near = jnp.concatenate(near, axis=0)
+    weights = [near] + [shift(near, "z", r) for r in range(1, depth)]
     last = depth - 1
     kept, others = {}, {}
     totals, home = {}, None
@@ -170,7 +172,7 @@
             after = after + [totals[j - 2]]
         sources = [(j, s) for s in range(1, subs)] + [(r, 0) for r in fresh]
         arrived = handed + [ring[r] for r in fresh]
-        partial = run_experts(after, weight, sources, arrived, tables, kinds, slots)
+        partial = run_experts(after, weights, sources, arrived, tables, kinds, slots)
         firsts.append(partial[0])
         if j + 2 < depth:
             ring.append(follow(shift(ring[-1], "z", 1), partial[0]))

time: 74.8 us -> 68.2 us (0.912)
  Pallas kernels: 23.8 us -> 16.5 us
  local copies, waits for them, and re-layouts: 10.8 us -> 3.56 us
  waiting for transfers between devices: 14 us -> 19.9 us
  starting transfers between devices: 23.8 us -> 26.1 us
    pallas_call x4, Pallas kernels: 23.1 us -> 15.8 us  [run_experts(): pl.pallas_call(functools.partial(expert_kernel, block, slots, unit, numbe...]
    unnamed x14 -> x6, local copies, waits for them, and re-layouts: 10.2 us -> 3.56 us
    ppermute x16 -> x20, starting transfers between devices: 20 us -> 26.1 us  [shift(): lax.ppermute(array, axis, [(i, (i + step) % size) for i in range(size)])]
    ppermute x16 -> x20, waiting for transfers between devices: 14 us -> 19.9 us  [shift(): lax.ppermute(array, axis, [(i, (i + step) % size) for i in range(size)])]
    all_to_all x1 -> x0, starting transfers between devices: 3.87 us -> none  [local(): lax.all_to_all(weight, ('z', 'sub'), split_axis=0, concat_axis=0, tiled=T...]
  transfers between devices with their start and end apart: 17 -> 20, of which waited for: 4 -> 8; matrix products, arithmetic and copies ran while one was open for 2% -> 1% of each run, Pallas kernels for 32% -> 24%
where the time goes in v12:
time: 68.2 us; the launch traced here: 68 us
  starting transfers between devices  26.1 us (38%)
  waiting for transfers between devices  19.9 us (29%)
  Pallas kernels  16.5 us (24%)
  local copies, waits for them, and re-layouts  3.56 us (5%)
  other arithmetic  1.85 us (3%)
    ppermute x20, starting transfers between devices, shift(): lax.ppermute(array, axis, [(i, (i + step) % size) for i in range(size)])  26.1 us
    ppermute x20, waiting for transfers between devices, shift(): lax.ppermute(array, axis, [(i, (i + step) % size) for i in range(size)])  19.9 us
    pallas_call x4, Pallas kernels, run_experts(): pl.pallas_call(functools.partial(expert_kernel, block, slots, unit, numbe...  15.8 us
    unnamed x6, local copies, waits for them, and re-layouts  3.56 us
  transfers between devices with their start and end apart: 20, of which 8 were waited for; matrix products, arithmetic and copies ran while one was open for 1% of the time, Pallas kernels for 24%

profile of v12, /device:TPU:0, one launch (start us, length us, event | category | flops | bytes accessed | tf_op | source)
XLA Modules:
  0.0 68.0 jit_solution(9784209029174868286)
XLA Ops:
  0.0 0.5 collective-permute-start.4
  0.5 0.1 collective-permute-start.5
  0.5 3.0 %collective-permute-start.3 = (bf16[128,1024]{1,0:T(8,128)(2,1)}, bf16[128,1024]{1,0:T(8,128)(2,1)S(1)}, u32[]{:S(2)}, u32[]{:S(2)}) collective-permute-start(bf16[128,1024]{1,0:T(8,128)(2,1)} %refs_3_.1), channel_id=1, source_target_pairs={{0,4},{4,8},{8,12},{12,0},{1,5},{5,9},{9,13},{13,1},{2,6},{6,10},{... | collective-permute-start | bytes 786440 | tf_op jit(solution)/shard_map/ppermute | solution.py:121
  3.5 1.5 %collective-permute-start.2 = (bf16[128,1024]{1,0:T(8,128)(2,1)}, bf16[128,1024]{1,0:T(8,128)(2,1)S(1)}, u32[]{:S(2)}, u32[]{:S(2)}) collective-permute-start(bf16[128,1024]{1,0:T(8,128)(2,1)} %refs_3_.1), channel_id=1, source_target_pairs={{0,1},{1,0},{2,3},{3,2},{4,5},{5,4},{6,7},{7,6},{8,9},{9,8},{10,11... | collective-permute-start | bytes 786440 | tf_op jit(solution)/shard_map/ppermute | solution.py:121
  5.0 0.7 %select_reduce_fusion = f32[8,128]{1,0:T(8,128)S(1)} fusion(f32[4,128]{1,0:T(4,128)} %bitcast.8, s32[4,128]{1,0:T(4,128)} %bitcast.9), kind=kLoop, calls=%fused_computation.5 | loop fusion | flops 11264 | bytes 8192 | tf_op jit(solution)/shard_map/reduce_sum | solution.py:140
  5.7 0.5 collective-permute-start
  6.3 1.8 %copy-done = bf16[1,1024,1344]{1,2,0:T(8,128)(2,1)S(1)} copy-done((bf16[1,1024,1344]{1,2,0:T(8,128)(2,1)S(1)}, bf16[1,1024,1344]{1,2,0:T(8,128)(2,1)}, u32[]{:S(2)}) %copy-start) | copy-done | bytes 2752536
  8.1 1.8 %copy-done.1 = bf16[1,1024,1344]{1,2,0:T(8,128)(2,1)S(1)} copy-done((bf16[1,1024,1344]{1,2,0:T(8,128)(2,1)S(1)}, bf16[1,1024,1344]{1,2,0:T(8,128)(2,1)}, u32[]{:S(2)}) %copy-start.1) | copy-done | bytes 2752536
  9.8 0.7 %shard_map.55 = (bf16[1,1344,1024]{2,1,0:T(8,128)(2,1)S(1)}, bf16[1,1344,1024]{2,1,0:T(8,128)(2,1)S(1)}) custom-call(bf16[1,1344,1024]{2,1,0:T(8,128)(2,1)S(1)} %bitcast.5, bf16[1,1344,1024]{2,1,0:T(8,128)(2,1)S(1)} %bitcast.7), custom_call_target="tpu_custom_call" | custom-call | tf_op jit(solution)/shard_map/pallas_call | solution.py:28
  10.5 1.2 %collective-permute-done = f32[8,128]{1,0:T(8,128)S(1)} collective-permute-done((f32[8,128]{1,0:T(8,128)S(1)}, f32[8,128]{1,0:T(8,128)S(1)}, u32[]{:S(2)}, u32[]{:S(2)}) %collective-permute-start) | collective-permute-done | bytes 4128 | tf_op jit(solution)/shard_map/ppermute | solution.py:121
  11.8 1.6 %collective-permute-start.1 = (f32[16,128]{1,0:T(8,128)S(1)}, f32[16,128]{1,0:T(8,128)S(1)}, u32[]{:S(2)}, u32[]{:S(2)}) collective-permute-start(f32[16,128]{1,0:T(8,128)S(1)} %pad_maximum_fusion.refs_0_), channel_id=1, source_target_pairs={{0,4},{4,8},{8,12},{12,0},{1,5},{5,9},{9,13},{13,1},{2,6},{6,10},{... | collective-permute-start | bytes 24584 | tf_op jit(solution)/shard_map/ppermute | solution.py:121
  13.3 0.0 collective-permute-done.3.refs_4_
  13.4 1.6 %collective-permute-start.10 = (bf16[128,1024]{1,0:T(8,128)(2,1)S(1)}, bf16[128,1024]{1,0:T(8,128)(2,1)S(1)}, u32[]{:S(2)}, u32[]{:S(2)}) collective-permute-start(bf16[128,1024]{1,0:T(8,128)(2,1)S(1)} %collective-permute-done.3.refs_4_), channel_id=1, source_target_pairs={{0,4},{4,8},{8,12},{12,0},{1,5},{5,9},{9,13},{13,1},{2,6},{6,10},{... | collective-permute-start | bytes 786440 | tf_op jit(solution)/shard_map/ppermute | solution.py:121
  14.9 2.3 %collective-permute-done.1.refs_1_.refs_0_ = f32[16,128]{1,0:T(8,128)S(1)} collective-permute-done((f32[16,128]{1,0:T(8,128)S(1)}, f32[16,128]{1,0:T(8,128)S(1)}, u32[]{:S(2)}, u32[]{:S(2)}) %collective-permute-start.1) | collective-permute-done | bytes 8224 | tf_op jit(solution)/shard_map/ppermute | solution.py:121
  17.3 1.5 %collective-permute-start.9 = (bf16[128,1024]{1,0:T(8,128)(2,1)S(1)}, bf16[128,1024]{1,0:T(8,128)(2,1)S(1)}, u32[]{:S(2)}, u32[]{:S(2)}) collective-permute-start(bf16[128,1024]{1,0:T(8,128)(2,1)S(1)} %collective-permute-done.3.refs_4_), channel_id=1, source_target_pairs={{0,1},{1,0},{2,3},{3,2},{4,5},{5,4},{6,7},{7,6},{8,9},{9,8},{10,11... | collective-permute-start | bytes 786440 | tf_op jit(solution)/shard_map/ppermute | solution.py:121
  18.8 0.0 collective-permute-done.2.refs_2_
  18.8 0.0 collective-permute-done.4.refs_7_.refs_6_
  18.8 0.0 collective-permute-done.5.refs_8_.refs_7_
  18.8 4.9 %shard_map.56 = (bf16[128,1024]{1,0:T(8,128)(2,1)S(1)}, f32[128,1024]{1,0:T(8,128)S(1)}, bf16[128,1024]{1,0:T(8,128)(2,1)S(1)}) custom-call(f32[16,128]{1,0:T(8,128)S(1)} %pad_maximum_fusion.refs_0_, f32[16,128]{1,0:T(8,128)S(1)} %collective-permute-done.1.refs_1_.refs_0_, bf16[128,1024]{1,0:T(8,128)(2,1)S(1)} %collective-permute-done.2.refs_2_, ...), custom_call_target="tpu_custom_call" | custom-call | flops 3472883712 | bytes 12976128 | tf_op jit(solution)/shard_map/pallas_call | solution.py:103
  23.7 0.0 collective-permute-done.10.refs_4_
  23.7 0.1 collective-permute-start.12
  23.7 0.6 collective-permute-start.11
  24.3 1.0 %collective-permute-start.7 = (f32[16,128]{1,0:T(8,128)S(1)}, f32[16,128]{1,0:T(8,128)S(1)}, u32[]{:S(2)}, u32[]{:S(2)}) collective-permute-start(f32[16,128]{1,0:T(8,128)S(1)} %pad_maximum_fusion.refs_0_), channel_id=1, source_target_pairs={{0,8},{4,12},{8,0},{12,4},{1,9},{5,13},{9,1},{13,5},{2,10},{6,14},... | collective-permute-start | bytes 24584 | tf_op jit(solution)/shard_map/ppermute | solution.py:121
  25.4 2.7 %collective-permute-start.8 = (f32[16,128]{1,0:T(8,128)S(1)}, f32[16,128]{1,0:T(8,128)S(1)}, u32[]{:S(2)}, u32[]{:S(2)}) collective-permute-start(f32[16,128]{1,0:T(8,128)S(1)} %pad_maximum_fusion.refs_0_), channel_id=1, source_target_pairs={{0,12},{4,0},{8,4},{12,8},{1,13},{5,1},{9,5},{13,9},{2,14},{6,2},{... | collective-permute-start | bytes 24584 | tf_op jit(solution)/shard_map/ppermute | solution.py:121
  28.1 0.8 %collective-permute-done.7.refs_1_.refs_0_ = f32[16,128]{1,0:T(8,128)S(1)} collective-permute-done((f32[16,128]{1,0:T(8,128)S(1)}, f32[16,128]{1,0:T(8,128)S(1)}, u32[]{:S(2)}, u32[]{:S(2)}) %collective-permute-start.7) | collective-permute-done | bytes 8224 | tf_op jit(solution)/shard_map/ppermute | solution.py:121
  28.9 5.1 %collective-permute-start.6 = (bf16[128,1024]{1,0:T(8,128)(2,1)S(1)}, bf16[128,1024]{1,0:T(8,128)(2,1)S(1)}, u32[]{:S(2)}, u32[]{:S(2)}) collective-permute-start(bf16[128,1024]{1,0:T(8,128)(2,1)S(1)} %get-tuple-element.32), channel_id=1, source_target_pairs={{0,12},{4,0},{8,4},{12,8},{1,13},{5,1},{9,5},{13,9},{2,14},{6,2},{... | collective-permute-start | bytes 786440 | tf_op jit(solution)/shard_map/ppermute | solution.py:121
  34.0 0.0 collective-permute-done.9.refs_3_
  34.0 3.8 %shard_map.57 = (bf16[128,1024]{1,0:T(8,128)(2,1)S(1)}, f32[128,1024]{1,0:T(8,128)S(1)}) custom-call(f32[16,128]{1,0:T(8,128)S(1)} %collective-permute-done.1.refs_1_.refs_0_, f32[16,128]{1,0:T(8,128)S(1)} %collective-permute-done.7.refs_1_.refs_0_, bf16[128,1024]{1,0:T(8,128)(2,1)S(1)} %get-tuple-element.33.refs_2_, ...), custom_call_target="tpu_custom_call" | custom-call | flops 2315255808 | bytes 12320768 | tf_op jit(solution)/shard_map/pallas_call | solution.py:103
  37.8 0.0 collective-permute-done.12.refs_4_
  37.8 0.2 collective-permute-start.14
  38.0 0.1 collective-permute-start.13
  38.2 3.8 %shard_map.58 = (bf16[128,1024]{1,0:T(8,128)(2,1)S(1)}, f32[128,1024]{1,0:T(8,128)S(1)}) custom-call(f32[16,128]{1,0:T(8,128)S(1)} %collective-permute-done.7.refs_1_.refs_0_, f32[16,128]{1,0:T(8,128)S(1)} %collective-permute-done.8.refs_1_.refs_0_, bf16[128,1024]{1,0:T(8,128)(2,1)S(1)} %get-tuple-element.39.refs_2_, ...), custom_call_target="tpu_custom_call" | custom-call | flops 2315255808 | bytes 12320768 | tf_op jit(solution)/shard_map/pallas_call | solution.py:103
  42.0 1.8 %collective-permute-start.16 = (bf16[128,1024]{1,0:T(8,128)(2,1)S(1)}, bf16[128,1024]{1,0:T(8,128)(2,1)S(1)}, u32[]{:S(2)}, u32[]{:S(2)}) collective-permute-start(bf16[128,1024]{1,0:T(8,128)(2,1)S(1)} %get-tuple-element.37.refs_1_), channel_id=1, source_target_pairs={{0,1},{1,0},{2,3},{3,2},{4,5},{5,4},{6,7},{7,6},{8,9},{9,8},{10,11... | collective-permute-start | bytes 786440 | tf_op jit(solution)/shard_map/ppermute | solution.py:121
  43.8 0.1 convert_add_fusion.refs_2_
  43.9 2.9 %collective-permute-done.14.refs_3_ = bf16[128,1024]{1,0:T(8,128)(2,1)S(1)} collective-permute-done((bf16[128,1024]{1,0:T(8,128)(2,1)S(1)}, bf16[128,1024]{1,0:T(8,128)(2,1)S(1)}, u32[]{:S(2)}, u32[]{:S(2)}) %collective-permute-start.14) | collective-permute-done | bytes 262176 | tf_op jit(solution)/shard_map/ppermute | solution.py:121
  46.8 3.3 %shard_map.59 = bf16[128,1024]{1,0:T(8,128)(2,1)S(1)} custom-call(f32[16,128]{1,0:T(8,128)S(1)} %collective-permute-done.8.refs_1_.refs_0_, bf16[128,1024]{1,0:T(8,128)(2,1)S(1)} %get-tuple-element.37.refs_1_, f32[128,1024]{1,0:T(8,128)S(1)} %convert_add_fusion.refs_2_, bf16[128,1024]{1,0:T(8,128)(2,1)S(1)} %collective-permute-done.14.refs_3_, ...), custom_call_target="tpu_custom_call" | custom-call | flops 1157627904 | bytes 11665408 | tf_op jit(solution)/shard_map/pallas_call | solution.py:103
  50.0 0.5 collective-permute-start.15
  50.5 0.1 add_convert_fusion.3
  50.6 0.3 collective-permute-done.16
  50.9 0.1 add_convert_fusion.2
  51.0 2.2 %collective-permute-start.19 = (bf16[128,1024]{1,0:T(8,128)(2,1)S(1)}, bf16[128,1024]{1,0:T(8,128)(2,1)S(1)}, u32[]{:S(2)}, u32[]{:S(2)}) collective-permute-start(bf16[128,1024]{1,0:T(8,128)(2,1)S(1)} %add_convert_fusion.2), channel_id=1, source_target_pairs={{0,8},{4,12},{8,0},{12,4},{1,9},{5,13},{9,1},{13,5},{2,10},{6,14},... | collective-permute-start | bytes 786440 | tf_op jit(solution)/shard_map/ppermute | solution.py:121
  53.2 5.7 %collective-permute-done.15 = bf16[128,1024]{1,0:T(8,128)(2,1)S(1)} collective-permute-done((bf16[128,1024]{1,0:T(8,128)(2,1)S(1)}, bf16[128,1024]{1,0:T(8,128)(2,1)S(1)}, u32[]{:S(2)}, u32[]{:S(2)}) %collective-permute-start.15) | collective-permute-done | bytes 262176 | tf_op jit(solution)/shard_map/ppermute | solution.py:121
  58.9 0.1 add_convert_fusion.1
  58.9 1.3 %collective-permute-start.18 = (bf16[128,1024]{1,0:T(8,128)(2,1)S(1)}, bf16[128,1024]{1,0:T(8,128)(2,1)S(1)}, u32[]{:S(2)}, u32[]{:S(2)}) collective-permute-start(bf16[128,1024]{1,0:T(8,128)(2,1)S(1)} %add_convert_fusion.1), channel_id=1, source_target_pairs={{0,4},{4,8},{8,12},{12,0},{1,5},{5,9},{9,13},{13,1},{2,6},{6,10},{... | collective-permute-start | bytes 786440 | tf_op jit(solution)/shard_map/ppermute | solution.py:121
  60.3 0.3 collective-permute-start.17
  60.6 1.9 %collective-permute-done.19 = bf16[128,1024]{1,0:T(8,128)(2,1)S(1)} collective-permute-done((bf16[128,1024]{1,0:T(8,128)(2,1)S(1)}, bf16[128,1024]{1,0:T(8,128)(2,1)S(1)}, u32[]{:S(2)}, u32[]{:S(2)}) %collective-permute-start.19) | collective-permute-done | bytes 262176 | tf_op jit(solution)/shard_map/ppermute | solution.py:121
  62.5 4.7 %collective-permute-done.18 = bf16[128,1024]{1,0:T(8,128)(2,1)S(1)} collective-permute-done((bf16[128,1024]{1,0:T(8,128)(2,1)S(1)}, bf16[128,1024]{1,0:T(8,128)(2,1)S(1)}, u32[]{:S(2)}, u32[]{:S(2)}) %collective-permute-start.18) | collective-permute-done | bytes 262176 | tf_op jit(solution)/shard_map/ppermute | solution.py:121
  67.2 0.9 %add_convert_fusion = bf16[128,1024]{1,0:T(8,128)(2,1)} fusion(bf16[128,1024]{1,0:T(8,128)(2,1)S(1)} %collective-permute-done.18, bf16[128,1024]{1,0:T(8,128)(2,1)S(1)} %collective-permute-done.19, f32[128,1024]{1,0:T(8,128)S(1)} %convert_add_fusion.refs_2_, bf16[128,1024]{1,0:T(8,128)(2,1)S(1)} %collective-permute-done.17), kind=kLoop, calls=%fused_computation | loop fusion | flops 917504 | bytes 1572864 | tf_op jit(solution)/shard_map/convert_element_type | solution.py:209
  (10 shorter events, 0.0 us)
Async XLA Ops:
  0.0 18.8 %collective-permute-start.4 = (bf16[1,1344,1024]{2,1,0:T(8,128)(2,1)}, bf16[1,1344,1024]{2,1,0:T(8,128)(2,1)S(1)}, u32[]{:S(2)}, u32[]{:S(2)}) collective-permute-start(bf16[1,1344,1024]{2,1,0:T(8,128)(2,1)} %bitcast.4), channel_id=1, source_target_pairs={{0,2},{2,0},{1,3},{3,1},{4,6},{6,4},{5,7},{7,5},{8,10},{10,8},{9,1... | collective-permute-start | bytes 8257544 | tf_op jit(solution)/shard_map/ppermute | solution.py:121
  0.5 18.3 %collective-permute-start.5 = (bf16[1,1344,1024]{2,1,0:T(8,128)(2,1)}, bf16[1,1344,1024]{2,1,0:T(8,128)(2,1)S(1)}, u32[]{:S(2)}, u32[]{:S(2)}) collective-permute-start(bf16[1,1344,1024]{2,1,0:T(8,128)(2,1)} %bitcast.6), channel_id=1, source_target_pairs={{0,2},{2,0},{1,3},{3,1},{4,6},{6,4},{5,7},{7,5},{8,10},{10,8},{9,1... | collective-permute-start | bytes 8257544 | tf_op jit(solution)/shard_map/ppermute | solution.py:121
  0.5 12.8 %collective-permute-start.3 = (bf16[128,1024]{1,0:T(8,128)(2,1)}, bf16[128,1024]{1,0:T(8,128)(2,1)S(1)}, u32[]{:S(2)}, u32[]{:S(2)}) collective-permute-start(bf16[128,1024]{1,0:T(8,128)(2,1)} %refs_3_.1), channel_id=1, source_target_pairs={{0,4},{4,8},{8,12},{12,0},{1,5},{5,9},{9,13},{13,1},{2,6},{6,10},{... | collective-permute-start | bytes 786440 | tf_op jit(solution)/shard_map/ppermute | solution.py:121
  3.5 15.2 %collective-permute-start.2 = (bf16[128,1024]{1,0:T(8,128)(2,1)}, bf16[128,1024]{1,0:T(8,128)(2,1)S(1)}, u32[]{:S(2)}, u32[]{:S(2)}) collective-permute-start(bf16[128,1024]{1,0:T(8,128)(2,1)} %refs_3_.1), channel_id=1, source_target_pairs={{0,1},{1,0},{2,3},{3,2},{4,5},{5,4},{6,7},{7,6},{8,9},{9,8},{10,11... | collective-permute-start | bytes 786440 | tf_op jit(solution)/shard_map/ppermute | solution.py:121
  5.7 6.0 %collective-permute-start = (f32[8,128]{1,0:T(8,128)S(1)}, f32[8,128]{1,0:T(8,128)S(1)}, u32[]{:S(2)}, u32[]{:S(2)}) collective-permute-start(f32[8,128]{1,0:T(8,128)S(1)} %select_reduce_fusion), channel_id=1, source_target_pairs={{0,1},{1,0},{2,3},{3,2},{4,5},{5,4},{6,7},{7,6},{8,9},{9,8},{10,11... | collective-permute-start | bytes 12296 | tf_op jit(solution)/shard_map/ppermute | solution.py:121
  6.3 1.8 %copy-start = (bf16[1,1024,1344]{1,2,0:T(8,128)(2,1)S(1)}, bf16[1,1024,1344]{1,2,0:T(8,128)(2,1)}, u32[]{:S(2)}) copy-start(bf16[1,1024,1344]{1,2,0:T(8,128)(2,1)} %param.8) | copy-start | bytes 8257540
  8.0 1.8 %copy-start.1 = (bf16[1,1024,1344]{1,2,0:T(8,128)(2,1)S(1)}, bf16[1,1024,1344]{1,2,0:T(8,128)(2,1)}, u32[]{:S(2)}) copy-start(bf16[1,1024,1344]{1,2,0:T(8,128)(2,1)} %param.9) | copy-start | bytes 8257540
  9.8 9.0 %copy-start.2 = (bf16[128,1024]{1,0:T(8,128)(2,1)S(1)}, bf16[128,1024]{1,0:T(8,128)(2,1)}, u32[]{:S(2)}) copy-start(bf16[128,1024]{1,0:T(8,128)(2,1)} %refs_3_.1) | copy-start | bytes 786436
  11.8 5.5 %collective-permute-start.1 = (f32[16,128]{1,0:T(8,128)S(1)}, f32[16,128]{1,0:T(8,128)S(1)}, u32[]{:S(2)}, u32[]{:S(2)}) collective-permute-start(f32[16,128]{1,0:T(8,128)S(1)} %pad_maximum_fusion.refs_0_), channel_id=1, source_target_pairs={{0,4},{4,8},{8,12},{12,0},{1,5},{5,9},{9,13},{13,1},{2,6},{6,10},{... | collective-permute-start | bytes 24584 | tf_op jit(solution)/shard_map/ppermute | solution.py:121
  13.4 10.3 %collective-permute-start.10 = (bf16[128,1024]{1,0:T(8,128)(2,1)S(1)}, bf16[128,1024]{1,0:T(8,128)(2,1)S(1)}, u32[]{:S(2)}, u32[]{:S(2)}) collective-permute-start(bf16[128,1024]{1,0:T(8,128)(2,1)S(1)} %collective-permute-done.3.refs_4_), channel_id=1, source_target_pairs={{0,4},{4,8},{8,12},{12,0},{1,5},{5,9},{9,13},{13,1},{2,6},{6,10},{... | collective-permute-start | bytes 786440 | tf_op jit(solution)/shard_map/ppermute | solution.py:121
  17.3 16.7 %collective-permute-start.9 = (bf16[128,1024]{1,0:T(8,128)(2,1)S(1)}, bf16[128,1024]{1,0:T(8,128)(2,1)S(1)}, u32[]{:S(2)}, u32[]{:S(2)}) collective-permute-start(bf16[128,1024]{1,0:T(8,128)(2,1)S(1)} %collective-permute-done.3.refs_4_), channel_id=1, source_target_pairs={{0,1},{1,0},{2,3},{3,2},{4,5},{5,4},{6,7},{7,6},{8,9},{9,8},{10,11... | collective-permute-start | bytes 786440 | tf_op jit(solution)/shard_map/ppermute | solution.py:121
  23.7 14.1 %collective-permute-start.12 = (bf16[128,1024]{1,0:T(8,128)(2,1)S(1)}, bf16[128,1024]{1,0:T(8,128)(2,1)S(1)}, u32[]{:S(2)}, u32[]{:S(2)}) collective-permute-start(bf16[128,1024]{1,0:T(8,128)(2,1)S(1)} %collective-permute-done.10.refs_4_), channel_id=1, source_target_pairs={{0,4},{4,8},{8,12},{12,0},{1,5},{5,9},{9,13},{13,1},{2,6},{6,10},{... | collective-permute-start | bytes 786440 | tf_op jit(solution)/shard_map/ppermute | solution.py:121
  23.7 14.4 %collective-permute-start.11 = (bf16[128,1024]{1,0:T(8,128)(2,1)S(1)}, bf16[128,1024]{1,0:T(8,128)(2,1)S(1)}, u32[]{:S(2)}, u32[]{:S(2)}) collective-permute-start(bf16[128,1024]{1,0:T(8,128)(2,1)S(1)} %collective-permute-done.10.refs_4_), channel_id=1, source_target_pairs={{0,1},{1,0},{2,3},{3,2},{4,5},{5,4},{6,7},{7,6},{8,9},{9,8},{10,11... | collective-permute-start | bytes 786440 | tf_op jit(solution)/shard_map/ppermute | solution.py:121
  24.3 4.5 %collective-permute-start.7 = (f32[16,128]{1,0:T(8,128)S(1)}, f32[16,128]{1,0:T(8,128)S(1)}, u32[]{:S(2)}, u32[]{:S(2)}) collective-permute-start(f32[16,128]{1,0:T(8,128)S(1)} %pad_maximum_fusion.refs_0_), channel_id=1, source_target_pairs={{0,8},{4,12},{8,0},{12,4},{1,9},{5,13},{9,1},{13,5},{2,10},{6,14},... | collective-permute-start | bytes 24584 | tf_op jit(solution)/shard_map/ppermute | solution.py:121
  25.4 12.8 %collective-permute-start.8 = (f32[16,128]{1,0:T(8,128)S(1)}, f32[16,128]{1,0:T(8,128)S(1)}, u32[]{:S(2)}, u32[]{:S(2)}) collective-permute-start(f32[16,128]{1,0:T(8,128)S(1)} %pad_maximum_fusion.refs_0_), channel_id=1, source_target_pairs={{0,12},{4,0},{8,4},{12,8},{1,13},{5,1},{9,5},{13,9},{2,14},{6,2},{... | collective-permute-start | bytes 24584 | tf_op jit(solution)/shard_map/ppermute | solution.py:121
  28.9 14.9 %collective-permute-start.6 = (bf16[128,1024]{1,0:T(8,128)(2,1)S(1)}, bf16[128,1024]{1,0:T(8,128)(2,1)S(1)}, u32[]{:S(2)}, u32[]{:S(2)}) collective-permute-start(bf16[128,1024]{1,0:T(8,128)(2,1)S(1)} %get-tuple-element.32), channel_id=1, source_target_pairs={{0,12},{4,0},{8,4},{12,8},{1,13},{5,1},{9,5},{13,9},{2,14},{6,2},{... | collective-permute-start | bytes 786440 | tf_op jit(solution)/shard_map/ppermute | solution.py:121
  37.8 9.0 %collective-permute-start.14 = (bf16[128,1024]{1,0:T(8,128)(2,1)S(1)}, bf16[128,1024]{1,0:T(8,128)(2,1)S(1)}, u32[]{:S(2)}, u32[]{:S(2)}) collective-permute-start(bf16[128,1024]{1,0:T(8,128)(2,1)S(1)} %collective-permute-done.12.refs_4_), channel_id=1, source_target_pairs={{0,1},{1,0},{2,3},{3,2},{4,5},{5,4},{6,7},{7,6},{8,9},{9,8},{10,11... | collective-permute-start | bytes 786440 | tf_op jit(solution)/shard_map/ppermute | solution.py:121
  38.0 12.5 %collective-permute-start.13 = (bf16[128,1024]{1,0:T(8,128)(2,1)S(1)}, bf16[128,1024]{1,0:T(8,128)(2,1)S(1)}, u32[]{:S(2)}, u32[]{:S(2)}) collective-permute-start(bf16[128,1024]{1,0:T(8,128)(2,1)S(1)} %get-tuple-element.39.refs_2_), channel_id=1, source_target_pairs={{0,12},{4,0},{8,4},{12,8},{1,13},{5,1},{9,5},{13,9},{2,14},{6,2},{... | collective-permute-start | bytes 786440 | tf_op jit(solution)/shard_map/ppermute | solution.py:121
  42.0 8.9 %collective-permute-start.16 = (bf16[128,1024]{1,0:T(8,128)(2,1)S(1)}, bf16[128,1024]{1,0:T(8,128)(2,1)S(1)}, u32[]{:S(2)}, u32[]{:S(2)}) collective-permute-start(bf16[128,1024]{1,0:T(8,128)(2,1)S(1)} %get-tuple-element.37.refs_1_), channel_id=1, source_target_pairs={{0,1},{1,0},{2,3},{3,2},{4,5},{5,4},{6,7},{7,6},{8,9},{9,8},{10,11... | collective-permute-start | bytes 786440 | tf_op jit(solution)/shard_map/ppermute | solution.py:121
  50.0 8.8 %collective-permute-start.15 = (bf16[128,1024]{1,0:T(8,128)(2,1)S(1)}, bf16[128,1024]{1,0:T(8,128)(2,1)S(1)}, u32[]{:S(2)}, u32[]{:S(2)}) collective-permute-start(bf16[128,1024]{1,0:T(8,128)(2,1)S(1)} %shard_map.59), channel_id=1, source_target_pairs={{0,1},{1,0},{2,3},{3,2},{4,5},{5,4},{6,7},{7,6},{8,9},{9,8},{10,11... | collective-permute-start | bytes 786440 | tf_op jit(solution)/shard_map/ppermute | solution.py:121
  51.0 11.5 %collective-permute-start.19 = (bf16[128,1024]{1,0:T(8,128)(2,1)S(1)}, bf16[128,1024]{1,0:T(8,128)(2,1)S(1)}, u32[]{:S(2)}, u32[]{:S(2)}) collective-permute-start(bf16[128,1024]{1,0:T(8,128)(2,1)S(1)} %add_convert_fusion.2), channel_id=1, source_target_pairs={{0,8},{4,12},{8,0},{12,4},{1,9},{5,13},{9,1},{13,5},{2,10},{6,14},... | collective-permute-start | bytes 786440 | tf_op jit(solution)/shard_map/ppermute | solution.py:121
  58.9 8.2 %collective-permute-start.18 = (bf16[128,1024]{1,0:T(8,128)(2,1)S(1)}, bf16[128,1024]{1,0:T(8,128)(2,1)S(1)}, u32[]{:S(2)}, u32[]{:S(2)}) collective-permute-start(bf16[128,1024]{1,0:T(8,128)(2,1)S(1)} %add_convert_fusion.1), channel_id=1, source_target_pairs={{0,4},{4,8},{8,12},{12,0},{1,5},{5,9},{9,13},{13,1},{2,6},{6,10},{... | collective-permute-start | bytes 786440 | tf_op jit(solution)/shard_map/ppermute | solution.py:121
  60.3 6.9 %collective-permute-start.17 = (bf16[128,1024]{1,0:T(8,128)(2,1)S(1)}, bf16[128,1024]{1,0:T(8,128)(2,1)S(1)}, u32[]{:S(2)}, u32[]{:S(2)}) collective-permute-start(bf16[128,1024]{1,0:T(8,128)(2,1)S(1)} %add_convert_fusion.3), channel_id=1, source_target_pairs={{0,1},{1,0},{2,3},{3,2},{4,5},{5,4},{6,7},{7,6},{8,9},{9,8},{10,11... | collective-permute-start | bytes 786440 | tf_op jit(solution)/shard_map/ppermute | solution.py:121

commit v13 on v12

--- a/solution.py
+++ b/solution.py
@@ -164,9 +164,7 @@
         kinds += [jnp.bfloat16 if r == 1 else jnp.float32 for r in fresh]
         after = firsts[-1:]
         if j == last and j > 1:
-            rows = follow(shift(kept[1], "z", -1), firsts[-1])
-            home = kept[0] + rows.astype(jnp.float32)
-            after = after + [home]
+            home = kept[0] + shift(follow(kept[1], ring[last]), "z", -1).astype(jnp.float32)
         if j > 3:
             totals[j - 2] = total(j - 2, firsts[-1]).astype(jnp.bfloat16)
             after = after + [totals[j - 2]]
@@ -192,7 +190,7 @@
         ]
     for r in range(2, depth):
         if r not in totals:
-            behind = [firsts[-1]] + (joined if r < last else [totals[r - 1]] * (r > 2))
+            behind = [firsts[-1]] + ([home, *joined] if r < last else [totals[r - 1]] * (r > 2))
             totals[r] = total(r, *behind).astype(jnp.bfloat16)
     came = []
     for r in range(2, depth):

time: 68.2 us -> 67.9 us (level)
  starting transfers between devices: 26.1 us -> 24.3 us
  waiting for transfers between devices: 19.9 us -> 21.4 us
    ppermute x20, starting transfers between devices: 26.1 us -> 24.3 us  [shift(): lax.ppermute(array, axis, [(i, (i + step) % size) for i in range(size)])]
    ppermute x20, waiting for transfers between devices: 19.9 us -> 21.4 us  [shift(): lax.ppermute(array, axis, [(i, (i + step) % size) for i in range(size)])]
where the time goes in v13:
time: 67.9 us; the launch traced here: 67.7 us
  starting transfers between devices  24.3 us (36%)
  waiting for transfers between devices  21.4 us (32%)
  Pallas kernels  16.5 us (24%)
  local copies, waits for them, and re-layouts  3.56 us (5%)
  other arithmetic  1.84 us (3%)
    ppermute x20, starting transfers between devices, shift(): lax.ppermute(array, axis, [(i, (i + step) % size) for i in range(size)])  24.3 us
    ppermute x20, waiting for transfers between devices, shift(): lax.ppermute(array, axis, [(i, (i + step) % size) for i in range(size)])  21.4 us
    pallas_call x4, Pallas kernels, run_experts(): pl.pallas_call(functools.partial(expert_kernel, block, slots, unit, numbe...  15.8 us
    unnamed x6, local copies, waits for them, and re-layouts  3.56 us
  transfers between devices with their start and end apart: 20, of which 8 were waited for; matrix products, arithmetic and copies ran while one was open for 1% of the time, Pallas kernels for 24%

profile of v13, /device:TPU:0, one launch (start us, length us, event | category | flops | bytes accessed | tf_op | source)
XLA Modules:
  0.0 67.7 jit_solution(2987186543098317334)
XLA Ops:
  0.0 0.5 collective-permute-start.4
  0.5 0.1 collective-permute-start.5
  0.5 3.0 %collective-permute-start.3 = (bf16[128,1024]{1,0:T(8,128)(2,1)}, bf16[128,1024]{1,0:T(8,128)(2,1)S(1)}, u32[]{:S(2)}, u32[]{:S(2)}) collective-permute-start(bf16[128,1024]{1,0:T(8,128)(2,1)} %refs_3_.1), channel_id=1, source_target_pairs={{0,4},{4,8},{8,12},{12,0},{1,5},{5,9},{9,13},{13,1},{2,6},{6,10},{... | collective-permute-start | bytes 786440 | tf_op jit(solution)/shard_map/ppermute | solution.py:121
  3.5 1.5 %collective-permute-start.2 = (bf16[128,1024]{1,0:T(8,128)(2,1)}, bf16[128,1024]{1,0:T(8,128)(2,1)S(1)}, u32[]{:S(2)}, u32[]{:S(2)}) collective-permute-start(bf16[128,1024]{1,0:T(8,128)(2,1)} %refs_3_.1), channel_id=1, source_target_pairs={{0,1},{1,0},{2,3},{3,2},{4,5},{5,4},{6,7},{7,6},{8,9},{9,8},{10,11... | collective-permute-start | bytes 786440 | tf_op jit(solution)/shard_map/ppermute | solution.py:121
  5.0 0.7 %select_reduce_fusion = f32[8,128]{1,0:T(8,128)S(1)} fusion(f32[4,128]{1,0:T(4,128)} %bitcast.8, s32[4,128]{1,0:T(4,128)} %bitcast.9), kind=kLoop, calls=%fused_computation.5 | loop fusion | flops 11264 | bytes 8192 | tf_op jit(solution)/shard_map/reduce_sum | solution.py:140
  5.7 0.5 collective-permute-start
  6.3 1.8 %copy-done = bf16[1,1024,1344]{1,2,0:T(8,128)(2,1)S(1)} copy-done((bf16[1,1024,1344]{1,2,0:T(8,128)(2,1)S(1)}, bf16[1,1024,1344]{1,2,0:T(8,128)(2,1)}, u32[]{:S(2)}) %copy-start) | copy-done | bytes 2752536
  8.1 1.8 %copy-done.1 = bf16[1,1024,1344]{1,2,0:T(8,128)(2,1)S(1)} copy-done((bf16[1,1024,1344]{1,2,0:T(8,128)(2,1)S(1)}, bf16[1,1024,1344]{1,2,0:T(8,128)(2,1)}, u32[]{:S(2)}) %copy-start.1) | copy-done | bytes 2752536
  9.8 0.7 %shard_map.55 = (bf16[1,1344,1024]{2,1,0:T(8,128)(2,1)S(1)}, bf16[1,1344,1024]{2,1,0:T(8,128)(2,1)S(1)}) custom-call(bf16[1,1344,1024]{2,1,0:T(8,128)(2,1)S(1)} %bitcast.5, bf16[1,1344,1024]{2,1,0:T(8,128)(2,1)S(1)} %bitcast.7), custom_call_target="tpu_custom_call" | custom-call | tf_op jit(solution)/shard_map/pallas_call | solution.py:28
  10.5 1.2 %collective-permute-done = f32[8,128]{1,0:T(8,128)S(1)} collective-permute-done((f32[8,128]{1,0:T(8,128)S(1)}, f32[8,128]{1,0:T(8,128)S(1)}, u32[]{:S(2)}, u32[]{:S(2)}) %collective-permute-start) | collective-permute-done | bytes 4128 | tf_op jit(solution)/shard_map/ppermute | solution.py:121
  11.8 1.6 %collective-permute-start.1 = (f32[16,128]{1,0:T(8,128)S(1)}, f32[16,128]{1,0:T(8,128)S(1)}, u32[]{:S(2)}, u32[]{:S(2)}) collective-permute-start(f32[16,128]{1,0:T(8,128)S(1)} %pad_maximum_fusion.refs_0_), channel_id=1, source_target_pairs={{0,4},{4,8},{8,12},{12,0},{1,5},{5,9},{9,13},{13,1},{2,6},{6,10},{... | collective-permute-start | bytes 24584 | tf_op jit(solution)/shard_map/ppermute | solution.py:121
  13.3 0.0 collective-permute-done.3.refs_4_
  13.4 1.5 %collective-permute-start.9 = (bf16[128,1024]{1,0:T(8,128)(2,1)S(1)}, bf16[128,1024]{1,0:T(8,128)(2,1)S(1)}, u32[]{:S(2)}, u32[]{:S(2)}) collective-permute-start(bf16[128,1024]{1,0:T(8,128)(2,1)S(1)} %collective-permute-done.3.refs_4_), channel_id=1, source_target_pairs={{0,1},{1,0},{2,3},{3,2},{4,5},{5,4},{6,7},{7,6},{8,9},{9,8},{10,11... | collective-permute-start | bytes 786440 | tf_op jit(solution)/shard_map/ppermute | solution.py:121
  14.8 2.4 %collective-permute-done.1.refs_1_.refs_0_ = f32[16,128]{1,0:T(8,128)S(1)} collective-permute-done((f32[16,128]{1,0:T(8,128)S(1)}, f32[16,128]{1,0:T(8,128)S(1)}, u32[]{:S(2)}, u32[]{:S(2)}) %collective-permute-start.1) | collective-permute-done | bytes 8224 | tf_op jit(solution)/shard_map/ppermute | solution.py:121
  17.2 0.0 collective-permute-start.6
  17.2 0.0 collective-permute-done.2.refs_2_
  17.2 0.0 collective-permute-done.4.refs_7_.refs_5_
  17.2 0.0 collective-permute-done.5.refs_8_.refs_6_
  17.3 4.9 %shard_map.56 = (bf16[128,1024]{1,0:T(8,128)(2,1)S(1)}, f32[128,1024]{1,0:T(8,128)S(1)}, bf16[128,1024]{1,0:T(8,128)(2,1)S(1)}) custom-call(f32[16,128]{1,0:T(8,128)S(1)} %pad_maximum_fusion.refs_0_, f32[16,128]{1,0:T(8,128)S(1)} %collective-permute-done.1.refs_1_.refs_0_, bf16[128,1024]{1,0:T(8,128)(2,1)S(1)} %collective-permute-done.2.refs_2_, ...), custom_call_target="tpu_custom_call" | custom-call | flops 3472883712 | bytes 12976128 | tf_op jit(solution)/shard_map/pallas_call | solution.py:103
  22.1 3.3 %collective-permute-done.6.refs_4_ = bf16[128,1024]{1,0:T(8,128)(2,1)S(1)} collective-permute-done((bf16[128,1024]{1,0:T(8,128)(2,1)S(1)}, bf16[128,1024]{1,0:T(8,128)(2,1)S(1)}, u32[]{:S(2)}, u32[]{:S(2)}) %collective-permute-start.6) | collective-permute-done | bytes 262176 | tf_op jit(solution)/shard_map/ppermute | solution.py:121
  25.4 1.2 %collective-permute-start.8 = (f32[16,128]{1,0:T(8,128)S(1)}, f32[16,128]{1,0:T(8,128)S(1)}, u32[]{:S(2)}, u32[]{:S(2)}) collective-permute-start(f32[16,128]{1,0:T(8,128)S(1)} %pad_maximum_fusion.refs_0_), channel_id=1, source_target_pairs={{0,8},{4,12},{8,0},{12,4},{1,9},{5,13},{9,1},{13,5},{2,10},{6,14},... | collective-permute-start | bytes 24584 | tf_op jit(solution)/shard_map/ppermute | solution.py:121
  26.6 1.5 %collective-permute-start.13 = (bf16[128,1024]{1,0:T(8,128)(2,1)S(1)}, bf16[128,1024]{1,0:T(8,128)(2,1)S(1)}, u32[]{:S(2)}, u32[]{:S(2)}) collective-permute-start(bf16[128,1024]{1,0:T(8,128)(2,1)S(1)} %collective-permute-done.6.refs_4_), channel_id=1, source_target_pairs={{0,1},{1,0},{2,3},{3,2},{4,5},{5,4},{6,7},{7,6},{8,9},{9,8},{10,11... | collective-permute-start | bytes 786440 | tf_op jit(solution)/shard_map/ppermute | solution.py:121
  28.1 1.9 %collective-permute-done.8.refs_1_.refs_0_ = f32[16,128]{1,0:T(8,128)S(1)} collective-permute-done((f32[16,128]{1,0:T(8,128)S(1)}, f32[16,128]{1,0:T(8,128)S(1)}, u32[]{:S(2)}, u32[]{:S(2)}) %collective-permute-start.8) | collective-permute-done | bytes 8224 | tf_op jit(solution)/shard_map/ppermute | solution.py:121
  29.9 0.0 collective-permute-done.9.refs_3_
  29.9 3.8 %shard_map.57 = (bf16[128,1024]{1,0:T(8,128)(2,1)S(1)}, f32[128,1024]{1,0:T(8,128)S(1)}) custom-call(f32[16,128]{1,0:T(8,128)S(1)} %collective-permute-done.1.refs_1_.refs_0_, f32[16,128]{1,0:T(8,128)S(1)} %collective-permute-done.8.refs_1_.refs_0_, bf16[128,1024]{1,0:T(8,128)(2,1)S(1)} %get-tuple-element.34.refs_2_, ...), custom_call_target="tpu_custom_call" | custom-call | flops 2315255808 | bytes 12320768 | tf_op jit(solution)/shard_map/pallas_call | solution.py:103
  33.8 0.0 collective-permute-done.7.refs_4_
  33.8 1.6 %collective-permute-start.14 = (bf16[128,1024]{1,0:T(8,128)(2,1)S(1)}, bf16[128,1024]{1,0:T(8,128)(2,1)S(1)}, u32[]{:S(2)}, u32[]{:S(2)}) collective-permute-start(bf16[128,1024]{1,0:T(8,128)(2,1)S(1)} %collective-permute-done.7.refs_4_), channel_id=1, source_target_pairs={{0,1},{1,0},{2,3},{3,2},{4,5},{5,4},{6,7},{7,6},{8,9},{9,8},{10,11... | collective-permute-start | bytes 786440 | tf_op jit(solution)/shard_map/ppermute | solution.py:121
  35.3 3.8 %collective-permute-start.12 = (f32[16,128]{1,0:T(8,128)S(1)}, f32[16,128]{1,0:T(8,128)S(1)}, u32[]{:S(2)}, u32[]{:S(2)}) collective-permute-start(f32[16,128]{1,0:T(8,128)S(1)} %pad_maximum_fusion.refs_0_), channel_id=1, source_target_pairs={{0,12},{4,0},{8,4},{12,8},{1,13},{5,1},{9,5},{13,9},{2,14},{6,2},{... | collective-permute-start | bytes 24584 | tf_op jit(solution)/shard_map/ppermute | solution.py:121
  39.2 0.5 collective-permute-start.11
  39.6 2.9 %collective-permute-start.10 = (bf16[128,1024]{1,0:T(8,128)(2,1)S(1)}, bf16[128,1024]{1,0:T(8,128)(2,1)S(1)}, u32[]{:S(2)}, u32[]{:S(2)}) collective-permute-start(bf16[128,1024]{1,0:T(8,128)(2,1)S(1)} %get-tuple-element.38), channel_id=1, source_target_pairs={{0,12},{4,0},{8,4},{12,8},{1,13},{5,1},{9,5},{13,9},{2,14},{6,2},{... | collective-permute-start | bytes 786440 | tf_op jit(solution)/shard_map/ppermute | solution.py:121
  42.5 0.0 collective-permute-done.12.refs_1_.refs_0_
  42.5 0.0 collective-permute-done.13.refs_3_
  42.5 3.8 %shard_map.58 = (bf16[128,1024]{1,0:T(8,128)(2,1)S(1)}, f32[128,1024]{1,0:T(8,128)S(1)}) custom-call(f32[16,128]{1,0:T(8,128)S(1)} %collective-permute-done.8.refs_1_.refs_0_, f32[16,128]{1,0:T(8,128)S(1)} %collective-permute-done.12.refs_1_.refs_0_, bf16[128,1024]{1,0:T(8,128)(2,1)S(1)} %get-tuple-element.39.refs_2_, ...), custom_call_target="tpu_custom_call" | custom-call | flops 2315255808 | bytes 12320768 | tf_op jit(solution)/shard_map/pallas_call | solution.py:103
  46.4 0.6 collective-permute-start.16
  47.0 3.3 %shard_map.59 = bf16[128,1024]{1,0:T(8,128)(2,1)S(1)} custom-call(f32[16,128]{1,0:T(8,128)S(1)} %collective-permute-done.12.refs_1_.refs_0_, bf16[128,1024]{1,0:T(8,128)(2,1)S(1)} %get-tuple-element.41.refs_1_, bf16[128,1024]{1,0:T(8,128)(2,1)S(1)} %collective-permute-done.14.refs_2_, bf16[1,1344,1024]{2,1,0:T(8,128)(2,1)S(1)} %get-tuple-element.28.refs_5_.refs_3_, ...), custom_call_target="tpu_custom_call" | custom-call | flops 1157627904 | bytes 11665408 | tf_op jit(solution)/shard_map/pallas_call | solution.py:103
  50.2 1.6 %collective-permute-start.15 = (bf16[128,1024]{1,0:T(8,128)(2,1)S(1)}, bf16[128,1024]{1,0:T(8,128)(2,1)S(1)}, u32[]{:S(2)}, u32[]{:S(2)}) collective-permute-start(bf16[128,1024]{1,0:T(8,128)(2,1)S(1)} %shard_map.59), channel_id=1, source_target_pairs={{0,1},{1,0},{2,3},{3,2},{4,5},{5,4},{6,7},{7,6},{8,9},{9,8},{10,11... | collective-permute-start | bytes 786440 | tf_op jit(solution)/shard_map/ppermute | solution.py:121
  51.8 0.1 add_convert_fusion.3
  52.0 0.9 %collective-permute-done.16 = bf16[128,1024]{1,0:T(8,128)(2,1)S(1)} collective-permute-done((bf16[128,1024]{1,0:T(8,128)(2,1)S(1)}, bf16[128,1024]{1,0:T(8,128)(2,1)S(1)}, u32[]{:S(2)}, u32[]{:S(2)}) %collective-permute-start.16) | collective-permute-done | bytes 262176 | tf_op jit(solution)/shard_map/ppermute | solution.py:121
  52.8 0.1 add_convert_fusion.2
  52.9 0.2 collective-permute-start.19
  53.1 5.5 %collective-permute-done.15 = bf16[128,1024]{1,0:T(8,128)(2,1)S(1)} collective-permute-done((bf16[128,1024]{1,0:T(8,128)(2,1)S(1)}, bf16[128,1024]{1,0:T(8,128)(2,1)S(1)}, u32[]{:S(2)}, u32[]{:S(2)}) %collective-permute-start.15) | collective-permute-done | bytes 262176 | tf_op jit(solution)/shard_map/ppermute | solution.py:121
  58.5 0.1 add_convert_fusion.1
  58.6 0.7 collective-permute-start.18
  59.3 1.3 %collective-permute-start.17 = (bf16[128,1024]{1,0:T(8,128)(2,1)S(1)}, bf16[128,1024]{1,0:T(8,128)(2,1)S(1)}, u32[]{:S(2)}, u32[]{:S(2)}) collective-permute-start(bf16[128,1024]{1,0:T(8,128)(2,1)S(1)} %get-tuple-element.48), channel_id=1, source_target_pairs={{0,1},{1,0},{2,3},{3,2},{4,5},{5,4},{6,7},{7,6},{8,9},{9,8},{10,11... | collective-permute-start | bytes 786440 | tf_op jit(solution)/shard_map/ppermute | solution.py:121
  60.5 3.4 %collective-permute-done.19 = bf16[128,1024]{1,0:T(8,128)(2,1)S(1)} collective-permute-done((bf16[128,1024]{1,0:T(8,128)(2,1)S(1)}, bf16[128,1024]{1,0:T(8,128)(2,1)S(1)}, u32[]{:S(2)}, u32[]{:S(2)}) %collective-permute-start.19) | collective-permute-done | bytes 262176 | tf_op jit(solution)/shard_map/ppermute | solution.py:121
  63.9 2.9 %collective-permute-done.18 = bf16[128,1024]{1,0:T(8,128)(2,1)S(1)} collective-permute-done((bf16[128,1024]{1,0:T(8,128)(2,1)S(1)}, bf16[128,1024]{1,0:T(8,128)(2,1)S(1)}, u32[]{:S(2)}, u32[]{:S(2)}) %collective-permute-start.18) | collective-permute-done | bytes 262176 | tf_op jit(solution)/shard_map/ppermute | solution.py:121
  66.8 0.0 collective-permute-done.17
  66.8 0.9 %add_convert_fusion = bf16[128,1024]{1,0:T(8,128)(2,1)} fusion(bf16[128,1024]{1,0:T(8,128)(2,1)S(1)} %collective-permute-done.18, bf16[128,1024]{1,0:T(8,128)(2,1)S(1)} %collective-permute-done.19, f32[128,1024]{1,0:T(8,128)S(1)} %get-tuple-element.52, bf16[128,1024]{1,0:T(8,128)(2,1)S(1)} %collective-permute-done.17), kind=kLoop, calls=%fused_computation | loop fusion | flops 917504 | bytes 1572864 | tf_op jit(solution)/shard_map/convert_element_type | solution.py:207
  (9 shorter events, 0.0 us)
Async XLA Ops:
  0.0 17.2 %collective-permute-start.4 = (bf16[1,1344,1024]{2,1,0:T(8,128)(2,1)}, bf16[1,1344,1024]{2,1,0:T(8,128)(2,1)S(1)}, u32[]{:S(2)}, u32[]{:S(2)}) collective-permute-start(bf16[1,1344,1024]{2,1,0:T(8,128)(2,1)} %bitcast.4), channel_id=1, source_target_pairs={{0,2},{2,0},{1,3},{3,1},{4,6},{6,4},{5,7},{7,5},{8,10},{10,8},{9,1... | collective-permute-start | bytes 8257544 | tf_op jit(solution)/shard_map/ppermute | solution.py:121
  0.5 16.8 %collective-permute-start.5 = (bf16[1,1344,1024]{2,1,0:T(8,128)(2,1)}, bf16[1,1344,1024]{2,1,0:T(8,128)(2,1)S(1)}, u32[]{:S(2)}, u32[]{:S(2)}) collective-permute-start(bf16[1,1344,1024]{2,1,0:T(8,128)(2,1)} %bitcast.6), channel_id=1, source_target_pairs={{0,2},{2,0},{1,3},{3,1},{4,6},{6,4},{5,7},{7,5},{8,10},{10,8},{9,1... | collective-permute-start | bytes 8257544 | tf_op jit(solution)/shard_map/ppermute | solution.py:121
  0.5 12.8 %collective-permute-start.3 = (bf16[128,1024]{1,0:T(8,128)(2,1)}, bf16[128,1024]{1,0:T(8,128)(2,1)S(1)}, u32[]{:S(2)}, u32[]{:S(2)}) collective-permute-start(bf16[128,1024]{1,0:T(8,128)(2,1)} %refs_3_.1), channel_id=1, source_target_pairs={{0,4},{4,8},{8,12},{12,0},{1,5},{5,9},{9,13},{13,1},{2,6},{6,10},{... | collective-permute-start | bytes 786440 | tf_op jit(solution)/shard_map/ppermute | solution.py:121
  3.5 13.7 %collective-permute-start.2 = (bf16[128,1024]{1,0:T(8,128)(2,1)}, bf16[128,1024]{1,0:T(8,128)(2,1)S(1)}, u32[]{:S(2)}, u32[]{:S(2)}) collective-permute-start(bf16[128,1024]{1,0:T(8,128)(2,1)} %refs_3_.1), channel_id=1, source_target_pairs={{0,1},{1,0},{2,3},{3,2},{4,5},{5,4},{6,7},{7,6},{8,9},{9,8},{10,11... | collective-permute-start | bytes 786440 | tf_op jit(solution)/shard_map/ppermute | solution.py:121
  5.7 6.0 %collective-permute-start = (f32[8,128]{1,0:T(8,128)S(1)}, f32[8,128]{1,0:T(8,128)S(1)}, u32[]{:S(2)}, u32[]{:S(2)}) collective-permute-start(f32[8,128]{1,0:T(8,128)S(1)} %select_reduce_fusion), channel_id=1, source_target_pairs={{0,1},{1,0},{2,3},{3,2},{4,5},{5,4},{6,7},{7,6},{8,9},{9,8},{10,11... | collective-permute-start | bytes 12296 | tf_op jit(solution)/shard_map/ppermute | solution.py:121
  6.3 1.8 %copy-start = (bf16[1,1024,1344]{1,2,0:T(8,128)(2,1)S(1)}, bf16[1,1024,1344]{1,2,0:T(8,128)(2,1)}, u32[]{:S(2)}) copy-start(bf16[1,1024,1344]{1,2,0:T(8,128)(2,1)} %param.8) | copy-start | bytes 8257540
  8.0 1.8 %copy-start.1 = (bf16[1,1024,1344]{1,2,0:T(8,128)(2,1)S(1)}, bf16[1,1024,1344]{1,2,0:T(8,128)(2,1)}, u32[]{:S(2)}) copy-start(bf16[1,1024,1344]{1,2,0:T(8,128)(2,1)} %param.9) | copy-start | bytes 8257540
  9.8 7.4 %copy-start.2 = (bf16[128,1024]{1,0:T(8,128)(2,1)S(1)}, bf16[128,1024]{1,0:T(8,128)(2,1)}, u32[]{:S(2)}) copy-start(bf16[128,1024]{1,0:T(8,128)(2,1)} %refs_3_.1) | copy-start | bytes 786436
  11.8 5.4 %collective-permute-start.1 = (f32[16,128]{1,0:T(8,128)S(1)}, f32[16,128]{1,0:T(8,128)S(1)}, u32[]{:S(2)}, u32[]{:S(2)}) collective-permute-start(f32[16,128]{1,0:T(8,128)S(1)} %pad_maximum_fusion.refs_0_), channel_id=1, source_target_pairs={{0,4},{4,8},{8,12},{12,0},{1,5},{5,9},{9,13},{13,1},{2,6},{6,10},{... | collective-permute-start | bytes 24584 | tf_op jit(solution)/shard_map/ppermute | solution.py:121
  13.4 16.6 %collective-permute-start.9 = (bf16[128,1024]{1,0:T(8,128)(2,1)S(1)}, bf16[128,1024]{1,0:T(8,128)(2,1)S(1)}, u32[]{:S(2)}, u32[]{:S(2)}) collective-permute-start(bf16[128,1024]{1,0:T(8,128)(2,1)S(1)} %collective-permute-done.3.refs_4_), channel_id=1, source_target_pairs={{0,1},{1,0},{2,3},{3,2},{4,5},{5,4},{6,7},{7,6},{8,9},{9,8},{10,11... | collective-permute-start | bytes 786440 | tf_op jit(solution)/shard_map/ppermute | solution.py:121
  17.2 8.2 %collective-permute-start.6 = (bf16[128,1024]{1,0:T(8,128)(2,1)S(1)}, bf16[128,1024]{1,0:T(8,128)(2,1)S(1)}, u32[]{:S(2)}, u32[]{:S(2)}) collective-permute-start(bf16[128,1024]{1,0:T(8,128)(2,1)S(1)} %collective-permute-done.3.refs_4_), channel_id=1, source_target_pairs={{0,4},{4,8},{8,12},{12,0},{1,5},{5,9},{9,13},{13,1},{2,6},{6,10},{... | collective-permute-start | bytes 786440 | tf_op jit(solution)/shard_map/ppermute | solution.py:121
  25.4 8.4 %collective-permute-start.7 = (bf16[128,1024]{1,0:T(8,128)(2,1)S(1)}, bf16[128,1024]{1,0:T(8,128)(2,1)S(1)}, u32[]{:S(2)}, u32[]{:S(2)}) collective-permute-start(bf16[128,1024]{1,0:T(8,128)(2,1)S(1)} %collective-permute-done.6.refs_4_), channel_id=1, source_target_pairs={{0,4},{4,8},{8,12},{12,0},{1,5},{5,9},{9,13},{13,1},{2,6},{6,10},{... | collective-permute-start | bytes 786440 | tf_op jit(solution)/shard_map/ppermute | solution.py:121
  25.4 4.6 %collective-permute-start.8 = (f32[16,128]{1,0:T(8,128)S(1)}, f32[16,128]{1,0:T(8,128)S(1)}, u32[]{:S(2)}, u32[]{:S(2)}) collective-permute-start(f32[16,128]{1,0:T(8,128)S(1)} %pad_maximum_fusion.refs_0_), channel_id=1, source_target_pairs={{0,8},{4,12},{8,0},{12,4},{1,9},{5,13},{9,1},{13,5},{2,10},{6,14},... | collective-permute-start | bytes 24584 | tf_op jit(solution)/shard_map/ppermute | solution.py:121
  26.6 16.0 %collective-permute-start.13 = (bf16[128,1024]{1,0:T(8,128)(2,1)S(1)}, bf16[128,1024]{1,0:T(8,128)(2,1)S(1)}, u32[]{:S(2)}, u32[]{:S(2)}) collective-permute-start(bf16[128,1024]{1,0:T(8,128)(2,1)S(1)} %collective-permute-done.6.refs_4_), channel_id=1, source_target_pairs={{0,1},{1,0},{2,3},{3,2},{4,5},{5,4},{6,7},{7,6},{8,9},{9,8},{10,11... | collective-permute-start | bytes 786440 | tf_op jit(solution)/shard_map/ppermute | solution.py:121
  33.8 13.2 %collective-permute-start.14 = (bf16[128,1024]{1,0:T(8,128)(2,1)S(1)}, bf16[128,1024]{1,0:T(8,128)(2,1)S(1)}, u32[]{:S(2)}, u32[]{:S(2)}) collective-permute-start(bf16[128,1024]{1,0:T(8,128)(2,1)S(1)} %collective-permute-done.7.refs_4_), channel_id=1, source_target_pairs={{0,1},{1,0},{2,3},{3,2},{4,5},{5,4},{6,7},{7,6},{8,9},{9,8},{10,11... | collective-permute-start | bytes 786440 | tf_op jit(solution)/shard_map/ppermute | solution.py:121
  35.3 7.2 %collective-permute-start.12 = (f32[16,128]{1,0:T(8,128)S(1)}, f32[16,128]{1,0:T(8,128)S(1)}, u32[]{:S(2)}, u32[]{:S(2)}) collective-permute-start(f32[16,128]{1,0:T(8,128)S(1)} %pad_maximum_fusion.refs_0_), channel_id=1, source_target_pairs={{0,12},{4,0},{8,4},{12,8},{1,13},{5,1},{9,5},{13,9},{2,14},{6,2},{... | collective-permute-start | bytes 24584 | tf_op jit(solution)/shard_map/ppermute | solution.py:121
  39.2 12.6 %collective-permute-start.11 = (bf16[128,1024]{1,0:T(8,128)(2,1)S(1)}, bf16[128,1024]{1,0:T(8,128)(2,1)S(1)}, u32[]{:S(2)}, u32[]{:S(2)}) collective-permute-start(bf16[128,1024]{1,0:T(8,128)(2,1)S(1)} %get-tuple-element.39.refs_2_), channel_id=1, source_target_pairs={{0,12},{4,0},{8,4},{12,8},{1,13},{5,1},{9,5},{13,9},{2,14},{6,2},{... | collective-permute-start | bytes 786440 | tf_op jit(solution)/shard_map/ppermute | solution.py:121
  39.6 12.2 %collective-permute-start.10 = (bf16[128,1024]{1,0:T(8,128)(2,1)S(1)}, bf16[128,1024]{1,0:T(8,128)(2,1)S(1)}, u32[]{:S(2)}, u32[]{:S(2)}) collective-permute-start(bf16[128,1024]{1,0:T(8,128)(2,1)S(1)} %get-tuple-element.38), channel_id=1, source_target_pairs={{0,12},{4,0},{8,4},{12,8},{1,13},{5,1},{9,5},{13,9},{2,14},{6,2},{... | collective-permute-start | bytes 786440 | tf_op jit(solution)/shard_map/ppermute | solution.py:121
  46.4 6.4 %collective-permute-start.16 = (bf16[128,1024]{1,0:T(8,128)(2,1)S(1)}, bf16[128,1024]{1,0:T(8,128)(2,1)S(1)}, u32[]{:S(2)}, u32[]{:S(2)}) collective-permute-start(bf16[128,1024]{1,0:T(8,128)(2,1)S(1)} %get-tuple-element.41.refs_1_), channel_id=1, source_target_pairs={{0,1},{1,0},{2,3},{3,2},{4,5},{5,4},{6,7},{7,6},{8,9},{9,8},{10,11... | collective-permute-start | bytes 786440 | tf_op jit(solution)/shard_map/ppermute | solution.py:121
  50.2 8.3 %collective-permute-start.15 = (bf16[128,1024]{1,0:T(8,128)(2,1)S(1)}, bf16[128,1024]{1,0:T(8,128)(2,1)S(1)}, u32[]{:S(2)}, u32[]{:S(2)}) collective-permute-start(bf16[128,1024]{1,0:T(8,128)(2,1)S(1)} %shard_map.59), channel_id=1, source_target_pairs={{0,1},{1,0},{2,3},{3,2},{4,5},{5,4},{6,7},{7,6},{8,9},{9,8},{10,11... | collective-permute-start | bytes 786440 | tf_op jit(solution)/shard_map/ppermute | solution.py:121
  52.9 11.0 %collective-permute-start.19 = (bf16[128,1024]{1,0:T(8,128)(2,1)S(1)}, bf16[128,1024]{1,0:T(8,128)(2,1)S(1)}, u32[]{:S(2)}, u32[]{:S(2)}) collective-permute-start(bf16[128,1024]{1,0:T(8,128)(2,1)S(1)} %add_convert_fusion.2), channel_id=1, source_target_pairs={{0,8},{4,12},{8,0},{12,4},{1,9},{5,13},{9,1},{13,5},{2,10},{6,14},... | collective-permute-start | bytes 786440 | tf_op jit(solution)/shard_map/ppermute | solution.py:121
  58.6 8.2 %collective-permute-start.18 = (bf16[128,1024]{1,0:T(8,128)(2,1)S(1)}, bf16[128,1024]{1,0:T(8,128)(2,1)S(1)}, u32[]{:S(2)}, u32[]{:S(2)}) collective-permute-start(bf16[128,1024]{1,0:T(8,128)(2,1)S(1)} %add_convert_fusion.1), channel_id=1, source_target_pairs={{0,4},{4,8},{8,12},{12,0},{1,5},{5,9},{9,13},{13,1},{2,6},{6,10},{... | collective-permute-start | bytes 786440 | tf_op jit(solution)/shard_map/ppermute | solution.py:121
  59.3 7.6 %collective-permute-start.17 = (bf16[128,1024]{1,0:T(8,128)(2,1)S(1)}, bf16[128,1024]{1,0:T(8,128)(2,1)S(1)}, u32[]{:S(2)}, u32[]{:S(2)}) collective-permute-start(bf16[128,1024]{1,0:T(8,128)(2,1)S(1)} %get-tuple-element.48), channel_id=1, source_target_pairs={{0,1},{1,0},{2,3},{3,2},{4,5},{5,4},{6,7},{7,6},{8,9},{9,8},{10,11... | collective-permute-start | bytes 786440 | tf_op jit(solution)/shard_map/ppermute | solution.py:121

commit v14 on v13

--- a/solution.py
+++ b/solution.py
@@ -162,9 +162,9 @@
         fresh = ([0] if j == 0 else []) + [j + 1] * (j < last)
         kinds = [jnp.bfloat16] * len(handed)
         kinds += [jnp.bfloat16 if r == 1 else jnp.float32 for r in fresh]
-        after = firsts[-1:]
+        after = firsts[-1:] + (weights[3:] if j == 1 else [])
         if j == last and j > 1:
-            home = kept[0] + shift(follow(kept[1], ring[last]), "z", -1).astype(jnp.float32)
+            home = kept[0] + shift(follow(kept[1], firsts[-1]), "z", -1).astype(jnp.float32)
         if j > 3:
             totals[j - 2] = total(j - 2, firsts[-1]).astype(jnp.bfloat16)
             after = after + [totals[j - 2]]
@@ -184,7 +184,7 @@
         joined = [
             (
                 mine.astype(jnp.float32)
-                + shift(follow(rows, ring[last]), "z", -1).astype(jnp.float32)
+                + shift(follow(rows, firsts[max(last - 1, 1)]), "z", -1).astype(jnp.float32)
             ).astype(jnp.bfloat16)
             for mine, rows in zip(others[0], others[1])
         ]

time: 67.9 us -> 70.8 us (1.043)
  starting transfers between devices: 24.3 us -> 27.1 us
    ppermute x20, starting transfers between devices: 24.3 us -> 27.1 us  [shift(): lax.ppermute(array, axis, [(i, (i + step) % size) for i in range(size)])]
  transfers between devices with their start and end apart: 20 -> 20, of which waited for: 8 -> 8; matrix products, arithmetic and copies ran while one was open for 1% -> 1% of each run, Pallas kernels for 24% -> 23%
where the time goes in v14:
time: 70.8 us; the launch traced here: 70.6 us
  starting transfers between devices  27.1 us (38%)
  waiting for transfers between devices  21.6 us (31%)
  Pallas kernels  16.5 us (23%)
  local copies, waits for them, and re-layouts  3.56 us (5%)
  other arithmetic  1.84 us (3%)
    ppermute x20, starting transfers between devices, shift(): lax.ppermute(array, axis, [(i, (i + step) % size) for i in range(size)])  27.1 us
    ppermute x20, waiting for transfers between devices, shift(): lax.ppermute(array, axis, [(i, (i + step) % size) for i in range(size)])  21.6 us
    pallas_call x4, Pallas kernels, run_experts(): pl.pallas_call(functools.partial(expert_kernel, block, slots, unit, numbe...  15.8 us
    unnamed x6, local copies, waits for them, and re-layouts  3.56 us
  transfers between devices with their start and end apart: 20, of which 8 were waited for; matrix products, arithmetic and copies ran while one was open for 1% of the time, Pallas kernels for 23%

profile of v14, /device:TPU:0, one launch (start us, length us, event | category | flops | bytes accessed | tf_op | source)
XLA Modules:
  0.0 70.6 jit_solution(14146219110959016192)
XLA Ops:
  0.0 0.5 collective-permute-start.4
  0.5 0.1 collective-permute-start.5
  0.5 3.0 %collective-permute-start.3 = (bf16[128,1024]{1,0:T(8,128)(2,1)}, bf16[128,1024]{1,0:T(8,128)(2,1)S(1)}, u32[]{:S(2)}, u32[]{:S(2)}) collective-permute-start(bf16[128,1024]{1,0:T(8,128)(2,1)} %refs_3_.1), channel_id=1, source_target_pairs={{0,4},{4,8},{8,12},{12,0},{1,5},{5,9},{9,13},{13,1},{2,6},{6,10},{... | collective-permute-start | bytes 786440 | tf_op jit(solution)/shard_map/ppermute | solution.py:121
  3.5 1.5 %collective-permute-start.2 = (bf16[128,1024]{1,0:T(8,128)(2,1)}, bf16[128,1024]{1,0:T(8,128)(2,1)S(1)}, u32[]{:S(2)}, u32[]{:S(2)}) collective-permute-start(bf16[128,1024]{1,0:T(8,128)(2,1)} %refs_3_.1), channel_id=1, source_target_pairs={{0,1},{1,0},{2,3},{3,2},{4,5},{5,4},{6,7},{7,6},{8,9},{9,8},{10,11... | collective-permute-start | bytes 786440 | tf_op jit(solution)/shard_map/ppermute | solution.py:121
  5.0 0.7 %select_reduce_fusion = f32[8,128]{1,0:T(8,128)S(1)} fusion(f32[4,128]{1,0:T(4,128)} %bitcast.8, s32[4,128]{1,0:T(4,128)} %bitcast.9), kind=kLoop, calls=%fused_computation.5 | loop fusion | flops 11264 | bytes 8192 | tf_op jit(solution)/shard_map/reduce_sum | solution.py:140
  5.7 0.5 collective-permute-start
  6.3 1.8 %copy-done = bf16[1,1024,1344]{1,2,0:T(8,128)(2,1)S(1)} copy-done((bf16[1,1024,1344]{1,2,0:T(8,128)(2,1)S(1)}, bf16[1,1024,1344]{1,2,0:T(8,128)(2,1)}, u32[]{:S(2)}) %copy-start) | copy-done | bytes 2752536
  8.1 1.8 %copy-done.1 = bf16[1,1024,1344]{1,2,0:T(8,128)(2,1)S(1)} copy-done((bf16[1,1024,1344]{1,2,0:T(8,128)(2,1)S(1)}, bf16[1,1024,1344]{1,2,0:T(8,128)(2,1)}, u32[]{:S(2)}) %copy-start.1) | copy-done | bytes 2752536
  9.8 0.7 %shard_map.55 = (bf16[1,1344,1024]{2,1,0:T(8,128)(2,1)S(1)}, bf16[1,1344,1024]{2,1,0:T(8,128)(2,1)S(1)}) custom-call(bf16[1,1344,1024]{2,1,0:T(8,128)(2,1)S(1)} %bitcast.5, bf16[1,1344,1024]{2,1,0:T(8,128)(2,1)S(1)} %bitcast.7), custom_call_target="tpu_custom_call" | custom-call | tf_op jit(solution)/shard_map/pallas_call | solution.py:28
  10.5 1.2 %collective-permute-done = f32[8,128]{1,0:T(8,128)S(1)} collective-permute-done((f32[8,128]{1,0:T(8,128)S(1)}, f32[8,128]{1,0:T(8,128)S(1)}, u32[]{:S(2)}, u32[]{:S(2)}) %collective-permute-start) | collective-permute-done | bytes 4128 | tf_op jit(solution)/shard_map/ppermute | solution.py:121
  11.8 1.6 %collective-permute-start.1 = (f32[16,128]{1,0:T(8,128)S(1)}, f32[16,128]{1,0:T(8,128)S(1)}, u32[]{:S(2)}, u32[]{:S(2)}) collective-permute-start(f32[16,128]{1,0:T(8,128)S(1)} %pad_maximum_fusion.refs_0_), channel_id=1, source_target_pairs={{0,4},{4,8},{8,12},{12,0},{1,5},{5,9},{9,13},{13,1},{2,6},{6,10},{... | collective-permute-start | bytes 24584 | tf_op jit(solution)/shard_map/ppermute | solution.py:121
  13.3 0.0 collective-permute-done.3.refs_4_
  13.4 1.5 %collective-permute-start.8 = (bf16[128,1024]{1,0:T(8,128)(2,1)S(1)}, bf16[128,1024]{1,0:T(8,128)(2,1)S(1)}, u32[]{:S(2)}, u32[]{:S(2)}) collective-permute-start(bf16[128,1024]{1,0:T(8,128)(2,1)S(1)} %collective-permute-done.3.refs_4_), channel_id=1, source_target_pairs={{0,1},{1,0},{2,3},{3,2},{4,5},{5,4},{6,7},{7,6},{8,9},{9,8},{10,11... | collective-permute-start | bytes 786440 | tf_op jit(solution)/shard_map/ppermute | solution.py:121
  14.8 2.4 %collective-permute-done.1.refs_1_.refs_0_ = f32[16,128]{1,0:T(8,128)S(1)} collective-permute-done((f32[16,128]{1,0:T(8,128)S(1)}, f32[16,128]{1,0:T(8,128)S(1)}, u32[]{:S(2)}, u32[]{:S(2)}) %collective-permute-start.1) | collective-permute-done | bytes 8224 | tf_op jit(solution)/shard_map/ppermute | solution.py:121
  17.2 0.0 collective-permute-start.9
  17.2 0.0 collective-permute-done.2.refs_2_
  17.2 0.0 collective-permute-done.4.refs_7_.refs_8_.refs_5_
  17.2 0.0 collective-permute-done.5.refs_8_.refs_9_.refs_6_
  17.3 4.9 %shard_map.56 = (bf16[128,1024]{1,0:T(8,128)(2,1)S(1)}, f32[128,1024]{1,0:T(8,128)S(1)}, bf16[128,1024]{1,0:T(8,128)(2,1)S(1)}) custom-call(f32[16,128]{1,0:T(8,128)S(1)} %pad_maximum_fusion.refs_0_, f32[16,128]{1,0:T(8,128)S(1)} %collective-permute-done.1.refs_1_.refs_0_, bf16[128,1024]{1,0:T(8,128)(2,1)S(1)} %collective-permute-done.2.refs_2_, ...), custom_call_target="tpu_custom_call" | custom-call | flops 3472883712 | bytes 12976128 | tf_op jit(solution)/shard_map/pallas_call | solution.py:103
  22.1 3.3 %collective-permute-done.9.refs_5_ = bf16[128,1024]{1,0:T(8,128)(2,1)S(1)} collective-permute-done((bf16[128,1024]{1,0:T(8,128)(2,1)S(1)}, bf16[128,1024]{1,0:T(8,128)(2,1)S(1)}, u32[]{:S(2)}, u32[]{:S(2)}) %collective-permute-start.9) | collective-permute-done | bytes 262176 | tf_op jit(solution)/shard_map/ppermute | solution.py:121
  25.4 1.5 %collective-permute-start.10 = (bf16[128,1024]{1,0:T(8,128)(2,1)S(1)}, bf16[128,1024]{1,0:T(8,128)(2,1)S(1)}, u32[]{:S(2)}, u32[]{:S(2)}) collective-permute-start(bf16[128,1024]{1,0:T(8,128)(2,1)S(1)} %collective-permute-done.9.refs_5_), channel_id=1, source_target_pairs={{0,1},{1,0},{2,3},{3,2},{4,5},{5,4},{6,7},{7,6},{8,9},{9,8},{10,11... | collective-permute-start | bytes 786440 | tf_op jit(solution)/shard_map/ppermute | solution.py:121
  26.9 1.2 %collective-permute-start.6 = (f32[16,128]{1,0:T(8,128)S(1)}, f32[16,128]{1,0:T(8,128)S(1)}, u32[]{:S(2)}, u32[]{:S(2)}) collective-permute-start(f32[16,128]{1,0:T(8,128)S(1)} %pad_maximum_fusion.refs_0_), channel_id=1, source_target_pairs={{0,8},{4,12},{8,0},{12,4},{1,9},{5,13},{9,1},{13,5},{2,10},{6,14},... | collective-permute-start | bytes 24584 | tf_op jit(solution)/shard_map/ppermute | solution.py:121
  28.1 2.6 %collective-permute-start.7 = (f32[16,128]{1,0:T(8,128)S(1)}, f32[16,128]{1,0:T(8,128)S(1)}, u32[]{:S(2)}, u32[]{:S(2)}) collective-permute-start(f32[16,128]{1,0:T(8,128)S(1)} %pad_maximum_fusion.refs_0_), channel_id=1, source_target_pairs={{0,12},{4,0},{8,4},{12,8},{1,13},{5,1},{9,5},{13,9},{2,14},{6,2},{... | collective-permute-start | bytes 24584 | tf_op jit(solution)/shard_map/ppermute | solution.py:121
  30.7 1.5 %collective-permute-done.6.refs_1_.refs_0_ = f32[16,128]{1,0:T(8,128)S(1)} collective-permute-done((f32[16,128]{1,0:T(8,128)S(1)}, f32[16,128]{1,0:T(8,128)S(1)}, u32[]{:S(2)}, u32[]{:S(2)}) %collective-permute-start.6) | collective-permute-done | bytes 8224 | tf_op jit(solution)/shard_map/ppermute | solution.py:121
  32.2 1.5 %collective-permute-done.7.refs_3_.refs_1_.refs_0_ = f32[16,128]{1,0:T(8,128)S(1)} collective-permute-done((f32[16,128]{1,0:T(8,128)S(1)}, f32[16,128]{1,0:T(8,128)S(1)}, u32[]{:S(2)}, u32[]{:S(2)}) %collective-permute-start.7) | collective-permute-done | bytes 8224 | tf_op jit(solution)/shard_map/ppermute | solution.py:121
  33.7 3.8 %shard_map.57 = (bf16[128,1024]{1,0:T(8,128)(2,1)S(1)}, f32[128,1024]{1,0:T(8,128)S(1)}) custom-call(f32[16,128]{1,0:T(8,128)S(1)} %collective-permute-done.1.refs_1_.refs_0_, f32[16,128]{1,0:T(8,128)S(1)} %collective-permute-done.6.refs_1_.refs_0_, bf16[128,1024]{1,0:T(8,128)(2,1)S(1)} %get-tuple-element.34.refs_2_, ...), custom_call_target="tpu_custom_call" | custom-call | flops 2315255808 | bytes 12320768 | tf_op jit(solution)/shard_map/pallas_call | solution.py:103
  37.5 0.0 collective-permute-done.11.refs_4_
  37.5 0.6 collective-permute-start.14
  38.1 0.0 collective-permute-done.10.refs_3_
  38.1 3.8 %shard_map.58 = (bf16[128,1024]{1,0:T(8,128)(2,1)S(1)}, f32[128,1024]{1,0:T(8,128)S(1)}) custom-call(f32[16,128]{1,0:T(8,128)S(1)} %collective-permute-done.6.refs_1_.refs_0_, f32[16,128]{1,0:T(8,128)S(1)} %collective-permute-done.7.refs_3_.refs_1_.refs_0_, bf16[128,1024]{1,0:T(8,128)(2,1)S(1)} %get-tuple-element.40.refs_2_, ...), custom_call_target="tpu_custom_call" | custom-call | flops 2315255808 | bytes 12320768 | tf_op jit(solution)/shard_map/pallas_call | solution.py:103
  42.0 2.5 %collective-permute-start.13 = (bf16[128,1024]{1,0:T(8,128)(2,1)S(1)}, bf16[128,1024]{1,0:T(8,128)(2,1)S(1)}, u32[]{:S(2)}, u32[]{:S(2)}) collective-permute-start(bf16[128,1024]{1,0:T(8,128)(2,1)S(1)} %get-tuple-element.40.refs_2_), channel_id=1, source_target_pairs={{0,12},{4,0},{8,4},{12,8},{1,13},{5,1},{9,5},{13,9},{2,14},{6,2},{... | collective-permute-start | bytes 786440 | tf_op jit(solution)/shard_map/ppermute | solution.py:121
  44.5 0.6 collective-permute-start.12
  45.0 1.2 %collective-permute-start.16 = (bf16[128,1024]{1,0:T(8,128)(2,1)S(1)}, bf16[128,1024]{1,0:T(8,128)(2,1)S(1)}, u32[]{:S(2)}, u32[]{:S(2)}) collective-permute-start(bf16[128,1024]{1,0:T(8,128)(2,1)S(1)} %get-tuple-element.38.refs_1_), channel_id=1, source_target_pairs={{0,1},{1,0},{2,3},{3,2},{4,5},{5,4},{6,7},{7,6},{8,9},{9,8},{10,11... | collective-permute-start | bytes 786440 | tf_op jit(solution)/shard_map/ppermute | solution.py:121
  46.2 0.0 collective-permute-done.14.refs_2_
  46.2 3.3 %shard_map.59 = bf16[128,1024]{1,0:T(8,128)(2,1)S(1)} custom-call(f32[16,128]{1,0:T(8,128)S(1)} %collective-permute-done.7.refs_3_.refs_1_.refs_0_, bf16[128,1024]{1,0:T(8,128)(2,1)S(1)} %get-tuple-element.38.refs_1_, bf16[128,1024]{1,0:T(8,128)(2,1)S(1)} %collective-permute-done.14.refs_2_, ...), custom_call_target="tpu_custom_call" | custom-call | flops 1157627904 | bytes 11665408 | tf_op jit(solution)/shard_map/pallas_call | solution.py:103
  49.5 0.9 %collective-permute-start.15 = (bf16[128,1024]{1,0:T(8,128)(2,1)S(1)}, bf16[128,1024]{1,0:T(8,128)(2,1)S(1)}, u32[]{:S(2)}, u32[]{:S(2)}) collective-permute-start(bf16[128,1024]{1,0:T(8,128)(2,1)S(1)} %shard_map.59), channel_id=1, source_target_pairs={{0,1},{1,0},{2,3},{3,2},{4,5},{5,4},{6,7},{7,6},{8,9},{9,8},{10,11... | collective-permute-start | bytes 786440 | tf_op jit(solution)/shard_map/ppermute | solution.py:121
  50.4 4.1 %collective-permute-done.12 = bf16[128,1024]{1,0:T(8,128)(2,1)S(1)} collective-permute-done((bf16[128,1024]{1,0:T(8,128)(2,1)S(1)}, bf16[128,1024]{1,0:T(8,128)(2,1)S(1)}, u32[]{:S(2)}, u32[]{:S(2)}) %collective-permute-start.12) | collective-permute-done | bytes 262176 | tf_op jit(solution)/shard_map/ppermute | solution.py:121
  54.5 0.1 add_convert_fusion.3
  54.7 0.0 collective-permute-done.16
  54.7 0.1 add_convert_fusion.2
  54.8 4.5 %collective-permute-start.19 = (bf16[128,1024]{1,0:T(8,128)(2,1)S(1)}, bf16[128,1024]{1,0:T(8,128)(2,1)S(1)}, u32[]{:S(2)}, u32[]{:S(2)}) collective-permute-start(bf16[128,1024]{1,0:T(8,128)(2,1)S(1)} %add_convert_fusion.2), channel_id=1, source_target_pairs={{0,8},{4,12},{8,0},{12,4},{1,9},{5,13},{9,1},{13,5},{2,10},{6,14},... | collective-permute-start | bytes 786440 | tf_op jit(solution)/shard_map/ppermute | solution.py:121
  59.2 0.0 collective-permute-done.15
  59.2 0.1 add_convert_fusion.1
  59.3 1.1 %collective-permute-start.18 = (bf16[128,1024]{1,0:T(8,128)(2,1)S(1)}, bf16[128,1024]{1,0:T(8,128)(2,1)S(1)}, u32[]{:S(2)}, u32[]{:S(2)}) collective-permute-start(bf16[128,1024]{1,0:T(8,128)(2,1)S(1)} %add_convert_fusion.1), channel_id=1, source_target_pairs={{0,4},{4,8},{8,12},{12,0},{1,5},{5,9},{9,13},{13,1},{2,6},{6,10},{... | collective-permute-start | bytes 786440 | tf_op jit(solution)/shard_map/ppermute | solution.py:121
  60.4 1.8 %collective-permute-start.17 = (bf16[128,1024]{1,0:T(8,128)(2,1)S(1)}, bf16[128,1024]{1,0:T(8,128)(2,1)S(1)}, u32[]{:S(2)}, u32[]{:S(2)}) collective-permute-start(bf16[128,1024]{1,0:T(8,128)(2,1)S(1)} %get-tuple-element.48), channel_id=1, source_target_pairs={{0,1},{1,0},{2,3},{3,2},{4,5},{5,4},{6,7},{7,6},{8,9},{9,8},{10,11... | collective-permute-start | bytes 786440 | tf_op jit(solution)/shard_map/ppermute | solution.py:121
  62.2 1.4 %collective-permute-done.19 = bf16[128,1024]{1,0:T(8,128)(2,1)S(1)} collective-permute-done((bf16[128,1024]{1,0:T(8,128)(2,1)S(1)}, bf16[128,1024]{1,0:T(8,128)(2,1)S(1)}, u32[]{:S(2)}, u32[]{:S(2)}) %collective-permute-start.19) | collective-permute-done | bytes 262176 | tf_op jit(solution)/shard_map/ppermute | solution.py:121
  63.6 6.2 %collective-permute-done.18 = bf16[128,1024]{1,0:T(8,128)(2,1)S(1)} collective-permute-done((bf16[128,1024]{1,0:T(8,128)(2,1)S(1)}, bf16[128,1024]{1,0:T(8,128)(2,1)S(1)}, u32[]{:S(2)}, u32[]{:S(2)}) %collective-permute-start.18) | collective-permute-done | bytes 262176 | tf_op jit(solution)/shard_map/ppermute | solution.py:121
  69.8 0.9 %add_convert_fusion = bf16[128,1024]{1,0:T(8,128)(2,1)} fusion(bf16[128,1024]{1,0:T(8,128)(2,1)S(1)} %collective-permute-done.18, bf16[128,1024]{1,0:T(8,128)(2,1)S(1)} %collective-permute-done.19, f32[128,1024]{1,0:T(8,128)S(1)} %get-tuple-element.52, bf16[128,1024]{1,0:T(8,128)(2,1)S(1)} %collective-permute-done.17), kind=kLoop, calls=%fused_computation | loop fusion | flops 917504 | bytes 1572864 | tf_op jit(solution)/shard_map/convert_element_type | solution.py:207
  (9 shorter events, 0.0 us)
Async XLA Ops:
  0.0 17.2 %collective-permute-start.4 = (bf16[1,1344,1024]{2,1,0:T(8,128)(2,1)}, bf16[1,1344,1024]{2,1,0:T(8,128)(2,1)S(1)}, u32[]{:S(2)}, u32[]{:S(2)}) collective-permute-start(bf16[1,1344,1024]{2,1,0:T(8,128)(2,1)} %bitcast.4), channel_id=1, source_target_pairs={{0,2},{2,0},{1,3},{3,1},{4,6},{6,4},{5,7},{7,5},{8,10},{10,8},{9,1... | collective-permute-start | bytes 8257544 | tf_op jit(solution)/shard_map/ppermute | solution.py:121
  0.5 16.8 %collective-permute-start.5 = (bf16[1,1344,1024]{2,1,0:T(8,128)(2,1)}, bf16[1,1344,1024]{2,1,0:T(8,128)(2,1)S(1)}, u32[]{:S(2)}, u32[]{:S(2)}) collective-permute-start(bf16[1,1344,1024]{2,1,0:T(8,128)(2,1)} %bitcast.6), channel_id=1, source_target_pairs={{0,2},{2,0},{1,3},{3,1},{4,6},{6,4},{5,7},{7,5},{8,10},{10,8},{9,1... | collective-permute-start | bytes 8257544 | tf_op jit(solution)/shard_map/ppermute | solution.py:121
  0.5 12.8 %collective-permute-start.3 = (bf16[128,1024]{1,0:T(8,128)(2,1)}, bf16[128,1024]{1,0:T(8,128)(2,1)S(1)}, u32[]{:S(2)}, u32[]{:S(2)}) collective-permute-start(bf16[128,1024]{1,0:T(8,128)(2,1)} %refs_3_.1), channel_id=1, source_target_pairs={{0,4},{4,8},{8,12},{12,0},{1,5},{5,9},{9,13},{13,1},{2,6},{6,10},{... | collective-permute-start | bytes 786440 | tf_op jit(solution)/shard_map/ppermute | solution.py:121
  3.5 13.7 %collective-permute-start.2 = (bf16[128,1024]{1,0:T(8,128)(2,1)}, bf16[128,1024]{1,0:T(8,128)(2,1)S(1)}, u32[]{:S(2)}, u32[]{:S(2)}) collective-permute-start(bf16[128,1024]{1,0:T(8,128)(2,1)} %refs_3_.1), channel_id=1, source_target_pairs={{0,1},{1,0},{2,3},{3,2},{4,5},{5,4},{6,7},{7,6},{8,9},{9,8},{10,11... | collective-permute-start | bytes 786440 | tf_op jit(solution)/shard_map/ppermute | solution.py:121
  5.7 6.0 %collective-permute-start = (f32[8,128]{1,0:T(8,128)S(1)}, f32[8,128]{1,0:T(8,128)S(1)}, u32[]{:S(2)}, u32[]{:S(2)}) collective-permute-start(f32[8,128]{1,0:T(8,128)S(1)} %select_reduce_fusion), channel_id=1, source_target_pairs={{0,1},{1,0},{2,3},{3,2},{4,5},{5,4},{6,7},{7,6},{8,9},{9,8},{10,11... | collective-permute-start | bytes 12296 | tf_op jit(solution)/shard_map/ppermute | solution.py:121
  6.3 1.8 %copy-start = (bf16[1,1024,1344]{1,2,0:T(8,128)(2,1)S(1)}, bf16[1,1024,1344]{1,2,0:T(8,128)(2,1)}, u32[]{:S(2)}) copy-start(bf16[1,1024,1344]{1,2,0:T(8,128)(2,1)} %param.8) | copy-start | bytes 8257540
  8.0 1.8 %copy-start.1 = (bf16[1,1024,1344]{1,2,0:T(8,128)(2,1)S(1)}, bf16[1,1024,1344]{1,2,0:T(8,128)(2,1)}, u32[]{:S(2)}) copy-start(bf16[1,1024,1344]{1,2,0:T(8,128)(2,1)} %param.9) | copy-start | bytes 8257540
  9.8 7.4 %copy-start.2 = (bf16[128,1024]{1,0:T(8,128)(2,1)S(1)}, bf16[128,1024]{1,0:T(8,128)(2,1)}, u32[]{:S(2)}) copy-start(bf16[128,1024]{1,0:T(8,128)(2,1)} %refs_3_.1) | copy-start | bytes 786436
  11.8 5.4 %collective-permute-start.1 = (f32[16,128]{1,0:T(8,128)S(1)}, f32[16,128]{1,0:T(8,128)S(1)}, u32[]{:S(2)}, u32[]{:S(2)}) collective-permute-start(f32[16,128]{1,0:T(8,128)S(1)} %pad_maximum_fusion.refs_0_), channel_id=1, source_target_pairs={{0,4},{4,8},{8,12},{12,0},{1,5},{5,9},{9,13},{13,1},{2,6},{6,10},{... | collective-permute-start | bytes 24584 | tf_op jit(solution)/shard_map/ppermute | solution.py:121
  13.4 20.4 %collective-permute-start.8 = (bf16[128,1024]{1,0:T(8,128)(2,1)S(1)}, bf16[128,1024]{1,0:T(8,128)(2,1)S(1)}, u32[]{:S(2)}, u32[]{:S(2)}) collective-permute-start(bf16[128,1024]{1,0:T(8,128)(2,1)S(1)} %collective-permute-done.3.refs_4_), channel_id=1, source_target_pairs={{0,1},{1,0},{2,3},{3,2},{4,5},{5,4},{6,7},{7,6},{8,9},{9,8},{10,11... | collective-permute-start | bytes 786440 | tf_op jit(solution)/shard_map/ppermute | solution.py:121
  17.2 8.2 %collective-permute-start.9 = (bf16[128,1024]{1,0:T(8,128)(2,1)S(1)}, bf16[128,1024]{1,0:T(8,128)(2,1)S(1)}, u32[]{:S(2)}, u32[]{:S(2)}) collective-permute-start(bf16[128,1024]{1,0:T(8,128)(2,1)S(1)} %collective-permute-done.3.refs_4_), channel_id=1, source_target_pairs={{0,4},{4,8},{8,12},{12,0},{1,5},{5,9},{9,13},{13,1},{2,6},{6,10},{... | collective-permute-start | bytes 786440 | tf_op jit(solution)/shard_map/ppermute | solution.py:121
  25.4 12.1 %collective-permute-start.11 = (bf16[128,1024]{1,0:T(8,128)(2,1)S(1)}, bf16[128,1024]{1,0:T(8,128)(2,1)S(1)}, u32[]{:S(2)}, u32[]{:S(2)}) collective-permute-start(bf16[128,1024]{1,0:T(8,128)(2,1)S(1)} %collective-permute-done.9.refs_5_), channel_id=1, source_target_pairs={{0,4},{4,8},{8,12},{12,0},{1,5},{5,9},{9,13},{13,1},{2,6},{6,10},{... | collective-permute-start | bytes 786440 | tf_op jit(solution)/shard_map/ppermute | solution.py:121
  25.4 12.7 %collective-permute-start.10 = (bf16[128,1024]{1,0:T(8,128)(2,1)S(1)}, bf16[128,1024]{1,0:T(8,128)(2,1)S(1)}, u32[]{:S(2)}, u32[]{:S(2)}) collective-permute-start(bf16[128,1024]{1,0:T(8,128)(2,1)S(1)} %collective-permute-done.9.refs_5_), channel_id=1, source_target_pairs={{0,1},{1,0},{2,3},{3,2},{4,5},{5,4},{6,7},{7,6},{8,9},{9,8},{10,11... | collective-permute-start | bytes 786440 | tf_op jit(solution)/shard_map/ppermute | solution.py:121
  26.9 5.3 %collective-permute-start.6 = (f32[16,128]{1,0:T(8,128)S(1)}, f32[16,128]{1,0:T(8,128)S(1)}, u32[]{:S(2)}, u32[]{:S(2)}) collective-permute-start(f32[16,128]{1,0:T(8,128)S(1)} %pad_maximum_fusion.refs_0_), channel_id=1, source_target_pairs={{0,8},{4,12},{8,0},{12,4},{1,9},{5,13},{9,1},{13,5},{2,10},{6,14},... | collective-permute-start | bytes 24584 | tf_op jit(solution)/shard_map/ppermute | solution.py:121
  28.1 5.6 %collective-permute-start.7 = (f32[16,128]{1,0:T(8,128)S(1)}, f32[16,128]{1,0:T(8,128)S(1)}, u32[]{:S(2)}, u32[]{:S(2)}) collective-permute-start(f32[16,128]{1,0:T(8,128)S(1)} %pad_maximum_fusion.refs_0_), channel_id=1, source_target_pairs={{0,12},{4,0},{8,4},{12,8},{1,13},{5,1},{9,5},{13,9},{2,14},{6,2},{... | collective-permute-start | bytes 24584 | tf_op jit(solution)/shard_map/ppermute | solution.py:121
  37.5 8.7 %collective-permute-start.14 = (bf16[128,1024]{1,0:T(8,128)(2,1)S(1)}, bf16[128,1024]{1,0:T(8,128)(2,1)S(1)}, u32[]{:S(2)}, u32[]{:S(2)}) collective-permute-start(bf16[128,1024]{1,0:T(8,128)(2,1)S(1)} %collective-permute-done.11.refs_4_), channel_id=1, source_target_pairs={{0,1},{1,0},{2,3},{3,2},{4,5},{5,4},{6,7},{7,6},{8,9},{9,8},{10,11... | collective-permute-start | bytes 786440 | tf_op jit(solution)/shard_map/ppermute | solution.py:121
  42.0 8.4 %collective-permute-start.13 = (bf16[128,1024]{1,0:T(8,128)(2,1)S(1)}, bf16[128,1024]{1,0:T(8,128)(2,1)S(1)}, u32[]{:S(2)}, u32[]{:S(2)}) collective-permute-start(bf16[128,1024]{1,0:T(8,128)(2,1)S(1)} %get-tuple-element.40.refs_2_), channel_id=1, source_target_pairs={{0,12},{4,0},{8,4},{12,8},{1,13},{5,1},{9,5},{13,9},{2,14},{6,2},{... | collective-permute-start | bytes 786440 | tf_op jit(solution)/shard_map/ppermute | solution.py:121
  44.5 10.1 %collective-permute-start.12 = (bf16[128,1024]{1,0:T(8,128)(2,1)S(1)}, bf16[128,1024]{1,0:T(8,128)(2,1)S(1)}, u32[]{:S(2)}, u32[]{:S(2)}) collective-permute-start(bf16[128,1024]{1,0:T(8,128)(2,1)S(1)} %get-tuple-element.39), channel_id=1, source_target_pairs={{0,12},{4,0},{8,4},{12,8},{1,13},{5,1},{9,5},{13,9},{2,14},{6,2},{... | collective-permute-start | bytes 786440 | tf_op jit(solution)/shard_map/ppermute | solution.py:121
  45.0 9.7 %collective-permute-start.16 = (bf16[128,1024]{1,0:T(8,128)(2,1)S(1)}, bf16[128,1024]{1,0:T(8,128)(2,1)S(1)}, u32[]{:S(2)}, u32[]{:S(2)}) collective-permute-start(bf16[128,1024]{1,0:T(8,128)(2,1)S(1)} %get-tuple-element.38.refs_1_), channel_id=1, source_target_pairs={{0,1},{1,0},{2,3},{3,2},{4,5},{5,4},{6,7},{7,6},{8,9},{9,8},{10,11... | collective-permute-start | bytes 786440 | tf_op jit(solution)/shard_map/ppermute | solution.py:121
  49.5 9.8 %collective-permute-start.15 = (bf16[128,1024]{1,0:T(8,128)(2,1)S(1)}, bf16[128,1024]{1,0:T(8,128)(2,1)S(1)}, u32[]{:S(2)}, u32[]{:S(2)}) collective-permute-start(bf16[128,1024]{1,0:T(8,128)(2,1)S(1)} %shard_map.59), channel_id=1, source_target_pairs={{0,1},{1,0},{2,3},{3,2},{4,5},{5,4},{6,7},{7,6},{8,9},{9,8},{10,11... | collective-permute-start | bytes 786440 | tf_op jit(solution)/shard_map/ppermute | solution.py:121
  54.8 8.8 %collective-permute-start.19 = (bf16[128,1024]{1,0:T(8,128)(2,1)S(1)}, bf16[128,1024]{1,0:T(8,128)(2,1)S(1)}, u32[]{:S(2)}, u32[]{:S(2)}) collective-permute-start(bf16[128,1024]{1,0:T(8,128)(2,1)S(1)} %add_convert_fusion.2), channel_id=1, source_target_pairs={{0,8},{4,12},{8,0},{12,4},{1,9},{5,13},{9,1},{13,5},{2,10},{6,14},... | collective-permute-start | bytes 786440 | tf_op jit(solution)/shard_map/ppermute | solution.py:121
  59.3 10.5 %collective-permute-start.18 = (bf16[128,1024]{1,0:T(8,128)(2,1)S(1)}, bf16[128,1024]{1,0:T(8,128)(2,1)S(1)}, u32[]{:S(2)}, u32[]{:S(2)}) collective-permute-start(bf16[128,1024]{1,0:T(8,128)(2,1)S(1)} %add_convert_fusion.1), channel_id=1, source_target_pairs={{0,4},{4,8},{8,12},{12,0},{1,5},{5,9},{9,13},{13,1},{2,6},{6,10},{... | collective-permute-start | bytes 786440 | tf_op jit(solution)/shard_map/ppermute | solution.py:121
  60.4 9.4 %collective-permute-start.17 = (bf16[128,1024]{1,0:T(8,128)(2,1)S(1)}, bf16[128,1024]{1,0:T(8,128)(2,1)S(1)}, u32[]{:S(2)}, u32[]{:S(2)}) collective-permute-start(bf16[128,1024]{1,0:T(8,128)(2,1)S(1)} %get-tuple-element.48), channel_id=1, source_target_pairs={{0,1},{1,0},{2,3},{3,2},{4,5},{5,4},{6,7},{7,6},{8,9},{9,8},{10,11... | collective-permute-start | bytes 786440 | tf_op jit(solution)/shard_map/ppermute | solution.py:121

commit v15 on v13

--- a/solution.py
+++ b/solution.py
@@ -36,10 +36,10 @@
 
 
 def expert_kernel(block, slots, unit, number, sources, waits, *refs):
-    rounds = sorted({r for r, _ in sources})
-    gate_refs, refs = refs[: len(rounds)], refs[len(rounds) :]
+    steps = sorted({r.bit_length() for r, _ in sources})
+    gate_refs, refs = refs[: len(steps)], refs[len(steps) :]
     first, core = lax.axis_index("z") * number, lax.axis_index("core")
-    blocks, experts = len(sources), gate_refs[0].shape[0] // lax.axis_size("sub")
+    blocks, experts, subs = len(sources), lax.axis_size("z") * number, lax.axis_size("sub")
     refs = refs[waits:]
     x_refs, tables, out_refs = refs[:blocks], refs[blocks : blocks + 2 * number], refs[blocks + 2 * number :]
     earlier = lax.broadcasted_iota(jnp.int32, (block, block), 0)
@@ -50,7 +50,8 @@
     row = lax.broadcasted_iota(jnp.int32, (experts, block), 0)
     gates, ranks = [], []
     for r, turn in sources:
-        gate = gate_refs[rounds.index(r)][turn * experts : (turn + 1) * experts, :]
+        place = ((r - (2 ** r.bit_length()) // 2 * (r > 0)) * subs + turn) * experts
+        gate = gate_refs[steps.index(r.bit_length())][place : place + experts, :]
         gates.append(gate)
         ranks.append(
             jnp.dot((gate > 0).astype(jnp.bfloat16), before, preferred_element_type=jnp.float32)
@@ -96,7 +97,7 @@
 
 def run_experts(after, gates, sources, arrived, tables, kinds, slots):
     blocks, number, block = len(arrived), len(tables) // 2, gates[0].shape[1]
-    gates = [gates[r] for r in sorted({r for r, _ in sources})]
+    gates = [gates[step] for step in sorted({r.bit_length() for r, _ in sources})]
     hidden, width = tables[0].shape[1:]
     unit = 16 // math.gcd(16, slots)
     whole = pl.BlockSpec(memory_space=pltpu.VMEM)
@@ -142,7 +143,10 @@
     )
     near = [weight] + [follow(shift(weight, "sub", s), tables[0]) for s in range(1, subs)]
     near = jnp.concatenate(near, axis=0)
-    weights = [near] + [shift(near, "z", r) for r in range(1, depth)]
+    weights, held = [near], near
+    while 2 ** len(weights) < 2 * depth:
+        weights.append(shift(held, "z", 2 ** (len(weights) - 1)))
+        held = jnp.concatenate([held, weights[-1]], axis=0)
     last = depth - 1
     kept, others = {}, {}
     totals, home = {}, None

time: 67.9 us -> 66.8 us (0.984)
  waiting for transfers between devices: 21.4 us -> 16.6 us
  starting transfers between devices: 24.3 us -> 28 us
    ppermute x20 -> x19, waiting for transfers between devices: 21.4 us -> 16.6 us  [shift(): lax.ppermute(array, axis, [(i, (i + step) % size) for i in range(size)])]
    ppermute x20 -> x19, starting transfers between devices: 24.3 us -> 28 us  [shift(): lax.ppermute(array, axis, [(i, (i + step) % size) for i in range(size)])]
  transfers between devices with their start and end apart: 20 -> 19, of which waited for: 8 -> 8; matrix products, arithmetic and copies ran while one was open for 1% -> 1% of each run, Pallas kernels for 24% -> 25%
where the time goes in v15:
time: 66.8 us; the launch traced here: 66.6 us
  starting transfers between devices  28 us (42%)
  waiting for transfers between devices  16.6 us (25%)
  Pallas kernels  16.5 us (25%)
  local copies, waits for them, and re-layouts  3.56 us (5%)
  other arithmetic  1.83 us (3%)
    ppermute x19, starting transfers between devices, shift(): lax.ppermute(array, axis, [(i, (i + step) % size) for i in range(size)])  28 us
    ppermute x19, waiting for transfers between devices, shift(): lax.ppermute(array, axis, [(i, (i + step) % size) for i in range(size)])  16.6 us
    pallas_call x4, Pallas kernels, run_experts(): pl.pallas_call(functools.partial(expert_kernel, block, slots, unit, numbe...  15.8 us
    unnamed x6, local copies, waits for them, and re-layouts  3.56 us
  transfers between devices with their start and end apart: 19, of which 8 were waited for; matrix products, arithmetic and copies ran while one was open for 1% of the time, Pallas kernels for 25%

profile of v15, /device:TPU:0, one launch (start us, length us, event | category | flops | bytes accessed | tf_op | source)
XLA Modules:
  0.0 66.6 jit_solution(6443633574794498545)
XLA Ops:
  0.0 0.5 collective-permute-start.4
  0.5 0.1 collective-permute-start.5
  0.5 3.0 %collective-permute-start.3 = (bf16[128,1024]{1,0:T(8,128)(2,1)}, bf16[128,1024]{1,0:T(8,128)(2,1)S(1)}, u32[]{:S(2)}, u32[]{:S(2)}) collective-permute-start(bf16[128,1024]{1,0:T(8,128)(2,1)} %refs_3_.1), channel_id=1, source_target_pairs={{0,4},{4,8},{8,12},{12,0},{1,5},{5,9},{9,13},{13,1},{2,6},{6,10},{... | collective-permute-start | bytes 786440 | tf_op jit(solution)/shard_map/ppermute | solution.py:122
  3.5 1.5 %collective-permute-start.2 = (bf16[128,1024]{1,0:T(8,128)(2,1)}, bf16[128,1024]{1,0:T(8,128)(2,1)S(1)}, u32[]{:S(2)}, u32[]{:S(2)}) collective-permute-start(bf16[128,1024]{1,0:T(8,128)(2,1)} %refs_3_.1), channel_id=1, source_target_pairs={{0,1},{1,0},{2,3},{3,2},{4,5},{5,4},{6,7},{7,6},{8,9},{9,8},{10,11... | collective-permute-start | bytes 786440 | tf_op jit(solution)/shard_map/ppermute | solution.py:122
  5.0 0.7 %select_reduce_fusion = f32[8,128]{1,0:T(8,128)S(1)} fusion(f32[4,128]{1,0:T(4,128)} %bitcast.8, s32[4,128]{1,0:T(4,128)} %bitcast.9), kind=kLoop, calls=%fused_computation.6 | loop fusion | flops 11264 | bytes 8192 | tf_op jit(solution)/shard_map/reduce_sum | solution.py:141
  5.7 0.5 collective-permute-start
  6.3 1.8 %copy-done = bf16[1,1024,1344]{1,2,0:T(8,128)(2,1)S(1)} copy-done((bf16[1,1024,1344]{1,2,0:T(8,128)(2,1)S(1)}, bf16[1,1024,1344]{1,2,0:T(8,128)(2,1)}, u32[]{:S(2)}) %copy-start) | copy-done | bytes 2752536
  8.1 1.8 %copy-done.1 = bf16[1,1024,1344]{1,2,0:T(8,128)(2,1)S(1)} copy-done((bf16[1,1024,1344]{1,2,0:T(8,128)(2,1)S(1)}, bf16[1,1024,1344]{1,2,0:T(8,128)(2,1)}, u32[]{:S(2)}) %copy-start.1) | copy-done | bytes 2752536
  9.8 0.7 %shard_map.55 = (bf16[1,1344,1024]{2,1,0:T(8,128)(2,1)S(1)}, bf16[1,1344,1024]{2,1,0:T(8,128)(2,1)S(1)}) custom-call(bf16[1,1344,1024]{2,1,0:T(8,128)(2,1)S(1)} %bitcast.5, bf16[1,1344,1024]{2,1,0:T(8,128)(2,1)S(1)} %bitcast.7), custom_call_target="tpu_custom_call" | custom-call | tf_op jit(solution)/shard_map/pallas_call | solution.py:28
  10.5 1.2 %collective-permute-done = f32[8,128]{1,0:T(8,128)S(1)} collective-permute-done((f32[8,128]{1,0:T(8,128)S(1)}, f32[8,128]{1,0:T(8,128)S(1)}, u32[]{:S(2)}, u32[]{:S(2)}) %collective-permute-start) | collective-permute-done | bytes 4128 | tf_op jit(solution)/shard_map/ppermute | solution.py:122
  11.8 1.6 %collective-permute-start.1 = (f32[16,128]{1,0:T(8,128)S(1)}, f32[16,128]{1,0:T(8,128)S(1)}, u32[]{:S(2)}, u32[]{:S(2)}) collective-permute-start(f32[16,128]{1,0:T(8,128)S(1)} %pad_maximum_fusion.1.refs_0_), channel_id=1, source_target_pairs={{0,4},{4,8},{8,12},{12,0},{1,5},{5,9},{9,13},{13,1},{2,6},{6,10},{... | collective-permute-start | bytes 24584 | tf_op jit(solution)/shard_map/ppermute | solution.py:122
  13.3 0.0 collective-permute-done.3.refs_4_
  13.4 1.5 %collective-permute-start.9 = (bf16[128,1024]{1,0:T(8,128)(2,1)S(1)}, bf16[128,1024]{1,0:T(8,128)(2,1)S(1)}, u32[]{:S(2)}, u32[]{:S(2)}) collective-permute-start(bf16[128,1024]{1,0:T(8,128)(2,1)S(1)} %collective-permute-done.3.refs_4_), channel_id=1, source_target_pairs={{0,1},{1,0},{2,3},{3,2},{4,5},{5,4},{6,7},{7,6},{8,9},{9,8},{10,11... | collective-permute-start | bytes 786440 | tf_op jit(solution)/shard_map/ppermute | solution.py:122
  14.8 2.4 %collective-permute-done.1.refs_1_.refs_0_ = f32[16,128]{1,0:T(8,128)S(1)} collective-permute-done((f32[16,128]{1,0:T(8,128)S(1)}, f32[16,128]{1,0:T(8,128)S(1)}, u32[]{:S(2)}, u32[]{:S(2)}) %collective-permute-start.1) | collective-permute-done | bytes 8224 | tf_op jit(solution)/shard_map/ppermute | solution.py:122
  17.2 0.0 collective-permute-start.6
  17.2 0.0 collective-permute-done.2.refs_2_
  17.2 0.0 collective-permute-done.4.refs_7_.refs_6_.refs_5_
  17.2 0.0 collective-permute-done.5.refs_8_.refs_7_.refs_6_
  17.3 4.9 %shard_map.56 = (bf16[128,1024]{1,0:T(8,128)(2,1)S(1)}, f32[128,1024]{1,0:T(8,128)S(1)}, bf16[128,1024]{1,0:T(8,128)(2,1)S(1)}) custom-call(f32[16,128]{1,0:T(8,128)S(1)} %pad_maximum_fusion.1.refs_0_, f32[16,128]{1,0:T(8,128)S(1)} %collective-permute-done.1.refs_1_.refs_0_, bf16[128,1024]{1,0:T(8,128)(2,1)S(1)} %collective-permute-done.2.refs_2_, ...), custom_call_target="tpu_custom_call" | custom-call | flops 3472883712 | bytes 12976128 | tf_op jit(solution)/shard_map/pallas_call | solution.py:104
  22.1 3.3 %collective-permute-done.6.refs_4_ = bf16[128,1024]{1,0:T(8,128)(2,1)S(1)} collective-permute-done((bf16[128,1024]{1,0:T(8,128)(2,1)S(1)}, bf16[128,1024]{1,0:T(8,128)(2,1)S(1)}, u32[]{:S(2)}, u32[]{:S(2)}) %collective-permute-start.6) | collective-permute-done | bytes 262176 | tf_op jit(solution)/shard_map/ppermute | solution.py:122
  25.4 0.0 collective-permute-start.7
  25.4 1.2 %collective-permute-start.8 = (f32[32,128]{1,0:T(8,128)S(1)}, f32[32,128]{1,0:T(8,128)S(1)}, u32[]{:S(2)}, u32[]{:S(2)}) collective-permute-start(f32[32,128]{1,0:T(8,128)S(1)} %pad_maximum_fusion), channel_id=1, source_target_pairs={{0,8},{4,12},{8,0},{12,4},{1,9},{5,13},{9,1},{13,5},{2,10},{6,14},... | collective-permute-start | bytes 49160 | tf_op jit(solution)/shard_map/ppermute | solution.py:122
  26.6 1.5 %collective-permute-start.12 = (bf16[128,1024]{1,0:T(8,128)(2,1)S(1)}, bf16[128,1024]{1,0:T(8,128)(2,1)S(1)}, u32[]{:S(2)}, u32[]{:S(2)}) collective-permute-start(bf16[128,1024]{1,0:T(8,128)(2,1)S(1)} %collective-permute-done.6.refs_4_), channel_id=1, source_target_pairs={{0,1},{1,0},{2,3},{3,2},{4,5},{5,4},{6,7},{7,6},{8,9},{9,8},{10,11... | collective-permute-start | bytes 786440 | tf_op jit(solution)/shard_map/ppermute | solution.py:122
  28.1 2.0 %collective-permute-done.8.refs_1_.refs_0_ = f32[32,128]{1,0:T(8,128)S(1)} collective-permute-done((f32[32,128]{1,0:T(8,128)S(1)}, f32[32,128]{1,0:T(8,128)S(1)}, u32[]{:S(2)}, u32[]{:S(2)}) %collective-permute-start.8) | collective-permute-done | bytes 16416 | tf_op jit(solution)/shard_map/ppermute | solution.py:122
  30.0 0.0 collective-permute-done.9.refs_3_
  30.0 3.8 %shard_map.57 = (bf16[128,1024]{1,0:T(8,128)(2,1)S(1)}, f32[128,1024]{1,0:T(8,128)S(1)}) custom-call(f32[16,128]{1,0:T(8,128)S(1)} %collective-permute-done.1.refs_1_.refs_0_, f32[32,128]{1,0:T(8,128)S(1)} %collective-permute-done.8.refs_1_.refs_0_, bf16[128,1024]{1,0:T(8,128)(2,1)S(1)} %get-tuple-element.34.refs_2_, ...), custom_call_target="tpu_custom_call" | custom-call | flops 2315255808 | bytes 12320768 | tf_op jit(solution)/shard_map/pallas_call | solution.py:104
  33.9 0.0 collective-permute-done.7.refs_3_
  33.9 1.6 %collective-permute-start.13 = (bf16[128,1024]{1,0:T(8,128)(2,1)S(1)}, bf16[128,1024]{1,0:T(8,128)(2,1)S(1)}, u32[]{:S(2)}, u32[]{:S(2)}) collective-permute-start(bf16[128,1024]{1,0:T(8,128)(2,1)S(1)} %collective-permute-done.7.refs_3_), channel_id=1, source_target_pairs={{0,1},{1,0},{2,3},{3,2},{4,5},{5,4},{6,7},{7,6},{8,9},{9,8},{10,11... | collective-permute-start | bytes 786440 | tf_op jit(solution)/shard_map/ppermute | solution.py:122
  35.4 3.9 %collective-permute-start.10 = (bf16[128,1024]{1,0:T(8,128)(2,1)S(1)}, bf16[128,1024]{1,0:T(8,128)(2,1)S(1)}, u32[]{:S(2)}, u32[]{:S(2)}) collective-permute-start(bf16[128,1024]{1,0:T(8,128)(2,1)S(1)} %get-tuple-element.38), channel_id=1, source_target_pairs={{0,12},{4,0},{8,4},{12,8},{1,13},{5,1},{9,5},{13,9},{2,14},{6,2},{... | collective-permute-start | bytes 786440 | tf_op jit(solution)/shard_map/ppermute | solution.py:122
  39.3 0.4 collective-permute-start.11
  39.7 0.0 collective-permute-done.12.refs_2_
  39.7 3.8 %shard_map.58 = (bf16[128,1024]{1,0:T(8,128)(2,1)S(1)}, f32[128,1024]{1,0:T(8,128)S(1)}) custom-call(f32[32,128]{1,0:T(8,128)S(1)} %collective-permute-done.8.refs_1_.refs_0_, bf16[128,1024]{1,0:T(8,128)(2,1)S(1)} %get-tuple-element.39.refs_1_, bf16[128,1024]{1,0:T(8,128)(2,1)S(1)} %collective-permute-done.12.refs_2_, ...), custom_call_target="tpu_custom_call" | custom-call | flops 2315255808 | bytes 12320768 | tf_op jit(solution)/shard_map/pallas_call | solution.py:104
  43.5 0.6 collective-permute-start.15
  44.1 0.0 collective-permute-done.13.refs_2_
  44.1 3.3 %shard_map.59 = bf16[128,1024]{1,0:T(8,128)(2,1)S(1)} custom-call(f32[32,128]{1,0:T(8,128)S(1)} %collective-permute-done.8.refs_1_.refs_0_, bf16[128,1024]{1,0:T(8,128)(2,1)S(1)} %get-tuple-element.41.refs_1_, bf16[128,1024]{1,0:T(8,128)(2,1)S(1)} %collective-permute-done.13.refs_2_, bf16[1,1344,1024]{2,1,0:T(8,128)(2,1)S(1)} %get-tuple-element.28.refs_5_.refs_4_.refs_3_, ...), custom_call_target="tpu_custom_call" | custom-call | flops 1157627904 | bytes 11665408 | tf_op jit(solution)/shard_map/pallas_call | solution.py:104
  47.4 1.5 %collective-permute-start.14 = (bf16[128,1024]{1,0:T(8,128)(2,1)S(1)}, bf16[128,1024]{1,0:T(8,128)(2,1)S(1)}, u32[]{:S(2)}, u32[]{:S(2)}) collective-permute-start(bf16[128,1024]{1,0:T(8,128)(2,1)S(1)} %shard_map.59), channel_id=1, source_target_pairs={{0,1},{1,0},{2,3},{3,2},{4,5},{5,4},{6,7},{7,6},{8,9},{9,8},{10,11... | collective-permute-start | bytes 786440 | tf_op jit(solution)/shard_map/ppermute | solution.py:122
  49.0 0.1 add_convert_fusion.3
  49.1 1.2 %collective-permute-done.15 = bf16[128,1024]{1,0:T(8,128)(2,1)S(1)} collective-permute-done((bf16[128,1024]{1,0:T(8,128)(2,1)S(1)}, bf16[128,1024]{1,0:T(8,128)(2,1)S(1)}, u32[]{:S(2)}, u32[]{:S(2)}) %collective-permute-start.15) | collective-permute-done | bytes 262176 | tf_op jit(solution)/shard_map/ppermute | solution.py:122
  50.3 0.1 add_convert_fusion.2
  50.4 1.5 %collective-permute-start.18 = (bf16[128,1024]{1,0:T(8,128)(2,1)S(1)}, bf16[128,1024]{1,0:T(8,128)(2,1)S(1)}, u32[]{:S(2)}, u32[]{:S(2)}) collective-permute-start(bf16[128,1024]{1,0:T(8,128)(2,1)S(1)} %add_convert_fusion.2), channel_id=1, source_target_pairs={{0,8},{4,12},{8,0},{12,4},{1,9},{5,13},{9,1},{13,5},{2,10},{6,14},... | collective-permute-start | bytes 786440 | tf_op jit(solution)/shard_map/ppermute | solution.py:122
  51.9 2.0 %collective-permute-done.14 = bf16[128,1024]{1,0:T(8,128)(2,1)S(1)} collective-permute-done((bf16[128,1024]{1,0:T(8,128)(2,1)S(1)}, bf16[128,1024]{1,0:T(8,128)(2,1)S(1)}, u32[]{:S(2)}, u32[]{:S(2)}) %collective-permute-start.14) | collective-permute-done | bytes 262176 | tf_op jit(solution)/shard_map/ppermute | solution.py:122
  53.8 0.1 add_convert_fusion.1
  53.9 5.5 %collective-permute-start.17 = (bf16[128,1024]{1,0:T(8,128)(2,1)S(1)}, bf16[128,1024]{1,0:T(8,128)(2,1)S(1)}, u32[]{:S(2)}, u32[]{:S(2)}) collective-permute-start(bf16[128,1024]{1,0:T(8,128)(2,1)S(1)} %add_convert_fusion.1), channel_id=1, source_target_pairs={{0,4},{4,8},{8,12},{12,0},{1,5},{5,9},{9,13},{13,1},{2,6},{6,10},{... | collective-permute-start | bytes 786440 | tf_op jit(solution)/shard_map/ppermute | solution.py:122
  59.4 1.8 %collective-permute-start.16 = (bf16[128,1024]{1,0:T(8,128)(2,1)S(1)}, bf16[128,1024]{1,0:T(8,128)(2,1)S(1)}, u32[]{:S(2)}, u32[]{:S(2)}) collective-permute-start(bf16[128,1024]{1,0:T(8,128)(2,1)S(1)} %get-tuple-element.48), channel_id=1, source_target_pairs={{0,1},{1,0},{2,3},{3,2},{4,5},{5,4},{6,7},{7,6},{8,9},{9,8},{10,11... | collective-permute-start | bytes 786440 | tf_op jit(solution)/shard_map/ppermute | solution.py:122
  61.2 3.9 %collective-permute-done.18 = bf16[128,1024]{1,0:T(8,128)(2,1)S(1)} collective-permute-done((bf16[128,1024]{1,0:T(8,128)(2,1)S(1)}, bf16[128,1024]{1,0:T(8,128)(2,1)S(1)}, u32[]{:S(2)}, u32[]{:S(2)}) %collective-permute-start.18) | collective-permute-done | bytes 262176 | tf_op jit(solution)/shard_map/ppermute | solution.py:122
  65.2 0.0 collective-permute-done.17
  65.2 0.6 collective-permute-done.16
  65.8 0.8 %add_convert_fusion = bf16[128,1024]{1,0:T(8,128)(2,1)} fusion(bf16[128,1024]{1,0:T(8,128)(2,1)S(1)} %collective-permute-done.17, bf16[128,1024]{1,0:T(8,128)(2,1)S(1)} %collective-permute-done.18, f32[128,1024]{1,0:T(8,128)S(1)} %get-tuple-element.52, bf16[128,1024]{1,0:T(8,128)(2,1)S(1)} %collective-permute-done.16), kind=kLoop, calls=%fused_computation | loop fusion | flops 917504 | bytes 1572864 | tf_op jit(solution)/shard_map/convert_element_type | solution.py:211
  (8 shorter events, 0.0 us)
Async XLA Ops:
  0.0 17.2 %collective-permute-start.4 = (bf16[1,1344,1024]{2,1,0:T(8,128)(2,1)}, bf16[1,1344,1024]{2,1,0:T(8,128)(2,1)S(1)}, u32[]{:S(2)}, u32[]{:S(2)}) collective-permute-start(bf16[1,1344,1024]{2,1,0:T(8,128)(2,1)} %bitcast.4), channel_id=1, source_target_pairs={{0,2},{2,0},{1,3},{3,1},{4,6},{6,4},{5,7},{7,5},{8,10},{10,8},{9,1... | collective-permute-start | bytes 8257544 | tf_op jit(solution)/shard_map/ppermute | solution.py:122
  0.5 16.8 %collective-permute-start.5 = (bf16[1,1344,1024]{2,1,0:T(8,128)(2,1)}, bf16[1,1344,1024]{2,1,0:T(8,128)(2,1)S(1)}, u32[]{:S(2)}, u32[]{:S(2)}) collective-permute-start(bf16[1,1344,1024]{2,1,0:T(8,128)(2,1)} %bitcast.6), channel_id=1, source_target_pairs={{0,2},{2,0},{1,3},{3,1},{4,6},{6,4},{5,7},{7,5},{8,10},{10,8},{9,1... | collective-permute-start | bytes 8257544 | tf_op jit(solution)/shard_map/ppermute | solution.py:122
  0.5 12.8 %collective-permute-start.3 = (bf16[128,1024]{1,0:T(8,128)(2,1)}, bf16[128,1024]{1,0:T(8,128)(2,1)S(1)}, u32[]{:S(2)}, u32[]{:S(2)}) collective-permute-start(bf16[128,1024]{1,0:T(8,128)(2,1)} %refs_3_.1), channel_id=1, source_target_pairs={{0,4},{4,8},{8,12},{12,0},{1,5},{5,9},{9,13},{13,1},{2,6},{6,10},{... | collective-permute-start | bytes 786440 | tf_op jit(solution)/shard_map/ppermute | solution.py:122
  3.5 13.7 %collective-permute-start.2 = (bf16[128,1024]{1,0:T(8,128)(2,1)}, bf16[128,1024]{1,0:T(8,128)(2,1)S(1)}, u32[]{:S(2)}, u32[]{:S(2)}) collective-permute-start(bf16[128,1024]{1,0:T(8,128)(2,1)} %refs_3_.1), channel_id=1, source_target_pairs={{0,1},{1,0},{2,3},{3,2},{4,5},{5,4},{6,7},{7,6},{8,9},{9,8},{10,11... | collective-permute-start | bytes 786440 | tf_op jit(solution)/shard_map/ppermute | solution.py:122
  5.7 6.0 %collective-permute-start = (f32[8,128]{1,0:T(8,128)S(1)}, f32[8,128]{1,0:T(8,128)S(1)}, u32[]{:S(2)}, u32[]{:S(2)}) collective-permute-start(f32[8,128]{1,0:T(8,128)S(1)} %select_reduce_fusion), channel_id=1, source_target_pairs={{0,1},{1,0},{2,3},{3,2},{4,5},{5,4},{6,7},{7,6},{8,9},{9,8},{10,11... | collective-permute-start | bytes 12296 | tf_op jit(solution)/shard_map/ppermute | solution.py:122
  6.3 1.8 %copy-start = (bf16[1,1024,1344]{1,2,0:T(8,128)(2,1)S(1)}, bf16[1,1024,1344]{1,2,0:T(8,128)(2,1)}, u32[]{:S(2)}) copy-start(bf16[1,1024,1344]{1,2,0:T(8,128)(2,1)} %param.8) | copy-start | bytes 8257540
  8.0 1.8 %copy-start.1 = (bf16[1,1024,1344]{1,2,0:T(8,128)(2,1)S(1)}, bf16[1,1024,1344]{1,2,0:T(8,128)(2,1)}, u32[]{:S(2)}) copy-start(bf16[1,1024,1344]{1,2,0:T(8,128)(2,1)} %param.9) | copy-start | bytes 8257540
  9.8 7.4 %copy-start.2 = (bf16[128,1024]{1,0:T(8,128)(2,1)S(1)}, bf16[128,1024]{1,0:T(8,128)(2,1)}, u32[]{:S(2)}) copy-start(bf16[128,1024]{1,0:T(8,128)(2,1)} %refs_3_.1) | copy-start | bytes 786436
  11.8 5.4 %collective-permute-start.1 = (f32[16,128]{1,0:T(8,128)S(1)}, f32[16,128]{1,0:T(8,128)S(1)}, u32[]{:S(2)}, u32[]{:S(2)}) collective-permute-start(f32[16,128]{1,0:T(8,128)S(1)} %pad_maximum_fusion.1.refs_0_), channel_id=1, source_target_pairs={{0,4},{4,8},{8,12},{12,0},{1,5},{5,9},{9,13},{13,1},{2,6},{6,10},{... | collective-permute-start | bytes 24584 | tf_op jit(solution)/shard_map/ppermute | solution.py:122
  13.4 16.7 %collective-permute-start.9 = (bf16[128,1024]{1,0:T(8,128)(2,1)S(1)}, bf16[128,1024]{1,0:T(8,128)(2,1)S(1)}, u32[]{:S(2)}, u32[]{:S(2)}) collective-permute-start(bf16[128,1024]{1,0:T(8,128)(2,1)S(1)} %collective-permute-done.3.refs_4_), channel_id=1, source_target_pairs={{0,1},{1,0},{2,3},{3,2},{4,5},{5,4},{6,7},{7,6},{8,9},{9,8},{10,11... | collective-permute-start | bytes 786440 | tf_op jit(solution)/shard_map/ppermute | solution.py:122
  17.2 8.2 %collective-permute-start.6 = (bf16[128,1024]{1,0:T(8,128)(2,1)S(1)}, bf16[128,1024]{1,0:T(8,128)(2,1)S(1)}, u32[]{:S(2)}, u32[]{:S(2)}) collective-permute-start(bf16[128,1024]{1,0:T(8,128)(2,1)S(1)} %collective-permute-done.3.refs_4_), channel_id=1, source_target_pairs={{0,4},{4,8},{8,12},{12,0},{1,5},{5,9},{9,13},{13,1},{2,6},{6,10},{... | collective-permute-start | bytes 786440 | tf_op jit(solution)/shard_map/ppermute | solution.py:122
  25.4 8.5 %collective-permute-start.7 = (bf16[128,1024]{1,0:T(8,128)(2,1)S(1)}, bf16[128,1024]{1,0:T(8,128)(2,1)S(1)}, u32[]{:S(2)}, u32[]{:S(2)}) collective-permute-start(bf16[128,1024]{1,0:T(8,128)(2,1)S(1)} %collective-permute-done.6.refs_4_), channel_id=1, source_target_pairs={{0,4},{4,8},{8,12},{12,0},{1,5},{5,9},{9,13},{13,1},{2,6},{6,10},{... | collective-permute-start | bytes 786440 | tf_op jit(solution)/shard_map/ppermute | solution.py:122
  25.4 4.6 %collective-permute-start.8 = (f32[32,128]{1,0:T(8,128)S(1)}, f32[32,128]{1,0:T(8,128)S(1)}, u32[]{:S(2)}, u32[]{:S(2)}) collective-permute-start(f32[32,128]{1,0:T(8,128)S(1)} %pad_maximum_fusion), channel_id=1, source_target_pairs={{0,8},{4,12},{8,0},{12,4},{1,9},{5,13},{9,1},{13,5},{2,10},{6,14},... | collective-permute-start | bytes 49160 | tf_op jit(solution)/shard_map/ppermute | solution.py:122
  26.6 13.1 %collective-permute-start.12 = (bf16[128,1024]{1,0:T(8,128)(2,1)S(1)}, bf16[128,1024]{1,0:T(8,128)(2,1)S(1)}, u32[]{:S(2)}, u32[]{:S(2)}) collective-permute-start(bf16[128,1024]{1,0:T(8,128)(2,1)S(1)} %collective-permute-done.6.refs_4_), channel_id=1, source_target_pairs={{0,1},{1,0},{2,3},{3,2},{4,5},{5,4},{6,7},{7,6},{8,9},{9,8},{10,11... | collective-permute-start | bytes 786440 | tf_op jit(solution)/shard_map/ppermute | solution.py:122
  33.9 10.3 %collective-permute-start.13 = (bf16[128,1024]{1,0:T(8,128)(2,1)S(1)}, bf16[128,1024]{1,0:T(8,128)(2,1)S(1)}, u32[]{:S(2)}, u32[]{:S(2)}) collective-permute-start(bf16[128,1024]{1,0:T(8,128)(2,1)S(1)} %collective-permute-done.7.refs_3_), channel_id=1, source_target_pairs={{0,1},{1,0},{2,3},{3,2},{4,5},{5,4},{6,7},{7,6},{8,9},{9,8},{10,11... | collective-permute-start | bytes 786440 | tf_op jit(solution)/shard_map/ppermute | solution.py:122
  35.4 13.5 %collective-permute-start.10 = (bf16[128,1024]{1,0:T(8,128)(2,1)S(1)}, bf16[128,1024]{1,0:T(8,128)(2,1)S(1)}, u32[]{:S(2)}, u32[]{:S(2)}) collective-permute-start(bf16[128,1024]{1,0:T(8,128)(2,1)S(1)} %get-tuple-element.38), channel_id=1, source_target_pairs={{0,12},{4,0},{8,4},{12,8},{1,13},{5,1},{9,5},{13,9},{2,14},{6,2},{... | collective-permute-start | bytes 786440 | tf_op jit(solution)/shard_map/ppermute | solution.py:122
  39.3 9.6 %collective-permute-start.11 = (bf16[128,1024]{1,0:T(8,128)(2,1)S(1)}, bf16[128,1024]{1,0:T(8,128)(2,1)S(1)}, u32[]{:S(2)}, u32[]{:S(2)}) collective-permute-start(bf16[128,1024]{1,0:T(8,128)(2,1)S(1)} %get-tuple-element.39.refs_1_), channel_id=1, source_target_pairs={{0,12},{4,0},{8,4},{12,8},{1,13},{5,1},{9,5},{13,9},{2,14},{6,2},{... | collective-permute-start | bytes 786440 | tf_op jit(solution)/shard_map/ppermute | solution.py:122
  43.5 6.8 %collective-permute-start.15 = (bf16[128,1024]{1,0:T(8,128)(2,1)S(1)}, bf16[128,1024]{1,0:T(8,128)(2,1)S(1)}, u32[]{:S(2)}, u32[]{:S(2)}) collective-permute-start(bf16[128,1024]{1,0:T(8,128)(2,1)S(1)} %get-tuple-element.41.refs_1_), channel_id=1, source_target_pairs={{0,1},{1,0},{2,3},{3,2},{4,5},{5,4},{6,7},{7,6},{8,9},{9,8},{10,11... | collective-permute-start | bytes 786440 | tf_op jit(solution)/shard_map/ppermute | solution.py:122
  47.4 6.4 %collective-permute-start.14 = (bf16[128,1024]{1,0:T(8,128)(2,1)S(1)}, bf16[128,1024]{1,0:T(8,128)(2,1)S(1)}, u32[]{:S(2)}, u32[]{:S(2)}) collective-permute-start(bf16[128,1024]{1,0:T(8,128)(2,1)S(1)} %shard_map.59), channel_id=1, source_target_pairs={{0,1},{1,0},{2,3},{3,2},{4,5},{5,4},{6,7},{7,6},{8,9},{9,8},{10,11... | collective-permute-start | bytes 786440 | tf_op jit(solution)/shard_map/ppermute | solution.py:122
  50.4 14.8 %collective-permute-start.18 = (bf16[128,1024]{1,0:T(8,128)(2,1)S(1)}, bf16[128,1024]{1,0:T(8,128)(2,1)S(1)}, u32[]{:S(2)}, u32[]{:S(2)}) collective-permute-start(bf16[128,1024]{1,0:T(8,128)(2,1)S(1)} %add_convert_fusion.2), channel_id=1, source_target_pairs={{0,8},{4,12},{8,0},{12,4},{1,9},{5,13},{9,1},{13,5},{2,10},{6,14},... | collective-permute-start | bytes 786440 | tf_op jit(solution)/shard_map/ppermute | solution.py:122
  53.9 11.3 %collective-permute-start.17 = (bf16[128,1024]{1,0:T(8,128)(2,1)S(1)}, bf16[128,1024]{1,0:T(8,128)(2,1)S(1)}, u32[]{:S(2)}, u32[]{:S(2)}) collective-permute-start(bf16[128,1024]{1,0:T(8,128)(2,1)S(1)} %add_convert_fusion.1), channel_id=1, source_target_pairs={{0,4},{4,8},{8,12},{12,0},{1,5},{5,9},{9,13},{13,1},{2,6},{6,10},{... | collective-permute-start | bytes 786440 | tf_op jit(solution)/shard_map/ppermute | solution.py:122
  59.4 6.4 %collective-permute-start.16 = (bf16[128,1024]{1,0:T(8,128)(2,1)S(1)}, bf16[128,1024]{1,0:T(8,128)(2,1)S(1)}, u32[]{:S(2)}, u32[]{:S(2)}) collective-permute-start(bf16[128,1024]{1,0:T(8,128)(2,1)S(1)} %get-tuple-element.48), channel_id=1, source_target_pairs={{0,1},{1,0},{2,3},{3,2},{4,5},{5,4},{6,7},{7,6},{8,9},{9,8},{10,11... | collective-permute-start | bytes 786440 | tf_op jit(solution)/shard_map/ppermute | solution.py:122

commit v16 on v15

--- a/solution.py
+++ b/solution.py
@@ -91,8 +91,11 @@
                 sums[b] = sums[b] + lax.dot_general(
                     picks[g][j], gated, TN, preferred_element_type=jnp.float32
                 )
-    for b in range(blocks):
-        out_refs[b][...] = sums[b].astype(out_refs[b].dtype)
+    b = 0
+    for out_ref in out_refs:
+        for start in range(0, out_ref.shape[0], block):
+            out_ref[start : start + block, :] = sums[b].astype(out_ref.dtype)
+            b += 1
 
 
 def run_experts(after, gates, sources, arrived, tables, kinds, slots):
@@ -103,11 +106,11 @@
     whole = pl.BlockSpec(memory_space=pltpu.VMEM)
     return pl.pallas_call(
         functools.partial(expert_kernel, block, slots, unit, number, sources, len(after)),
-        out_shape=[jax.ShapeDtypeStruct((block, width), kind) for kind in kinds],
+        out_shape=[jax.ShapeDtypeStruct((count * block, width), kind) for kind, count in kinds],
         in_specs=[whole] * len(gates)
         + [pl.BlockSpec(memory_space=pl.ANY)] * len(after)
         + [whole] * (blocks + len(tables)),
-        out_specs=[whole] * blocks,
+        out_specs=[whole] * len(kinds),
         compiler_params=pltpu.CompilerParams(vmem_limit_bytes=30 * 1024 * 1024),
         cost_estimate=pl.CostEstimate(
             flops=4 * number * blocks * slots * width * (hidden + block),
@@ -149,7 +152,7 @@
         held = jnp.concatenate([held, weights[-1]], axis=0)
     last = depth - 1
     kept, others = {}, {}
-    totals, home = {}, None
+    totals = {}
     firsts = []
 
     def total(r, *behind):
@@ -163,12 +166,11 @@
 
     for j in range(depth):
         handed = [shift(ring[j], "sub", s) for s in range(1, subs)]
-        fresh = ([0] if j == 0 else []) + [j + 1] * (j < last)
-        kinds = [jnp.bfloat16] * len(handed)
-        kinds += [jnp.bfloat16 if r == 1 else jnp.float32 for r in fresh]
+        fresh = [[0], [1, 2][:last]][j] if j < 2 else [j + 1][: last - j]
+        kinds = [(jnp.bfloat16, 1)] * len(handed) + [(jnp.float32, 1)] * len(fresh)
+        if j == 1:
+            kinds = [(jnp.bfloat16, subs)] + kinds[subs:]
         after = firsts[-1:]
-        if j == last and j > 1:
-            home = kept[0] + shift(follow(kept[1], ring[last]), "z", -1).astype(jnp.float32)
         if j > 3:
             totals[j - 2] = total(j - 2, firsts[-1]).astype(jnp.bfloat16)
             after = after + [totals[j - 2]]
@@ -178,23 +180,25 @@
         firsts.append(partial[0])
         if j + 2 < depth:
             ring.append(follow(shift(ring[-1], "z", 1), partial[0]))
-        for r, rows in zip(fresh, partial[subs - 1 :]):
+        if j == 1:
+            joint, *partial = partial
+            fresh = fresh[1:]
+        else:
+            others[j], partial = partial[: subs - 1], partial[subs - 1 :]
+        for r, rows in zip(fresh, partial):
             kept[r] = rows
-        others[j] = partial[: subs - 1]
-    if home is None:
-        home = kept[0] + sum(shift(kept[r], "z", -r).astype(jnp.float32) for r in range(1, depth))
-    joined = others[0]
+    home, joined = kept[0], others[0]
     if depth > 1:
+        sent = follow(shift(follow(joint, ring[last]), "z", -1), firsts[-1])
+        sent = [sent[s * block : (s + 1) * block].astype(jnp.float32) for s in range(subs)]
         joined = [
-            (
-                mine.astype(jnp.float32)
-                + shift(follow(rows, ring[last]), "z", -1).astype(jnp.float32)
-            ).astype(jnp.bfloat16)
-            for mine, rows in zip(others[0], others[1])
+            (mine.astype(jnp.float32) + rows).astype(jnp.bfloat16)
+            for mine, rows in zip(others[0], sent)
         ]
+        home = home + sent[-1]
     for r in range(2, depth):
         if r not in totals:
-            behind = [firsts[-1]] + ([home, *joined] if r < last else [totals[r - 1]] * (r > 2))
+            behind = [firsts[-1]] + ([totals[r - 1]] * (r > 2) + [home, *joined] if r == last else [])
             totals[r] = total(r, *behind).astype(jnp.bfloat16)
     came = []
     for r in range(2, depth):

time: 66.8 us -> 64.2 us (0.961)
  starting transfers between devices: 28 us -> 18.3 us
  waiting for transfers between devices: 16.6 us -> 23.6 us
    ppermute x19 -> x18, starting transfers between devices: 28 us -> 18.3 us  [shift(): lax.ppermute(array, axis, [(i, (i + step) % size) for i in range(size)])]
    ppermute x19 -> x18, waiting for transfers between devices: 16.6 us -> 23.6 us  [shift(): lax.ppermute(array, axis, [(i, (i + step) % size) for i in range(size)])]
  transfers between devices with their start and end apart: 19 -> 18, of which waited for: 8 -> 7; matrix products, arithmetic and copies ran while one was open for 1% -> 2% of each run, Pallas kernels for 25% -> 26%
where the time goes in v16:
time: 64.2 us; the launch traced here: 64 us
  waiting for transfers between devices  23.6 us (37%)
  starting transfers between devices  18.3 us (29%)
  Pallas kernels  16.5 us (26%)
  local copies, waits for them, and re-layouts  3.56 us (6%)
  other arithmetic  1.83 us (3%)
    ppermute x18, waiting for transfers between devices, shift(): lax.ppermute(array, axis, [(i, (i + step) % size) for i in range(size)])  23.6 us
    ppermute x18, starting transfers between devices, shift(): lax.ppermute(array, axis, [(i, (i + step) % size) for i in range(size)])  18.3 us
    pallas_call x4, Pallas kernels, run_experts(): pl.pallas_call(functools.partial(expert_kernel, block, slots, unit, numbe...  15.8 us
    unnamed x6, local copies, waits for them, and re-layouts  3.56 us
  transfers between devices with their start and end apart: 18, of which 7 were waited for; matrix products, arithmetic and copies ran while one was open for 2% of the time, Pallas kernels for 26%

profile of v16, /device:TPU:0, one launch (start us, length us, event | category | flops | bytes accessed | tf_op | source)
XLA Modules:
  0.0 64.0 jit_solution(3486455433908303293)
XLA Ops:
  0.0 0.5 collective-permute-start.2
  0.5 0.1 collective-permute-start.3
  0.5 3.0 %collective-permute-start.6 = (bf16[128,1024]{1,0:T(8,128)(2,1)}, bf16[128,1024]{1,0:T(8,128)(2,1)S(1)}, u32[]{:S(2)}, u32[]{:S(2)}) collective-permute-start(bf16[128,1024]{1,0:T(8,128)(2,1)} %refs_2_.1), channel_id=1, source_target_pairs={{0,4},{4,8},{8,12},{12,0},{1,5},{5,9},{9,13},{13,1},{2,6},{6,10},{... | collective-permute-start | bytes 786440 | tf_op jit(solution)/shard_map/ppermute | solution.py:125
  3.5 1.5 %collective-permute-start.1 = (bf16[128,1024]{1,0:T(8,128)(2,1)}, bf16[128,1024]{1,0:T(8,128)(2,1)S(1)}, u32[]{:S(2)}, u32[]{:S(2)}) collective-permute-start(bf16[128,1024]{1,0:T(8,128)(2,1)} %refs_2_.1), channel_id=1, source_target_pairs={{0,1},{1,0},{2,3},{3,2},{4,5},{5,4},{6,7},{7,6},{8,9},{9,8},{10,11... | collective-permute-start | bytes 786440 | tf_op jit(solution)/shard_map/ppermute | solution.py:125
  5.0 0.7 %select_reduce_fusion = f32[8,128]{1,0:T(8,128)S(1)} fusion(f32[4,128]{1,0:T(4,128)} %bitcast.8, s32[4,128]{1,0:T(4,128)} %bitcast.9), kind=kLoop, calls=%fused_computation.6 | loop fusion | flops 11264 | bytes 8192 | tf_op jit(solution)/shard_map/reduce_sum | solution.py:144
  5.7 0.5 collective-permute-start
  6.3 1.8 %copy-done = bf16[1,1024,1344]{1,2,0:T(8,128)(2,1)S(1)} copy-done((bf16[1,1024,1344]{1,2,0:T(8,128)(2,1)S(1)}, bf16[1,1024,1344]{1,2,0:T(8,128)(2,1)}, u32[]{:S(2)}) %copy-start) | copy-done | bytes 2752536
  8.1 1.8 %copy-done.1 = bf16[1,1024,1344]{1,2,0:T(8,128)(2,1)S(1)} copy-done((bf16[1,1024,1344]{1,2,0:T(8,128)(2,1)S(1)}, bf16[1,1024,1344]{1,2,0:T(8,128)(2,1)}, u32[]{:S(2)}) %copy-start.1) | copy-done | bytes 2752536
  9.8 0.7 %shard_map.55 = (bf16[1,1344,1024]{2,1,0:T(8,128)(2,1)S(1)}, bf16[1,1344,1024]{2,1,0:T(8,128)(2,1)S(1)}) custom-call(bf16[1,1344,1024]{2,1,0:T(8,128)(2,1)S(1)} %bitcast.5, bf16[1,1344,1024]{2,1,0:T(8,128)(2,1)S(1)} %bitcast.7), custom_call_target="tpu_custom_call" | custom-call | tf_op jit(solution)/shard_map/pallas_call | solution.py:28
  10.5 1.2 %collective-permute-done = f32[8,128]{1,0:T(8,128)S(1)} collective-permute-done((f32[8,128]{1,0:T(8,128)S(1)}, f32[8,128]{1,0:T(8,128)S(1)}, u32[]{:S(2)}, u32[]{:S(2)}) %collective-permute-start) | collective-permute-done | bytes 4128 | tf_op jit(solution)/shard_map/ppermute | solution.py:125
  11.8 1.6 %collective-permute-start.4 = (f32[16,128]{1,0:T(8,128)S(1)}, f32[16,128]{1,0:T(8,128)S(1)}, u32[]{:S(2)}, u32[]{:S(2)}) collective-permute-start(f32[16,128]{1,0:T(8,128)S(1)} %pad_maximum_fusion.1.refs_0_), channel_id=1, source_target_pairs={{0,4},{4,8},{8,12},{12,0},{1,5},{5,9},{9,13},{13,1},{2,6},{6,10},{... | collective-permute-start | bytes 24584 | tf_op jit(solution)/shard_map/ppermute | solution.py:125
  13.3 0.0 collective-permute-done.6.refs_4_
  13.4 1.6 %collective-permute-start.8 = (bf16[128,1024]{1,0:T(8,128)(2,1)S(1)}, bf16[128,1024]{1,0:T(8,128)(2,1)S(1)}, u32[]{:S(2)}, u32[]{:S(2)}) collective-permute-start(bf16[128,1024]{1,0:T(8,128)(2,1)S(1)} %collective-permute-done.6.refs_4_), channel_id=1, source_target_pairs={{0,4},{4,8},{8,12},{12,0},{1,5},{5,9},{9,13},{13,1},{2,6},{6,10},{... | collective-permute-start | bytes 786440 | tf_op jit(solution)/shard_map/ppermute | solution.py:125
  14.9 2.3 %collective-permute-done.4.refs_0_ = f32[16,128]{1,0:T(8,128)S(1)} collective-permute-done((f32[16,128]{1,0:T(8,128)S(1)}, f32[16,128]{1,0:T(8,128)S(1)}, u32[]{:S(2)}, u32[]{:S(2)}) %collective-permute-start.4) | collective-permute-done | bytes 8224 | tf_op jit(solution)/shard_map/ppermute | solution.py:125
  17.3 1.5 %collective-permute-start.7 = (bf16[128,1024]{1,0:T(8,128)(2,1)S(1)}, bf16[128,1024]{1,0:T(8,128)(2,1)S(1)}, u32[]{:S(2)}, u32[]{:S(2)}) collective-permute-start(bf16[128,1024]{1,0:T(8,128)(2,1)S(1)} %collective-permute-done.6.refs_4_), channel_id=1, source_target_pairs={{0,1},{1,0},{2,3},{3,2},{4,5},{5,4},{6,7},{7,6},{8,9},{9,8},{10,11... | collective-permute-start | bytes 786440 | tf_op jit(solution)/shard_map/ppermute | solution.py:125
  18.8 0.0 collective-permute-done.1.refs_1_
  18.8 0.9 %collective-permute-start.5 = (f32[32,128]{1,0:T(8,128)S(1)}, f32[32,128]{1,0:T(8,128)S(1)}, u32[]{:S(2)}, u32[]{:S(2)}) collective-permute-start(f32[32,128]{1,0:T(8,128)S(1)} %pad_maximum_fusion), channel_id=1, source_target_pairs={{0,8},{4,12},{8,0},{12,4},{1,9},{5,13},{9,1},{13,5},{2,10},{6,14},... | collective-permute-start | bytes 49160 | tf_op jit(solution)/shard_map/ppermute | solution.py:125
  19.7 0.0 collective-permute-done.2.refs_5_.refs_8_.refs_6_
  19.7 0.0 collective-permute-done.3.refs_6_.refs_9_.refs_7_
  19.7 3.8 %shard_map.56 = (bf16[128,1024]{1,0:T(8,128)(2,1)S(1)}, f32[128,1024]{1,0:T(8,128)S(1)}) custom-call(f32[16,128]{1,0:T(8,128)S(1)} %pad_maximum_fusion.1.refs_0_, bf16[128,1024]{1,0:T(8,128)(2,1)S(1)} %collective-permute-done.1.refs_1_, bf16[128,1024]{1,0:T(8,128)(2,1)S(1)} %copy-done.2, ...), custom_call_target="tpu_custom_call" | custom-call | flops 2315255808 | bytes 12320768 | tf_op jit(solution)/shard_map/pallas_call | solution.py:107
  23.5 0.0 collective-permute-done.8.refs_5_
  23.5 0.6 collective-permute-start.11
  24.1 0.2 collective-permute-start.9
  24.3 0.0 collective-permute-done.5.refs_1_.refs_0_
  24.3 0.0 collective-permute-done.7.refs_3_
  24.3 4.9 %shard_map.57 = (bf16[256,1024]{1,0:T(8,128)(2,1)S(1)}, f32[128,1024]{1,0:T(8,128)S(1)}) custom-call(f32[16,128]{1,0:T(8,128)S(1)} %collective-permute-done.4.refs_0_, f32[32,128]{1,0:T(8,128)S(1)} %collective-permute-done.5.refs_1_.refs_0_, bf16[128,1024]{1,0:T(8,128)(2,1)S(1)} %get-tuple-element.31.refs_2_, ...), custom_call_target="tpu_custom_call" | custom-call | flops 3472883712 | bytes 12976128 | tf_op jit(solution)/shard_map/pallas_call | solution.py:107
  29.2 3.6 %collective-permute-done.9.refs_3_ = bf16[128,1024]{1,0:T(8,128)(2,1)S(1)} collective-permute-done((bf16[128,1024]{1,0:T(8,128)(2,1)S(1)}, bf16[128,1024]{1,0:T(8,128)(2,1)S(1)}, u32[]{:S(2)}, u32[]{:S(2)}) %collective-permute-start.9) | collective-permute-done | bytes 262176 | tf_op jit(solution)/shard_map/ppermute | solution.py:125
  32.8 2.7 %collective-permute-start.12 = (bf16[128,1024]{1,0:T(8,128)(2,1)S(1)}, bf16[128,1024]{1,0:T(8,128)(2,1)S(1)}, u32[]{:S(2)}, u32[]{:S(2)}) collective-permute-start(bf16[128,1024]{1,0:T(8,128)(2,1)S(1)} %collective-permute-done.9.refs_3_), channel_id=1, source_target_pairs={{0,1},{1,0},{2,3},{3,2},{4,5},{5,4},{6,7},{7,6},{8,9},{9,8},{10,11... | collective-permute-start | bytes 786440 | tf_op jit(solution)/shard_map/ppermute | solution.py:125
  35.5 0.0 collective-permute-start.10
  35.5 0.0 collective-permute-done.11.refs_2_
  35.5 3.8 %shard_map.58 = (bf16[128,1024]{1,0:T(8,128)(2,1)S(1)}, f32[128,1024]{1,0:T(8,128)S(1)}) custom-call(f32[32,128]{1,0:T(8,128)S(1)} %collective-permute-done.5.refs_1_.refs_0_, bf16[256,1024]{1,0:T(8,128)(2,1)S(1)} %get-tuple-element.36.refs_1_, bf16[128,1024]{1,0:T(8,128)(2,1)S(1)} %collective-permute-done.11.refs_2_, ...), custom_call_target="tpu_custom_call" | custom-call | flops 2315255808 | bytes 12320768 | tf_op jit(solution)/shard_map/pallas_call | solution.py:107
  39.4 0.1 collective-permute-start.14
  39.4 3.2 %collective-permute-done.12.refs_2_ = bf16[128,1024]{1,0:T(8,128)(2,1)S(1)} collective-permute-done((bf16[128,1024]{1,0:T(8,128)(2,1)S(1)}, bf16[128,1024]{1,0:T(8,128)(2,1)S(1)}, u32[]{:S(2)}, u32[]{:S(2)}) %collective-permute-start.12) | collective-permute-done | bytes 262176 | tf_op jit(solution)/shard_map/ppermute | solution.py:125
  42.7 3.3 %shard_map.59 = bf16[128,1024]{1,0:T(8,128)(2,1)S(1)} custom-call(f32[32,128]{1,0:T(8,128)S(1)} %collective-permute-done.5.refs_1_.refs_0_, bf16[128,1024]{1,0:T(8,128)(2,1)S(1)} %get-tuple-element.37.refs_1_, bf16[128,1024]{1,0:T(8,128)(2,1)S(1)} %collective-permute-done.12.refs_2_, bf16[1,1344,1024]{2,1,0:T(8,128)(2,1)S(1)} %get-tuple-element.27.refs_3_.refs_6_.refs_4_, ...), custom_call_target="tpu_custom_call" | custom-call | flops 1157627904 | bytes 11665408 | tf_op jit(solution)/shard_map/pallas_call | solution.py:107
  45.9 1.6 %collective-permute-start.13 = (bf16[128,1024]{1,0:T(8,128)(2,1)S(1)}, bf16[128,1024]{1,0:T(8,128)(2,1)S(1)}, u32[]{:S(2)}, u32[]{:S(2)}) collective-permute-start(bf16[128,1024]{1,0:T(8,128)(2,1)S(1)} %shard_map.59), channel_id=1, source_target_pairs={{0,1},{1,0},{2,3},{3,2},{4,5},{5,4},{6,7},{7,6},{8,9},{9,8},{10,11... | collective-permute-start | bytes 786440 | tf_op jit(solution)/shard_map/ppermute | solution.py:125
  47.5 0.5 collective-permute-done.14
  48.0 0.1 add_convert_fusion.2
  48.1 0.1 collective-permute-start.17
  48.1 6.2 %collective-permute-done.13 = bf16[128,1024]{1,0:T(8,128)(2,1)S(1)} collective-permute-done((bf16[128,1024]{1,0:T(8,128)(2,1)S(1)}, bf16[128,1024]{1,0:T(8,128)(2,1)S(1)}, u32[]{:S(2)}, u32[]{:S(2)}) %collective-permute-start.13) | collective-permute-done | bytes 262176 | tf_op jit(solution)/shard_map/ppermute | solution.py:125
  54.4 0.0 collective-permute-done.10
  54.4 0.2 add_convert_fusion.3
  54.5 0.1 add_convert_fusion.1
  54.6 0.1 collective-permute-start.16
  54.7 2.0 %collective-permute-start.15 = (bf16[128,1024]{1,0:T(8,128)(2,1)S(1)}, bf16[128,1024]{1,0:T(8,128)(2,1)S(1)}, u32[]{:S(2)}, u32[]{:S(2)}) collective-permute-start(bf16[128,1024]{1,0:T(8,128)(2,1)S(1)} %get-tuple-element.46), channel_id=1, source_target_pairs={{0,1},{1,0},{2,3},{3,2},{4,5},{5,4},{6,7},{7,6},{8,9},{9,8},{10,11... | collective-permute-start | bytes 786440 | tf_op jit(solution)/shard_map/ppermute | solution.py:125
  56.7 6.4 %collective-permute-done.17 = bf16[128,1024]{1,0:T(8,128)(2,1)S(1)} collective-permute-done((bf16[128,1024]{1,0:T(8,128)(2,1)S(1)}, bf16[128,1024]{1,0:T(8,128)(2,1)S(1)}, u32[]{:S(2)}, u32[]{:S(2)}) %collective-permute-start.17) | collective-permute-done | bytes 262176 | tf_op jit(solution)/shard_map/ppermute | solution.py:125
  63.1 0.0 collective-permute-done.16
  63.1 0.0 collective-permute-done.15
  63.1 0.9 %add_convert_fusion = bf16[128,1024]{1,0:T(8,128)(2,1)} fusion(bf16[128,1024]{1,0:T(8,128)(2,1)S(1)} %collective-permute-done.16, bf16[128,1024]{1,0:T(8,128)(2,1)S(1)} %collective-permute-done.17, f32[128,1024]{1,0:T(8,128)S(1)} %get-tuple-element.50, bf16[128,1024]{1,0:T(8,128)(2,1)S(1)} %collective-permute-done.15), kind=kLoop, calls=%fused_computation | loop fusion | flops 917504 | bytes 1572864 | tf_op jit(solution)/shard_map/convert_element_type | solution.py:215
  (6 shorter events, 0.0 us)
Async XLA Ops:
  0.0 19.7 %collective-permute-start.2 = (bf16[1,1344,1024]{2,1,0:T(8,128)(2,1)}, bf16[1,1344,1024]{2,1,0:T(8,128)(2,1)S(1)}, u32[]{:S(2)}, u32[]{:S(2)}) collective-permute-start(bf16[1,1344,1024]{2,1,0:T(8,128)(2,1)} %bitcast.4), channel_id=1, source_target_pairs={{0,2},{2,0},{1,3},{3,1},{4,6},{6,4},{5,7},{7,5},{8,10},{10,8},{9,1... | collective-permute-start | bytes 8257544 | tf_op jit(solution)/shard_map/ppermute | solution.py:125
  0.5 19.2 %collective-permute-start.3 = (bf16[1,1344,1024]{2,1,0:T(8,128)(2,1)}, bf16[1,1344,1024]{2,1,0:T(8,128)(2,1)S(1)}, u32[]{:S(2)}, u32[]{:S(2)}) collective-permute-start(bf16[1,1344,1024]{2,1,0:T(8,128)(2,1)} %bitcast.6), channel_id=1, source_target_pairs={{0,2},{2,0},{1,3},{3,1},{4,6},{6,4},{5,7},{7,5},{8,10},{10,8},{9,1... | collective-permute-start | bytes 8257544 | tf_op jit(solution)/shard_map/ppermute | solution.py:125
  0.5 12.8 %collective-permute-start.6 = (bf16[128,1024]{1,0:T(8,128)(2,1)}, bf16[128,1024]{1,0:T(8,128)(2,1)S(1)}, u32[]{:S(2)}, u32[]{:S(2)}) collective-permute-start(bf16[128,1024]{1,0:T(8,128)(2,1)} %refs_2_.1), channel_id=1, source_target_pairs={{0,4},{4,8},{8,12},{12,0},{1,5},{5,9},{9,13},{13,1},{2,6},{6,10},{... | collective-permute-start | bytes 786440 | tf_op jit(solution)/shard_map/ppermute | solution.py:125
  3.5 15.2 %collective-permute-start.1 = (bf16[128,1024]{1,0:T(8,128)(2,1)}, bf16[128,1024]{1,0:T(8,128)(2,1)S(1)}, u32[]{:S(2)}, u32[]{:S(2)}) collective-permute-start(bf16[128,1024]{1,0:T(8,128)(2,1)} %refs_2_.1), channel_id=1, source_target_pairs={{0,1},{1,0},{2,3},{3,2},{4,5},{5,4},{6,7},{7,6},{8,9},{9,8},{10,11... | collective-permute-start | bytes 786440 | tf_op jit(solution)/shard_map/ppermute | solution.py:125
  5.7 6.0 %collective-permute-start = (f32[8,128]{1,0:T(8,128)S(1)}, f32[8,128]{1,0:T(8,128)S(1)}, u32[]{:S(2)}, u32[]{:S(2)}) collective-permute-start(f32[8,128]{1,0:T(8,128)S(1)} %select_reduce_fusion), channel_id=1, source_target_pairs={{0,1},{1,0},{2,3},{3,2},{4,5},{5,4},{6,7},{7,6},{8,9},{9,8},{10,11... | collective-permute-start | bytes 12296 | tf_op jit(solution)/shard_map/ppermute | solution.py:125
  6.3 1.8 %copy-start = (bf16[1,1024,1344]{1,2,0:T(8,128)(2,1)S(1)}, bf16[1,1024,1344]{1,2,0:T(8,128)(2,1)}, u32[]{:S(2)}) copy-start(bf16[1,1024,1344]{1,2,0:T(8,128)(2,1)} %param.8) | copy-start | bytes 8257540
  8.0 1.8 %copy-start.1 = (bf16[1,1024,1344]{1,2,0:T(8,128)(2,1)S(1)}, bf16[1,1024,1344]{1,2,0:T(8,128)(2,1)}, u32[]{:S(2)}) copy-start(bf16[1,1024,1344]{1,2,0:T(8,128)(2,1)} %param.9) | copy-start | bytes 8257540
  9.8 9.8 %copy-start.2 = (bf16[128,1024]{1,0:T(8,128)(2,1)S(1)}, bf16[128,1024]{1,0:T(8,128)(2,1)}, u32[]{:S(2)}) copy-start(bf16[128,1024]{1,0:T(8,128)(2,1)} %refs_2_.1) | copy-start | bytes 786436
  11.8 5.5 %collective-permute-start.4 = (f32[16,128]{1,0:T(8,128)S(1)}, f32[16,128]{1,0:T(8,128)S(1)}, u32[]{:S(2)}, u32[]{:S(2)}) collective-permute-start(f32[16,128]{1,0:T(8,128)S(1)} %pad_maximum_fusion.1.refs_0_), channel_id=1, source_target_pairs={{0,4},{4,8},{8,12},{12,0},{1,5},{5,9},{9,13},{13,1},{2,6},{6,10},{... | collective-permute-start | bytes 24584 | tf_op jit(solution)/shard_map/ppermute | solution.py:125
  13.4 10.2 %collective-permute-start.8 = (bf16[128,1024]{1,0:T(8,128)(2,1)S(1)}, bf16[128,1024]{1,0:T(8,128)(2,1)S(1)}, u32[]{:S(2)}, u32[]{:S(2)}) collective-permute-start(bf16[128,1024]{1,0:T(8,128)(2,1)S(1)} %collective-permute-done.6.refs_4_), channel_id=1, source_target_pairs={{0,4},{4,8},{8,12},{12,0},{1,5},{5,9},{9,13},{13,1},{2,6},{6,10},{... | collective-permute-start | bytes 786440 | tf_op jit(solution)/shard_map/ppermute | solution.py:125
  17.3 7.1 %collective-permute-start.7 = (bf16[128,1024]{1,0:T(8,128)(2,1)S(1)}, bf16[128,1024]{1,0:T(8,128)(2,1)S(1)}, u32[]{:S(2)}, u32[]{:S(2)}) collective-permute-start(bf16[128,1024]{1,0:T(8,128)(2,1)S(1)} %collective-permute-done.6.refs_4_), channel_id=1, source_target_pairs={{0,1},{1,0},{2,3},{3,2},{4,5},{5,4},{6,7},{7,6},{8,9},{9,8},{10,11... | collective-permute-start | bytes 786440 | tf_op jit(solution)/shard_map/ppermute | solution.py:125
  18.8 5.6 %collective-permute-start.5 = (f32[32,128]{1,0:T(8,128)S(1)}, f32[32,128]{1,0:T(8,128)S(1)}, u32[]{:S(2)}, u32[]{:S(2)}) collective-permute-start(f32[32,128]{1,0:T(8,128)S(1)} %pad_maximum_fusion), channel_id=1, source_target_pairs={{0,8},{4,12},{8,0},{12,4},{1,9},{5,13},{9,1},{13,5},{2,10},{6,14},... | collective-permute-start | bytes 49160 | tf_op jit(solution)/shard_map/ppermute | solution.py:125
  23.5 12.0 %collective-permute-start.11 = (bf16[128,1024]{1,0:T(8,128)(2,1)S(1)}, bf16[128,1024]{1,0:T(8,128)(2,1)S(1)}, u32[]{:S(2)}, u32[]{:S(2)}) collective-permute-start(bf16[128,1024]{1,0:T(8,128)(2,1)S(1)} %collective-permute-done.8.refs_5_), channel_id=1, source_target_pairs={{0,1},{1,0},{2,3},{3,2},{4,5},{5,4},{6,7},{7,6},{8,9},{9,8},{10,11... | collective-permute-start | bytes 786440 | tf_op jit(solution)/shard_map/ppermute | solution.py:125
  24.1 8.7 %collective-permute-start.9 = (bf16[128,1024]{1,0:T(8,128)(2,1)S(1)}, bf16[128,1024]{1,0:T(8,128)(2,1)S(1)}, u32[]{:S(2)}, u32[]{:S(2)}) collective-permute-start(bf16[128,1024]{1,0:T(8,128)(2,1)S(1)} %collective-permute-done.8.refs_5_), channel_id=1, source_target_pairs={{0,4},{4,8},{8,12},{12,0},{1,5},{5,9},{9,13},{13,1},{2,6},{6,10},{... | collective-permute-start | bytes 786440 | tf_op jit(solution)/shard_map/ppermute | solution.py:125
  32.8 9.9 %collective-permute-start.12 = (bf16[128,1024]{1,0:T(8,128)(2,1)S(1)}, bf16[128,1024]{1,0:T(8,128)(2,1)S(1)}, u32[]{:S(2)}, u32[]{:S(2)}) collective-permute-start(bf16[128,1024]{1,0:T(8,128)(2,1)S(1)} %collective-permute-done.9.refs_3_), channel_id=1, source_target_pairs={{0,1},{1,0},{2,3},{3,2},{4,5},{5,4},{6,7},{7,6},{8,9},{9,8},{10,11... | collective-permute-start | bytes 786440 | tf_op jit(solution)/shard_map/ppermute | solution.py:125
  35.5 18.9 %collective-permute-start.10 = (bf16[256,1024]{1,0:T(8,128)(2,1)S(1)}, bf16[256,1024]{1,0:T(8,128)(2,1)S(1)}, u32[]{:S(2)}, u32[]{:S(2)}) collective-permute-start(bf16[256,1024]{1,0:T(8,128)(2,1)S(1)} %get-tuple-element.36.refs_1_), channel_id=1, source_target_pairs={{0,12},{4,0},{8,4},{12,8},{1,13},{5,1},{9,5},{13,9},{2,14},{6,2},{... | collective-permute-start | bytes 1572872 | tf_op jit(solution)/shard_map/ppermute | solution.py:125
  39.4 8.6 %collective-permute-start.14 = (bf16[128,1024]{1,0:T(8,128)(2,1)S(1)}, bf16[128,1024]{1,0:T(8,128)(2,1)S(1)}, u32[]{:S(2)}, u32[]{:S(2)}) collective-permute-start(bf16[128,1024]{1,0:T(8,128)(2,1)S(1)} %get-tuple-element.37.refs_1_), channel_id=1, source_target_pairs={{0,1},{1,0},{2,3},{3,2},{4,5},{5,4},{6,7},{7,6},{8,9},{9,8},{10,11... | collective-permute-start | bytes 786440 | tf_op jit(solution)/shard_map/ppermute | solution.py:125
  45.9 8.4 %collective-permute-start.13 = (bf16[128,1024]{1,0:T(8,128)(2,1)S(1)}, bf16[128,1024]{1,0:T(8,128)(2,1)S(1)}, u32[]{:S(2)}, u32[]{:S(2)}) collective-permute-start(bf16[128,1024]{1,0:T(8,128)(2,1)S(1)} %shard_map.59), channel_id=1, source_target_pairs={{0,1},{1,0},{2,3},{3,2},{4,5},{5,4},{6,7},{7,6},{8,9},{9,8},{10,11... | collective-permute-start | bytes 786440 | tf_op jit(solution)/shard_map/ppermute | solution.py:125
  48.1 15.0 %collective-permute-start.17 = (bf16[128,1024]{1,0:T(8,128)(2,1)S(1)}, bf16[128,1024]{1,0:T(8,128)(2,1)S(1)}, u32[]{:S(2)}, u32[]{:S(2)}) collective-permute-start(bf16[128,1024]{1,0:T(8,128)(2,1)S(1)} %add_convert_fusion.2), channel_id=1, source_target_pairs={{0,8},{4,12},{8,0},{12,4},{1,9},{5,13},{9,1},{13,5},{2,10},{6,14},... | collective-permute-start | bytes 786440 | tf_op jit(solution)/shard_map/ppermute | solution.py:125
  54.6 8.5 %collective-permute-start.16 = (bf16[128,1024]{1,0:T(8,128)(2,1)S(1)}, bf16[128,1024]{1,0:T(8,128)(2,1)S(1)}, u32[]{:S(2)}, u32[]{:S(2)}) collective-permute-start(bf16[128,1024]{1,0:T(8,128)(2,1)S(1)} %add_convert_fusion.1), channel_id=1, source_target_pairs={{0,4},{4,8},{8,12},{12,0},{1,5},{5,9},{9,13},{13,1},{2,6},{6,10},{... | collective-permute-start | bytes 786440 | tf_op jit(solution)/shard_map/ppermute | solution.py:125
  54.7 8.4 %collective-permute-start.15 = (bf16[128,1024]{1,0:T(8,128)(2,1)S(1)}, bf16[128,1024]{1,0:T(8,128)(2,1)S(1)}, u32[]{:S(2)}, u32[]{:S(2)}) collective-permute-start(bf16[128,1024]{1,0:T(8,128)(2,1)S(1)} %get-tuple-element.46), channel_id=1, source_target_pairs={{0,1},{1,0},{2,3},{3,2},{4,5},{5,4},{6,7},{7,6},{8,9},{9,8},{10,11... | collective-permute-start | bytes 786440 | tf_op jit(solution)/shard_map/ppermute | solution.py:125

commit v17 on v16

--- a/solution.py
+++ b/solution.py
@@ -144,12 +144,9 @@
     weight = jnp.sum(
         jnp.where(routes.T[None] == ids[:, None, None], gates.T[None], 0.0), axis=1
     )
-    near = [weight] + [follow(shift(weight, "sub", s), tables[0]) for s in range(1, subs)]
+    near = [weight] + [follow(shift(weight, "sub", s), ring[1]) for s in range(1, subs)]
     near = jnp.concatenate(near, axis=0)
-    weights, held = [near], near
-    while 2 ** len(weights) < 2 * depth:
-        weights.append(shift(held, "z", 2 ** (len(weights) - 1)))
-        held = jnp.concatenate([held, weights[-1]], axis=0)
+    weights = [near]
     last = depth - 1
     kept, others = {}, {}
     totals = {}
@@ -178,6 +175,12 @@
         arrived = handed + [ring[r] for r in fresh]
         partial = run_experts(after, weights, sources, arrived, tables, kinds, slots)
         firsts.append(partial[0])
+        if j == 0:
+            held = near
+            while 2 ** len(weights) < 2 * depth:
+                moved = shift(held, "z", 2 ** (len(weights) - 1))
+                weights.append(follow(moved, partial[0]))
+                held = jnp.concatenate([held, weights[-1]], axis=0)
         if j + 2 < depth:
             ring.append(follow(shift(ring[-1], "z", 1), partial[0]))
         if j == 1:

time: 64.2 us -> 64.4 us (level)
  waiting for transfers between devices: 23.6 us -> 26.3 us
  starting transfers between devices: 18.3 us -> 15.8 us
    ppermute x18, waiting for transfers between devices: 23.6 us -> 26.3 us  [shift(): lax.ppermute(array, axis, [(i, (i + step) % size) for i in range(size)])]
    ppermute x18, starting transfers between devices: 18.3 us -> 15.8 us  [shift(): lax.ppermute(array, axis, [(i, (i + step) % size) for i in range(size)])]
where the time goes in v17:
time: 64.4 us; the launch traced here: 64.2 us
  waiting for transfers between devices  26.3 us (41%)
  Pallas kernels  16.5 us (26%)
  starting transfers between devices  15.8 us (25%)
  local copies, waits for them, and re-layouts  3.56 us (6%)
  other arithmetic  1.83 us (3%)
    ppermute x18, waiting for transfers between devices, shift(): lax.ppermute(array, axis, [(i, (i + step) % size) for i in range(size)])  26.3 us
    ppermute x18, starting transfers between devices, shift(): lax.ppermute(array, axis, [(i, (i + step) % size) for i in range(size)])  15.8 us
    pallas_call x4, Pallas kernels, run_experts(): pl.pallas_call(functools.partial(expert_kernel, block, slots, unit, numbe...  15.8 us
    unnamed x6, local copies, waits for them, and re-layouts  3.56 us
  transfers between devices with their start and end apart: 18, of which 7 were waited for; matrix products, arithmetic and copies ran while one was open for 2% of the time, Pallas kernels for 26%

profile of v17, /device:TPU:0, one launch (start us, length us, event | category | flops | bytes accessed | tf_op | source)
XLA Modules:
  0.0 64.2 jit_solution(8368506523893312675)
XLA Ops:
  0.0 0.5 collective-permute-start.3
  0.5 0.1 collective-permute-start.4
  0.5 3.0 %collective-permute-start.1 = (bf16[128,1024]{1,0:T(8,128)(2,1)}, bf16[128,1024]{1,0:T(8,128)(2,1)S(1)}, u32[]{:S(2)}, u32[]{:S(2)}) collective-permute-start(bf16[128,1024]{1,0:T(8,128)(2,1)} %refs_2_.1), channel_id=1, source_target_pairs={{0,4},{4,8},{8,12},{12,0},{1,5},{5,9},{9,13},{13,1},{2,6},{6,10},{... | collective-permute-start | bytes 786440 | tf_op jit(solution)/shard_map/ppermute | solution.py:125
  3.5 1.5 %collective-permute-start.2 = (bf16[128,1024]{1,0:T(8,128)(2,1)}, bf16[128,1024]{1,0:T(8,128)(2,1)S(1)}, u32[]{:S(2)}, u32[]{:S(2)}) collective-permute-start(bf16[128,1024]{1,0:T(8,128)(2,1)} %refs_2_.1), channel_id=1, source_target_pairs={{0,1},{1,0},{2,3},{3,2},{4,5},{5,4},{6,7},{7,6},{8,9},{9,8},{10,11... | collective-permute-start | bytes 786440 | tf_op jit(solution)/shard_map/ppermute | solution.py:125
  5.0 0.7 %select_reduce_fusion = f32[8,128]{1,0:T(8,128)S(1)} fusion(f32[4,128]{1,0:T(4,128)} %bitcast.8, s32[4,128]{1,0:T(4,128)} %bitcast.9), kind=kLoop, calls=%fused_computation.6 | loop fusion | flops 11264 | bytes 8192 | tf_op jit(solution)/shard_map/reduce_sum | solution.py:144
  5.7 0.5 collective-permute-start
  6.3 1.8 %copy-done = bf16[1,1024,1344]{1,2,0:T(8,128)(2,1)S(1)} copy-done((bf16[1,1024,1344]{1,2,0:T(8,128)(2,1)S(1)}, bf16[1,1024,1344]{1,2,0:T(8,128)(2,1)}, u32[]{:S(2)}) %copy-start) | copy-done | bytes 2752536
  8.1 1.8 %copy-done.1 = bf16[1,1024,1344]{1,2,0:T(8,128)(2,1)S(1)} copy-done((bf16[1,1024,1344]{1,2,0:T(8,128)(2,1)S(1)}, bf16[1,1024,1344]{1,2,0:T(8,128)(2,1)}, u32[]{:S(2)}) %copy-start.1) | copy-done | bytes 2752536
  9.8 0.7 %shard_map.55 = (bf16[1,1344,1024]{2,1,0:T(8,128)(2,1)S(1)}, bf16[1,1344,1024]{2,1,0:T(8,128)(2,1)S(1)}) custom-call(bf16[1,1344,1024]{2,1,0:T(8,128)(2,1)S(1)} %bitcast.5, bf16[1,1344,1024]{2,1,0:T(8,128)(2,1)S(1)} %bitcast.7), custom_call_target="tpu_custom_call" | custom-call | tf_op jit(solution)/shard_map/pallas_call | solution.py:28
  10.5 1.7 %collective-permute-done.1.refs_4_ = bf16[128,1024]{1,0:T(8,128)(2,1)S(1)} collective-permute-done((bf16[128,1024]{1,0:T(8,128)(2,1)}, bf16[128,1024]{1,0:T(8,128)(2,1)S(1)}, u32[]{:S(2)}, u32[]{:S(2)}) %collective-permute-start.1) | collective-permute-done | bytes 262176 | tf_op jit(solution)/shard_map/ppermute | solution.py:125
  12.2 0.0 collective-permute-start.8
  12.2 0.0 collective-permute-done
  12.2 1.5 %collective-permute-start.7 = (bf16[128,1024]{1,0:T(8,128)(2,1)S(1)}, bf16[128,1024]{1,0:T(8,128)(2,1)S(1)}, u32[]{:S(2)}, u32[]{:S(2)}) collective-permute-start(bf16[128,1024]{1,0:T(8,128)(2,1)S(1)} %collective-permute-done.1.refs_4_), channel_id=1, source_target_pairs={{0,1},{1,0},{2,3},{3,2},{4,5},{5,4},{6,7},{7,6},{8,9},{9,8},{10,11... | collective-permute-start | bytes 786440 | tf_op jit(solution)/shard_map/ppermute | solution.py:125
  13.7 0.0 collective-permute-done.2.refs_1_
  13.7 1.5 %collective-permute-start.5 = (f32[16,128]{1,0:T(8,128)S(1)}, f32[16,128]{1,0:T(8,128)S(1)}, u32[]{:S(2)}, u32[]{:S(2)}) collective-permute-start(f32[16,128]{1,0:T(8,128)S(1)} %pad_maximum_fusion.1.refs_0_), channel_id=1, source_target_pairs={{0,4},{4,8},{8,12},{12,0},{1,5},{5,9},{9,13},{13,1},{2,6},{6,10},{... | collective-permute-start | bytes 24584 | tf_op jit(solution)/shard_map/ppermute | solution.py:125
  15.3 0.0 collective-permute-done.3.refs_5_.refs_8_.refs_6_
  15.3 0.0 collective-permute-done.4.refs_6_.refs_9_.refs_7_
  15.3 3.8 %shard_map.56 = (bf16[128,1024]{1,0:T(8,128)(2,1)S(1)}, f32[128,1024]{1,0:T(8,128)S(1)}) custom-call(f32[16,128]{1,0:T(8,128)S(1)} %pad_maximum_fusion.1.refs_0_, bf16[128,1024]{1,0:T(8,128)(2,1)S(1)} %collective-permute-done.2.refs_1_, bf16[128,1024]{1,0:T(8,128)(2,1)S(1)} %copy-done.2, ...), custom_call_target="tpu_custom_call" | custom-call | flops 2315255808 | bytes 12320768 | tf_op jit(solution)/shard_map/pallas_call | solution.py:107
  19.1 2.8 %collective-permute-done.5.refs_0_ = f32[16,128]{1,0:T(8,128)S(1)} collective-permute-done((f32[16,128]{1,0:T(8,128)S(1)}, f32[16,128]{1,0:T(8,128)S(1)}, u32[]{:S(2)}, u32[]{:S(2)}) %collective-permute-start.5) | collective-permute-done | bytes 8224 | tf_op jit(solution)/shard_map/ppermute | solution.py:125
  21.9 0.2 collective-permute-start.6
  22.1 0.0 collective-permute-done.8.refs_5_
  22.1 1.1 %collective-permute-start.11 = (bf16[128,1024]{1,0:T(8,128)(2,1)S(1)}, bf16[128,1024]{1,0:T(8,128)(2,1)S(1)}, u32[]{:S(2)}, u32[]{:S(2)}) collective-permute-start(bf16[128,1024]{1,0:T(8,128)(2,1)S(1)} %collective-permute-done.8.refs_5_), channel_id=1, source_target_pairs={{0,1},{1,0},{2,3},{3,2},{4,5},{5,4},{6,7},{7,6},{8,9},{9,8},{10,11... | collective-permute-start | bytes 786440 | tf_op jit(solution)/shard_map/ppermute | solution.py:125
  23.2 0.4 collective-permute-start.9
  23.6 7.8 %collective-permute-done.6.refs_1_.refs_0_ = f32[32,128]{1,0:T(8,128)S(1)} collective-permute-done((f32[32,128]{1,0:T(8,128)S(1)}, f32[32,128]{1,0:T(8,128)S(1)}, u32[]{:S(2)}, u32[]{:S(2)}) %collective-permute-start.6) | collective-permute-done | bytes 16416 | tf_op jit(solution)/shard_map/ppermute | solution.py:125
  31.4 0.0 collective-permute-done.7.refs_3_
  31.4 4.9 %shard_map.57 = (bf16[256,1024]{1,0:T(8,128)(2,1)S(1)}, f32[128,1024]{1,0:T(8,128)S(1)}) custom-call(f32[16,128]{1,0:T(8,128)S(1)} %collective-permute-done.5.refs_0_, f32[32,128]{1,0:T(8,128)S(1)} %collective-permute-done.6.refs_1_.refs_0_, bf16[128,1024]{1,0:T(8,128)(2,1)S(1)} %get-tuple-element.34.refs_2_, ...), custom_call_target="tpu_custom_call" | custom-call | flops 3472883712 | bytes 12976128 | tf_op jit(solution)/shard_map/pallas_call | solution.py:107
  36.3 0.0 collective-permute-done.9.refs_3_
  36.3 1.1 %collective-permute-start.12 = (bf16[128,1024]{1,0:T(8,128)(2,1)S(1)}, bf16[128,1024]{1,0:T(8,128)(2,1)S(1)}, u32[]{:S(2)}, u32[]{:S(2)}) collective-permute-start(bf16[128,1024]{1,0:T(8,128)(2,1)S(1)} %collective-permute-done.9.refs_3_), channel_id=1, source_target_pairs={{0,1},{1,0},{2,3},{3,2},{4,5},{5,4},{6,7},{7,6},{8,9},{9,8},{10,11... | collective-permute-start | bytes 786440 | tf_op jit(solution)/shard_map/ppermute | solution.py:125
  37.4 0.0 collective-permute-start.10
  37.4 0.0 collective-permute-done.11.refs_2_
  37.4 3.8 %shard_map.58 = (bf16[128,1024]{1,0:T(8,128)(2,1)S(1)}, f32[128,1024]{1,0:T(8,128)S(1)}) custom-call(f32[32,128]{1,0:T(8,128)S(1)} %collective-permute-done.6.refs_1_.refs_0_, bf16[256,1024]{1,0:T(8,128)(2,1)S(1)} %get-tuple-element.40.refs_1_, bf16[128,1024]{1,0:T(8,128)(2,1)S(1)} %collective-permute-done.11.refs_2_, ...), custom_call_target="tpu_custom_call" | custom-call | flops 2315255808 | bytes 12320768 | tf_op jit(solution)/shard_map/pallas_call | solution.py:107
  41.3 1.1 %collective-permute-start.14 = (bf16[128,1024]{1,0:T(8,128)(2,1)S(1)}, bf16[128,1024]{1,0:T(8,128)(2,1)S(1)}, u32[]{:S(2)}, u32[]{:S(2)}) collective-permute-start(bf16[128,1024]{1,0:T(8,128)(2,1)S(1)} %get-tuple-element.41.refs_1_), channel_id=1, source_target_pairs={{0,1},{1,0},{2,3},{3,2},{4,5},{5,4},{6,7},{7,6},{8,9},{9,8},{10,11... | collective-permute-start | bytes 786440 | tf_op jit(solution)/shard_map/ppermute | solution.py:125
  42.3 2.5 %collective-permute-done.12.refs_2_ = bf16[128,1024]{1,0:T(8,128)(2,1)S(1)} collective-permute-done((bf16[128,1024]{1,0:T(8,128)(2,1)S(1)}, bf16[128,1024]{1,0:T(8,128)(2,1)S(1)}, u32[]{:S(2)}, u32[]{:S(2)}) %collective-permute-start.12) | collective-permute-done | bytes 262176 | tf_op jit(solution)/shard_map/ppermute | solution.py:125
  44.8 3.3 %shard_map.59 = bf16[128,1024]{1,0:T(8,128)(2,1)S(1)} custom-call(f32[32,128]{1,0:T(8,128)S(1)} %collective-permute-done.6.refs_1_.refs_0_, bf16[128,1024]{1,0:T(8,128)(2,1)S(1)} %get-tuple-element.41.refs_1_, bf16[128,1024]{1,0:T(8,128)(2,1)S(1)} %collective-permute-done.12.refs_2_, bf16[1,1344,1024]{2,1,0:T(8,128)(2,1)S(1)} %get-tuple-element.29.refs_3_.refs_6_.refs_4_, ...), custom_call_target="tpu_custom_call" | custom-call | flops 1157627904 | bytes 11665408 | tf_op jit(solution)/shard_map/pallas_call | solution.py:107
  48.0 1.1 %collective-permute-start.13 = (bf16[128,1024]{1,0:T(8,128)(2,1)S(1)}, bf16[128,1024]{1,0:T(8,128)(2,1)S(1)}, u32[]{:S(2)}, u32[]{:S(2)}) collective-permute-start(bf16[128,1024]{1,0:T(8,128)(2,1)S(1)} %shard_map.59), channel_id=1, source_target_pairs={{0,1},{1,0},{2,3},{3,2},{4,5},{5,4},{6,7},{7,6},{8,9},{9,8},{10,11... | collective-permute-start | bytes 786440 | tf_op jit(solution)/shard_map/ppermute | solution.py:125
  49.1 0.0 collective-permute-done.14
  49.1 0.1 add_convert_fusion.2
  49.2 0.1 collective-permute-start.17
  49.3 5.6 %collective-permute-done.13 = bf16[128,1024]{1,0:T(8,128)(2,1)S(1)} collective-permute-done((bf16[128,1024]{1,0:T(8,128)(2,1)S(1)}, bf16[128,1024]{1,0:T(8,128)(2,1)S(1)}, u32[]{:S(2)}, u32[]{:S(2)}) %collective-permute-start.13) | collective-permute-done | bytes 262176 | tf_op jit(solution)/shard_map/ppermute | solution.py:125
  54.9 0.0 collective-permute-done.10
  54.9 0.2 add_convert_fusion.3
  55.0 0.1 add_convert_fusion.1
  55.1 1.5 %collective-permute-start.16 = (bf16[128,1024]{1,0:T(8,128)(2,1)S(1)}, bf16[128,1024]{1,0:T(8,128)(2,1)S(1)}, u32[]{:S(2)}, u32[]{:S(2)}) collective-permute-start(bf16[128,1024]{1,0:T(8,128)(2,1)S(1)} %add_convert_fusion.1), channel_id=1, source_target_pairs={{0,4},{4,8},{8,12},{12,0},{1,5},{5,9},{9,13},{13,1},{2,6},{6,10},{... | collective-permute-start | bytes 786440 | tf_op jit(solution)/shard_map/ppermute | solution.py:125
  56.6 0.7 %collective-permute-start.15 = (bf16[128,1024]{1,0:T(8,128)(2,1)S(1)}, bf16[128,1024]{1,0:T(8,128)(2,1)S(1)}, u32[]{:S(2)}, u32[]{:S(2)}) collective-permute-start(bf16[128,1024]{1,0:T(8,128)(2,1)S(1)} %get-tuple-element.50), channel_id=1, source_target_pairs={{0,1},{1,0},{2,3},{3,2},{4,5},{5,4},{6,7},{7,6},{8,9},{9,8},{10,11... | collective-permute-start | bytes 786440 | tf_op jit(solution)/shard_map/ppermute | solution.py:125
  57.4 2.0 %collective-permute-done.17 = bf16[128,1024]{1,0:T(8,128)(2,1)S(1)} collective-permute-done((bf16[128,1024]{1,0:T(8,128)(2,1)S(1)}, bf16[128,1024]{1,0:T(8,128)(2,1)S(1)}, u32[]{:S(2)}, u32[]{:S(2)}) %collective-permute-start.17) | collective-permute-done | bytes 262176 | tf_op jit(solution)/shard_map/ppermute | solution.py:125
  59.4 3.9 %collective-permute-done.16 = bf16[128,1024]{1,0:T(8,128)(2,1)S(1)} collective-permute-done((bf16[128,1024]{1,0:T(8,128)(2,1)S(1)}, bf16[128,1024]{1,0:T(8,128)(2,1)S(1)}, u32[]{:S(2)}, u32[]{:S(2)}) %collective-permute-start.16) | collective-permute-done | bytes 262176 | tf_op jit(solution)/shard_map/ppermute | solution.py:125
  63.3 0.0 collective-permute-done.15
  63.3 0.9 %add_convert_fusion = bf16[128,1024]{1,0:T(8,128)(2,1)} fusion(bf16[128,1024]{1,0:T(8,128)(2,1)S(1)} %collective-permute-done.16, bf16[128,1024]{1,0:T(8,128)(2,1)S(1)} %collective-permute-done.17, f32[128,1024]{1,0:T(8,128)S(1)} %get-tuple-element.54, bf16[128,1024]{1,0:T(8,128)(2,1)S(1)} %collective-permute-done.15), kind=kLoop, calls=%fused_computation | loop fusion | flops 917504 | bytes 1572864 | tf_op jit(solution)/shard_map/convert_element_type | solution.py:218
  (6 shorter events, 0.0 us)
Async XLA Ops:
  0.0 15.3 %collective-permute-start.3 = (bf16[1,1344,1024]{2,1,0:T(8,128)(2,1)}, bf16[1,1344,1024]{2,1,0:T(8,128)(2,1)S(1)}, u32[]{:S(2)}, u32[]{:S(2)}) collective-permute-start(bf16[1,1344,1024]{2,1,0:T(8,128)(2,1)} %bitcast.4), channel_id=1, source_target_pairs={{0,2},{2,0},{1,3},{3,1},{4,6},{6,4},{5,7},{7,5},{8,10},{10,8},{9,1... | collective-permute-start | bytes 8257544 | tf_op jit(solution)/shard_map/ppermute | solution.py:125
  0.5 14.8 %collective-permute-start.4 = (bf16[1,1344,1024]{2,1,0:T(8,128)(2,1)}, bf16[1,1344,1024]{2,1,0:T(8,128)(2,1)S(1)}, u32[]{:S(2)}, u32[]{:S(2)}) collective-permute-start(bf16[1,1344,1024]{2,1,0:T(8,128)(2,1)} %bitcast.6), channel_id=1, source_target_pairs={{0,2},{2,0},{1,3},{3,1},{4,6},{6,4},{5,7},{7,5},{8,10},{10,8},{9,1... | collective-permute-start | bytes 8257544 | tf_op jit(solution)/shard_map/ppermute | solution.py:125
  0.5 11.7 %collective-permute-start.1 = (bf16[128,1024]{1,0:T(8,128)(2,1)}, bf16[128,1024]{1,0:T(8,128)(2,1)S(1)}, u32[]{:S(2)}, u32[]{:S(2)}) collective-permute-start(bf16[128,1024]{1,0:T(8,128)(2,1)} %refs_2_.1), channel_id=1, source_target_pairs={{0,4},{4,8},{8,12},{12,0},{1,5},{5,9},{9,13},{13,1},{2,6},{6,10},{... | collective-permute-start | bytes 786440 | tf_op jit(solution)/shard_map/ppermute | solution.py:125
  3.5 10.2 %collective-permute-start.2 = (bf16[128,1024]{1,0:T(8,128)(2,1)}, bf16[128,1024]{1,0:T(8,128)(2,1)S(1)}, u32[]{:S(2)}, u32[]{:S(2)}) collective-permute-start(bf16[128,1024]{1,0:T(8,128)(2,1)} %refs_2_.1), channel_id=1, source_target_pairs={{0,1},{1,0},{2,3},{3,2},{4,5},{5,4},{6,7},{7,6},{8,9},{9,8},{10,11... | collective-permute-start | bytes 786440 | tf_op jit(solution)/shard_map/ppermute | solution.py:125
  5.7 6.5 %collective-permute-start = (f32[8,128]{1,0:T(8,128)S(1)}, f32[8,128]{1,0:T(8,128)S(1)}, u32[]{:S(2)}, u32[]{:S(2)}) collective-permute-start(f32[8,128]{1,0:T(8,128)S(1)} %select_reduce_fusion), channel_id=1, source_target_pairs={{0,1},{1,0},{2,3},{3,2},{4,5},{5,4},{6,7},{7,6},{8,9},{9,8},{10,11... | collective-permute-start | bytes 12296 | tf_op jit(solution)/shard_map/ppermute | solution.py:125
  6.3 1.8 %copy-start = (bf16[1,1024,1344]{1,2,0:T(8,128)(2,1)S(1)}, bf16[1,1024,1344]{1,2,0:T(8,128)(2,1)}, u32[]{:S(2)}) copy-start(bf16[1,1024,1344]{1,2,0:T(8,128)(2,1)} %param.8) | copy-start | bytes 8257540
  8.0 1.8 %copy-start.1 = (bf16[1,1024,1344]{1,2,0:T(8,128)(2,1)S(1)}, bf16[1,1024,1344]{1,2,0:T(8,128)(2,1)}, u32[]{:S(2)}) copy-start(bf16[1,1024,1344]{1,2,0:T(8,128)(2,1)} %param.9) | copy-start | bytes 8257540
  9.8 5.4 %copy-start.2 = (bf16[128,1024]{1,0:T(8,128)(2,1)S(1)}, bf16[128,1024]{1,0:T(8,128)(2,1)}, u32[]{:S(2)}) copy-start(bf16[128,1024]{1,0:T(8,128)(2,1)} %refs_2_.1) | copy-start | bytes 786436
  12.2 9.8 %collective-permute-start.8 = (bf16[128,1024]{1,0:T(8,128)(2,1)S(1)}, bf16[128,1024]{1,0:T(8,128)(2,1)S(1)}, u32[]{:S(2)}, u32[]{:S(2)}) collective-permute-start(bf16[128,1024]{1,0:T(8,128)(2,1)S(1)} %collective-permute-done.1.refs_4_), channel_id=1, source_target_pairs={{0,4},{4,8},{8,12},{12,0},{1,5},{5,9},{9,13},{13,1},{2,6},{6,10},{... | collective-permute-start | bytes 786440 | tf_op jit(solution)/shard_map/ppermute | solution.py:125
  12.2 19.2 %collective-permute-start.7 = (bf16[128,1024]{1,0:T(8,128)(2,1)S(1)}, bf16[128,1024]{1,0:T(8,128)(2,1)S(1)}, u32[]{:S(2)}, u32[]{:S(2)}) collective-permute-start(bf16[128,1024]{1,0:T(8,128)(2,1)S(1)} %collective-permute-done.1.refs_4_), channel_id=1, source_target_pairs={{0,1},{1,0},{2,3},{3,2},{4,5},{5,4},{6,7},{7,6},{8,9},{9,8},{10,11... | collective-permute-start | bytes 786440 | tf_op jit(solution)/shard_map/ppermute | solution.py:125
  13.7 8.1 %collective-permute-start.5 = (f32[16,128]{1,0:T(8,128)S(1)}, f32[16,128]{1,0:T(8,128)S(1)}, u32[]{:S(2)}, u32[]{:S(2)}) collective-permute-start(f32[16,128]{1,0:T(8,128)S(1)} %pad_maximum_fusion.1.refs_0_), channel_id=1, source_target_pairs={{0,4},{4,8},{8,12},{12,0},{1,5},{5,9},{9,13},{13,1},{2,6},{6,10},{... | collective-permute-start | bytes 24584 | tf_op jit(solution)/shard_map/ppermute | solution.py:125
  21.9 9.5 %collective-permute-start.6 = (f32[32,128]{1,0:T(8,128)S(1)}, f32[32,128]{1,0:T(8,128)S(1)}, u32[]{:S(2)}, u32[]{:S(2)}) collective-permute-start(f32[32,128]{1,0:T(8,128)S(1)} %pad_maximum_fusion), channel_id=1, source_target_pairs={{0,8},{4,12},{8,0},{12,4},{1,9},{5,13},{9,1},{13,5},{2,10},{6,14},... | collective-permute-start | bytes 49160 | tf_op jit(solution)/shard_map/ppermute | solution.py:125
  22.1 15.4 %collective-permute-start.11 = (bf16[128,1024]{1,0:T(8,128)(2,1)S(1)}, bf16[128,1024]{1,0:T(8,128)(2,1)S(1)}, u32[]{:S(2)}, u32[]{:S(2)}) collective-permute-start(bf16[128,1024]{1,0:T(8,128)(2,1)S(1)} %collective-permute-done.8.refs_5_), channel_id=1, source_target_pairs={{0,1},{1,0},{2,3},{3,2},{4,5},{5,4},{6,7},{7,6},{8,9},{9,8},{10,11... | collective-permute-start | bytes 786440 | tf_op jit(solution)/shard_map/ppermute | solution.py:125
  23.2 13.1 %collective-permute-start.9 = (bf16[128,1024]{1,0:T(8,128)(2,1)S(1)}, bf16[128,1024]{1,0:T(8,128)(2,1)S(1)}, u32[]{:S(2)}, u32[]{:S(2)}) collective-permute-start(bf16[128,1024]{1,0:T(8,128)(2,1)S(1)} %collective-permute-done.8.refs_5_), channel_id=1, source_target_pairs={{0,4},{4,8},{8,12},{12,0},{1,5},{5,9},{9,13},{13,1},{2,6},{6,10},{... | collective-permute-start | bytes 786440 | tf_op jit(solution)/shard_map/ppermute | solution.py:125
  36.3 8.5 %collective-permute-start.12 = (bf16[128,1024]{1,0:T(8,128)(2,1)S(1)}, bf16[128,1024]{1,0:T(8,128)(2,1)S(1)}, u32[]{:S(2)}, u32[]{:S(2)}) collective-permute-start(bf16[128,1024]{1,0:T(8,128)(2,1)S(1)} %collective-permute-done.9.refs_3_), channel_id=1, source_target_pairs={{0,1},{1,0},{2,3},{3,2},{4,5},{5,4},{6,7},{7,6},{8,9},{9,8},{10,11... | collective-permute-start | bytes 786440 | tf_op jit(solution)/shard_map/ppermute | solution.py:125
  37.4 17.5 %collective-permute-start.10 = (bf16[256,1024]{1,0:T(8,128)(2,1)S(1)}, bf16[256,1024]{1,0:T(8,128)(2,1)S(1)}, u32[]{:S(2)}, u32[]{:S(2)}) collective-permute-start(bf16[256,1024]{1,0:T(8,128)(2,1)S(1)} %get-tuple-element.40.refs_1_), channel_id=1, source_target_pairs={{0,12},{4,0},{8,4},{12,8},{1,13},{5,1},{9,5},{13,9},{2,14},{6,2},{... | collective-permute-start | bytes 1572872 | tf_op jit(solution)/shard_map/ppermute | solution.py:125
  41.3 7.9 %collective-permute-start.14 = (bf16[128,1024]{1,0:T(8,128)(2,1)S(1)}, bf16[128,1024]{1,0:T(8,128)(2,1)S(1)}, u32[]{:S(2)}, u32[]{:S(2)}) collective-permute-start(bf16[128,1024]{1,0:T(8,128)(2,1)S(1)} %get-tuple-element.41.refs_1_), channel_id=1, source_target_pairs={{0,1},{1,0},{2,3},{3,2},{4,5},{5,4},{6,7},{7,6},{8,9},{9,8},{10,11... | collective-permute-start | bytes 786440 | tf_op jit(solution)/shard_map/ppermute | solution.py:125
  48.0 6.8 %collective-permute-start.13 = (bf16[128,1024]{1,0:T(8,128)(2,1)S(1)}, bf16[128,1024]{1,0:T(8,128)(2,1)S(1)}, u32[]{:S(2)}, u32[]{:S(2)}) collective-permute-start(bf16[128,1024]{1,0:T(8,128)(2,1)S(1)} %shard_map.59), channel_id=1, source_target_pairs={{0,1},{1,0},{2,3},{3,2},{4,5},{5,4},{6,7},{7,6},{8,9},{9,8},{10,11... | collective-permute-start | bytes 786440 | tf_op jit(solution)/shard_map/ppermute | solution.py:125
  49.2 10.2 %collective-permute-start.17 = (bf16[128,1024]{1,0:T(8,128)(2,1)S(1)}, bf16[128,1024]{1,0:T(8,128)(2,1)S(1)}, u32[]{:S(2)}, u32[]{:S(2)}) collective-permute-start(bf16[128,1024]{1,0:T(8,128)(2,1)S(1)} %add_convert_fusion.2), channel_id=1, source_target_pairs={{0,8},{4,12},{8,0},{12,4},{1,9},{5,13},{9,1},{13,5},{2,10},{6,14},... | collective-permute-start | bytes 786440 | tf_op jit(solution)/shard_map/ppermute | solution.py:125
  55.1 8.2 %collective-permute-start.16 = (bf16[128,1024]{1,0:T(8,128)(2,1)S(1)}, bf16[128,1024]{1,0:T(8,128)(2,1)S(1)}, u32[]{:S(2)}, u32[]{:S(2)}) collective-permute-start(bf16[128,1024]{1,0:T(8,128)(2,1)S(1)} %add_convert_fusion.1), channel_id=1, source_target_pairs={{0,4},{4,8},{8,12},{12,0},{1,5},{5,9},{9,13},{13,1},{2,6},{6,10},{... | collective-permute-start | bytes 786440 | tf_op jit(solution)/shard_map/ppermute | solution.py:125
  56.6 6.7 %collective-permute-start.15 = (bf16[128,1024]{1,0:T(8,128)(2,1)S(1)}, bf16[128,1024]{1,0:T(8,128)(2,1)S(1)}, u32[]{:S(2)}, u32[]{:S(2)}) collective-permute-start(bf16[128,1024]{1,0:T(8,128)(2,1)S(1)} %get-tuple-element.50), channel_id=1, source_target_pairs={{0,1},{1,0},{2,3},{3,2},{4,5},{5,4},{6,7},{7,6},{8,9},{9,8},{10,11... | collective-permute-start | bytes 786440 | tf_op jit(solution)/shard_map/ppermute | solution.py:125

commit v18 on v17

--- a/solution.py
+++ b/solution.py
@@ -171,6 +171,9 @@
         if j > 3:
             totals[j - 2] = total(j - 2, firsts[-1]).astype(jnp.bfloat16)
             after = after + [totals[j - 2]]
+        if j == 1 and depth > 3:
+            ring.append(follow(shift(ring[-1], "z", 1), firsts[-1]))
+            after = after + [ring[-1]]
         sources = [(j, s) for s in range(1, subs)] + [(r, 0) for r in fresh]
         arrived = handed + [ring[r] for r in fresh]
         partial = run_experts(after, weights, sources, arrived, tables, kinds, slots)
@@ -181,7 +184,7 @@
                 moved = shift(held, "z", 2 ** (len(weights) - 1))
                 weights.append(follow(moved, partial[0]))
                 held = jnp.concatenate([held, weights[-1]], axis=0)
-        if j + 2 < depth:
+        if len(ring) == j + 2 < depth:
             ring.append(follow(shift(ring[-1], "z", 1), partial[0]))
         if j == 1:
             joint, *partial = partial

time: 64.4 us -> 69.9 us (1.085)
  waiting for transfers between devices: 26.3 us -> 32 us
    ppermute x18, waiting for transfers between devices: 26.3 us -> 32 us  [shift(): lax.ppermute(array, axis, [(i, (i + step) % size) for i in range(size)])]
  transfers between devices with their start and end apart: 18 -> 18, of which waited for: 7 -> 7; matrix products, arithmetic and copies ran while one was open for 2% -> 1% of each run, Pallas kernels for 26% -> 24%
where the time goes in v18:
time: 69.9 us; the launch traced here: 69.7 us
  waiting for transfers between devices  32 us (46%)
  Pallas kernels  16.5 us (24%)
  starting transfers between devices  15.6 us (22%)
  local copies, waits for them, and re-layouts  3.56 us (5%)
  other arithmetic  1.84 us (3%)
    ppermute x18, waiting for transfers between devices, shift(): lax.ppermute(array, axis, [(i, (i + step) % size) for i in range(size)])  32 us
    pallas_call x4, Pallas kernels, run_experts(): pl.pallas_call(functools.partial(expert_kernel, block, slots, unit, numbe...  15.8 us
    ppermute x18, starting transfers between devices, shift(): lax.ppermute(array, axis, [(i, (i + step) % size) for i in range(size)])  15.6 us
    unnamed x6, local copies, waits for them, and re-layouts  3.56 us
  transfers between devices with their start and end apart: 18, of which 7 were waited for; matrix products, arithmetic and copies ran while one was open for 1% of the time, Pallas kernels for 24%

profile of v18, /device:TPU:0, one launch (start us, length us, event | category | flops | bytes accessed | tf_op | source)
XLA Modules:
  0.0 69.7 jit_solution(11910528258094746641)
XLA Ops:
  0.0 0.5 collective-permute-start.3
  0.5 0.1 collective-permute-start.4
  0.5 3.0 %collective-permute-start.1 = (bf16[128,1024]{1,0:T(8,128)(2,1)}, bf16[128,1024]{1,0:T(8,128)(2,1)S(1)}, u32[]{:S(2)}, u32[]{:S(2)}) collective-permute-start(bf16[128,1024]{1,0:T(8,128)(2,1)} %refs_2_.1), channel_id=1, source_target_pairs={{0,4},{4,8},{8,12},{12,0},{1,5},{5,9},{9,13},{13,1},{2,6},{6,10},{... | collective-permute-start | bytes 786440 | tf_op jit(solution)/shard_map/ppermute | solution.py:125
  3.5 1.5 %collective-permute-start.2 = (bf16[128,1024]{1,0:T(8,128)(2,1)}, bf16[128,1024]{1,0:T(8,128)(2,1)S(1)}, u32[]{:S(2)}, u32[]{:S(2)}) collective-permute-start(bf16[128,1024]{1,0:T(8,128)(2,1)} %refs_2_.1), channel_id=1, source_target_pairs={{0,1},{1,0},{2,3},{3,2},{4,5},{5,4},{6,7},{7,6},{8,9},{9,8},{10,11... | collective-permute-start | bytes 786440 | tf_op jit(solution)/shard_map/ppermute | solution.py:125
  5.0 0.7 %select_reduce_fusion = f32[8,128]{1,0:T(8,128)S(1)} fusion(f32[4,128]{1,0:T(4,128)} %bitcast.8, s32[4,128]{1,0:T(4,128)} %bitcast.9), kind=kLoop, calls=%fused_computation.6 | loop fusion | flops 11264 | bytes 8192 | tf_op jit(solution)/shard_map/reduce_sum | solution.py:144
  5.7 0.5 collective-permute-start
  6.3 1.8 %copy-done = bf16[1,1024,1344]{1,2,0:T(8,128)(2,1)S(1)} copy-done((bf16[1,1024,1344]{1,2,0:T(8,128)(2,1)S(1)}, bf16[1,1024,1344]{1,2,0:T(8,128)(2,1)}, u32[]{:S(2)}) %copy-start) | copy-done | bytes 2752536
  8.1 1.8 %copy-done.1 = bf16[1,1024,1344]{1,2,0:T(8,128)(2,1)S(1)} copy-done((bf16[1,1024,1344]{1,2,0:T(8,128)(2,1)S(1)}, bf16[1,1024,1344]{1,2,0:T(8,128)(2,1)}, u32[]{:S(2)}) %copy-start.1) | copy-done | bytes 2752536
  9.8 0.7 %shard_map.55 = (bf16[1,1344,1024]{2,1,0:T(8,128)(2,1)S(1)}, bf16[1,1344,1024]{2,1,0:T(8,128)(2,1)S(1)}) custom-call(bf16[1,1344,1024]{2,1,0:T(8,128)(2,1)S(1)} %bitcast.5, bf16[1,1344,1024]{2,1,0:T(8,128)(2,1)S(1)} %bitcast.7), custom_call_target="tpu_custom_call" | custom-call | tf_op jit(solution)/shard_map/pallas_call | solution.py:28
  10.5 1.7 %collective-permute-done.1.refs_5_ = bf16[128,1024]{1,0:T(8,128)(2,1)S(1)} collective-permute-done((bf16[128,1024]{1,0:T(8,128)(2,1)}, bf16[128,1024]{1,0:T(8,128)(2,1)S(1)}, u32[]{:S(2)}, u32[]{:S(2)}) %collective-permute-start.1) | collective-permute-done | bytes 262176 | tf_op jit(solution)/shard_map/ppermute | solution.py:125
  12.2 0.0 collective-permute-start.7
  12.2 0.0 collective-permute-done
  12.3 0.0 collective-permute-done.2.refs_1_
  12.3 0.0 collective-permute-done.3.refs_5_.refs_9_.refs_6_
  12.3 0.0 collective-permute-done.4.refs_6_.refs_10_.refs_7_
  12.3 3.8 %shard_map.56 = (bf16[128,1024]{1,0:T(8,128)(2,1)S(1)}, f32[128,1024]{1,0:T(8,128)S(1)}) custom-call(f32[16,128]{1,0:T(8,128)S(1)} %pad_maximum_fusion.1.refs_0_, bf16[128,1024]{1,0:T(8,128)(2,1)S(1)} %collective-permute-done.2.refs_1_, bf16[128,1024]{1,0:T(8,128)(2,1)S(1)} %copy-done.2, ...), custom_call_target="tpu_custom_call" | custom-call | flops 2315255808 | bytes 12320768 | tf_op jit(solution)/shard_map/pallas_call | solution.py:107
  16.1 5.6 %collective-permute-done.7.refs_6_ = bf16[128,1024]{1,0:T(8,128)(2,1)S(1)} collective-permute-done((bf16[128,1024]{1,0:T(8,128)(2,1)S(1)}, bf16[128,1024]{1,0:T(8,128)(2,1)S(1)}, u32[]{:S(2)}, u32[]{:S(2)}) %collective-permute-start.7) | collective-permute-done | bytes 262176 | tf_op jit(solution)/shard_map/ppermute | solution.py:125
  21.7 0.0 collective-permute-start.8
  21.7 1.2 %collective-permute-start.9 = (bf16[128,1024]{1,0:T(8,128)(2,1)S(1)}, bf16[128,1024]{1,0:T(8,128)(2,1)S(1)}, u32[]{:S(2)}, u32[]{:S(2)}) collective-permute-start(bf16[128,1024]{1,0:T(8,128)(2,1)S(1)} %collective-permute-done.1.refs_5_), channel_id=1, source_target_pairs={{0,1},{1,0},{2,3},{3,2},{4,5},{5,4},{6,7},{7,6},{8,9},{9,8},{10,11... | collective-permute-start | bytes 786440 | tf_op jit(solution)/shard_map/ppermute | solution.py:125
  23.0 0.0 collective-permute-start.5
  23.0 7.7 %collective-permute-done.5.refs_0_ = f32[16,128]{1,0:T(8,128)S(1)} collective-permute-done((f32[16,128]{1,0:T(8,128)S(1)}, f32[16,128]{1,0:T(8,128)S(1)}, u32[]{:S(2)}, u32[]{:S(2)}) %collective-permute-start.5) | collective-permute-done | bytes 8224 | tf_op jit(solution)/shard_map/ppermute | solution.py:125
  30.6 0.0 collective-permute-start.6
  30.6 1.0 %collective-permute-start.11 = (bf16[128,1024]{1,0:T(8,128)(2,1)S(1)}, bf16[128,1024]{1,0:T(8,128)(2,1)S(1)}, u32[]{:S(2)}, u32[]{:S(2)}) collective-permute-start(bf16[128,1024]{1,0:T(8,128)(2,1)S(1)} %collective-permute-done.7.refs_6_), channel_id=1, source_target_pairs={{0,1},{1,0},{2,3},{3,2},{4,5},{5,4},{6,7},{7,6},{8,9},{9,8},{10,11... | collective-permute-start | bytes 786440 | tf_op jit(solution)/shard_map/ppermute | solution.py:125
  31.6 3.6 %collective-permute-done.6.refs_1_.refs_0_ = f32[32,128]{1,0:T(8,128)S(1)} collective-permute-done((f32[32,128]{1,0:T(8,128)S(1)}, f32[32,128]{1,0:T(8,128)S(1)}, u32[]{:S(2)}, u32[]{:S(2)}) %collective-permute-start.6) | collective-permute-done | bytes 16416 | tf_op jit(solution)/shard_map/ppermute | solution.py:125
  35.3 0.0 collective-permute-done.8.refs_3_
  35.3 1.0 %collective-permute-start.12 = (bf16[128,1024]{1,0:T(8,128)(2,1)S(1)}, bf16[128,1024]{1,0:T(8,128)(2,1)S(1)}, u32[]{:S(2)}, u32[]{:S(2)}) collective-permute-start(bf16[128,1024]{1,0:T(8,128)(2,1)S(1)} %collective-permute-done.8.refs_3_), channel_id=1, source_target_pairs={{0,1},{1,0},{2,3},{3,2},{4,5},{5,4},{6,7},{7,6},{8,9},{9,8},{10,11... | collective-permute-start | bytes 786440 | tf_op jit(solution)/shard_map/ppermute | solution.py:125
  36.3 0.0 collective-permute-done.9.refs_4_
  36.3 4.9 %shard_map.57 = (bf16[256,1024]{1,0:T(8,128)(2,1)S(1)}, f32[128,1024]{1,0:T(8,128)S(1)}) custom-call(f32[16,128]{1,0:T(8,128)S(1)} %collective-permute-done.5.refs_0_, f32[32,128]{1,0:T(8,128)S(1)} %collective-permute-done.6.refs_1_.refs_0_, bf16[128,1024]{1,0:T(8,128)(2,1)S(1)} %get-tuple-element.34.refs_2_, ...), custom_call_target="tpu_custom_call" | custom-call | flops 3472883712 | bytes 12976128 | tf_op jit(solution)/shard_map/pallas_call | solution.py:107
  41.2 0.2 collective-permute-start.10
  41.4 0.0 collective-permute-done.11.refs_2_
  41.4 3.8 %shard_map.58 = (bf16[128,1024]{1,0:T(8,128)(2,1)S(1)}, f32[128,1024]{1,0:T(8,128)S(1)}) custom-call(f32[32,128]{1,0:T(8,128)S(1)} %collective-permute-done.6.refs_1_.refs_0_, bf16[256,1024]{1,0:T(8,128)(2,1)S(1)} %get-tuple-element.40.refs_1_, bf16[128,1024]{1,0:T(8,128)(2,1)S(1)} %collective-permute-done.11.refs_2_, ...), custom_call_target="tpu_custom_call" | custom-call | flops 2315255808 | bytes 12320768 | tf_op jit(solution)/shard_map/pallas_call | solution.py:107
  45.3 1.1 %collective-permute-start.14 = (bf16[128,1024]{1,0:T(8,128)(2,1)S(1)}, bf16[128,1024]{1,0:T(8,128)(2,1)S(1)}, u32[]{:S(2)}, u32[]{:S(2)}) collective-permute-start(bf16[128,1024]{1,0:T(8,128)(2,1)S(1)} %get-tuple-element.41.refs_1_), channel_id=1, source_target_pairs={{0,1},{1,0},{2,3},{3,2},{4,5},{5,4},{6,7},{7,6},{8,9},{9,8},{10,11... | collective-permute-start | bytes 786440 | tf_op jit(solution)/shard_map/ppermute | solution.py:125
  46.4 0.0 collective-permute-done.12.refs_2_
  46.4 3.3 %shard_map.59 = bf16[128,1024]{1,0:T(8,128)(2,1)S(1)} custom-call(f32[32,128]{1,0:T(8,128)S(1)} %collective-permute-done.6.refs_1_.refs_0_, bf16[128,1024]{1,0:T(8,128)(2,1)S(1)} %get-tuple-element.41.refs_1_, bf16[128,1024]{1,0:T(8,128)(2,1)S(1)} %collective-permute-done.12.refs_2_, bf16[1,1344,1024]{2,1,0:T(8,128)(2,1)S(1)} %get-tuple-element.29.refs_3_.refs_7_.refs_4_, ...), custom_call_target="tpu_custom_call" | custom-call | flops 1157627904 | bytes 11665408 | tf_op jit(solution)/shard_map/pallas_call | solution.py:107
  49.6 1.1 %collective-permute-start.13 = (bf16[128,1024]{1,0:T(8,128)(2,1)S(1)}, bf16[128,1024]{1,0:T(8,128)(2,1)S(1)}, u32[]{:S(2)}, u32[]{:S(2)}) collective-permute-start(bf16[128,1024]{1,0:T(8,128)(2,1)S(1)} %shard_map.59), channel_id=1, source_target_pairs={{0,1},{1,0},{2,3},{3,2},{4,5},{5,4},{6,7},{7,6},{8,9},{9,8},{10,11... | collective-permute-start | bytes 786440 | tf_op jit(solution)/shard_map/ppermute | solution.py:125
  50.7 2.9 %collective-permute-done.14 = bf16[128,1024]{1,0:T(8,128)(2,1)S(1)} collective-permute-done((bf16[128,1024]{1,0:T(8,128)(2,1)S(1)}, bf16[128,1024]{1,0:T(8,128)(2,1)S(1)}, u32[]{:S(2)}, u32[]{:S(2)}) %collective-permute-start.14) | collective-permute-done | bytes 262176 | tf_op jit(solution)/shard_map/ppermute | solution.py:125
  53.6 0.1 add_convert_fusion.2
  53.7 0.3 collective-permute-start.17
  54.1 2.4 %collective-permute-done.13 = bf16[128,1024]{1,0:T(8,128)(2,1)S(1)} collective-permute-done((bf16[128,1024]{1,0:T(8,128)(2,1)S(1)}, bf16[128,1024]{1,0:T(8,128)(2,1)S(1)}, u32[]{:S(2)}, u32[]{:S(2)}) %collective-permute-start.13) | collective-permute-done | bytes 262176 | tf_op jit(solution)/shard_map/ppermute | solution.py:125
  56.5 0.0 collective-permute-done.10
  56.5 0.1 add_convert_fusion.3
  56.6 0.1 add_convert_fusion.1
  56.7 2.6 %collective-permute-start.16 = (bf16[128,1024]{1,0:T(8,128)(2,1)S(1)}, bf16[128,1024]{1,0:T(8,128)(2,1)S(1)}, u32[]{:S(2)}, u32[]{:S(2)}) collective-permute-start(bf16[128,1024]{1,0:T(8,128)(2,1)S(1)} %add_convert_fusion.1), channel_id=1, source_target_pairs={{0,4},{4,8},{8,12},{12,0},{1,5},{5,9},{9,13},{13,1},{2,6},{6,10},{... | collective-permute-start | bytes 786440 | tf_op jit(solution)/shard_map/ppermute | solution.py:125
  59.3 1.4 %collective-permute-start.15 = (bf16[128,1024]{1,0:T(8,128)(2,1)S(1)}, bf16[128,1024]{1,0:T(8,128)(2,1)S(1)}, u32[]{:S(2)}, u32[]{:S(2)}) collective-permute-start(bf16[128,1024]{1,0:T(8,128)(2,1)S(1)} %get-tuple-element.50), channel_id=1, source_target_pairs={{0,1},{1,0},{2,3},{3,2},{4,5},{5,4},{6,7},{7,6},{8,9},{9,8},{10,11... | collective-permute-start | bytes 786440 | tf_op jit(solution)/shard_map/ppermute | solution.py:125
  60.7 8.1 %collective-permute-done.17 = bf16[128,1024]{1,0:T(8,128)(2,1)S(1)} collective-permute-done((bf16[128,1024]{1,0:T(8,128)(2,1)S(1)}, bf16[128,1024]{1,0:T(8,128)(2,1)S(1)}, u32[]{:S(2)}, u32[]{:S(2)}) %collective-permute-start.17) | collective-permute-done | bytes 262176 | tf_op jit(solution)/shard_map/ppermute | solution.py:125
  68.8 0.0 collective-permute-done.16
  68.8 0.0 collective-permute-done.15
  68.8 0.9 %add_convert_fusion = bf16[128,1024]{1,0:T(8,128)(2,1)} fusion(bf16[128,1024]{1,0:T(8,128)(2,1)S(1)} %collective-permute-done.16, bf16[128,1024]{1,0:T(8,128)(2,1)S(1)} %collective-permute-done.17, f32[128,1024]{1,0:T(8,128)S(1)} %get-tuple-element.54, bf16[128,1024]{1,0:T(8,128)(2,1)S(1)} %collective-permute-done.15), kind=kLoop, calls=%fused_computation | loop fusion | flops 917504 | bytes 1572864 | tf_op jit(solution)/shard_map/convert_element_type | solution.py:221
  (6 shorter events, 0.0 us)
Async XLA Ops:
  0.0 12.3 %collective-permute-start.3 = (bf16[1,1344,1024]{2,1,0:T(8,128)(2,1)}, bf16[1,1344,1024]{2,1,0:T(8,128)(2,1)S(1)}, u32[]{:S(2)}, u32[]{:S(2)}) collective-permute-start(bf16[1,1344,1024]{2,1,0:T(8,128)(2,1)} %bitcast.4), channel_id=1, source_target_pairs={{0,2},{2,0},{1,3},{3,1},{4,6},{6,4},{5,7},{7,5},{8,10},{10,8},{9,1... | collective-permute-start | bytes 8257544 | tf_op jit(solution)/shard_map/ppermute | solution.py:125
  0.5 11.8 %collective-permute-start.4 = (bf16[1,1344,1024]{2,1,0:T(8,128)(2,1)}, bf16[1,1344,1024]{2,1,0:T(8,128)(2,1)S(1)}, u32[]{:S(2)}, u32[]{:S(2)}) collective-permute-start(bf16[1,1344,1024]{2,1,0:T(8,128)(2,1)} %bitcast.6), channel_id=1, source_target_pairs={{0,2},{2,0},{1,3},{3,1},{4,6},{6,4},{5,7},{7,5},{8,10},{10,8},{9,1... | collective-permute-start | bytes 8257544 | tf_op jit(solution)/shard_map/ppermute | solution.py:125
  0.5 11.7 %collective-permute-start.1 = (bf16[128,1024]{1,0:T(8,128)(2,1)}, bf16[128,1024]{1,0:T(8,128)(2,1)S(1)}, u32[]{:S(2)}, u32[]{:S(2)}) collective-permute-start(bf16[128,1024]{1,0:T(8,128)(2,1)} %refs_2_.1), channel_id=1, source_target_pairs={{0,4},{4,8},{8,12},{12,0},{1,5},{5,9},{9,13},{13,1},{2,6},{6,10},{... | collective-permute-start | bytes 786440 | tf_op jit(solution)/shard_map/ppermute | solution.py:125
  3.5 8.7 %collective-permute-start.2 = (bf16[128,1024]{1,0:T(8,128)(2,1)}, bf16[128,1024]{1,0:T(8,128)(2,1)S(1)}, u32[]{:S(2)}, u32[]{:S(2)}) collective-permute-start(bf16[128,1024]{1,0:T(8,128)(2,1)} %refs_2_.1), channel_id=1, source_target_pairs={{0,1},{1,0},{2,3},{3,2},{4,5},{5,4},{6,7},{7,6},{8,9},{9,8},{10,11... | collective-permute-start | bytes 786440 | tf_op jit(solution)/shard_map/ppermute | solution.py:125
  5.7 6.5 %collective-permute-start = (f32[8,128]{1,0:T(8,128)S(1)}, f32[8,128]{1,0:T(8,128)S(1)}, u32[]{:S(2)}, u32[]{:S(2)}) collective-permute-start(f32[8,128]{1,0:T(8,128)S(1)} %select_reduce_fusion), channel_id=1, source_target_pairs={{0,1},{1,0},{2,3},{3,2},{4,5},{5,4},{6,7},{7,6},{8,9},{9,8},{10,11... | collective-permute-start | bytes 12296 | tf_op jit(solution)/shard_map/ppermute | solution.py:125
  6.3 1.8 %copy-start = (bf16[1,1024,1344]{1,2,0:T(8,128)(2,1)S(1)}, bf16[1,1024,1344]{1,2,0:T(8,128)(2,1)}, u32[]{:S(2)}) copy-start(bf16[1,1024,1344]{1,2,0:T(8,128)(2,1)} %param.8) | copy-start | bytes 8257540
  8.0 1.8 %copy-start.1 = (bf16[1,1024,1344]{1,2,0:T(8,128)(2,1)S(1)}, bf16[1,1024,1344]{1,2,0:T(8,128)(2,1)}, u32[]{:S(2)}) copy-start(bf16[1,1024,1344]{1,2,0:T(8,128)(2,1)} %param.9) | copy-start | bytes 8257540
  9.8 2.5 %copy-start.2 = (bf16[128,1024]{1,0:T(8,128)(2,1)S(1)}, bf16[128,1024]{1,0:T(8,128)(2,1)}, u32[]{:S(2)}) copy-start(bf16[128,1024]{1,0:T(8,128)(2,1)} %refs_2_.1) | copy-start | bytes 786436
  12.2 9.5 %collective-permute-start.7 = (bf16[128,1024]{1,0:T(8,128)(2,1)S(1)}, bf16[128,1024]{1,0:T(8,128)(2,1)S(1)}, u32[]{:S(2)}, u32[]{:S(2)}) collective-permute-start(bf16[128,1024]{1,0:T(8,128)(2,1)S(1)} %collective-permute-done.1.refs_5_), channel_id=1, source_target_pairs={{0,4},{4,8},{8,12},{12,0},{1,5},{5,9},{9,13},{13,1},{2,6},{6,10},{... | collective-permute-start | bytes 786440 | tf_op jit(solution)/shard_map/ppermute | solution.py:125
  21.7 13.6 %collective-permute-start.8 = (bf16[128,1024]{1,0:T(8,128)(2,1)S(1)}, bf16[128,1024]{1,0:T(8,128)(2,1)S(1)}, u32[]{:S(2)}, u32[]{:S(2)}) collective-permute-start(bf16[128,1024]{1,0:T(8,128)(2,1)S(1)} %collective-permute-done.7.refs_6_), channel_id=1, source_target_pairs={{0,4},{4,8},{8,12},{12,0},{1,5},{5,9},{9,13},{13,1},{2,6},{6,10},{... | collective-permute-start | bytes 786440 | tf_op jit(solution)/shard_map/ppermute | solution.py:125
  21.7 14.6 %collective-permute-start.9 = (bf16[128,1024]{1,0:T(8,128)(2,1)S(1)}, bf16[128,1024]{1,0:T(8,128)(2,1)S(1)}, u32[]{:S(2)}, u32[]{:S(2)}) collective-permute-start(bf16[128,1024]{1,0:T(8,128)(2,1)S(1)} %collective-permute-done.1.refs_5_), channel_id=1, source_target_pairs={{0,1},{1,0},{2,3},{3,2},{4,5},{5,4},{6,7},{7,6},{8,9},{9,8},{10,11... | collective-permute-start | bytes 786440 | tf_op jit(solution)/shard_map/ppermute | solution.py:125
  23.0 7.7 %collective-permute-start.5 = (f32[16,128]{1,0:T(8,128)S(1)}, f32[16,128]{1,0:T(8,128)S(1)}, u32[]{:S(2)}, u32[]{:S(2)}) collective-permute-start(f32[16,128]{1,0:T(8,128)S(1)} %pad_maximum_fusion.1.refs_0_), channel_id=1, source_target_pairs={{0,4},{4,8},{8,12},{12,0},{1,5},{5,9},{9,13},{13,1},{2,6},{6,10},{... | collective-permute-start | bytes 24584 | tf_op jit(solution)/shard_map/ppermute | solution.py:125
  30.6 4.6 %collective-permute-start.6 = (f32[32,128]{1,0:T(8,128)S(1)}, f32[32,128]{1,0:T(8,128)S(1)}, u32[]{:S(2)}, u32[]{:S(2)}) collective-permute-start(f32[32,128]{1,0:T(8,128)S(1)} %pad_maximum_fusion), channel_id=1, source_target_pairs={{0,8},{4,12},{8,0},{12,4},{1,9},{5,13},{9,1},{13,5},{2,10},{6,14},... | collective-permute-start | bytes 49160 | tf_op jit(solution)/shard_map/ppermute | solution.py:125
  30.6 10.8 %collective-permute-start.11 = (bf16[128,1024]{1,0:T(8,128)(2,1)S(1)}, bf16[128,1024]{1,0:T(8,128)(2,1)S(1)}, u32[]{:S(2)}, u32[]{:S(2)}) collective-permute-start(bf16[128,1024]{1,0:T(8,128)(2,1)S(1)} %collective-permute-done.7.refs_6_), channel_id=1, source_target_pairs={{0,1},{1,0},{2,3},{3,2},{4,5},{5,4},{6,7},{7,6},{8,9},{9,8},{10,11... | collective-permute-start | bytes 786440 | tf_op jit(solution)/shard_map/ppermute | solution.py:125
  35.3 11.1 %collective-permute-start.12 = (bf16[128,1024]{1,0:T(8,128)(2,1)S(1)}, bf16[128,1024]{1,0:T(8,128)(2,1)S(1)}, u32[]{:S(2)}, u32[]{:S(2)}) collective-permute-start(bf16[128,1024]{1,0:T(8,128)(2,1)S(1)} %collective-permute-done.8.refs_3_), channel_id=1, source_target_pairs={{0,1},{1,0},{2,3},{3,2},{4,5},{5,4},{6,7},{7,6},{8,9},{9,8},{10,11... | collective-permute-start | bytes 786440 | tf_op jit(solution)/shard_map/ppermute | solution.py:125
  41.2 15.3 %collective-permute-start.10 = (bf16[256,1024]{1,0:T(8,128)(2,1)S(1)}, bf16[256,1024]{1,0:T(8,128)(2,1)S(1)}, u32[]{:S(2)}, u32[]{:S(2)}) collective-permute-start(bf16[256,1024]{1,0:T(8,128)(2,1)S(1)} %get-tuple-element.40.refs_1_), channel_id=1, source_target_pairs={{0,12},{4,0},{8,4},{12,8},{1,13},{5,1},{9,5},{13,9},{2,14},{6,2},{... | collective-permute-start | bytes 1572872 | tf_op jit(solution)/shard_map/ppermute | solution.py:125
  45.3 8.4 %collective-permute-start.14 = (bf16[128,1024]{1,0:T(8,128)(2,1)S(1)}, bf16[128,1024]{1,0:T(8,128)(2,1)S(1)}, u32[]{:S(2)}, u32[]{:S(2)}) collective-permute-start(bf16[128,1024]{1,0:T(8,128)(2,1)S(1)} %get-tuple-element.41.refs_1_), channel_id=1, source_target_pairs={{0,1},{1,0},{2,3},{3,2},{4,5},{5,4},{6,7},{7,6},{8,9},{9,8},{10,11... | collective-permute-start | bytes 786440 | tf_op jit(solution)/shard_map/ppermute | solution.py:125
  49.6 6.8 %collective-permute-start.13 = (bf16[128,1024]{1,0:T(8,128)(2,1)S(1)}, bf16[128,1024]{1,0:T(8,128)(2,1)S(1)}, u32[]{:S(2)}, u32[]{:S(2)}) collective-permute-start(bf16[128,1024]{1,0:T(8,128)(2,1)S(1)} %shard_map.59), channel_id=1, source_target_pairs={{0,1},{1,0},{2,3},{3,2},{4,5},{5,4},{6,7},{7,6},{8,9},{9,8},{10,11... | collective-permute-start | bytes 786440 | tf_op jit(solution)/shard_map/ppermute | solution.py:125
  53.7 15.1 %collective-permute-start.17 = (bf16[128,1024]{1,0:T(8,128)(2,1)S(1)}, bf16[128,1024]{1,0:T(8,128)(2,1)S(1)}, u32[]{:S(2)}, u32[]{:S(2)}) collective-permute-start(bf16[128,1024]{1,0:T(8,128)(2,1)S(1)} %add_convert_fusion.2), channel_id=1, source_target_pairs={{0,8},{4,12},{8,0},{12,4},{1,9},{5,13},{9,1},{13,5},{2,10},{6,14},... | collective-permute-start | bytes 786440 | tf_op jit(solution)/shard_map/ppermute | solution.py:125
  56.7 12.1 %collective-permute-start.16 = (bf16[128,1024]{1,0:T(8,128)(2,1)S(1)}, bf16[128,1024]{1,0:T(8,128)(2,1)S(1)}, u32[]{:S(2)}, u32[]{:S(2)}) collective-permute-start(bf16[128,1024]{1,0:T(8,128)(2,1)S(1)} %add_convert_fusion.1), channel_id=1, source_target_pairs={{0,4},{4,8},{8,12},{12,0},{1,5},{5,9},{9,13},{13,1},{2,6},{6,10},{... | collective-permute-start | bytes 786440 | tf_op jit(solution)/shard_map/ppermute | solution.py:125
  59.3 9.5 %collective-permute-start.15 = (bf16[128,1024]{1,0:T(8,128)(2,1)S(1)}, bf16[128,1024]{1,0:T(8,128)(2,1)S(1)}, u32[]{:S(2)}, u32[]{:S(2)}) collective-permute-start(bf16[128,1024]{1,0:T(8,128)(2,1)S(1)} %get-tuple-element.50), channel_id=1, source_target_pairs={{0,1},{1,0},{2,3},{3,2},{4,5},{5,4},{6,7},{7,6},{8,9},{9,8},{10,11... | collective-permute-start | bytes 786440 | tf_op jit(solution)/shard_map/ppermute | solution.py:125
